TPU v7x, 32 devices: a whole 2x2x4 slice. The times are simulated.
32 devices in a mesh: groups: 2 (over y), curve: 4 (over z), cross: 2 (over x), sub: 2 (over core).
Axes of the slice: x: 2, y: 2, z: 4, core: 2. Of those that a mesh axis runs over, the one named last changes fastest.
Arguments:
- node_features: bfloat16 [512, 8192], P('sub', ('groups', 'curve', 'cross')), parts along dimension 1, may hold values from -6 to 6
- inward_weight: bfloat16 [2, 512, 1024], P(None, 'sub'), may hold values from -0.1875 to 0.1875
- outward_weight: bfloat16 [2, 512, 512], P(None, 'sub'), may hold values from -0.25 to 0.25
- coarse_weight: bfloat16 [512, 512], P('sub'), may hold values from -0.25 to 0.25
- tile_index: int32 [64, 3], P(('groups', 'curve', 'cross')), parts along dimension 0, may hold values from 0 to 5, as said below
- tile_mask: int32 [64, 3, 128, 128], P(('groups', 'curve', 'cross')), parts along dimension 0, may hold values from 0 to 1, as said below
- send_rows: int32 [16, 2, 128], P(('groups', 'curve', 'cross')), parts along dimension 0, may hold values from 0 to 511, as said below
- parent: int32 [8192], P(('groups', 'curve', 'cross')), parts along dimension 0, may hold values from 0 to 1023, as said below
- cotangent: bfloat16 [512, 8192], P('sub', ('groups', 'curve', 'cross')), parts along dimension 1, may hold values from -6 to 6
Outputs:
- new_features: bfloat16 [512, 8192], P('sub', ('groups', 'curve', 'cross')), parts along dimension 1
- feature_grad: float32 [512, 8192], P('sub', ('groups', 'curve', 'cross')), parts along dimension 1
- grad_inward: float32 [4, 512, 1024], P('groups', 'sub', ('curve', 'cross')), parts along dimension 0
- grad_outward: float32 [4, 512, 512], P('groups', 'sub', ('curve', 'cross')), parts along dimension 0
- grad_coarse: float32 [1024, 512], P(('groups', 'sub'), ('curve', 'cross')), parts along dimension 0
There are 2 independent parts, one for each index of `groups`. A program takes and returns all parts, laid end to end along the dimension named above; an argument that names none is the same for every part. Nothing has to cross between parts.
Inputs may be any that keep to these rules, and one draw needn't show every extreme that they name: `tile_index`: slot 0 of block t names the block itself (t % 4), slot 1 the block before it, or 4 (the rows received from the previous domain) for a domain's first block; the 3 slots of a block name different sources. Values 4 and 5 stand for the rows received from the previous and the next domain. tile_mask[t, 0, r, r] is 1 for every block and row. `send_rows`: the 128 entries of one row are distinct; row 0 lies in the last 256 rows of a domain, row 1 in the first 256. Domain o owns coarse nodes o * 128 to (o + 1) * 128 - 1. The parent of a cell of domain p is owned by domain p, p - 1, p + 1, p - 2 or p + 2. At most 32 cells of domain p have parents owned by each of p - 2, p - 1, p + 1 and p + 2, and exactly 32 by p + 1 for every domain but the last.
All inputs are finite; a program needn't handle non-finite values.
Results may differ from a plain program's by a relative error of at most 0.0068.
Values may be sent and summed in bfloat16 or wider, within the bound.
No kernel may reach another device: no remote copies, remote signals or barrier semaphores. Data moves between devices by JAX's collectives and lax.ppermute only.
A program may use at most 64 MiB of HBM per device.

v0:
```python
import jax
import jax.numpy as jnp
from jax import lax
from jax.sharding import PartitionSpec as P


def shifted(value, axis, steps):
    count = lax.axis_size(axis)
    first, last = (max(0, -steps), min(count, count - steps))
    return lax.ppermute(value, axis, [(source, source + steps) for source in range(first, last)])


def silu_slope(preact):
    sigmoid_value = jax.nn.sigmoid(preact)
    return sigmoid_value * (1.0 + preact * (1.0 - sigmoid_value))


def gather_width(operand):
    return lax.all_gather(operand, "sub", axis=0, tiled=True)


def gather_pair(first_item, second_item):
    return (
        lax.all_gather(first_item, "sub", axis=0, tiled=True),
        lax.all_gather(second_item, "sub", axis=0, tiled=True),
    )


def neighbours(operand, step_by):
    return shifted(operand, ("curve", "cross"), step_by)


def carry(values, labels, step_by):
    moved_values, moved_labels = shifted((values, labels + 1), ("curve", "cross"), step_by)
    return (moved_values, (moved_labels - 1).astype(jnp.int32))


def deliver(pieces, labels):
    result = {}
    for offset in (1, -1, 2, -2):
        result[offset] = carry(pieces[offset], labels[offset], offset)
    return result


def reduce_grads(inward, outward, coarse_part):
    return (
        lax.psum_scatter(inward, ("curve", "cross"), scatter_dimension=2, tiled=True),
        lax.psum_scatter(outward, ("curve", "cross"), scatter_dimension=2, tiled=True),
        lax.psum_scatter(coarse_part, ("curve", "cross"), scatter_dimension=1, tiled=True),
    )


def local(
    node_features,
    inward_weight,
    outward_weight,
    coarse_weight,
    tile_index,
    tile_mask,
    send_rows,
    parent,
    cotangent,
):
    feature_width = node_features.shape[0]
    cell_rows = node_features.shape[1]
    block_count = tile_index.shape[0]
    block_len = tile_mask.shape[2]
    domain_count = lax.axis_size(("curve", "cross"))
    capacity = cell_rows // 16
    coarse_nodes = cell_rows // 4
    sub_index = lax.axis_index("sub")
    my_domain = lax.axis_index(("curve", "cross"))
    grad_scale = float(cell_rows * domain_count) ** (-0.5)
    tile_masks = tile_mask.astype(jnp.bfloat16)
    degree = jnp.sum(tile_mask, axis=(1, 3)).astype(jnp.float32)
    selector = (tile_index[:, :, None] == jnp.arange(block_count + 2)).astype(jnp.float32)
    next_rows = send_rows[0, 0]
    prev_rows = send_rows[0, 1]
    contract_cells = (((1,), (1,)), ((), ()))
    contract_hidden = (((0,), (0,)), ((), ()))
    offsets = (1, -1, 2, -2)

    def aggregate(features):
        before_rows = neighbours(jnp.take(features, next_rows, axis=1), 1)
        after_rows = neighbours(jnp.take(features, prev_rows, axis=1), -1)
        sources = jnp.concatenate([features, before_rows, after_rows], axis=1).reshape(
            feature_width, block_count + 2, block_len
        )
        picked = sources[:, tile_index, :]
        summed = jnp.einsum(
            "fbkc,bkrc->fbr", picked, tile_masks, preferred_element_type=jnp.float32
        )
        return (summed / degree[None]).astype(jnp.bfloat16).reshape(feature_width, cell_rows)

    def forward_layer(features, layer_id):
        aggregated = aggregate(features)
        features_full, aggregated_full = gather_pair(features, aggregated)
        model_width = features_full.shape[0]
        inward = inward_weight[layer_id]
        preact = jnp.dot(
            inward[:, :model_width], features_full, preferred_element_type=jnp.float32
        ) + jnp.dot(inward[:, model_width:], aggregated_full, preferred_element_type=jnp.float32)
        hidden_full = gather_width(jax.nn.silu(preact).astype(jnp.bfloat16))
        output = jnp.dot(outward_weight[layer_id], hidden_full, preferred_element_type=jnp.float32)
        updated = (features.astype(jnp.float32) + output).astype(jnp.bfloat16)
        return (updated, (features_full, aggregated_full, preact, hidden_full))

    def backward_layer(incoming, stored, layer_id):
        features_full, aggregated_full, preact, hidden_full = stored
        hidden_part = preact.shape[0]
        model_width = features_full.shape[0]
        inward_full, outward_full = gather_pair(inward_weight[layer_id], outward_weight[layer_id])
        incoming_full = gather_width(incoming)
        out_columns = lax.dynamic_slice_in_dim(
            outward_full, sub_index * hidden_part, hidden_part, 1
        )
        hidden_grad = lax.dot_general(
            out_columns, incoming_full, contract_hidden, preferred_element_type=jnp.float32
        )
        preact_grad = (hidden_grad * silu_slope(preact)).astype(jnp.bfloat16)
        grad_out = (
            lax.dot_general(
                incoming, hidden_full, contract_cells, preferred_element_type=jnp.float32
            )
            * grad_scale
        )
        grad_in = (
            jnp.concatenate(
                [
                    lax.dot_general(
                        preact_grad,
                        features_full,
                        contract_cells,
                        preferred_element_type=jnp.float32,
                    ),
                    lax.dot_general(
                        preact_grad,
                        aggregated_full,
                        contract_cells,
                        preferred_element_type=jnp.float32,
                    ),
                ],
                axis=1,
            )
            * grad_scale
        )
        preact_full = gather_width(preact_grad)
        feature_cols = lax.dynamic_slice_in_dim(
            inward_full, sub_index * feature_width, feature_width, 1
        )
        aggregated_cols = lax.dynamic_slice_in_dim(
            inward_full, model_width + sub_index * feature_width, feature_width, 1
        )
        direct_grad = lax.dot_general(
            feature_cols, preact_full, contract_hidden, preferred_element_type=jnp.float32
        )
        aggregated_grad = lax.dot_general(
            aggregated_cols, preact_full, contract_hidden, preferred_element_type=jnp.float32
        )
        scaled = (
            aggregated_grad.reshape(feature_width, block_count, block_len) / degree[None]
        ).astype(jnp.bfloat16)
        contrib = jnp.einsum(
            "fbr,bkrc->fbkc", scaled, tile_masks, preferred_element_type=jnp.float32
        )
        per_source = jnp.einsum("fbkc,bkj->fjc", contrib, selector, precision=lax.Precision.HIGHEST)
        from_after = neighbours(per_source[:, block_count].astype(jnp.bfloat16), -1)
        from_before = neighbours(per_source[:, block_count + 1].astype(jnp.bfloat16), 1)
        combined = (
            incoming.astype(jnp.float32)
            + direct_grad
            + per_source[:, :block_count].reshape(feature_width, cell_rows)
        )
        combined = combined.at[:, next_rows].add(from_after.astype(jnp.float32))
        combined = combined.at[:, prev_rows].add(from_before.astype(jnp.float32))
        return (combined, grad_in, grad_out)

    owner_of = parent // coarse_nodes
    node_of = parent % coarse_nodes
    offset_of = owner_of - my_domain
    node_range = jnp.arange(coarse_nodes)
    own_hot = ((offset_of == 0)[:, None] & (node_of[:, None] == node_range)).astype(jnp.bfloat16)
    own_count = jnp.sum(own_hot.astype(jnp.float32), axis=0)
    placings = {}
    slot_tags = {}
    for offset in offsets:
        chosen = (offset_of == offset).astype(jnp.int32)
        ranking = jnp.cumsum(chosen) - chosen
        fits = (chosen[:, None] == 1) & (ranking[:, None] == jnp.arange(capacity))
        placings[offset] = fits.astype(jnp.bfloat16)
        slot_tags[offset] = jnp.sum(fits.astype(jnp.int32) * (node_of[:, None] + 1), axis=0) - 1

    def to_slots(features):
        return {
            offset: jnp.dot(features, placings[offset], preferred_element_type=jnp.float32).astype(
                jnp.bfloat16
            )
            for offset in offsets
        }

    def pool(features, arrived, hits):
        total = jnp.dot(features, own_hot, preferred_element_type=jnp.float32)
        for offset in offsets:
            total = total + jnp.dot(
                arrived[offset][0], hits[offset], preferred_element_type=jnp.float32
            )
        return total

    def answers(values, hits):
        return {
            -offset: lax.dot_general(
                values, hits[offset], contract_cells, preferred_element_type=jnp.float32
            ).astype(jnp.bfloat16)
            for offset in offsets
        }

    def spread(values, returned):
        total = lax.dot_general(values, own_hot, contract_cells, preferred_element_type=jnp.float32)
        for offset in offsets:
            total = total + lax.dot_general(
                returned[-offset][0],
                placings[offset],
                contract_cells,
                preferred_element_type=jnp.float32,
            )
        return total

    first_out, first_stored = forward_layer(node_features, 0)
    arrived = deliver(to_slots(first_out), slot_tags)
    hits = {
        offset: (arrived[offset][1][:, None] == node_range).astype(jnp.bfloat16)
        for offset in offsets
    }
    back_tags = {-offset: arrived[offset][1] for offset in offsets}
    node_count = own_count
    for offset in offsets:
        node_count = node_count + jnp.sum(hits[offset].astype(jnp.float32), axis=0)
    node_count = jnp.maximum(node_count, 1.0)
    coarse = (pool(first_out, arrived, hits) / node_count[None]).astype(jnp.bfloat16)
    coarse_full = gather_width(coarse)
    coarse_pre = jnp.dot(coarse_weight, coarse_full, preferred_element_type=jnp.float32)
    correction = jax.nn.silu(coarse_pre).astype(jnp.bfloat16)
    returned = deliver(answers(correction, hits), back_tags)
    lifted = (first_out.astype(jnp.float32) + spread(correction, returned)).astype(jnp.bfloat16)
    final_out, second_stored = forward_layer(lifted, 1)
    second_grad, second_inward, second_outward = backward_layer(cotangent, second_stored, 1)
    lifted_grad = second_grad.astype(jnp.bfloat16)
    arrived_grad = deliver(to_slots(lifted_grad), slot_tags)
    correction_grad = pool(lifted_grad, arrived_grad, hits)
    pooled_grad = (correction_grad * silu_slope(coarse_pre)).astype(jnp.bfloat16)
    coarse_weights, pooled_full = gather_pair(coarse_weight, pooled_grad)
    weight_cols = lax.dynamic_slice_in_dim(
        coarse_weights, sub_index * feature_width, feature_width, 1
    )
    coarse_grad = lax.dot_general(
        weight_cols, pooled_full, contract_hidden, preferred_element_type=jnp.float32
    )
    spread_grad = (coarse_grad / node_count[None]).astype(jnp.bfloat16)
    weight_grad = (
        lax.dot_general(
            pooled_grad, coarse_full, contract_cells, preferred_element_type=jnp.float32
        )
        * grad_scale
    )
    returned_grad = deliver(answers(spread_grad, hits), back_tags)
    first_back = (lifted_grad.astype(jnp.float32) + spread(spread_grad, returned_grad)).astype(
        jnp.bfloat16
    )
    feature_grad, first_inward, first_outward = backward_layer(first_back, first_stored, 0)
    grad_inward, grad_outward, grad_coarse = reduce_grads(
        jnp.stack([first_inward, second_inward]),
        jnp.stack([first_outward, second_outward]),
        weight_grad,
    )
    return (final_out, feature_grad, grad_inward, grad_outward, grad_coarse)


def solution(mesh):
    in_specs = (
        P("sub", ("groups", "curve", "cross")),
        P(None, "sub", None),
        P(None, "sub", None),
        P("sub", None),
        P(("groups", "curve", "cross"), None),
        P(("groups", "curve", "cross"), None, None, None),
        P(("groups", "curve", "cross"), None, None),
        P(("groups", "curve", "cross")),
        P("sub", ("groups", "curve", "cross")),
    )
    out_specs = (
        P("sub", ("groups", "curve", "cross")),
        P("sub", ("groups", "curve", "cross")),
        P("groups", "sub", ("curve", "cross")),
        P("groups", "sub", ("curve", "cross")),
        P(("groups", "sub"), ("curve", "cross")),
    )
    return jax.shard_map(local, mesh=mesh, in_specs=in_specs, out_specs=out_specs, check_vma=False)
```

profile of v0, /device:TPU:0, one launch (start us, length us, event | category | flops | bytes accessed | tf_op | source)
XLA Modules:
  0.0 413.5 jit_solution(586925872455614781)
XLA Ops:
  7.2 2.5 fusion.189
  14.3 5.5 %collective-permute-start.3 = (s32[32]{0:T(128)}, s32[32]{0:T(128)}, u32[]{:S(2)}, u32[]{:S(2)}) collective-permute-start(s32[32]{0:T(128)} %get-tuple-element.29), channel_id=1, source_target_pairs={{0,2},{2,4},{4,6},{6,8},{8,10},{10,12},{12,14},{1,3},{3,5},{5,7},{... | collective-permute-start | bytes 392 | tf_op jit(solution)/shard_map/ppermute | solution.py:10
  21.6 3.5 collective-permute-start
  28.0 5.5 %collective-permute-start.7 = (s32[32]{0:T(128)}, s32[32]{0:T(128)}, u32[]{:S(2)}, u32[]{:S(2)}) collective-permute-start(s32[32]{0:T(128)} %get-tuple-element.27), channel_id=1, source_target_pairs={{0,4},{2,6},{4,8},{6,10},{8,12},{10,14},{1,5},{3,7},{5,9},{7,11},{... | collective-permute-start | bytes 392 | tf_op jit(solution)/shard_map/ppermute | solution.py:10
  34.9 2.2 all_gather.51
  40.5 2.3 all-gather.1
  42.8 2.7 all_gather.60
  45.5 2.3 all_gather.62
  52.0 2.6 collective-permute-done.5
  58.8 2.2 all_gather.52
  62.1 2.2 all_gather.53
  65.6 3.6 collective-permute-start.2
  69.4 4.4 %collective-permute-start.6 = (bf16[256,32]{0,1:T(8,128)(2,1)S(1)}, bf16[256,32]{0,1:T(8,128)(2,1)S(1)}, u32[]{:S(2)}, u32[]{:S(2)}) collective-permute-start(bf16[256,32]{0,1:T(8,128)(2,1)S(1)} %convolution_convert_fusion.13), channel_id=1, source_target_pairs={{0,4},{2,6},{4,8},{6,10},{8,12},{10,14},{1,5},{3,7},{5,9},{7,11},{... | collective-permute-start | bytes 49160 | tf_op jit(solution)/shard_map/ppermute | solution.py:10
  76.9 2.6 collective-permute-done.8
  81.0 1.9 all_gather.54
  87.5 6.7 %collective-permute-start.13 = (bf16[256,32]{0,1:T(8,128)(2,1)S(1)}, bf16[256,32]{0,1:T(8,128)(2,1)S(1)}, u32[]{:S(2)}, u32[]{:S(2)}) collective-permute-start(bf16[256,32]{0,1:T(8,128)(2,1)S(1)} %convolution_convert_fusion.8), channel_id=1, source_target_pairs={{0,4},{2,6},{4,8},{6,10},{8,12},{10,14},{1,5},{3,7},{5,9},{7,11},{... | collective-permute-start | bytes 49160 | tf_op jit(solution)/shard_map/ppermute | solution.py:10
  94.2 3.0 collective-permute-start.11
  101.0 2.2 all_gather.55
  103.3 4.4 %collective-permute-start.14 = (bf16[256,128]{0,1:T(8,128)(2,1)S(1)}, bf16[256,128]{0,1:T(8,128)(2,1)S(1)}, u32[]{:S(2)}, u32[]{:S(2)}) collective-permute-start(bf16[256,128]{0,1:T(8,128)(2,1)S(1)} %select_bitcast_fusion.1), channel_id=1, source_target_pairs={{0,2},{2,4},{4,6},{6,8},{8,10},{10,12},{12,14},{1,3},{3,5},{5,7},{... | collective-permute-start | bytes 196616 | tf_op jit(solution)/shard_map/ppermute | solution.py:10
  110.3 4.9 %collective-permute-done.15 = bf16[256,128]{0,1:T(8,128)(2,1)S(1)} collective-permute-done((bf16[256,128]{0,1:T(8,128)(2,1)S(1)}, bf16[256,128]{0,1:T(8,128)(2,1)S(1)}, u32[]{:S(2)}, u32[]{:S(2)}) %collective-permute-start.15) | collective-permute-done | bytes 65568 | tf_op jit(solution)/shard_map/ppermute | solution.py:10
  117.2 1.6 fusion.39
  118.8 2.2 all_gather.56
  122.8 2.3 all_gather.61
  125.1 2.4 all_gather.57
  130.9 2.6 fusion.194
  135.2 2.1 fusion.20
  138.6 5.4 %collective-permute-start.17 = (bf16[256,128]{1,0:T(8,128)(2,1)S(1)}, bf16[256,128]{1,0:T(8,128)(2,1)S(1)}, u32[]{:S(2)}, u32[]{:S(2)}) collective-permute-start(bf16[256,128]{1,0:T(8,128)(2,1)S(1)} %bitcast.291), channel_id=1, source_target_pairs={{0,2},{2,4},{4,6},{6,8},{8,10},{10,12},{12,14},{1,3},{3,5},{5,7},{... | collective-permute-start | bytes 196616 | tf_op jit(solution)/shard_map/ppermute | solution.py:10
  144.2 1.8 collective-permute-done.17
  146.1 1.6 scatter_fusion
  147.7 1.6 scatter_fusion.1
  150.6 4.8 %collective-permute-start.18 = (bf16[256,32]{0,1:T(8,128)(2,1)S(1)}, bf16[256,32]{0,1:T(8,128)(2,1)S(1)}, u32[]{:S(2)}, u32[]{:S(2)}) collective-permute-start(bf16[256,32]{0,1:T(8,128)(2,1)S(1)} %convolution_convert_fusion.7), channel_id=1, source_target_pairs={{0,2},{2,4},{4,6},{6,8},{8,10},{10,12},{12,14},{1,3},{3,5},{5,7},{... | collective-permute-start | bytes 49160 | tf_op jit(solution)/shard_map/ppermute | solution.py:10
  155.6 3.9 collective-permute-start.20
  162.8 2.4 collective-permute-done.21
  165.5 2.3 collective-permute-done.19
  168.0 1.9 all_gather.63
  174.0 7.5 %collective-permute-start.25 = (bf16[256,32]{0,1:T(8,128)(2,1)S(1)}, bf16[256,32]{0,1:T(8,128)(2,1)S(1)}, u32[]{:S(2)}, u32[]{:S(2)}) collective-permute-start(bf16[256,32]{0,1:T(8,128)(2,1)S(1)} %convolution_convert_fusion), channel_id=1, source_target_pairs={{0,4},{2,6},{4,8},{6,10},{8,12},{10,14},{1,5},{3,7},{5,9},{7,11},{... | collective-permute-start | bytes 49160 | tf_op jit(solution)/shard_map/ppermute | solution.py:10
  181.5 3.1 collective-permute-start.23
  188.9 2.4 all-gather.3
  194.2 2.2 all_gather.66
  198.3 1.5 pad_maximum_fusion
  202.9 2.4 all_gather.67
  207.2 2.6 fusion.195
  213.1 5.3 %collective-permute-start.27 = (bf16[256,128]{1,0:T(8,128)(2,1)S(1)}, bf16[256,128]{1,0:T(8,128)(2,1)S(1)}, u32[]{:S(2)}, u32[]{:S(2)}) collective-permute-start(bf16[256,128]{1,0:T(8,128)(2,1)S(1)} %bitcast.292), channel_id=1, source_target_pairs={{0,2},{2,4},{4,6},{6,8},{8,10},{10,12},{12,14},{1,3},{3,5},{5,7},{... | collective-permute-start | bytes 196616 | tf_op jit(solution)/shard_map/ppermute | solution.py:10
  218.5 2.8 collective-permute-done.27
  221.5 1.5 scatter_fusion.2
  225.5 44.6 %all-reduce.3.cloned.1.call-done = f32[2,256,512]{1,0,2:T(2,128)} async-done(((f32[2,256,512]{1,0,2:T(2,128)}), f32[2,256,512]{1,0,2:T(2,128)}) %all-reduce.3.cloned.1.call-update) | async-done | bytes 1048592
  271.6 64.1 %reduce-scatter.7.cloned.1.call-done = f32[64,256]{1,0:T(8,128)} async-done(((f32[512,256]{1,0:T(8,128)}), f32[64,256]{1,0:T(8,128)}) %reduce-scatter.7.cloned.1.call-update) | async-done | bytes 65552
  335.7 71.2 %reduce-scatter.5.cloned.1.call-done = f32[2,256,128]{2,1,0:T(8,128)} async-done(((f32[2,256,1024]{2,1,0:T(8,128)}), f32[2,256,128]{2,1,0:T(8,128)}) %reduce-scatter.5.cloned.1.call-update) | async-done | bytes 262160 | tf_op jit(solution)/shard_map/reduce_scatter | solution.py:47
  (366 shorter events, 80.0 us)
Async XLA Ops:
  7.2 121.4 %all-gather.7.cloned.1.call-start = ((), (), s32[]{:S(2)}) async-start(), calls=%async_computation.3 | async-start | bytes 1572864 | tf_op jit(solution)/shard_map/all_gather | solution.py:24
  9.8 195.5 %all-gather.9.cloned.1.call-start = ((), (), s32[]{:S(2)}) async-start(), calls=%async_computation.4 | async-start | bytes 1572864 | tf_op jit(solution)/shard_map/all_gather | solution.py:24
  14.3 22.8 %copy-start.55 = (s32[4,3]{1,0:T(4,128)S(1)}, s32[4,3]{1,0:T(4,128)}, u32[]{:S(2)}) copy-start(s32[4,3]{1,0:T(4,128)} %param.15) | copy-start | bytes 148
  14.3 24.7 %copy-start.19 = (s32[4,3,128,128]{3,2,1,0:T(8,128)S(1)}, s32[4,3,128,128]{3,2,1,0:T(8,128)}, u32[]{:S(2)}) copy-start(s32[4,3,128,128]{3,2,1,0:T(8,128)} %param.16) | copy-start | bytes 2359300
  14.3 40.9 %collective-permute-start.3 = (s32[32]{0:T(128)}, s32[32]{0:T(128)}, u32[]{:S(2)}, u32[]{:S(2)}) collective-permute-start(s32[32]{0:T(128)} %get-tuple-element.29), channel_id=1, source_target_pairs={{0,2},{2,4},{4,6},{6,8},{8,10},{10,12},{12,14},{1,3},{3,5},{5,7},{... | collective-permute-start | bytes 392 | tf_op jit(solution)/shard_map/ppermute | solution.py:10
  20.0 19.2 %copy-start.60 = (pred[128]{0:T(512)(128)(4,1)}, pred[128]{0:T(512)(128)(4,1)S(1)}, u32[]{:S(2)}) copy-start(pred[128]{0:T(512)(128)(4,1)S(1)} %get-tuple-element.66) | copy-start | bytes 388
  21.6 34.9 %collective-permute-start = (bf16[256,128]{0,1:T(8,128)(2,1)}, bf16[256,128]{0,1:T(8,128)(2,1)}, u32[]{:S(2)}, u32[]{:S(2)}) collective-permute-start(bf16[256,128]{0,1:T(8,128)(2,1)} %select_bitcast_fusion.3), channel_id=1, source_target_pairs={{0,2},{2,4},{4,6},{6,8},{8,10},{10,12},{12,14},{1,3},{3,5},{5,7},{... | collective-permute-start | bytes 196616 | tf_op jit(solution)/shard_map/ppermute | solution.py:10
  25.2 14.0 %copy-start.57 = (s32[1024]{0:T(1024)}, s32[1024]{0:T(1024)S(1)}, u32[]{:S(2)}) copy-start(s32[1024]{0:T(1024)S(1)} %pad_clamp_fusion.1) | copy-start | bytes 12292
  25.2 14.6 %copy-start.8 = (bf16[2,256,512]{2,1,0:T(8,128)(2,1)S(1)}, bf16[2,256,512]{2,1,0:T(8,128)(2,1)}, u32[]{:S(2)}) copy-start(bf16[2,256,512]{2,1,0:T(8,128)(2,1)} %param.13) | copy-start | bytes 1572868
  26.8 29.7 %collective-permute-start.1 = (bf16[256,128]{0,1:T(8,128)(2,1)}, bf16[256,128]{0,1:T(8,128)(2,1)}, u32[]{:S(2)}, u32[]{:S(2)}) collective-permute-start(bf16[256,128]{0,1:T(8,128)(2,1)} %select_bitcast_fusion.2), channel_id=1, source_target_pairs={{2,0},{4,2},{6,4},{8,6},{10,8},{12,10},{14,12},{3,1},{5,3},{7,5},{... | collective-permute-start | bytes 196616 | tf_op jit(solution)/shard_map/ppermute | solution.py:10
  28.0 23.2 %collective-permute-start.7 = (s32[32]{0:T(128)}, s32[32]{0:T(128)}, u32[]{:S(2)}, u32[]{:S(2)}) collective-permute-start(s32[32]{0:T(128)} %get-tuple-element.27), channel_id=1, source_target_pairs={{0,4},{2,6},{4,8},{6,10},{8,12},{10,14},{1,5},{3,7},{5,9},{7,11},{... | collective-permute-start | bytes 392 | tf_op jit(solution)/shard_map/ppermute | solution.py:10
  33.5 15.6 %collective-permute-start.9 = (s32[32]{0:T(128)}, s32[32]{0:T(128)}, u32[]{:S(2)}, u32[]{:S(2)}) collective-permute-start(s32[32]{0:T(128)} %get-tuple-element.28), channel_id=1, source_target_pairs={{4,0},{6,2},{8,4},{10,6},{12,8},{14,10},{5,1},{7,3},{9,5},{11,7},{... | collective-permute-start | bytes 392 | tf_op jit(solution)/shard_map/ppermute | solution.py:10
  34.8 235.2 %all-reduce.3.cloned.1.call-start = ((), (), s32[]{:S(2)}) async-start(), calls=%async_computation.6 | async-start | bytes 2097152
  39.2 90.7 %copy-start.2 = (bf16[4,3,128,128]{3,2,1,0:T(8,128)(2,1)}, bf16[4,3,128,128]{3,2,1,0:T(8,128)(2,1)S(1)}, u32[]{:S(2)}) copy-start(bf16[4,3,128,128]{3,2,1,0:T(8,128)(2,1)S(1)} %get-tuple-element.51) | copy-start | bytes 1179652
  49.2 5.4 %collective-permute-start.5 = (s32[32]{0:T(128)S(1)}, s32[32]{0:T(128)S(1)}, u32[]{:S(2)}, u32[]{:S(2)}) collective-permute-start(s32[32]{0:T(128)S(1)} %copy-done.74), channel_id=1, source_target_pairs={{2,0},{4,2},{6,4},{8,6},{10,8},{12,10},{14,12},{3,1},{5,3},{7,5},{... | collective-permute-start | bytes 392 | tf_op jit(solution)/shard_map/ppermute | solution.py:10
  64.3 15.2 %copy-start.66 = (s32[32]{0:T(128)S(1)}, s32[32]{0:T(128)}, u32[]{:S(2)}) copy-start(s32[32]{0:T(128)} %copy-done.65) | copy-start | bytes 388
  64.3 16.4 %copy-start.75 = (f32[128]{0:T(128)S(1)}, f32[128]{0:T(128)}, u32[]{:S(2)}) copy-start(f32[128]{0:T(128)} %add_maximum_fusion) | copy-start | bytes 1540
  64.3 16.4 %copy-start.79 = (s32[32]{0:T(128)S(1)}, s32[32]{0:T(128)}, u32[]{:S(2)}) copy-start(s32[32]{0:T(128)} %copy-done.78) | copy-start | bytes 388
  64.7 18.2 %copy-start.29 = (bf16[256,512]{1,0:T(8,128)(2,1)S(1)}, bf16[256,512]{1,0:T(8,128)(2,1)}, u32[]{:S(2)}) copy-start(bf16[256,512]{1,0:T(8,128)(2,1)} %param.14) | copy-start | bytes 786436
  65.6 10.8 %collective-permute-start.2 = (bf16[256,32]{0,1:T(8,128)(2,1)S(1)}, bf16[256,32]{0,1:T(8,128)(2,1)S(1)}, u32[]{:S(2)}, u32[]{:S(2)}) collective-permute-start(bf16[256,32]{0,1:T(8,128)(2,1)S(1)} %convolution_convert_fusion.15), channel_id=1, source_target_pairs={{0,2},{2,4},{4,6},{6,8},{8,10},{10,12},{12,14},{1,3},{3,5},{5,7},{... | collective-permute-start | bytes 49160 | tf_op jit(solution)/shard_map/ppermute | solution.py:10
  69.4 7.2 %collective-permute-start.6 = (bf16[256,32]{0,1:T(8,128)(2,1)S(1)}, bf16[256,32]{0,1:T(8,128)(2,1)S(1)}, u32[]{:S(2)}, u32[]{:S(2)}) collective-permute-start(bf16[256,32]{0,1:T(8,128)(2,1)S(1)} %convolution_convert_fusion.13), channel_id=1, source_target_pairs={{0,4},{2,6},{4,8},{6,10},{8,12},{10,14},{1,5},{3,7},{5,9},{7,11},{... | collective-permute-start | bytes 49160 | tf_op jit(solution)/shard_map/ppermute | solution.py:10
  73.8 5.6 %collective-permute-start.8 = (bf16[256,32]{0,1:T(8,128)(2,1)S(1)}, bf16[256,32]{0,1:T(8,128)(2,1)S(1)}, u32[]{:S(2)}, u32[]{:S(2)}) collective-permute-start(bf16[256,32]{0,1:T(8,128)(2,1)S(1)} %convolution_convert_fusion.12), channel_id=1, source_target_pairs={{4,0},{6,2},{8,4},{10,6},{12,8},{14,10},{5,1},{7,3},{9,5},{11,7},{... | collective-permute-start | bytes 49160 | tf_op jit(solution)/shard_map/ppermute | solution.py:10
  75.1 5.6 %collective-permute-start.4 = (bf16[256,32]{0,1:T(8,128)(2,1)S(1)}, bf16[256,32]{0,1:T(8,128)(2,1)S(1)}, u32[]{:S(2)}, u32[]{:S(2)}) collective-permute-start(bf16[256,32]{0,1:T(8,128)(2,1)S(1)} %convolution_convert_fusion.14), channel_id=1, source_target_pairs={{2,0},{4,2},{6,4},{8,6},{10,8},{12,10},{14,12},{3,1},{5,3},{7,5},{... | collective-permute-start | bytes 49160 | tf_op jit(solution)/shard_map/ppermute | solution.py:10
  84.7 12.5 %collective-permute-start.10 = (bf16[256,32]{0,1:T(8,128)(2,1)S(1)}, bf16[256,32]{0,1:T(8,128)(2,1)S(1)}, u32[]{:S(2)}, u32[]{:S(2)}) collective-permute-start(bf16[256,32]{0,1:T(8,128)(2,1)S(1)} %convolution_convert_fusion.11), channel_id=1, source_target_pairs={{2,0},{4,2},{6,4},{8,6},{10,8},{12,10},{14,12},{3,1},{5,3},{7,5},{... | collective-permute-start | bytes 49160 | tf_op jit(solution)/shard_map/ppermute | solution.py:10
  86.2 11.3 %collective-permute-start.12 = (bf16[256,32]{0,1:T(8,128)(2,1)S(1)}, bf16[256,32]{0,1:T(8,128)(2,1)S(1)}, u32[]{:S(2)}, u32[]{:S(2)}) collective-permute-start(bf16[256,32]{0,1:T(8,128)(2,1)S(1)} %convolution_convert_fusion.9), channel_id=1, source_target_pairs={{4,0},{6,2},{8,4},{10,6},{12,8},{14,10},{5,1},{7,3},{9,5},{11,7},{... | collective-permute-start | bytes 49160 | tf_op jit(solution)/shard_map/ppermute | solution.py:10
  87.5 10.3 %collective-permute-start.13 = (bf16[256,32]{0,1:T(8,128)(2,1)S(1)}, bf16[256,32]{0,1:T(8,128)(2,1)S(1)}, u32[]{:S(2)}, u32[]{:S(2)}) collective-permute-start(bf16[256,32]{0,1:T(8,128)(2,1)S(1)} %convolution_convert_fusion.8), channel_id=1, source_target_pairs={{0,4},{2,6},{4,8},{6,10},{8,12},{10,14},{1,5},{3,7},{5,9},{7,11},{... | collective-permute-start | bytes 49160 | tf_op jit(solution)/shard_map/ppermute | solution.py:10
  94.2 4.5 %collective-permute-start.11 = (bf16[256,32]{0,1:T(8,128)(2,1)S(1)}, bf16[256,32]{0,1:T(8,128)(2,1)S(1)}, u32[]{:S(2)}, u32[]{:S(2)}) collective-permute-start(bf16[256,32]{0,1:T(8,128)(2,1)S(1)} %convolution_convert_fusion.10), channel_id=1, source_target_pairs={{0,2},{2,4},{4,6},{6,8},{8,10},{10,12},{12,14},{1,3},{3,5},{5,7},{... | collective-permute-start | bytes 49160 | tf_op jit(solution)/shard_map/ppermute | solution.py:10
  103.3 7.0 %collective-permute-start.14 = (bf16[256,128]{0,1:T(8,128)(2,1)S(1)}, bf16[256,128]{0,1:T(8,128)(2,1)S(1)}, u32[]{:S(2)}, u32[]{:S(2)}) collective-permute-start(bf16[256,128]{0,1:T(8,128)(2,1)S(1)} %select_bitcast_fusion.1), channel_id=1, source_target_pairs={{0,2},{2,4},{4,6},{6,8},{8,10},{10,12},{12,14},{1,3},{3,5},{5,7},{... | collective-permute-start | bytes 196616 | tf_op jit(solution)/shard_map/ppermute | solution.py:10
  107.8 7.3 %collective-permute-start.15 = (bf16[256,128]{0,1:T(8,128)(2,1)S(1)}, bf16[256,128]{0,1:T(8,128)(2,1)S(1)}, u32[]{:S(2)}, u32[]{:S(2)}) collective-permute-start(bf16[256,128]{0,1:T(8,128)(2,1)S(1)} %select_bitcast_fusion), channel_id=1, source_target_pairs={{2,0},{4,2},{6,4},{8,6},{10,8},{12,10},{14,12},{3,1},{5,3},{7,5},{... | collective-permute-start | bytes 196616 | tf_op jit(solution)/shard_map/ppermute | solution.py:10
  133.9 10.1 %collective-permute-start.16 = (bf16[256,128]{1,0:T(8,128)(2,1)S(1)}, bf16[256,128]{1,0:T(8,128)(2,1)S(1)}, u32[]{:S(2)}, u32[]{:S(2)}) collective-permute-start(bf16[256,128]{1,0:T(8,128)(2,1)S(1)} %bitcast.290), channel_id=1, source_target_pairs={{2,0},{4,2},{6,4},{8,6},{10,8},{12,10},{14,12},{3,1},{5,3},{7,5},{... | collective-permute-start | bytes 196616 | tf_op jit(solution)/shard_map/ppermute | solution.py:10
  138.6 7.3 %collective-permute-start.17 = (bf16[256,128]{1,0:T(8,128)(2,1)S(1)}, bf16[256,128]{1,0:T(8,128)(2,1)S(1)}, u32[]{:S(2)}, u32[]{:S(2)}) collective-permute-start(bf16[256,128]{1,0:T(8,128)(2,1)S(1)} %bitcast.291), channel_id=1, source_target_pairs={{0,2},{2,4},{4,6},{6,8},{8,10},{10,12},{12,14},{1,3},{3,5},{5,7},{... | collective-permute-start | bytes 196616 | tf_op jit(solution)/shard_map/ppermute | solution.py:10
  149.4 15.8 %copy-start.67 = (s32[32]{0:T(128)S(1)}, s32[32]{0:T(128)}, u32[]{:S(2)}) copy-start(s32[32]{0:T(128)} %copy-done.65) | copy-start | bytes 388
  149.4 18.4 %copy-start.80 = (s32[32]{0:T(128)S(1)}, s32[32]{0:T(128)}, u32[]{:S(2)}) copy-start(s32[32]{0:T(128)} %copy-done.78) | copy-start | bytes 388
  149.4 18.3 %copy-start.81 = (f32[256,128]{0,1:T(8,128)S(1)}, f32[256,128]{0,1:T(8,128)}, u32[]{:S(2)}) copy-start(f32[256,128]{0,1:T(8,128)} %get-tuple-element.71) | copy-start | bytes 393220
  149.6 20.4 %copy-start.20 = (bf16[512,512]{1,0:T(8,128)(2,1)S(1)}, bf16[512,512]{1,0:T(8,128)(2,1)}, u32[]{:S(2)}) copy-start(bf16[512,512]{1,0:T(8,128)(2,1)} %all_gather.62) | copy-start | bytes 1572868
  149.6 20.4 %copy-start.76 = (f32[128]{0:T(128)S(1)}, f32[128]{0:T(128)}, u32[]{:S(2)}) copy-start(f32[128]{0:T(128)} %add_maximum_fusion) | copy-start | bytes 1540
  150.6 11.6 %collective-permute-start.18 = (bf16[256,32]{0,1:T(8,128)(2,1)S(1)}, bf16[256,32]{0,1:T(8,128)(2,1)S(1)}, u32[]{:S(2)}, u32[]{:S(2)}) collective-permute-start(bf16[256,32]{0,1:T(8,128)(2,1)S(1)} %convolution_convert_fusion.7), channel_id=1, source_target_pairs={{0,2},{2,4},{4,6},{6,8},{8,10},{10,12},{12,14},{1,3},{3,5},{5,7},{... | collective-permute-start | bytes 49160 | tf_op jit(solution)/shard_map/ppermute | solution.py:10
  155.6 6.9 %collective-permute-start.20 = (bf16[256,32]{0,1:T(8,128)(2,1)S(1)}, bf16[256,32]{0,1:T(8,128)(2,1)S(1)}, u32[]{:S(2)}, u32[]{:S(2)}) collective-permute-start(bf16[256,32]{0,1:T(8,128)(2,1)S(1)} %convolution_convert_fusion.5), channel_id=1, source_target_pairs={{0,4},{2,6},{4,8},{6,10},{8,12},{10,14},{1,5},{3,7},{5,9},{7,11},{... | collective-permute-start | bytes 49160 | tf_op jit(solution)/shard_map/ppermute | solution.py:10
  159.6 5.6 %collective-permute-start.21 = (bf16[256,32]{0,1:T(8,128)(2,1)S(1)}, bf16[256,32]{0,1:T(8,128)(2,1)S(1)}, u32[]{:S(2)}, u32[]{:S(2)}) collective-permute-start(bf16[256,32]{0,1:T(8,128)(2,1)S(1)} %convolution_convert_fusion.4), channel_id=1, source_target_pairs={{4,0},{6,2},{8,4},{10,6},{12,8},{14,10},{5,1},{7,3},{9,5},{11,7},{... | collective-permute-start | bytes 49160 | tf_op jit(solution)/shard_map/ppermute | solution.py:10
  160.9 6.9 %collective-permute-start.19 = (bf16[256,32]{0,1:T(8,128)(2,1)S(1)}, bf16[256,32]{0,1:T(8,128)(2,1)S(1)}, u32[]{:S(2)}, u32[]{:S(2)}) collective-permute-start(bf16[256,32]{0,1:T(8,128)(2,1)S(1)} %convolution_convert_fusion.6), channel_id=1, source_target_pairs={{2,0},{4,2},{6,4},{8,6},{10,8},{12,10},{14,12},{3,1},{5,3},{7,5},{... | collective-permute-start | bytes 49160 | tf_op jit(solution)/shard_map/ppermute | solution.py:10
  171.2 13.4 %collective-permute-start.22 = (bf16[256,32]{0,1:T(8,128)(2,1)S(1)}, bf16[256,32]{0,1:T(8,128)(2,1)S(1)}, u32[]{:S(2)}, u32[]{:S(2)}) collective-permute-start(bf16[256,32]{0,1:T(8,128)(2,1)S(1)} %convolution_convert_fusion.3), channel_id=1, source_target_pairs={{2,0},{4,2},{6,4},{8,6},{10,8},{12,10},{14,12},{3,1},{5,3},{7,5},{... | collective-permute-start | bytes 49160 | tf_op jit(solution)/shard_map/ppermute | solution.py:10
  172.7 12.2 %collective-permute-start.24 = (bf16[256,32]{0,1:T(8,128)(2,1)S(1)}, bf16[256,32]{0,1:T(8,128)(2,1)S(1)}, u32[]{:S(2)}, u32[]{:S(2)}) collective-permute-start(bf16[256,32]{0,1:T(8,128)(2,1)S(1)} %convolution_convert_fusion.1), channel_id=1, source_target_pairs={{4,0},{6,2},{8,4},{10,6},{12,8},{14,10},{5,1},{7,3},{9,5},{11,7},{... | collective-permute-start | bytes 49160 | tf_op jit(solution)/shard_map/ppermute | solution.py:10
  174.0 11.2 %collective-permute-start.25 = (bf16[256,32]{0,1:T(8,128)(2,1)S(1)}, bf16[256,32]{0,1:T(8,128)(2,1)S(1)}, u32[]{:S(2)}, u32[]{:S(2)}) collective-permute-start(bf16[256,32]{0,1:T(8,128)(2,1)S(1)} %convolution_convert_fusion), channel_id=1, source_target_pairs={{0,4},{2,6},{4,8},{6,10},{8,12},{10,14},{1,5},{3,7},{5,9},{7,11},{... | collective-permute-start | bytes 49160 | tf_op jit(solution)/shard_map/ppermute | solution.py:10
  181.5 4.5 %collective-permute-start.23 = (bf16[256,32]{0,1:T(8,128)(2,1)S(1)}, bf16[256,32]{0,1:T(8,128)(2,1)S(1)}, u32[]{:S(2)}, u32[]{:S(2)}) collective-permute-start(bf16[256,32]{0,1:T(8,128)(2,1)S(1)} %convolution_convert_fusion.2), channel_id=1, source_target_pairs={{0,2},{2,4},{4,6},{6,8},{8,10},{10,12},{12,14},{1,3},{3,5},{5,7},{... | collective-permute-start | bytes 49160 | tf_op jit(solution)/shard_map/ppermute | solution.py:10
  188.8 146.9 %reduce-scatter.7.cloned.1.call-start = ((), (), s32[]{:S(2)}) async-start(), calls=%async_computation.5 | async-start | bytes 589824
  193.2 213.7 %reduce-scatter.5.cloned.1.call-start = ((), (), s32[]{:S(2)}) async-start(), calls=%async_computation.2 | async-start | bytes 2359296 | tf_op jit(solution)/shard_map/reduce_scatter | solution.py:47
  210.2 8.2 %collective-permute-start.26 = (bf16[256,128]{1,0:T(8,128)(2,1)S(1)}, bf16[256,128]{1,0:T(8,128)(2,1)S(1)}, u32[]{:S(2)}, u32[]{:S(2)}) collective-permute-start(bf16[256,128]{1,0:T(8,128)(2,1)S(1)} %bitcast.289), channel_id=1, source_target_pairs={{2,0},{4,2},{6,4},{8,6},{10,8},{12,10},{14,12},{3,1},{5,3},{7,5},{... | collective-permute-start | bytes 196616 | tf_op jit(solution)/shard_map/ppermute | solution.py:10
  213.1 8.3 %collective-permute-start.27 = (bf16[256,128]{1,0:T(8,128)(2,1)S(1)}, bf16[256,128]{1,0:T(8,128)(2,1)S(1)}, u32[]{:S(2)}, u32[]{:S(2)}) collective-permute-start(bf16[256,128]{1,0:T(8,128)(2,1)S(1)} %bitcast.292), channel_id=1, source_target_pairs={{0,2},{2,4},{4,6},{6,8},{8,10},{10,12},{12,14},{1,3},{3,5},{5,7},{... | collective-permute-start | bytes 196616 | tf_op jit(solution)/shard_map/ppermute | solution.py:10
  (68 other events, 303.2 us)
Sparse Core Ops, SparseCore 0:
  9.9 11.7 all-gather.6
  34.9 10.7 all-gather.8
  189.0 81.0 all-reduce.2
  274.2 61.5 reduce-scatter.6
  339.7 67.1 reduce-scatter.4
where the time goes:
time: 415 us; the launch traced here: 413 us
  waiting for transfers between devices  202 us (49%)
  starting transfers between devices  85.1 us (21%)
  blocking collectives  33.6 us (8%)
  matrix products  32.4 us (8%)
  local copies, waits for them, and re-layouts  25.5 us (6%)
  other arithmetic  19.1 us (5%)
  between operations  16.1 us (4%)
    unnamed x7, waiting for transfers between devices  109 us
    ppermute x28, starting transfers between devices, shifted(): lax.ppermute(value, axis, [(source, source + steps) for source in range(f...  84.9 us
    reduce_scatter x1, waiting for transfers between devices, reduce_grads(): lax.psum_scatter(inward, ('curve', 'cross'), scatter_dimension=2, tiled=T...  71.2 us
    ppermute x28, waiting for transfers between devices, shifted(): lax.ppermute(value, axis, [(source, source + steps) for source in range(f...  21.6 us
    all_gather x7, blocking collectives, gather_width(): return lax.all_gather(operand, 'sub', axis=0, tiled=True)  16 us
    all_gather x5, blocking collectives, gather_pair(): lax.all_gather(second_item, 'sub', axis=0, tiled=True)  11 us
    unnamed x178, local copies, waits for them, and re-layouts  10.8 us
  transfers between devices with their start and end apart: 33, of which 13 were waited for; matrix products, arithmetic and copies ran while one was open for 17% of the time, Pallas kernels for 0%

commit v1 on v0

v1 whole, which is shorter than its diff:
```python
import jax
import jax.numpy as jnp
from jax import lax
from jax.experimental import pallas as pl
from jax.experimental.pallas import tpu as pltpu
from jax.sharding import PartitionSpec as P

BF = jnp.bfloat16
F32 = jnp.float32
I32 = jnp.int32
DOM = ("curve", "cross")
LINE = ("curve", "cross", "sub")
NN = (((1,), (0,)), ((), ()))
NT = (((1,), (1,)), ((), ()))
TN = (((0,), (0,)), ((), ()))


def dot(a, b, dims=NN):
    return lax.dot_general(a, b, dims, preferred_element_type=F32)


def sds(shape, dtype):
    return jax.ShapeDtypeStruct(shape, dtype)


def call(body, outs, scalars, arrays, name, flops=0, scratch=()):
    scalars, arrays = list(scalars), list(arrays)
    moved = sum(a.size * a.dtype.itemsize for a in arrays) + sum(
        o.size * o.dtype.itemsize for o in outs
    )
    return pl.pallas_call(
        body,
        out_shape=tuple(outs),
        in_specs=[pl.BlockSpec(memory_space=pltpu.SMEM)] * len(scalars)
        + [pl.BlockSpec(memory_space=pltpu.VMEM)] * len(arrays),
        out_specs=tuple(pl.BlockSpec(memory_space=pltpu.VMEM) for _ in outs),
        scratch_shapes=list(scratch),
        compiler_params=pltpu.CompilerParams(vmem_limit_bytes=40 * 2**20),
        cost_estimate=pl.CostEstimate(flops=flops, bytes_accessed=moved, transcendentals=0),
        name=name,
    )(*scalars, *arrays)


def shifted(value, steps):
    count = lax.axis_size(DOM)
    first, last = (max(0, -steps), min(count, count - steps))
    return lax.ppermute(value, DOM, [(s, s + steps) for s in range(first, last)])


def two_way(value, steps):
    count = lax.axis_size(DOM)
    pairs = [(2 * p, 2 * (p + steps)) for p in range(count - steps)]
    pairs += [(2 * p + 1, 2 * (p - steps) + 1) for p in range(steps, count)]
    return lax.ppermute(value, LINE, pairs)


def gather(value):
    return lax.all_gather(value, "sub", axis=0, tiled=True)


def sigmoid(v):
    return 1.0 / (1.0 + jnp.exp(-v))


def slope_of(v):
    s = sigmoid(v)
    return s * (1.0 + v * (1.0 - s))


def wide(col, width):
    return jnp.concatenate([col] * (width // col.shape[1]), axis=1)


def k_halo(rows_ref, x_ref, next_ref, prev_ref):
    x = x_ref[...]
    n = x.shape[1]
    at = lax.broadcasted_iota(I32, (n, rows_ref.shape[1]), 0)
    next_ref[...] = dot(x, (at == rows_ref[0:1, :]).astype(BF)).astype(BF)
    prev_ref[...] = dot(x, (at == rows_ref[1:2, :]).astype(BF)).astype(BF)


def k_prep(tile_ref, me_ref, mask_ref, rows_ref, rowc_ref, par_ref, parc_ref,
           adj_ref, adjt_ref, inv_ref, hott_ref, hot_ref, slot_ref, slott_ref,
           pick_ref, place_ref, tags_ref, ocount_ref):
    blocks, k_slots, length, _ = mask_ref.shape
    n = adj_ref.shape[0]
    nodes = hott_ref.shape[0]
    slots = slot_ref.shape[0]
    cap = slots // 4
    adj_ref[...] = jnp.zeros(adj_ref.shape, BF)
    adjt_ref[...] = jnp.zeros(adjt_ref.shape, BF)
    for b in range(blocks):
        degree = jnp.zeros((length, 1), F32)
        for k in range(k_slots):
            bits = mask_ref[b, k].astype(F32)
            start = pl.multiple_of(tile_ref[b, k] * length, length)
            adj_ref[b * length:(b + 1) * length, pl.ds(start, length)] = bits.astype(BF)
            adjt_ref[pl.ds(start, length), b * length:(b + 1) * length] = bits.T.astype(BF)
            degree = degree + jnp.sum(bits, axis=1, keepdims=True)
        inv_ref[b * length:(b + 1) * length, :] = jnp.broadcast_to(1.0 / degree, (length, 128))
    base = me_ref[0] * nodes
    rel_row = par_ref[...] - base
    rel_col = parc_ref[...] - base
    hott = (lax.broadcasted_iota(I32, (nodes, n), 0) == rel_row).astype(F32)
    hott_ref[...] = hott.astype(BF)
    ocount_ref[...] = jnp.broadcast_to(jnp.sum(hott, axis=1, keepdims=True), (nodes, 128))
    hot_ref[...] = (lax.broadcasted_iota(I32, (n, nodes), 1) == rel_col).astype(F32).astype(BF)

    def offsets(shape, dim):
        j = lax.broadcasted_iota(I32, shape, dim)
        off = jnp.where(j < cap, 1, jnp.where(j < 2 * cap, -1, jnp.where(j < 3 * cap, 2, -2)))
        start = jnp.where(j < cap, 0, jnp.where(j < 2 * cap, cap, jnp.where(j < 3 * cap, 2 * cap, 3 * cap)))
        return off * nodes, (j - start).astype(F32)

    i0 = lax.broadcasted_iota(I32, (n, n), 0)
    i1 = lax.broadcasted_iota(I32, (n, n), 1)
    off, rank_want = offsets((slots, n), 0)
    node = rel_row - off
    chosen = ((node >= 0) & (node < nodes)).astype(F32)
    rank = dot(chosen.astype(BF), (i0 < i1).astype(F32).astype(BF))
    slot_ref[...] = jnp.where(rank == rank_want, chosen, 0.0).astype(BF)
    off, rank_want = offsets((n, slots), 1)
    node = rel_col - off
    chosen = ((node >= 0) & (node < nodes)).astype(F32)
    rank = dot((i0 > i1).astype(F32).astype(BF), chosen.astype(BF))
    fits = jnp.where(rank == rank_want, chosen, 0.0)
    slott_ref[...] = fits.astype(BF)
    tags = jnp.sum(fits * (node + 1).astype(F32), axis=0, keepdims=True)
    tags_ref[...] = jnp.broadcast_to(tags, tags_ref.shape).astype(BF)
    width = rows_ref.shape[1]
    at1 = lax.broadcasted_iota(I32, (width, n), 1)
    at0 = lax.broadcasted_iota(I32, (n, width), 0)
    for c in range(2):
        pick_ref[c * width:(c + 1) * width, :] = (at1 == rowc_ref[:, c:c + 1]).astype(F32).astype(BF)
        place_ref[:, c * width:(c + 1) * width] = (at0 == rows_ref[c:c + 1, :]).astype(F32).astype(BF)


def forward(xc, src, adj_ref, inv_ref, wx_ref, wa_ref, wo_ref):
    width = xc.shape[1]
    agg = (dot(adj_ref[...], src) * wide(inv_ref[...], width)).astype(BF)
    pre = dot(xc, wx_ref[...], NT) + dot(agg, wa_ref[...], NT)
    hid = (pre * sigmoid(pre)).astype(BF)
    out = (xc.astype(F32) + dot(hid, wo_ref[...], NT)).astype(BF)
    return agg, pre, hid, out


def send_slots(sub, values, slot_ref, one_ref, two_ref):
    cap = slot_ref.shape[0] // 4
    a = pl.multiple_of(sub * cap, cap)
    one_ref[0:cap, :] = dot(slot_ref[pl.ds(a, cap), :], values).astype(BF)
    two_ref[0:cap, :] = dot(slot_ref[pl.ds(a + 2 * cap, cap), :], values).astype(BF)


def k_first(me_ref, x_ref, before_ref, after_ref, adj_ref, inv_ref, wx_ref, wa_ref, wo_ref,
            slot_ref, tags_ref,
            xc_ref, agg_ref, pre_ref, hid_ref, first_ref, one_ref, two_ref, src):
    n = x_ref.shape[1]
    rim = before_ref.shape[1]
    xc = x_ref[...].T
    xc_ref[...] = xc
    src[0:n, :] = xc
    src[n:n + rim, :] = before_ref[...].T
    src[n + rim:, :] = after_ref[...].T
    agg, pre, hid, out = forward(xc, src[...], adj_ref, inv_ref, wx_ref, wa_ref, wo_ref)
    agg_ref[...] = agg
    pre_ref[...] = pre
    hid_ref[...] = hid
    first_ref[...] = out
    send_slots(me_ref[1], out, slot_ref, one_ref, two_ref)
    cap = slot_ref.shape[0] // 4
    pad = wide(tags_ref[...], one_ref.shape[1])
    one_ref[cap:, :] = pad
    two_ref[cap:, :] = pad


def k_own(hott_ref, v_ref, pre_ref, pool_ref, slope_ref):
    pool_ref[...] = dot(hott_ref[...], v_ref[...])
    slope_ref[...] = slope_of(pre_ref[...])


def k_pool(hott_ref, v_ref, pool_ref):
    pool_ref[...] = dot(hott_ref[...], v_ref[...])


def k_cot(ct_ref, wo_ref, ctc_ref, hg_ref):
    ctc = ct_ref[...].T
    ctc_ref[...] = ctc
    hg_ref[...] = dot(ctc, wo_ref[...])


def arrived_of(one_ref, two_ref, cap, rows):
    return jnp.concatenate(
        [one_ref[0:cap, :], one_ref[rows:rows + cap, :], two_ref[0:cap, :], two_ref[rows:rows + cap, :]],
        axis=0,
    )


def send_answers(sub, hits, values, one_ref, two_ref):
    cap = hits.shape[1] // 4
    ans = dot(hits.T, values).astype(BF)
    one_ref[...] = jnp.where(sub == 0, ans[cap:2 * cap], ans[0:cap])
    two_ref[...] = jnp.where(sub == 0, ans[3 * cap:], ans[2 * cap:3 * cap])


def k_coarse(me_ref, pool_ref, ocount_ref, one_ref, two_ref, cw_ref,
             hits_ref, icount_ref, coarse_ref, cpre_ref, corr_ref, out1_ref, out2_ref):
    nodes, width = pool_ref.shape
    cap = out1_ref.shape[0]
    rows = one_ref.shape[0] // 2
    slots = 4 * cap
    lane = lax.broadcasted_iota(I32, (1, slots), 1)
    t = [r[o + cap:o + cap + 1, 0:slots].astype(F32) for r in (one_ref, two_ref) for o in (0, rows)]
    tags = jnp.where(lane < cap, t[0], jnp.where(lane < 2 * cap, t[1], jnp.where(lane < 3 * cap, t[2], t[3])))
    node = (lax.broadcasted_iota(I32, (nodes, slots), 0) + 1).astype(F32)
    hits = (node == tags).astype(F32)
    count = jnp.maximum(ocount_ref[...] + jnp.sum(hits, axis=1, keepdims=True), 1.0)
    icount = 1.0 / count
    hits_ref[...] = hits
    icount_ref[...] = icount
    hb = hits.astype(BF)
    total = pool_ref[...] + dot(hb, arrived_of(one_ref, two_ref, cap, rows))
    coarse = (total * wide(icount, width)).astype(BF)
    cpre = dot(coarse, cw_ref[...], NT)
    corr = (cpre * sigmoid(cpre)).astype(BF)
    coarse_ref[...] = coarse
    cpre_ref[...] = cpre
    corr_ref[...] = corr
    ans = dot(hits.T.astype(BF), corr).astype(BF)
    sub = me_ref[1]
    out1_ref[...] = jnp.where(sub == 0, ans[cap:2 * cap], ans[0:cap])
    out2_ref[...] = jnp.where(sub == 0, ans[3 * cap:], ans[2 * cap:3 * cap])


def spread_back(first, hot_ref, slott_ref, corr, one_ref, two_ref):
    cap = one_ref.shape[0] // 2
    returned = jnp.concatenate(
        [one_ref[cap:, :], one_ref[0:cap, :], two_ref[cap:, :], two_ref[0:cap, :]], axis=0
    )
    total = first.astype(F32) + dot(hot_ref[...], corr) + dot(slott_ref[...], returned)
    return total.astype(BF)


def k_lift(me_ref, first_ref, hot_ref, slott_ref, corr_ref, one_ref, two_ref, pick_ref,
           lift_ref, msg_ref):
    lifted = spread_back(first_ref[...], hot_ref, slott_ref, corr_ref[...], one_ref, two_ref)
    lift_ref[...] = lifted
    rim = msg_ref.shape[0]
    at = pl.multiple_of(me_ref[1] * rim, rim)
    msg_ref[...] = dot(pick_ref[pl.ds(at, rim), :], lifted).astype(BF)


def rim_grads(sub, pg, wa_ref, inv_ref, adjt_ref, scaled_ref, msg_ref):
    n = pg.shape[0]
    rim = msg_ref.shape[0]
    scaled = (dot(pg, wa_ref[...]) * wide(inv_ref[...], wa_ref.shape[1])).astype(BF)
    scaled_ref[...] = scaled
    at = pl.multiple_of(n + (1 - sub) * rim, rim)
    msg_ref[...] = dot(adjt_ref[pl.ds(at, rim), :], scaled).astype(BF)


def k_second(me_ref, lift_ref, rim_ref, adj_ref, adjt_ref, inv_ref, wx_ref, wa_ref, wo_ref, hg_ref,
             agg_ref, hid_ref, new_ref, pg_ref, scaled_ref, msg_ref, src):
    n = lift_ref.shape[0]
    lifted = lift_ref[...]
    src[0:n, :] = lifted
    src[n:, :] = rim_ref[...]
    agg, pre, hid, out = forward(lifted, src[...], adj_ref, inv_ref, wx_ref, wa_ref, wo_ref)
    agg_ref[...] = agg
    hid_ref[...] = hid
    new_ref[...] = out
    pg = (hg_ref[...] * slope_of(pre)).astype(BF)
    pg_ref[...] = pg
    rim_grads(me_ref[1], pg, wa_ref, inv_ref, adjt_ref, scaled_ref, msg_ref)


def combine(g, pg, wx_ref, scaled, adjt_ref):
    n = g.shape[0]
    return g.astype(F32) + dot(pg, wx_ref[...]) + dot(adjt_ref[0:n, :], scaled)


def k_combine(g_ref, pg_ref, wx_ref, scaled_ref, adjt_ref, comb_ref):
    comb_ref[...] = combine(g_ref[...], pg_ref[...], wx_ref, scaled_ref[...], adjt_ref)


def k_newt(me_ref, new_ref, out_ref):
    half = out_ref.shape[0]
    at = pl.multiple_of(me_ref[1] * half, half)
    out_ref[...] = new_ref[:, pl.ds(at, half)].T


def k_grads(scale, me_ref, pg_ref, h_ref, agg_ref, g_ref, hid_ref, gin_ref, gout_ref):
    half = gin_ref.shape[0]
    width = h_ref.shape[1]
    at = pl.multiple_of(me_ref[1] * half, half)
    pgt = pg_ref[:, pl.ds(at, half)].T
    gin_ref[:, 0:width] = dot(pgt, h_ref[...]) * scale
    gin_ref[:, width:] = dot(pgt, agg_ref[...]) * scale
    gt = g_ref[:, pl.ds(at, half)].T
    gout_ref[...] = dot(gt, hid_ref[...]) * scale


def k_packed(scale, order, me_ref, pg_ref, h_ref, agg_ref, g_ref, hid_ref, *rest):
    out_ref = rest[-1]
    extra_ref = rest[0] if len(rest) > 1 else None
    parts = out_ref.shape[0]
    width = h_ref.shape[1]
    hidden = hid_ref.shape[1]
    half = width // 2
    at = pl.multiple_of(me_ref[1] * half, half)
    pgt = pg_ref[:, pl.ds(at, half)].T
    lo = (dot(pgt, h_ref[...]) * scale).astype(BF)
    hi = (dot(pgt, agg_ref[...]) * scale).astype(BF)
    gt = g_ref[:, pl.ds(at, half)].T
    go = (dot(gt, hid_ref[...]) * scale).astype(BF)
    piece = 2 * width // parts
    small = hidden // parts
    for d in range(parts):
        row = order[d]
        src, c = (lo, d * piece) if d * piece < width else (hi, d * piece - width)
        out_ref[row, 0:half, :] = src[:, c:c + piece]
        mine = go[:, d * small:(d + 1) * small]
        if extra_ref is None:
            quarter = half // 2
            out_ref[row, half:half + quarter, :] = jnp.concatenate([mine[:quarter], mine[quarter:]], axis=1)
        else:
            other = extra_ref[:, d * small:(d + 1) * small].astype(BF)
            out_ref[row, half:2 * half, :] = jnp.concatenate([mine, other], axis=1)


def k_lgrad(me_ref, comb_ref, rim_ref, place_ref, slot_ref, lg_ref, one_ref, two_ref):
    rim = rim_ref.shape[0] // 2
    lg = comb_ref[...] + dot(place_ref[:, 0:rim], rim_ref[rim:, :]) + dot(place_ref[:, rim:], rim_ref[0:rim, :])
    lg = lg.astype(BF)
    lg_ref[...] = lg
    send_slots(me_ref[1], lg, slot_ref, one_ref, two_ref)


def k_cgrad(me_ref, pool_ref, one_ref, two_ref, hits_ref, icount_ref, cpre_ref, cw_ref,
            pgrad_ref, spread_ref, out1_ref, out2_ref):
    cap = out1_ref.shape[0]
    hits = hits_ref[...]
    total = pool_ref[...] + dot(hits.astype(BF), arrived_of(one_ref, two_ref, cap, cap))
    pgrad = (total * slope_of(cpre_ref[...])).astype(BF)
    pgrad_ref[...] = pgrad
    spread = (dot(pgrad, cw_ref[...]) * wide(icount_ref[...], pgrad.shape[1])).astype(BF)
    spread_ref[...] = spread
    ans = dot(hits.T.astype(BF), spread).astype(BF)
    sub = me_ref[1]
    out1_ref[...] = jnp.where(sub == 0, ans[cap:2 * cap], ans[0:cap])
    out2_ref[...] = jnp.where(sub == 0, ans[3 * cap:], ans[2 * cap:3 * cap])


def k_cweight(scale, me_ref, pgrad_ref, coarse_ref, out_ref):
    half = out_ref.shape[0]
    at = pl.multiple_of(me_ref[1] * half, half)
    out_ref[...] = dot(pgrad_ref[:, pl.ds(at, half)].T, coarse_ref[...]) * scale


def k_third(me_ref, lg_ref, hot_ref, slott_ref, spread_ref, one_ref, two_ref, wo_ref, slope_ref,
            wa_ref, inv_ref, adjt_ref,
            fb_ref, pg_ref, scaled_ref, before_ref, after_ref):
    fb = spread_back(lg_ref[...], hot_ref, slott_ref, spread_ref[...], one_ref, two_ref)
    fb_ref[...] = fb
    pg = (dot(fb, wo_ref[...]) * slope_ref[...]).astype(BF)
    pg_ref[...] = pg
    n, width = fb.shape
    half = width // 2
    rim = before_ref.shape[0]
    scaled = (dot(pg, wa_ref[...]) * wide(inv_ref[...], width)).astype(BF)
    scaled_ref[...] = scaled
    at = pl.multiple_of(me_ref[1] * half, half)
    mine = scaled_ref[:, pl.ds(at, half)]
    both = dot(adjt_ref[n:, :], mine).astype(BF)
    before_ref[...] = both[0:rim]
    after_ref[...] = both[rim:]


def k_last(comb_ref, after_ref, before_ref, place_ref, out_ref):
    rim = after_ref.shape[0]
    total = comb_ref[...] + dot(place_ref[:, 0:rim], after_ref[...]) + dot(place_ref[:, rim:], before_ref[...])
    out_ref[...] = total.T


def k_halfcomb(me_ref, fb_ref, pg_ref, wx_ref, scaled_ref, adjt_ref, comb_ref):
    n, half = comb_ref.shape
    at = pl.multiple_of(me_ref[1] * half, half)
    cols = pl.ds(at, half)
    comb_ref[...] = (
        fb_ref[:, cols].astype(F32)
        + dot(pg_ref[...], wx_ref[:, cols])
        + dot(adjt_ref[0:n, :], scaled_ref[:, cols])
    )


def k_sum(early_ref, late_ref, gin_ref, gout_ref, gco_ref):
    half = gin_ref.shape[1]
    small = gout_ref.shape[2]
    e = early_ref[...].astype(F32)
    gin_ref[1] = e[0:half]
    gout_ref[1] = e[half:, 0:small]
    gco_ref[...] = e[half:, small:]
    t = late_ref[0].astype(F32)
    for d in range(1, late_ref.shape[0]):
        t = t + late_ref[d].astype(F32)
    gin_ref[0] = t[0:half]
    quarter = half // 2
    gout_ref[0, 0:quarter, :] = t[half:, 0:small]
    gout_ref[0, quarter:, :] = t[half:, small:]


def local(node_features, inward_weight, outward_weight, coarse_weight, tile_index, tile_mask,
          send_rows, parent, cotangent):
    half, n = node_features.shape
    width = 2 * half
    blocks, k_slots = tile_index.shape
    rim = tile_mask.shape[2]
    src_rows = (blocks + 2) * rim
    domains = lax.axis_size(DOM)
    cross = lax.axis_size("cross")
    curve = lax.axis_size("curve")
    cap = n // 16
    nodes = n // 4
    slots = 4 * cap
    hidden = 2 * inward_weight.shape[1]
    scale = float(n * domains) ** -0.5
    me = jnp.stack([lax.axis_index(DOM), lax.axis_index("sub")]).astype(I32)
    rows = send_rows[0]
    packed = 2 * width // domains == 128

    halo_next, halo_prev = call(
        k_halo, [sds((half, rim), BF)] * 2, [], [rows, node_features], "halo")
    before_half = shifted(halo_next, 1)
    after_half = shifted(halo_prev, -1)
    x_full = gather(node_features)
    wx = [gather(inward_weight[l, :, :width]) for l in range(2)]
    wa = [gather(inward_weight[l, :, width:]) for l in range(2)]
    wo = [gather(outward_weight[l]) for l in range(2)]
    (adj, adjt, inv, hott, hot, slot, slott, pick, place, tags, ocount) = call(
        k_prep,
        [sds((n, src_rows), BF), sds((src_rows, n), BF), sds((n, 128), F32), sds((nodes, n), BF),
         sds((n, nodes), BF), sds((slots, n), BF), sds((n, slots), BF), sds((2 * rim, n), BF),
         sds((n, 2 * rim), BF), sds((16, slots), BF), sds((nodes, 128), F32)],
        [tile_index, me],
        [tile_mask, rows, rows.T, parent[None, :], parent[:, None]], "prep")
    before = gather(before_half)
    after = gather(after_half)
    msg = sds((cap + 16, width), BF)
    plain = sds((cap, width), BF)
    cell_bf, cell_f32 = sds((n, width), BF), sds((n, width), F32)
    xc, agg0, pre0, hid0, first, one, two = call(
        k_first,
        [cell_bf, cell_bf, sds((n, hidden), F32), sds((n, hidden), BF), cell_bf, msg, msg],
        [me], [x_full, before, after, adj, inv, wx[0], wa[0], wo[0], slot, tags], "first",
        flops=2 * n * width * (src_rows + 3 * width),
        scratch=[pltpu.VMEM((src_rows, width), BF)])
    one, two = two_way(one, 1), two_way(two, 2)
    own, slope0 = call(k_own, [sds((nodes, width), F32), sds((n, hidden), F32)], [], [hott, first, pre0],
                       "own")
    ct_full = gather(cotangent)
    ctc, hg1 = call(k_cot, [cell_bf, sds((n, hidden), F32)], [], [ct_full, wo[1]], "cot")
    cw = gather(coarse_weight)
    one, two = gather(one), gather(two)
    node_bf, node_f32 = sds((nodes, width), BF), sds((nodes, width), F32)
    hits, icount, coarse, cpre, corr, one, two = call(
        k_coarse, [sds((nodes, slots), F32), sds((nodes, 128), F32), node_bf, node_f32, node_bf, plain, plain],
        [me], [own, ocount, one, two, cw], "coarse")
    one, two = gather(two_way(one, 1)), gather(two_way(two, 2))
    lifted, rims = call(
        k_lift, [cell_bf, sds((rim, width), BF)], [me],
        [first, hot, slott, corr, one, two, pick], "lift")
    rims = gather(two_way(rims, 1))
    agg1, hid1, new, pg1, scaled1, rims = call(
        k_second,
        [cell_bf, sds((n, hidden), BF), cell_bf, sds((n, hidden), BF), cell_bf, sds((rim, width), BF)],
        [me], [lifted, rims, adj, adjt, inv, wx[1], wa[1], wo[1], hg1], "second",
        scratch=[pltpu.VMEM((src_rows, width), BF)])
    rims = two_way(rims, 1)
    comb1, = call(k_combine, [cell_f32], [], [ctc, pg1, wx[1], scaled1, adjt], "combine")
    rims = gather(rims)
    lg, one, two = call(
        k_lgrad, [cell_bf, plain, plain], [me], [comb1, rims, place, slot], "lgrad")
    one, two = two_way(one, 1), two_way(two, 2)
    own_g, = call(k_pool, [node_f32], [], [hott, lg], "own_grad")
    new_t, = call(k_newt, [sds((half, n), BF)], [me], [new], "new")
    one, two = gather(one), gather(two)
    pgrad, spread, one, two = call(
        k_cgrad, [node_bf, node_bf, plain, plain], [me],
        [own_g, one, two, hits, icount, cpre, cw], "cgrad")
    one, two = two_way(one, 1), two_way(two, 2)
    gco, = call(lambda *r: k_cweight(scale, *r), [sds((half, width), F32)], [me], [pgrad, coarse], "cweight")
    one, two = gather(one), gather(two)
    fb, pg0, scaled0, to_before, to_after = call(
        k_third,
        [cell_bf, sds((n, hidden), BF), cell_bf, sds((rim, half), BF), sds((rim, half), BF)],
        [me], [lg, hot, slott, spread, one, two, wo[0], slope0, wa[0], inv, adjt], "third")
    from_after = shifted(to_before, -1)
    from_before = shifted(to_after, 1)
    comb0, = call(k_halfcomb, [sds((n, half), F32)], [me], [fb, pg0, wx[0], scaled0, adjt], "halfcomb")
    if packed:
        order = [(d % cross) * curve + d // cross for d in range(domains)]
        piece = 2 * width // domains
        early, = call(lambda *r: k_packed(scale, order, *r), [sds((domains, 2 * half, piece), BF)], [me],
                      [pg1, lifted, agg1, ctc, hid1, gco], "grads1")
        early = lax.psum_scatter(early, "cross", scatter_dimension=0, tiled=True)
        early = lax.psum_scatter(early, "curve", scatter_dimension=0, tiled=True)[0]
        late, = call(lambda *r: k_packed(scale, list(range(domains)), *r),
                     [sds((domains, half + half // 2, piece), BF)], [me],
                     [pg0, xc, agg0, fb, hid0], "grads0")
        late = lax.all_to_all(late, DOM, 0, 0, tiled=True)
        small = hidden // domains
        gin, gout, gco = call(
            k_sum, [sds((2, half, piece), F32), sds((2, half, small), F32), sds((half, small), F32)],
            [], [early, late], "sums")
    else:
        shapes = [sds((half, 2 * width), F32), sds((half, hidden), F32)]
        gi1, go1 = call(lambda *r: k_grads(scale, *r), shapes, [me], [pg1, lifted, agg1, ctc, hid1], "grads1")
        gi0, go0 = call(lambda *r: k_grads(scale, *r), shapes, [me], [pg0, xc, agg0, fb, hid0], "grads0")
        gin = lax.psum_scatter(jnp.stack([gi0, gi1]), DOM, scatter_dimension=2, tiled=True)
        gout = lax.psum_scatter(jnp.stack([go0, go1]), DOM, scatter_dimension=2, tiled=True)
        gco = lax.psum_scatter(gco, DOM, scatter_dimension=1, tiled=True)
    fgrad, = call(k_last, [sds((half, n), F32)], [], [comb0, from_after, from_before, place], "last")
    return new_t, fgrad, gin, gout, gco


def solution(mesh):
    cells = ("groups", "curve", "cross")
    in_specs = (
        P("sub", cells),
        P(None, "sub", None),
        P(None, "sub", None),
        P("sub", None),
        P(cells, None),
        P(cells, None, None, None),
        P(cells, None, None),
        P(cells),
        P("sub", cells),
    )
    out_specs = (
        P("sub", cells),
        P("sub", cells),
        P("groups", "sub", ("curve", "cross")),
        P("groups", "sub", ("curve", "cross")),
        P(("groups", "sub"), ("curve", "cross")),
    )
    return jax.shard_map(local, mesh=mesh, in_specs=in_specs, out_specs=out_specs, check_vma=False)
```

time: 415 us -> 177 us (0.43)
  waiting for transfers between devices: 202 us -> 24.4 us
  starting transfers between devices: 85.1 us -> 52.3 us
  matrix products: 32.4 us -> 0 us
  Pallas kernels: 0 us -> 26.1 us
  other arithmetic: 19.1 us -> 0.07 us
  local copies, waits for them, and re-layouts: 25.5 us -> 15.6 us
  blocking collectives: 33.6 us -> 43.5 us
    unnamed x7 -> x2, waiting for transfers between devices: 109 us -> 0.68 us
    reduce_scatter x1 -> x2, waiting for transfers between devices: 71.2 us -> 0.59 us  [the longest x1 0.57 us: local(): early = lax.psum_scatter(early, 'curve', scatter_dimension=0, tiled=True)[0]]
    ppermute x28 -> x14, starting transfers between devices: 84.9 us -> 47.8 us  [the longest x10 35.1 us: two_way(): return lax.ppermute(value, LINE, pairs)]
    dot_general x63 -> x0, matrix products: 32.4 us -> none  [the longest x2 5.28 us: backward_layer(): jnp.einsum('fbkc,bkj->fjc', contrib, selector, precision=lax.Precision.HI...]
    pallas_call x0 -> x20, Pallas kernels: none -> 26.1 us  [call(): pl.pallas_call(body, out_shape=tuple(outs), in_specs=[pl.BlockSpec(memory...]
    all_to_all x0 -> x1, waiting for transfers between devices: none -> 17.9 us  [local(): late = lax.all_to_all(late, DOM, 0, 0, tiled=True)]
    ppermute x28 -> x14, waiting for transfers between devices: 21.6 us -> 5.25 us  [the longest x10 4.84 us: two_way(): return lax.ppermute(value, LINE, pairs)]
    all_gather x15 -> x21, blocking collectives: 33.6 us -> 43.5 us  [gather(): return lax.all_gather(value, 'sub', axis=0, tiled=True)]
  transfers between devices with their start and end apart: 33 -> 17, of which waited for: 13 -> 5; matrix products, arithmetic and copies ran while one was open for 17% -> 1% of each run, Pallas kernels for 0% -> 7%
where the time goes in v1:
time: 177 us; the launch traced here: 176 us
  starting transfers between devices  52.3 us (30%)
  blocking collectives  43.5 us (25%)
  Pallas kernels  26.1 us (15%)
  waiting for transfers between devices  24.4 us (14%)
  local copies, waits for them, and re-layouts  15.6 us (9%)
  between operations  14.5 us (8%)
    all_gather x21, blocking collectives, gather(): return lax.all_gather(value, 'sub', axis=0, tiled=True)  43.5 us
    ppermute x10, starting transfers between devices, two_way(): return lax.ppermute(value, LINE, pairs)  35.1 us
    pallas_call x20, Pallas kernels, call(): pl.pallas_call(body, out_shape=tuple(outs), in_specs=[pl.BlockSpec(memory...  26.1 us
    all_to_all x1, waiting for transfers between devices, local(): late = lax.all_to_all(late, DOM, 0, 0, tiled=True)  17.9 us
    unnamed x89, local copies, waits for them, and re-layouts  13.1 us
    ppermute x4, starting transfers between devices, shifted(): lax.ppermute(value, DOM, [(s, s + steps) for s in range(first, last)])  12.7 us
    ppermute x10, waiting for transfers between devices, two_way(): return lax.ppermute(value, LINE, pairs)  4.84 us
    all_to_all x1, starting transfers between devices, local(): late = lax.all_to_all(late, DOM, 0, 0, tiled=True)  4.4 us
  transfers between devices with their start and end apart: 17, of which 5 were waited for; matrix products, arithmetic and copies ran while one was open for 1% of the time, Pallas kernels for 7%

profile of v1, /device:TPU:0, one launch (start us, length us, event | category | flops | bytes accessed | tf_op | source)
XLA Modules:
  0.0 176.4 jit_solution(13755440326908047786)
XLA Ops:
  9.9 5.5 %collective-permute-start = (bf16[256,128]{1,0:T(8,128)(2,1)}, bf16[256,128]{1,0:T(8,128)(2,1)}, u32[]{:S(2)}, u32[]{:S(2)}) collective-permute-start(bf16[256,128]{1,0:T(8,128)(2,1)} %get-tuple-element.59), channel_id=1, source_target_pairs={{0,2},{2,4},{4,6},{6,8},{8,10},{10,12},{12,14},{1,3},{3,5},{5,7},{... | collective-permute-start | bytes 196616 | tf_op jit(solution)/shard_map/ppermute | solution.py:47
  15.4 1.3 collective-permute-start.1
  16.7 2.4 %all_gather.63.x_ref = bf16[512,512]{1,0:T(8,128)(2,1)} all-gather(bf16[256,512]{1,0:T(8,128)(2,1)S(1)} %copy-done.7), channel_id=1, replica_groups=mesh['groups'=2,'curve'=4,'cross'=2,'sub'=2] {'sub'}, dimensions={0}, use_global_device_ids=true | all-gather | bytes 786432 | tf_op jit(solution)/shard_map/all_gather | solution.py:58
  19.2 2.3 %all_gather.71.cw_ref = bf16[512,512]{1,0:T(8,128)(2,1)S(1)} all-gather(bf16[256,512]{1,0:T(8,128)(2,1)S(1)} %copy-done.41), channel_id=1, replica_groups=mesh['groups'=2,'curve'=4,'cross'=2,'sub'=2] {'sub'}, dimensions={0}, use_global_device_ids=true | all-gather | bytes 786432 | tf_op jit(solution)/shard_map/all_gather | solution.py:58
  21.5 2.3 %all_gather.78.ct_ref = bf16[512,512]{1,0:T(8,128)(2,1)S(1)} all-gather(bf16[256,512]{1,0:T(8,128)(2,1)S(1)} %copy-done.42), channel_id=1, replica_groups=mesh['groups'=2,'curve'=4,'cross'=2,'sub'=2] {'sub'}, dimensions={0}, use_global_device_ids=true | all-gather | bytes 786432 | tf_op jit(solution)/shard_map/all_gather | solution.py:58
  24.5 2.2 %all-gather.2 = bf16[1,512,512]{2,1,0:T(8,128)(2,1)S(1)} all-gather(bf16[1,256,512]{2,1,0:T(8,128)(2,1)S(1)} %get-tuple-element.128), channel_id=4, replica_groups=mesh['groups'=2,'curve'=4,'cross'=2,'sub'=2] {'sub'}, dimensions={1}, use_global_device_ids=true | all-gather | bytes 786432 | tf_op jit(solution)/shard_map/all_gather | solution.py:58
  27.6 2.2 %all-gather.1 = bf16[1,512,512]{2,1,0:T(8,128)(2,1)S(1)} all-gather(bf16[1,256,512]{2,1,0:T(8,128)(2,1)S(1)} %get-tuple-element.124), channel_id=3, replica_groups=mesh['groups'=2,'curve'=4,'cross'=2,'sub'=2] {'sub'}, dimensions={1}, use_global_device_ids=true | all-gather | bytes 786432 | tf_op jit(solution)/shard_map/all_gather | solution.py:58
  29.7 2.2 %all-gather = bf16[1,512,512]{2,1,0:T(8,128)(2,1)S(1)} all-gather(bf16[1,256,512]{2,1,0:T(8,128)(2,1)S(1)} %get-tuple-element.125), channel_id=2, replica_groups=mesh['groups'=2,'curve'=4,'cross'=2,'sub'=2] {'sub'}, dimensions={1}, use_global_device_ids=true | all-gather | bytes 786432 | tf_op jit(solution)/shard_map/all_gather | solution.py:58
  36.2 1.5 prep.1
  37.8 2.1 %all_gather.64.before_ref = bf16[512,128]{1,0:T(8,128)(2,1)S(1)} all-gather(bf16[256,128]{1,0:T(8,128)(2,1)} %collective-permute-done), channel_id=1, replica_groups=mesh['groups'=2,'curve'=4,'cross'=2,'sub'=2] {'sub'}, dimensions={0}, use_global_device_ids=true | all-gather | bytes 196608 | tf_op jit(solution)/shard_map/all_gather | solution.py:58
  39.9 2.1 %all_gather.65.after_ref = bf16[512,128]{1,0:T(8,128)(2,1)S(1)} all-gather(bf16[256,128]{1,0:T(8,128)(2,1)} %collective-permute-done.1), channel_id=1, replica_groups=mesh['groups'=2,'curve'=4,'cross'=2,'sub'=2] {'sub'}, dimensions={0}, use_global_device_ids=true | all-gather | bytes 196608 | tf_op jit(solution)/shard_map/all_gather | solution.py:58
  42.0 2.4 %first.1 = (bf16[512,512]{1,0:T(8,128)(2,1)S(1)}, bf16[512,512]{1,0:T(8,128)(2,1)S(1)}, f32[512,512]{1,0:T(8,128)S(1)}, bf16[512,512]{1,0:T(8,128)(2,1)S(1)}, bf...) custom-call(s32[2]{0:T(128)S(1)} %pad_add_fusion.me_ref.r_0_, ...), custom_call_target="tpu_custom_call" | custom-call | flops 1207959552 | bytes 6787072 | tf_op jit(solution)/shard_map/first/pallas_call | solution.py:31
  44.4 4.5 %collective-permute-start.2 = (bf16[48,512]{1,0:T(8,128)(2,1)S(1)}, bf16[48,512]{1,0:T(8,128)(2,1)S(1)}, u32[]{:S(2)}, u32[]{:S(2)}) collective-permute-start(bf16[48,512]{1,0:T(8,128)(2,1)S(1)} %get-tuple-element.72), channel_id=1, source_target_pairs={{0,2},{2,4},{4,6},{6,8},{8,10},{10,12},{12,14},{3,1},{5,3},{7,5},{... | collective-permute-start | bytes 147464 | tf_op jit(solution)/shard_map/ppermute | solution.py:54
  49.0 2.9 %collective-permute-start.3 = (bf16[48,512]{1,0:T(8,128)(2,1)S(1)}, bf16[48,512]{1,0:T(8,128)(2,1)S(1)}, u32[]{:S(2)}, u32[]{:S(2)}) collective-permute-start(bf16[48,512]{1,0:T(8,128)(2,1)S(1)} %get-tuple-element.73), channel_id=1, source_target_pairs={{0,4},{2,6},{4,8},{6,10},{8,12},{10,14},{5,1},{7,3},{9,5},{11,7},{... | collective-permute-start | bytes 147464 | tf_op jit(solution)/shard_map/ppermute | solution.py:54
  51.9 2.2 %all-gather.5 = bf16[1,512,512]{2,1,0:T(8,128)(2,1)S(1)} all-gather(bf16[1,256,512]{2,1,0:T(8,128)(2,1)S(1)} %copy-done.37), channel_id=7, replica_groups=mesh['groups'=2,'curve'=4,'cross'=2,'sub'=2] {'sub'}, dimensions={1}, use_global_device_ids=true | all-gather | bytes 786432 | tf_op jit(solution)/shard_map/all_gather | solution.py:58
  54.8 1.9 %all_gather.69.one_ref = bf16[96,512]{1,0:T(8,128)(2,1)S(1)} all-gather(bf16[48,512]{1,0:T(8,128)(2,1)S(1)} %collective-permute-done.2), channel_id=1, replica_groups=mesh['groups'=2,'curve'=4,'cross'=2,'sub'=2] {'sub'}, dimensions={0}, use_global_device_ids=true | all-gather | bytes 147456 | tf_op jit(solution)/shard_map/all_gather | solution.py:58
  56.7 1.9 %all_gather.70.two_ref = bf16[96,512]{1,0:T(8,128)(2,1)S(1)} all-gather(bf16[48,512]{1,0:T(8,128)(2,1)S(1)} %collective-permute-done.3), channel_id=1, replica_groups=mesh['groups'=2,'curve'=4,'cross'=2,'sub'=2] {'sub'}, dimensions={0}, use_global_device_ids=true | all-gather | bytes 147456 | tf_op jit(solution)/shard_map/all_gather | solution.py:58
  59.7 4.3 %collective-permute-start.4 = (bf16[32,512]{1,0:T(8,128)(2,1)S(1)}, bf16[32,512]{1,0:T(8,128)(2,1)S(1)}, u32[]{:S(2)}, u32[]{:S(2)}) collective-permute-start(bf16[32,512]{1,0:T(8,128)(2,1)S(1)} %get-tuple-element.75), channel_id=1, source_target_pairs={{0,2},{2,4},{4,6},{6,8},{8,10},{10,12},{12,14},{3,1},{5,3},{7,5},{... | collective-permute-start | bytes 98312 | tf_op jit(solution)/shard_map/ppermute | solution.py:54
  64.1 3.5 %collective-permute-start.5 = (bf16[32,512]{1,0:T(8,128)(2,1)S(1)}, bf16[32,512]{1,0:T(8,128)(2,1)S(1)}, u32[]{:S(2)}, u32[]{:S(2)}) collective-permute-start(bf16[32,512]{1,0:T(8,128)(2,1)S(1)} %get-tuple-element.76), channel_id=1, source_target_pairs={{0,4},{2,6},{4,8},{6,10},{8,12},{10,14},{5,1},{7,3},{9,5},{11,7},{... | collective-permute-start | bytes 98312 | tf_op jit(solution)/shard_map/ppermute | solution.py:54
  67.6 2.2 %all-gather.4 = bf16[1,512,512]{2,1,0:T(8,128)(2,1)S(1)} all-gather(bf16[1,256,512]{2,1,0:T(8,128)(2,1)S(1)} %copy-done.39), channel_id=6, replica_groups=mesh['groups'=2,'curve'=4,'cross'=2,'sub'=2] {'sub'}, dimensions={1}, use_global_device_ids=true | all-gather | bytes 786432 | tf_op jit(solution)/shard_map/all_gather | solution.py:58
  70.3 1.9 %all_gather.72.one_ref = bf16[64,512]{1,0:T(8,128)(2,1)S(1)} all-gather(bf16[32,512]{1,0:T(8,128)(2,1)S(1)} %collective-permute-done.4), channel_id=1, replica_groups=mesh['groups'=2,'curve'=4,'cross'=2,'sub'=2] {'sub'}, dimensions={0}, use_global_device_ids=true | all-gather | bytes 98304 | tf_op jit(solution)/shard_map/all_gather | solution.py:58
  72.1 1.8 %all_gather.73.two_ref = bf16[64,512]{1,0:T(8,128)(2,1)S(1)} all-gather(bf16[32,512]{1,0:T(8,128)(2,1)S(1)} %collective-permute-done.5), channel_id=1, replica_groups=mesh['groups'=2,'curve'=4,'cross'=2,'sub'=2] {'sub'}, dimensions={0}, use_global_device_ids=true | all-gather | bytes 98304 | tf_op jit(solution)/shard_map/all_gather | solution.py:58
  75.1 3.1 %collective-permute-start.6 = (bf16[128,512]{1,0:T(8,128)(2,1)S(1)}, bf16[128,512]{1,0:T(8,128)(2,1)S(1)}, u32[]{:S(2)}, u32[]{:S(2)}) collective-permute-start(bf16[128,512]{1,0:T(8,128)(2,1)S(1)} %get-tuple-element.79), channel_id=1, source_target_pairs={{0,2},{2,4},{4,6},{6,8},{8,10},{10,12},{12,14},{3,1},{5,3},{7,5},{... | collective-permute-start | bytes 393224 | tf_op jit(solution)/shard_map/ppermute | solution.py:54
  78.2 2.2 %all-gather.3 = bf16[1,512,512]{2,1,0:T(8,128)(2,1)S(1)} all-gather(bf16[1,256,512]{2,1,0:T(8,128)(2,1)S(1)} %copy-done.38), channel_id=5, replica_groups=mesh['groups'=2,'curve'=4,'cross'=2,'sub'=2] {'sub'}, dimensions={1}, use_global_device_ids=true | all-gather | bytes 786432 | tf_op jit(solution)/shard_map/all_gather | solution.py:58
  80.4 1.7 collective-permute-done.6
  82.1 2.0 %all_gather.74.rim_ref = bf16[256,512]{1,0:T(8,128)(2,1)S(1)} all-gather(bf16[128,512]{1,0:T(8,128)(2,1)S(1)} %collective-permute-done.6), channel_id=1, replica_groups=mesh['groups'=2,'curve'=4,'cross'=2,'sub'=2] {'sub'}, dimensions={0}, use_global_device_ids=true | all-gather | bytes 393216 | tf_op jit(solution)/shard_map/all_gather | solution.py:58
  84.0 2.7 %second.1 = (bf16[512,512]{1,0:T(8,128)(2,1)S(1)}, bf16[512,512]{1,0:T(8,128)(2,1)S(1)}, bf16[512,512]{1,0:T(8,128)(2,1)S(1)}, bf16[512,512]{1,0:T(8,128)(2,1)S(...) custom-call(s32[2]{0:T(128)S(1)} %pad_add_fusion.me_ref.r_0_, ...), custom_call_target="tpu_custom_call" | custom-call | bytes 7995392 | tf_op jit(solution)/shard_map/second/pallas_call | solution.py:31
  86.7 4.4 %collective-permute-start.7 = (bf16[128,512]{1,0:T(8,128)(2,1)S(1)}, bf16[128,512]{1,0:T(8,128)(2,1)S(1)}, u32[]{:S(2)}, u32[]{:S(2)}) collective-permute-start(bf16[128,512]{1,0:T(8,128)(2,1)S(1)} %get-tuple-element.86), channel_id=1, source_target_pairs={{0,2},{2,4},{4,6},{6,8},{8,10},{10,12},{12,14},{3,1},{5,3},{7,5},{... | collective-permute-start | bytes 393224 | tf_op jit(solution)/shard_map/ppermute | solution.py:54
  91.9 3.1 %collective-permute-done.7 = bf16[128,512]{1,0:T(8,128)(2,1)S(1)} collective-permute-done((bf16[128,512]{1,0:T(8,128)(2,1)S(1)}, bf16[128,512]{1,0:T(8,128)(2,1)S(1)}, u32[]{:S(2)}, u32[]{:S(2)}) %collective-permute-start.7) | collective-permute-done | bytes 131104 | tf_op jit(solution)/shard_map/ppermute | solution.py:54
  95.0 2.0 %all_gather.79.rim_ref = bf16[256,512]{1,0:T(8,128)(2,1)S(1)} all-gather(bf16[128,512]{1,0:T(8,128)(2,1)S(1)} %collective-permute-done.7), channel_id=1, replica_groups=mesh['groups'=2,'curve'=4,'cross'=2,'sub'=2] {'sub'}, dimensions={0}, use_global_device_ids=true | all-gather | bytes 393216 | tf_op jit(solution)/shard_map/all_gather | solution.py:58
  97.0 1.2 lgrad.1
  98.2 4.4 %collective-permute-start.8 = (bf16[32,512]{1,0:T(8,128)(2,1)S(1)}, bf16[32,512]{1,0:T(8,128)(2,1)S(1)}, u32[]{:S(2)}, u32[]{:S(2)}) collective-permute-start(bf16[32,512]{1,0:T(8,128)(2,1)S(1)} %get-tuple-element.89), channel_id=1, source_target_pairs={{0,2},{2,4},{4,6},{6,8},{8,10},{10,12},{12,14},{3,1},{5,3},{7,5},{... | collective-permute-start | bytes 98312 | tf_op jit(solution)/shard_map/ppermute | solution.py:54
  102.6 1.9 %collective-permute-start.9 = (bf16[32,512]{1,0:T(8,128)(2,1)S(1)}, bf16[32,512]{1,0:T(8,128)(2,1)S(1)}, u32[]{:S(2)}, u32[]{:S(2)}) collective-permute-start(bf16[32,512]{1,0:T(8,128)(2,1)S(1)} %get-tuple-element.90), channel_id=1, source_target_pairs={{0,4},{2,6},{4,8},{6,10},{8,12},{10,14},{5,1},{7,3},{9,5},{11,7},{... | collective-permute-start | bytes 98312 | tf_op jit(solution)/shard_map/ppermute | solution.py:54
  104.7 1.9 %all_gather.80.one_ref = bf16[64,512]{1,0:T(8,128)(2,1)S(1)} all-gather(bf16[32,512]{1,0:T(8,128)(2,1)S(1)} %collective-permute-done.8), channel_id=1, replica_groups=mesh['groups'=2,'curve'=4,'cross'=2,'sub'=2] {'sub'}, dimensions={0}, use_global_device_ids=true | all-gather | bytes 98304 | tf_op jit(solution)/shard_map/all_gather | solution.py:58
  106.6 1.8 %all_gather.81.two_ref = bf16[64,512]{1,0:T(8,128)(2,1)S(1)} all-gather(bf16[32,512]{1,0:T(8,128)(2,1)S(1)} %collective-permute-done.9), channel_id=1, replica_groups=mesh['groups'=2,'curve'=4,'cross'=2,'sub'=2] {'sub'}, dimensions={0}, use_global_device_ids=true | all-gather | bytes 98304 | tf_op jit(solution)/shard_map/all_gather | solution.py:58
  110.3 2.2 %grads1.1 = bf16[8,512,128]{2,1,0:T(8,128)(2,1)} custom-call(s32[2]{0:T(128)S(1)} %pad_add_fusion.me_ref.r_0_, bf16[512,512]{1,0:T(8,128)(2,1)S(1)} %get-tuple-element.84.pg_ref.r_1_, bf16[512,512]{1,0:T(8,128)(2,1)S(1)} %get-tuple-element.78.lift_ref.r_2_, bf16[512,512]{1,0:T(8,128)(2,1)S(1)} %get-tuple-element.103.r_3_, ...), custom_call_target="tpu_custom_call" | custom-call | bytes 4194304 | tf_op jit(solution)/shard_map/grads1/pallas_call | solution.py:31
  113.3 4.0 %collective-permute-start.10 = (bf16[32,512]{1,0:T(8,128)(2,1)S(1)}, bf16[32,512]{1,0:T(8,128)(2,1)S(1)}, u32[]{:S(2)}, u32[]{:S(2)}) collective-permute-start(bf16[32,512]{1,0:T(8,128)(2,1)S(1)} %copy-done.35), channel_id=1, source_target_pairs={{0,2},{2,4},{4,6},{6,8},{8,10},{10,12},{12,14},{3,1},{5,3},{7,5},{... | collective-permute-start | bytes 98312 | tf_op jit(solution)/shard_map/ppermute | solution.py:54
  117.3 2.1 %collective-permute-start.11 = (bf16[32,512]{1,0:T(8,128)(2,1)S(1)}, bf16[32,512]{1,0:T(8,128)(2,1)S(1)}, u32[]{:S(2)}, u32[]{:S(2)}) collective-permute-start(bf16[32,512]{1,0:T(8,128)(2,1)S(1)} %copy-done.33), channel_id=1, source_target_pairs={{0,4},{2,6},{4,8},{6,10},{8,12},{10,14},{5,1},{7,3},{9,5},{11,7},{... | collective-permute-start | bytes 98312 | tf_op jit(solution)/shard_map/ppermute | solution.py:54
  119.4 1.9 %all_gather.82.one_ref = bf16[64,512]{1,0:T(8,128)(2,1)S(1)} all-gather(bf16[32,512]{1,0:T(8,128)(2,1)S(1)} %collective-permute-done.10), channel_id=1, replica_groups=mesh['groups'=2,'curve'=4,'cross'=2,'sub'=2] {'sub'}, dimensions={0}, use_global_device_ids=true | all-gather | bytes 98304 | tf_op jit(solution)/shard_map/all_gather | solution.py:58
  121.3 2.2 %all_gather.83.two_ref = bf16[64,512]{1,0:T(8,128)(2,1)S(1)} all-gather(bf16[32,512]{1,0:T(8,128)(2,1)S(1)} %collective-permute-done.11), channel_id=1, replica_groups=mesh['groups'=2,'curve'=4,'cross'=2,'sub'=2] {'sub'}, dimensions={0}, use_global_device_ids=true | all-gather | bytes 98304 | tf_op jit(solution)/shard_map/all_gather | solution.py:58
  123.5 1.2 copy-done.5
  124.8 2.5 %third.1 = (bf16[512,512]{1,0:T(8,128)(2,1)S(1)}, bf16[512,512]{1,0:T(8,128)(2,1)S(1)}, bf16[512,512]{1,0:T(8,128)(2,1)S(1)}, bf16[128,256]{1,0:T(8,128)(2,1)}, bf16[128,256]{1,0:T(8,128)(2,1)}) custom-call(s32[2]{0:T(128)S(1)} %pad_add_fusion.me_ref.r_0_, bf16[512,512]{1,0:T(8,128)(2,1)S(1)} %get-tuple-element.88.v_ref.lg_ref, ...), custom_call_target="tpu_custom_call" | custom-call | bytes 5898240 | tf_op jit(solution)/shard_map/third/pallas_call | solution.py:31
  128.1 2.1 %grads0.1 = bf16[8,384,128]{2,1,0:T(8,128)(2,1)} custom-call(s32[2]{0:T(128)S(1)} %pad_add_fusion.me_ref.r_0_, bf16[512,512]{1,0:T(8,128)(2,1)S(1)} %get-tuple-element.99.pg_ref.r_1_, bf16[512,512]{1,0:T(8,128)(2,1)S(1)} %copy-done.22, bf16[512,512]{1,0:T(8,128)(2,1)S(1)} %copy-done.24, bf16[512,512]{1,0:T(8,128)(2,1)S(1)} %get-tuple-element.98.fb_ref.r_4_, ...), custom_call_target="tpu_custom_call" | custom-call | bytes 3407872 | tf_op jit(solution)/shard_map/grads0/pallas_call | solution.py:31
  131.8 4.4 %all-to-all-start = ((bf16[8,384,128]{2,1,0:T(8,128)(2,1)}), bf16[8,384,128]{2,1,0:T(8,128)(2,1)S(1)}, u32[]{:S(2)}, u32[]{:S(2)}) async-start(bf16[8,384,128]{2,1,0:T(8,128)(2,1)} %grads0.1), calls=%async_computation.2 | async-start | bytes 1572864 | tf_op jit(solution)/shard_map/all_to_all | solution.py:509
  136.9 1.4 collective-permute-start.12
  138.4 4.5 %collective-permute-start.13 = (bf16[128,256]{1,0:T(8,128)(2,1)}, bf16[128,256]{1,0:T(8,128)(2,1)S(1)}, u32[]{:S(2)}, u32[]{:S(2)}) collective-permute-start(bf16[128,256]{1,0:T(8,128)(2,1)} %get-tuple-element.102), channel_id=1, source_target_pairs={{0,2},{2,4},{4,6},{6,8},{8,10},{10,12},{12,14},{1,3},{3,5},{5,7},{... | collective-permute-start | bytes 196616 | tf_op jit(solution)/shard_map/ppermute | solution.py:47
  142.9 1.4 new.1
  147.9 17.9 %all-to-all-done.late_ref = bf16[8,384,128]{2,1,0:T(8,128)(2,1)S(1)} async-done(((bf16[8,384,128]{2,1,0:T(8,128)(2,1)}), bf16[8,384,128]{2,1,0:T(8,128)(2,1)S(1)}, u32[]{:S(2)}, u32[]{:S(2)}) %all-to-all-start) | async-done | bytes 786464 | tf_op jit(solution)/shard_map/all_to_all | solution.py:509
  (123 shorter events, 26.3 us)
Async XLA Ops:
  7.2 129.1 %reduce-scatter.3.cloned.1.call-start = ((), (), s32[]{:S(2)}) async-start(), calls=%async_computation.3 | async-start | bytes 1572864 | tf_op jit(solution)/shard_map/reduce_scatter | solution.py:504
  9.0 7.7 %copy-start.7 = (bf16[256,512]{1,0:T(8,128)(2,1)S(1)}, bf16[256,512]{1,0:T(8,128)(2,1)}, u32[]{:S(2)}) copy-start(bf16[256,512]{1,0:T(8,128)(2,1)} %x_ref.1) | copy-start | bytes 786436
  9.9 27.8 %collective-permute-start = (bf16[256,128]{1,0:T(8,128)(2,1)}, bf16[256,128]{1,0:T(8,128)(2,1)}, u32[]{:S(2)}, u32[]{:S(2)}) collective-permute-start(bf16[256,128]{1,0:T(8,128)(2,1)} %get-tuple-element.59), channel_id=1, source_target_pairs={{0,2},{2,4},{4,6},{6,8},{8,10},{10,12},{12,14},{1,3},{3,5},{5,7},{... | collective-permute-start | bytes 196616 | tf_op jit(solution)/shard_map/ppermute | solution.py:47
  15.4 24.5 %collective-permute-start.1 = (bf16[256,128]{1,0:T(8,128)(2,1)}, bf16[256,128]{1,0:T(8,128)(2,1)}, u32[]{:S(2)}, u32[]{:S(2)}) collective-permute-start(bf16[256,128]{1,0:T(8,128)(2,1)} %get-tuple-element.60), channel_id=1, source_target_pairs={{2,0},{4,2},{6,4},{8,6},{10,8},{12,10},{14,12},{3,1},{5,3},{7,5},{... | collective-permute-start | bytes 196616 | tf_op jit(solution)/shard_map/ppermute | solution.py:47
  16.7 2.5 %copy-start.41 = (bf16[256,512]{1,0:T(8,128)(2,1)S(1)}, bf16[256,512]{1,0:T(8,128)(2,1)}, u32[]{:S(2)}) copy-start(bf16[256,512]{1,0:T(8,128)(2,1)} %param.12) | copy-start | bytes 786436
  19.2 2.3 %copy-start.42 = (bf16[256,512]{1,0:T(8,128)(2,1)S(1)}, bf16[256,512]{1,0:T(8,128)(2,1)}, u32[]{:S(2)}) copy-start(bf16[256,512]{1,0:T(8,128)(2,1)} %param.17) | copy-start | bytes 786436
  21.5 2.3 %copy-start.40 = (bf16[2,256,512]{2,1,0:T(8,128)(2,1)S(1)}, bf16[2,256,512]{2,1,0:T(8,128)(2,1)}, u32[]{:S(2)}) copy-start(bf16[2,256,512]{2,1,0:T(8,128)(2,1)} %param.11) | copy-start | bytes 1572868
  23.8 2.9 %copy-start.36 = (bf16[2,256,1024]{2,1,0:T(8,128)(2,1)S(1)}, bf16[2,256,1024]{2,1,0:T(8,128)(2,1)}, u32[]{:S(2)}) copy-start(bf16[2,256,1024]{2,1,0:T(8,128)(2,1)} %param.10) | copy-start | bytes 3145732
  35.1 1.1 copy-start.13
  36.2 5.8 %copy-start.18 = (bf16[512,512]{1,0:T(8,128)(2,1)S(1)}, bf16[512,512]{1,0:T(8,128)(2,1)}, u32[]{:S(2)}) copy-start(bf16[512,512]{1,0:T(8,128)(2,1)} %all_gather.63.x_ref) | copy-start | bytes 1572868
  37.7 36.2 %copy-start.14 = (bf16[512,128]{1,0:T(8,128)(2,1)}, bf16[512,128]{1,0:T(8,128)(2,1)S(1)}, u32[]{:S(2)}) copy-start(bf16[512,128]{1,0:T(8,128)(2,1)S(1)} %get-tuple-element.66.hot_ref) | copy-start | bytes 393220
  37.7 36.2 %copy-start.16 = (bf16[512,128]{1,0:T(8,128)(2,1)}, bf16[512,128]{1,0:T(8,128)(2,1)S(1)}, u32[]{:S(2)}) copy-start(bf16[512,128]{1,0:T(8,128)(2,1)S(1)} %get-tuple-element.67.slott_ref) | copy-start | bytes 393220
  37.7 46.3 %copy-start.11 = (f32[512,128]{1,0:T(8,128)}, f32[512,128]{1,0:T(8,128)S(1)}, u32[]{:S(2)}) copy-start(f32[512,128]{1,0:T(8,128)S(1)} %get-tuple-element.62.inv_ref) | copy-start | bytes 786436
  37.8 59.3 %copy-start.9 = (bf16[512,256]{1,0:T(8,128)(2,1)}, bf16[512,256]{1,0:T(8,128)(2,1)S(1)}, u32[]{:S(2)}) copy-start(bf16[512,256]{1,0:T(8,128)(2,1)S(1)} %get-tuple-element.87.place_ref) | copy-start | bytes 786436
  42.0 9.9 %copy-start.37 = (bf16[1,256,512]{2,1,0:T(8,128)(2,1)S(1)}, bf16[1,256,512]{2,1,0:T(8,128)(2,1)}, u32[]{:S(2)}) copy-start(bf16[1,256,512]{2,1,0:T(8,128)(2,1)} %get-tuple-element.127) | copy-start | bytes 786436
  44.4 10.4 %copy-start.21 = (bf16[512,512]{1,0:T(8,128)(2,1)}, bf16[512,512]{1,0:T(8,128)(2,1)S(1)}, u32[]{:S(2)}) copy-start(bf16[512,512]{1,0:T(8,128)(2,1)S(1)} %get-tuple-element.107.r_2_) | copy-start | bytes 1572868
  44.4 10.4 %copy-start.23 = (bf16[512,512]{1,0:T(8,128)(2,1)}, bf16[512,512]{1,0:T(8,128)(2,1)S(1)}, u32[]{:S(2)}) copy-start(bf16[512,512]{1,0:T(8,128)(2,1)S(1)} %get-tuple-element.108.r_3_) | copy-start | bytes 1572868
  44.4 10.4 %copy-start.25 = (bf16[512,512]{1,0:T(8,128)(2,1)}, bf16[512,512]{1,0:T(8,128)(2,1)S(1)}, u32[]{:S(2)}) copy-start(bf16[512,512]{1,0:T(8,128)(2,1)S(1)} %get-tuple-element.109.r_5_) | copy-start | bytes 1572868
  44.4 10.4 %collective-permute-start.2 = (bf16[48,512]{1,0:T(8,128)(2,1)S(1)}, bf16[48,512]{1,0:T(8,128)(2,1)S(1)}, u32[]{:S(2)}, u32[]{:S(2)}) collective-permute-start(bf16[48,512]{1,0:T(8,128)(2,1)S(1)} %get-tuple-element.72), channel_id=1, source_target_pairs={{0,2},{2,4},{4,6},{6,8},{8,10},{10,12},{12,14},{3,1},{5,3},{7,5},{... | collective-permute-start | bytes 147464 | tf_op jit(solution)/shard_map/ppermute | solution.py:54
  49.0 7.7 %collective-permute-start.3 = (bf16[48,512]{1,0:T(8,128)(2,1)S(1)}, bf16[48,512]{1,0:T(8,128)(2,1)S(1)}, u32[]{:S(2)}, u32[]{:S(2)}) collective-permute-start(bf16[48,512]{1,0:T(8,128)(2,1)S(1)} %get-tuple-element.73), channel_id=1, source_target_pairs={{0,4},{2,6},{4,8},{6,10},{8,12},{10,14},{5,1},{7,3},{9,5},{11,7},{... | collective-permute-start | bytes 147464 | tf_op jit(solution)/shard_map/ppermute | solution.py:54
  54.8 15.0 %copy-start.4 = (f32[512,512]{1,0:T(8,128)}, f32[512,512]{1,0:T(8,128)S(1)}, u32[]{:S(2)}) copy-start(f32[512,512]{1,0:T(8,128)S(1)} %get-tuple-element.97.slope_ref) | copy-start | bytes 3145732
  58.6 9.0 %copy-start.39 = (bf16[1,256,512]{2,1,0:T(8,128)(2,1)S(1)}, bf16[1,256,512]{2,1,0:T(8,128)(2,1)}, u32[]{:S(2)}) copy-start(bf16[1,256,512]{2,1,0:T(8,128)(2,1)} %get-tuple-element.123) | copy-start | bytes 786436
  59.7 10.5 %collective-permute-start.4 = (bf16[32,512]{1,0:T(8,128)(2,1)S(1)}, bf16[32,512]{1,0:T(8,128)(2,1)S(1)}, u32[]{:S(2)}, u32[]{:S(2)}) collective-permute-start(bf16[32,512]{1,0:T(8,128)(2,1)S(1)} %get-tuple-element.75), channel_id=1, source_target_pairs={{0,2},{2,4},{4,6},{6,8},{8,10},{10,12},{12,14},{3,1},{5,3},{7,5},{... | collective-permute-start | bytes 98312 | tf_op jit(solution)/shard_map/ppermute | solution.py:54
  64.1 8.0 %collective-permute-start.5 = (bf16[32,512]{1,0:T(8,128)(2,1)S(1)}, bf16[32,512]{1,0:T(8,128)(2,1)S(1)}, u32[]{:S(2)}, u32[]{:S(2)}) collective-permute-start(bf16[32,512]{1,0:T(8,128)(2,1)S(1)} %get-tuple-element.76), channel_id=1, source_target_pairs={{0,4},{2,6},{4,8},{6,10},{8,12},{10,14},{5,1},{7,3},{9,5},{11,7},{... | collective-permute-start | bytes 98312 | tf_op jit(solution)/shard_map/ppermute | solution.py:54
  74.0 4.2 %copy-start.38 = (bf16[1,256,512]{2,1,0:T(8,128)(2,1)S(1)}, bf16[1,256,512]{2,1,0:T(8,128)(2,1)}, u32[]{:S(2)}) copy-start(bf16[1,256,512]{2,1,0:T(8,128)(2,1)} %get-tuple-element.126) | copy-start | bytes 786436
  75.1 6.9 %collective-permute-start.6 = (bf16[128,512]{1,0:T(8,128)(2,1)S(1)}, bf16[128,512]{1,0:T(8,128)(2,1)S(1)}, u32[]{:S(2)}, u32[]{:S(2)}) collective-permute-start(bf16[128,512]{1,0:T(8,128)(2,1)S(1)} %get-tuple-element.79), channel_id=1, source_target_pairs={{0,2},{2,4},{4,6},{6,8},{8,10},{10,12},{12,14},{3,1},{5,3},{7,5},{... | collective-permute-start | bytes 393224 | tf_op jit(solution)/shard_map/ppermute | solution.py:54
  86.7 5.1 %copy-start.19 = (bf16[512,512]{1,0:T(8,128)(2,1)}, bf16[512,512]{1,0:T(8,128)(2,1)S(1)}, u32[]{:S(2)}) copy-start(bf16[512,512]{1,0:T(8,128)(2,1)S(1)} %get-tuple-element.82.new_ref) | copy-start | bytes 1572868
  86.7 8.3 %collective-permute-start.7 = (bf16[128,512]{1,0:T(8,128)(2,1)S(1)}, bf16[128,512]{1,0:T(8,128)(2,1)S(1)}, u32[]{:S(2)}, u32[]{:S(2)}) collective-permute-start(bf16[128,512]{1,0:T(8,128)(2,1)S(1)} %get-tuple-element.86), channel_id=1, source_target_pairs={{0,2},{2,4},{4,6},{6,8},{8,10},{10,12},{12,14},{3,1},{5,3},{7,5},{... | collective-permute-start | bytes 393224 | tf_op jit(solution)/shard_map/ppermute | solution.py:54
  98.2 6.6 %collective-permute-start.8 = (bf16[32,512]{1,0:T(8,128)(2,1)S(1)}, bf16[32,512]{1,0:T(8,128)(2,1)S(1)}, u32[]{:S(2)}, u32[]{:S(2)}) collective-permute-start(bf16[32,512]{1,0:T(8,128)(2,1)S(1)} %get-tuple-element.89), channel_id=1, source_target_pairs={{0,2},{2,4},{4,6},{6,8},{8,10},{10,12},{12,14},{3,1},{5,3},{7,5},{... | collective-permute-start | bytes 98312 | tf_op jit(solution)/shard_map/ppermute | solution.py:54
  102.6 4.0 %collective-permute-start.9 = (bf16[32,512]{1,0:T(8,128)(2,1)S(1)}, bf16[32,512]{1,0:T(8,128)(2,1)S(1)}, u32[]{:S(2)}, u32[]{:S(2)}) collective-permute-start(bf16[32,512]{1,0:T(8,128)(2,1)S(1)} %get-tuple-element.90), channel_id=1, source_target_pairs={{0,4},{2,6},{4,8},{6,10},{8,12},{10,14},{5,1},{7,3},{9,5},{11,7},{... | collective-permute-start | bytes 98312 | tf_op jit(solution)/shard_map/ppermute | solution.py:54
  112.6 4.7 %copy-start.33 = (bf16[32,512]{1,0:T(8,128)(2,1)S(1)}, bf16[32,512]{1,0:T(8,128)(2,1)}, u32[]{:S(2)}) copy-start(bf16[32,512]{1,0:T(8,128)(2,1)} %copy-done.32) | copy-start | bytes 98308
  112.6 10.9 %copy-start.12 = (f32[512,128]{1,0:T(8,128)S(1)}, f32[512,128]{1,0:T(8,128)}, u32[]{:S(2)}) copy-start(f32[512,128]{1,0:T(8,128)} %copy-done.11) | copy-start | bytes 786436
  112.6 10.9 %copy-start.17 = (bf16[512,128]{1,0:T(8,128)(2,1)S(1)}, bf16[512,128]{1,0:T(8,128)(2,1)}, u32[]{:S(2)}) copy-start(bf16[512,128]{1,0:T(8,128)(2,1)} %copy-done.16) | copy-start | bytes 393220
  112.6 10.9 %copy-start.15 = (bf16[512,128]{1,0:T(8,128)(2,1)S(1)}, bf16[512,128]{1,0:T(8,128)(2,1)}, u32[]{:S(2)}) copy-start(bf16[512,128]{1,0:T(8,128)(2,1)} %copy-done.14) | copy-start | bytes 393220
  113.3 6.1 %collective-permute-start.10 = (bf16[32,512]{1,0:T(8,128)(2,1)S(1)}, bf16[32,512]{1,0:T(8,128)(2,1)S(1)}, u32[]{:S(2)}, u32[]{:S(2)}) collective-permute-start(bf16[32,512]{1,0:T(8,128)(2,1)S(1)} %copy-done.35), channel_id=1, source_target_pairs={{0,2},{2,4},{4,6},{6,8},{8,10},{10,12},{12,14},{3,1},{5,3},{7,5},{... | collective-permute-start | bytes 98312 | tf_op jit(solution)/shard_map/ppermute | solution.py:54
  117.3 4.0 %collective-permute-start.11 = (bf16[32,512]{1,0:T(8,128)(2,1)S(1)}, bf16[32,512]{1,0:T(8,128)(2,1)S(1)}, u32[]{:S(2)}, u32[]{:S(2)}) collective-permute-start(bf16[32,512]{1,0:T(8,128)(2,1)S(1)} %copy-done.33), channel_id=1, source_target_pairs={{0,4},{2,6},{4,8},{6,10},{8,12},{10,14},{5,1},{7,3},{9,5},{11,7},{... | collective-permute-start | bytes 98312 | tf_op jit(solution)/shard_map/ppermute | solution.py:54
  123.5 1.2 copy-start.5
  124.8 3.3 %copy-start.22 = (bf16[512,512]{1,0:T(8,128)(2,1)S(1)}, bf16[512,512]{1,0:T(8,128)(2,1)}, u32[]{:S(2)}) copy-start(bf16[512,512]{1,0:T(8,128)(2,1)} %copy-done.21) | copy-start | bytes 1572868
  124.8 3.3 %copy-start.24 = (bf16[512,512]{1,0:T(8,128)(2,1)S(1)}, bf16[512,512]{1,0:T(8,128)(2,1)}, u32[]{:S(2)}) copy-start(bf16[512,512]{1,0:T(8,128)(2,1)} %copy-done.23) | copy-start | bytes 1572868
  124.8 3.3 %copy-start.26 = (bf16[512,512]{1,0:T(8,128)(2,1)S(1)}, bf16[512,512]{1,0:T(8,128)(2,1)}, u32[]{:S(2)}) copy-start(bf16[512,512]{1,0:T(8,128)(2,1)} %copy-done.25) | copy-start | bytes 1572868
  131.8 11.2 %copy-start.20 = (bf16[512,512]{1,0:T(8,128)(2,1)S(1)}, bf16[512,512]{1,0:T(8,128)(2,1)}, u32[]{:S(2)}) copy-start(bf16[512,512]{1,0:T(8,128)(2,1)} %copy-done.19) | copy-start | bytes 1572868
  131.8 34.0 %all-to-all-start = ((bf16[8,384,128]{2,1,0:T(8,128)(2,1)}), bf16[8,384,128]{2,1,0:T(8,128)(2,1)S(1)}, u32[]{:S(2)}, u32[]{:S(2)}) async-start(bf16[8,384,128]{2,1,0:T(8,128)(2,1)} %grads0.1), calls=%async_computation.2 | async-start | bytes 1572864 | tf_op jit(solution)/shard_map/all_to_all | solution.py:509
  136.2 30.2 %reduce-scatter.5.cloned.1.call-start = ((), (), s32[]{:S(2)}) async-start(), calls=%async_computation.4 | async-start | bytes 655360 | tf_op jit(solution)/shard_map/reduce_scatter | solution.py:505
  136.2 8.1 %copy-start.3 = (bf16[512,512]{1,0:T(8,128)(2,1)S(1)}, bf16[512,512]{1,0:T(8,128)(2,1)}, u32[]{:S(2)}) copy-start(bf16[512,512]{1,0:T(8,128)(2,1)} %copy-done.2) | copy-start | bytes 1572868
  136.9 7.4 %copy-start.1 = (bf16[512,512]{1,0:T(8,128)(2,1)S(1)}, bf16[512,512]{1,0:T(8,128)(2,1)}, u32[]{:S(2)}) copy-start(bf16[512,512]{1,0:T(8,128)(2,1)} %copy-done) | copy-start | bytes 1572868
  136.9 9.4 %collective-permute-start.12 = (bf16[128,256]{1,0:T(8,128)(2,1)}, bf16[128,256]{1,0:T(8,128)(2,1)S(1)}, u32[]{:S(2)}, u32[]{:S(2)}) collective-permute-start(bf16[128,256]{1,0:T(8,128)(2,1)} %get-tuple-element.101), channel_id=1, source_target_pairs={{2,0},{4,2},{6,4},{8,6},{10,8},{12,10},{14,12},{3,1},{5,3},{7,5},{... | collective-permute-start | bytes 196616 | tf_op jit(solution)/shard_map/ppermute | solution.py:47
  138.4 8.4 %collective-permute-start.13 = (bf16[128,256]{1,0:T(8,128)(2,1)}, bf16[128,256]{1,0:T(8,128)(2,1)S(1)}, u32[]{:S(2)}, u32[]{:S(2)}) collective-permute-start(bf16[128,256]{1,0:T(8,128)(2,1)} %get-tuple-element.102), channel_id=1, source_target_pairs={{0,2},{2,4},{4,6},{6,8},{8,10},{10,12},{12,14},{1,3},{3,5},{5,7},{... | collective-permute-start | bytes 196616 | tf_op jit(solution)/shard_map/ppermute | solution.py:47
  145.3 1.4 copy-start.10
  (12 other events, 10.0 us)
Sparse Core Ops, SparseCore 0:
  112.7 19.7 reduce-scatter.2
  139.4 26.9 reduce-scatter.4

commit v2 on v1

v2 whole, which is shorter than its diff:
```python
import jax
import jax.numpy as jnp
from jax import lax
from jax.experimental import pallas as pl
from jax.experimental.pallas import tpu as pltpu
from jax.sharding import PartitionSpec as P

BF = jnp.bfloat16
F32 = jnp.float32
I32 = jnp.int32
DOM = ("curve", "cross")
LINE = ("curve", "cross", "sub")
NN = (((1,), (0,)), ((), ()))
NT = (((1,), (1,)), ((), ()))
TN = (((0,), (0,)), ((), ()))


def dot(a, b, dims=NN):
    return lax.dot_general(a, b, dims, preferred_element_type=F32)


def sds(shape, dtype):
    return jax.ShapeDtypeStruct(shape, dtype)


def call(body, outs, scalars, arrays, name, flops=0, scratch=()):
    scalars, arrays = list(scalars), list(arrays)
    moved = sum(a.size * a.dtype.itemsize for a in arrays) + sum(
        o.size * o.dtype.itemsize for o in outs
    )
    return pl.pallas_call(
        body,
        out_shape=tuple(outs),
        in_specs=[pl.BlockSpec(memory_space=pltpu.SMEM)] * len(scalars)
        + [pl.BlockSpec(memory_space=pltpu.VMEM)] * len(arrays),
        out_specs=tuple(pl.BlockSpec(memory_space=pltpu.VMEM) for _ in outs),
        scratch_shapes=list(scratch),
        compiler_params=pltpu.CompilerParams(vmem_limit_bytes=20 * 2**20),
        cost_estimate=pl.CostEstimate(flops=flops, bytes_accessed=moved, transcendentals=0),
        name=name,
    )(*scalars, *arrays)


def shifted(value, steps):
    count = lax.axis_size(DOM)
    first, last = (max(0, -steps), min(count, count - steps))
    return lax.ppermute(value, DOM, [(s, s + steps) for s in range(first, last)])


def two_way(value, steps):
    count = lax.axis_size(DOM)
    pairs = [(2 * p, 2 * (p + steps)) for p in range(count - steps)]
    pairs += [(2 * p + 1, 2 * (p - steps) + 1) for p in range(steps, count)]
    return lax.ppermute(value, LINE, pairs)


def gather(value):
    return lax.all_gather(value, "sub", axis=0, tiled=True)


def swap(value):
    return lax.ppermute(value, "sub", [(0, 1), (1, 0)])


def sigmoid(v):
    return 1.0 / (1.0 + jnp.exp(-v))


def slope_of(v):
    s = sigmoid(v)
    return s * (1.0 + v * (1.0 - s))


def wide(col, width):
    return jnp.concatenate([col] * (width // col.shape[1]), axis=1)


def k_halo(rows_ref, x_ref, next_ref, prev_ref):
    x = x_ref[...]
    n = x.shape[1]
    at = lax.broadcasted_iota(I32, (n, rows_ref.shape[1]), 0)
    next_ref[...] = dot(x, (at == rows_ref[0:1, :]).astype(BF)).astype(BF)
    prev_ref[...] = dot(x, (at == rows_ref[1:2, :]).astype(BF)).astype(BF)


def k_weights(me_ref, win_ref, wout_ref, win2_ref, wout2_ref, *outs):
    half = win_ref.shape[1]
    own = pl.multiple_of(me_ref[1] * half, half)
    other = pl.multiple_of((1 - me_ref[1]) * half, half)
    for layer in range(2):
        outs[layer][pl.ds(own, half), :] = win_ref[layer]
        outs[layer][pl.ds(other, half), :] = win2_ref[layer]
        outs[2 + layer][pl.ds(own, half), :] = wout_ref[layer]
        outs[2 + layer][pl.ds(other, half), :] = wout2_ref[layer]


def k_prep(tile_ref, me_ref, mask_ref, rows_ref, par_ref,
           adj_ref, adjt_ref, inv_ref, hott_ref, hot_ref, slot_ref, slott_ref,
           pick_ref, place_ref, tags_ref, ocount_ref):
    blocks, k_slots, length, _ = mask_ref.shape
    n = adj_ref.shape[0]
    nodes = hott_ref.shape[0]
    slots = slot_ref.shape[0]
    cap = slots // 4
    adj_ref[...] = jnp.zeros(adj_ref.shape, BF)
    adjt_ref[...] = jnp.zeros(adjt_ref.shape, BF)
    for b in range(blocks):
        degree = jnp.zeros((length, 1), F32)
        for k in range(k_slots):
            bits = mask_ref[b, k].astype(F32)
            start = pl.multiple_of(tile_ref[b, k] * length, length)
            adj_ref[b * length:(b + 1) * length, pl.ds(start, length)] = bits.astype(BF)
            adjt_ref[pl.ds(start, length), b * length:(b + 1) * length] = bits.T.astype(BF)
            degree = degree + jnp.sum(bits, axis=1, keepdims=True)
        inv_ref[b * length:(b + 1) * length, :] = jnp.broadcast_to(1.0 / degree, (length, 128))
    rel_row = par_ref[...] - me_ref[0] * nodes
    hott = (lax.broadcasted_iota(I32, (nodes, n), 0) == rel_row).astype(F32)
    hott_ref[...] = hott.astype(BF)
    ocount_ref[...] = jnp.broadcast_to(jnp.sum(hott, axis=1, keepdims=True), (nodes, 128))
    hot_ref[...] = hott.T.astype(BF)
    j = lax.broadcasted_iota(I32, (slots, n), 0)
    off = jnp.where(j < cap, 1, jnp.where(j < 2 * cap, -1, jnp.where(j < 3 * cap, 2, -2)))
    start = jnp.where(j < cap, 0, jnp.where(j < 2 * cap, cap, jnp.where(j < 3 * cap, 2 * cap, 3 * cap)))
    node = rel_row - off * nodes
    chosen = ((node >= 0) & (node < nodes)).astype(F32)
    before = lax.broadcasted_iota(I32, (n, n), 0) < lax.broadcasted_iota(I32, (n, n), 1)
    rank = dot(chosen.astype(BF), before.astype(F32).astype(BF))
    fits = jnp.where(rank == (j - start).astype(F32), chosen, 0.0)
    slot_ref[...] = fits.astype(BF)
    slott_ref[...] = fits.T.astype(BF)
    tags = jnp.sum(fits * (node + 1).astype(F32), axis=1, keepdims=True)
    tags_ref[...] = jnp.broadcast_to(tags, (slots, slots)).T[0:tags_ref.shape[0], :].astype(BF)
    width = rows_ref.shape[1]
    at = lax.broadcasted_iota(I32, (n, width), 0)
    for c in range(2):
        place = (at == rows_ref[c:c + 1, :]).astype(F32)
        place_ref[:, c * width:(c + 1) * width] = place.astype(BF)
        pick_ref[c * width:(c + 1) * width, :] = place.T.astype(BF)


def forward(xc, src, adj_ref, inv_ref, win_ref, wo_ref):
    width = xc.shape[1]
    agg = (dot(adj_ref[...], src) * wide(inv_ref[...], width)).astype(BF)
    pre = dot(xc, win_ref[:, 0:width], NT) + dot(agg, win_ref[:, width:], NT)
    hid = (pre * sigmoid(pre)).astype(BF)
    out = (xc.astype(F32) + dot(hid, wo_ref[...], NT)).astype(BF)
    return agg, pre, hid, out


def send_slots(sub, values, slot_ref, one_ref, two_ref):
    cap = slot_ref.shape[0] // 4
    a = pl.multiple_of(sub * cap, cap)
    one_ref[0:cap, :] = dot(slot_ref[pl.ds(a, cap), :], values).astype(BF)
    two_ref[0:cap, :] = dot(slot_ref[pl.ds(a + 2 * cap, cap), :], values).astype(BF)


def k_first(me_ref, x_ref, rims_ref, adj_ref, inv_ref, win_ref, wo_ref,
            slot_ref, tags_ref,
            xc_ref, agg_ref, pre_ref, hid_ref, first_ref, one_ref, two_ref, src):
    n = x_ref.shape[1]
    rim = rims_ref.shape[2]
    half = rims_ref.shape[1] // 2
    xc = x_ref[...].T
    xc_ref[...] = xc
    src[0:n, :] = xc
    for c in range(2):
        src[n:n + rim, c * half:(c + 1) * half] = rims_ref[c, 0:half, :].T
        src[n + rim:, c * half:(c + 1) * half] = rims_ref[c, half:, :].T
    agg, pre, hid, out = forward(xc, src[...], adj_ref, inv_ref, win_ref, wo_ref)
    agg_ref[...] = agg
    pre_ref[...] = pre
    hid_ref[...] = hid
    first_ref[...] = out
    send_slots(me_ref[1], out, slot_ref, one_ref, two_ref)
    cap = slot_ref.shape[0] // 4
    pad = wide(tags_ref[...], one_ref.shape[1])
    one_ref[cap:, :] = pad
    two_ref[cap:, :] = pad


def k_own(hott_ref, v_ref, pre_ref, pool_ref, slope_ref):
    pool_ref[...] = dot(hott_ref[...], v_ref[...])
    slope_ref[...] = slope_of(pre_ref[...])


def k_pool(hott_ref, v_ref, pool_ref):
    pool_ref[...] = dot(hott_ref[...], v_ref[...])


def k_cot(ct_ref, wo_ref, ctc_ref, hg_ref):
    ctc = ct_ref[...].T
    ctc_ref[...] = ctc
    hg_ref[...] = dot(ctc, wo_ref[...])


def arrived_of(got_ref, cap):
    rows = got_ref.shape[1] // 2
    return jnp.concatenate(
        [got_ref[0, 0:cap], got_ref[1, 0:cap], got_ref[0, rows:rows + cap], got_ref[1, rows:rows + cap]],
        axis=0,
    )


def k_coarse(me_ref, pool_ref, ocount_ref, got_ref, cw_ref,
             hits_ref, icount_ref, coarse_ref, cpre_ref, corr_ref, out1_ref, out2_ref):
    nodes, width = pool_ref.shape
    cap = out1_ref.shape[0]
    rows = got_ref.shape[1] // 2
    slots = 4 * cap
    lane = lax.broadcasted_iota(I32, (1, slots), 1)
    t = [got_ref[c, o + cap:o + cap + 1, 0:slots].astype(F32) for o in (0, rows) for c in range(2)]
    tags = jnp.where(lane < cap, t[0], jnp.where(lane < 2 * cap, t[1], jnp.where(lane < 3 * cap, t[2], t[3])))
    node = (lax.broadcasted_iota(I32, (nodes, slots), 0) + 1).astype(F32)
    hits = (node == tags).astype(F32)
    count = jnp.maximum(ocount_ref[...] + jnp.sum(hits, axis=1, keepdims=True), 1.0)
    icount = 1.0 / count
    hits_ref[...] = hits
    icount_ref[...] = icount
    hb = hits.astype(BF)
    total = pool_ref[...] + dot(hb, arrived_of(got_ref, cap))
    coarse = (total * wide(icount, width)).astype(BF)
    cpre = dot(coarse, cw_ref[...], NT)
    corr = (cpre * sigmoid(cpre)).astype(BF)
    coarse_ref[...] = coarse
    cpre_ref[...] = cpre
    corr_ref[...] = corr
    ans = dot(hits.T.astype(BF), corr).astype(BF)
    sub = me_ref[1]
    out1_ref[...] = jnp.where(sub == 0, ans[cap:2 * cap], ans[0:cap])
    out2_ref[...] = jnp.where(sub == 0, ans[3 * cap:], ans[2 * cap:3 * cap])


def spread_back(first, hot_ref, slott_ref, corr, got_ref):
    cap = got_ref.shape[1] // 2
    returned = jnp.concatenate(
        [got_ref[1, 0:cap], got_ref[0, 0:cap], got_ref[1, cap:], got_ref[0, cap:]], axis=0
    )
    total = first.astype(F32) + dot(hot_ref[...], corr) + dot(slott_ref[...], returned)
    return total.astype(BF)


def k_lift(me_ref, first_ref, hot_ref, slott_ref, corr_ref, got_ref, pick_ref,
           lift_ref, msg_ref):
    lifted = spread_back(first_ref[...], hot_ref, slott_ref, corr_ref[...], got_ref)
    lift_ref[...] = lifted
    rim = msg_ref.shape[0]
    at = pl.multiple_of(me_ref[1] * rim, rim)
    msg_ref[...] = dot(pick_ref[pl.ds(at, rim), :], lifted).astype(BF)


def rim_grads(sub, pg, win_ref, inv_ref, adjt_ref, scaled_ref, msg_ref):
    n = pg.shape[0]
    width = win_ref.shape[1] // 2
    rim = msg_ref.shape[0]
    scaled = (dot(pg, win_ref[:, width:]) * wide(inv_ref[...], width)).astype(BF)
    scaled_ref[...] = scaled
    at = pl.multiple_of(n + (1 - sub) * rim, rim)
    msg_ref[...] = dot(adjt_ref[pl.ds(at, rim), :], scaled).astype(BF)


def k_second(me_ref, lift_ref, rim_ref, adj_ref, adjt_ref, inv_ref, win_ref, wo_ref, hg_ref,
             agg_ref, hid_ref, new_ref, pg_ref, scaled_ref, msg_ref, src):
    n = lift_ref.shape[0]
    lifted = lift_ref[...]
    src[0:n, :] = lifted
    src[n:, :] = rim_ref[...]
    agg, pre, hid, out = forward(lifted, src[...], adj_ref, inv_ref, win_ref, wo_ref)
    agg_ref[...] = agg
    hid_ref[...] = hid
    new_ref[...] = out
    pg = (hg_ref[...] * slope_of(pre)).astype(BF)
    pg_ref[...] = pg
    rim_grads(me_ref[1], pg, win_ref, inv_ref, adjt_ref, scaled_ref, msg_ref)


def k_combine(g_ref, pg_ref, win_ref, scaled_ref, adjt_ref, comb_ref):
    n, width = comb_ref.shape
    comb_ref[...] = (
        g_ref[...].astype(F32)
        + dot(pg_ref[...], win_ref[:, 0:width])
        + dot(adjt_ref[0:n, :], scaled_ref[...])
    )


def k_newt(me_ref, new_ref, out_ref):
    half = out_ref.shape[0]
    at = pl.multiple_of(me_ref[1] * half, half)
    out_ref[...] = new_ref[:, pl.ds(at, half)].T


def k_grads(scale, me_ref, pg_ref, h_ref, agg_ref, g_ref, hid_ref, gin_ref, gout_ref):
    half = gin_ref.shape[0]
    width = h_ref.shape[1]
    at = pl.multiple_of(me_ref[1] * half, half)
    pgt = pg_ref[:, pl.ds(at, half)].T
    gin_ref[:, 0:width] = dot(pgt, h_ref[...]) * scale
    gin_ref[:, width:] = dot(pgt, agg_ref[...]) * scale
    gt = g_ref[:, pl.ds(at, half)].T
    gout_ref[...] = dot(gt, hid_ref[...]) * scale


def pack_grads(scale, sub, pg_ref, h_ref, agg_ref, g_ref, hid_ref, out_ref):
    parts, _, piece = out_ref.shape
    width = h_ref.shape[1]
    hidden = hid_ref.shape[1]
    half = width // 2
    at = pl.multiple_of(sub * half, half)
    pgt = pg_ref[:, pl.ds(at, half)].T
    lo = (dot(pgt, h_ref[...]) * scale).astype(BF)
    hi = (dot(pgt, agg_ref[...]) * scale).astype(BF)
    for d in range(parts):
        src, c = (lo, d * piece) if d * piece < width else (hi, d * piece - width)
        out_ref[d, 0:half, :] = src[:, c:c + piece]
    pack_small((dot(hid_ref[...].T, g_ref[:, pl.ds(at, half)]) * scale).astype(BF), out_ref, half)


def pack_small(values, out_ref, row):
    parts, _, piece = out_ref.shape
    small = values.shape[0] // parts
    for d in range(parts):
        for c in range(values.shape[1] // piece):
            start = row + c * small
            out_ref[d, start:start + small, :] = values[d * small:(d + 1) * small, c * piece:(c + 1) * piece]


def k_combine_pack(scale, me_ref, pg_ref, h_ref, agg_ref, g_ref, hid_ref, win_ref, scaled_ref, adjt_ref,
                   comb_ref, out_ref):
    k_combine(g_ref, pg_ref, win_ref, scaled_ref, adjt_ref, comb_ref)
    pack_grads(scale, me_ref[1], pg_ref, h_ref, agg_ref, g_ref, hid_ref, out_ref)


def k_cweight_pack(scale, me_ref, pgrad_ref, coarse_ref, out_ref):
    half = pgrad_ref.shape[1] // 2
    at = pl.multiple_of(me_ref[1] * half, half)
    values = (dot(coarse_ref[...].T, pgrad_ref[:, pl.ds(at, half)]) * scale).astype(BF)
    pack_small(values, out_ref, 0)


def k_lgrad(me_ref, comb_ref, rim_ref, place_ref, slot_ref, lg_ref, one_ref, two_ref):
    rim = rim_ref.shape[0] // 2
    lg = comb_ref[...] + dot(place_ref[:, 0:rim], rim_ref[rim:, :]) + dot(place_ref[:, rim:], rim_ref[0:rim, :])
    lg = lg.astype(BF)
    lg_ref[...] = lg
    send_slots(me_ref[1], lg, slot_ref, one_ref, two_ref)


def k_cgrad(me_ref, pool_ref, got_ref, hits_ref, icount_ref, cpre_ref, cw_ref,
            pgrad_ref, spread_ref, out1_ref, out2_ref):
    cap = out1_ref.shape[0]
    hits = hits_ref[...]
    total = pool_ref[...] + dot(hits.astype(BF), arrived_of(got_ref, cap))
    pgrad = (total * slope_of(cpre_ref[...])).astype(BF)
    pgrad_ref[...] = pgrad
    spread = (dot(pgrad, cw_ref[...]) * wide(icount_ref[...], pgrad.shape[1])).astype(BF)
    spread_ref[...] = spread
    ans = dot(hits.T.astype(BF), spread).astype(BF)
    sub = me_ref[1]
    out1_ref[...] = jnp.where(sub == 0, ans[cap:2 * cap], ans[0:cap])
    out2_ref[...] = jnp.where(sub == 0, ans[3 * cap:], ans[2 * cap:3 * cap])


def k_cweight(scale, me_ref, pgrad_ref, coarse_ref, out_ref):
    half = out_ref.shape[0]
    at = pl.multiple_of(me_ref[1] * half, half)
    out_ref[...] = dot(pgrad_ref[:, pl.ds(at, half)].T, coarse_ref[...]) * scale


def k_third(me_ref, lg_ref, hot_ref, slott_ref, spread_ref, got_ref, wo_ref, slope_ref,
            win_ref, inv_ref, adjt_ref, *rest, scale=None):
    fb_ref, pg_ref, scaled_ref, before_ref, after_ref = rest[-5:] if scale is None else rest[3:8]
    fb = spread_back(lg_ref[...], hot_ref, slott_ref, spread_ref[...], got_ref)
    fb_ref[...] = fb
    pg = (dot(fb, wo_ref[...]) * slope_ref[...]).astype(BF)
    pg_ref[...] = pg
    if scale is not None:
        xc_ref, agg_ref, hid_ref = rest[:3]
        pack_grads(scale, me_ref[1], pg_ref, xc_ref, agg_ref, fb_ref, hid_ref, rest[8])
    n, width = fb.shape
    half = width // 2
    rim = before_ref.shape[0]
    scaled = (dot(pg, win_ref[:, width:]) * wide(inv_ref[...], width)).astype(BF)
    scaled_ref[...] = scaled
    at = pl.multiple_of(me_ref[1] * half, half)
    both = dot(adjt_ref[n:, :], scaled_ref[:, pl.ds(at, half)]).astype(BF)
    before_ref[...] = both[0:rim]
    after_ref[...] = both[rim:]


def k_last(comb_ref, after_ref, before_ref, place_ref, out_ref):
    rim = after_ref.shape[0]
    total = comb_ref[...] + dot(place_ref[:, 0:rim], after_ref[...]) + dot(place_ref[:, rim:], before_ref[...])
    out_ref[...] = total.T


def k_halfcomb(me_ref, fb_ref, pg_ref, win_ref, scaled_ref, adjt_ref, comb_ref):
    n, half = comb_ref.shape
    at = pl.multiple_of(me_ref[1] * half, half)
    cols = pl.ds(at, half)
    comb_ref[...] = (
        fb_ref[:, cols].astype(F32)
        + dot(pg_ref[...], win_ref[:, cols])
        + dot(adjt_ref[0:n, :], scaled_ref[:, cols])
    )


def summed(ref):
    total = ref[0].astype(F32)
    for d in range(1, ref.shape[0]):
        total = total + ref[d].astype(F32)
    return total


def unpack_small(total):
    small = total.shape[0] // 2
    return jnp.concatenate([total[0:small], total[small:]], axis=1)


def k_sum(early_ref, coarse_ref, ein_ref, eout_ref, gco_ref):
    half = ein_ref.shape[0]
    total = summed(early_ref)
    ein_ref[...] = total[0:half]
    eout_ref[...] = unpack_small(total[half:])
    gco_ref[...] = unpack_small(summed(coarse_ref))


def k_sum_late(late_ref, ein_ref, eout_ref, gin_ref, gout_ref):
    half = ein_ref.shape[0]
    total = summed(late_ref)
    gin_ref[0] = total[0:half]
    gin_ref[1] = ein_ref[...]
    gout_ref[0] = unpack_small(total[half:])
    gout_ref[1] = eout_ref[...]


def local(node_features, inward_weight, outward_weight, coarse_weight, tile_index, tile_mask,
          send_rows, parent, cotangent):
    half, n = node_features.shape
    width = 2 * half
    blocks, k_slots = tile_index.shape
    rim = tile_mask.shape[2]
    src_rows = (blocks + 2) * rim
    domains = lax.axis_size(DOM)
    cross = lax.axis_size("cross")
    curve = lax.axis_size("curve")
    cap = n // 16
    nodes = n // 4
    slots = 4 * cap
    hidden = 2 * inward_weight.shape[1]
    scale = float(n * domains) ** -0.5
    me = jnp.stack([lax.axis_index(DOM), lax.axis_index("sub")]).astype(I32)
    rows = send_rows[0]
    packed = 2 * width // domains == 128

    halo_next, halo_prev = call(
        k_halo, [sds((half, rim), BF)] * 2, [], [rows, node_features], "halo")
    before_half = shifted(halo_next, 1)
    after_half = shifted(halo_prev, -1)
    win2, wout2 = swap(inward_weight), swap(outward_weight)
    x_full = gather(node_features)
    (adj, adjt, inv, hott, hot, slot, slott, pick, place, tags, ocount) = call(
        k_prep,
        [sds((n, src_rows), BF), sds((src_rows, n), BF), sds((n, 128), F32), sds((nodes, n), BF),
         sds((n, nodes), BF), sds((slots, n), BF), sds((n, slots), BF), sds((2 * rim, n), BF),
         sds((n, 2 * rim), BF), sds((16, slots), BF), sds((nodes, 128), F32)],
        [tile_index, me], [tile_mask, rows, parent[None, :]], "prep")
    win0, win1, wo0, wo1 = call(
        k_weights, [sds((hidden, 2 * width), BF)] * 2 + [sds((width, hidden), BF)] * 2,
        [me], [inward_weight, outward_weight, win2, wout2], "weights")
    rims = gather(jnp.concatenate([before_half, after_half], axis=0)).reshape(2, width, rim)
    msg = sds((cap + 16, width), BF)
    plain = sds((cap, width), BF)
    cell_bf, cell_f32 = sds((n, width), BF), sds((n, width), F32)
    hid_bf, hid_f32 = sds((n, hidden), BF), sds((n, hidden), F32)
    xc, agg0, pre0, hid0, first, one, two = call(
        k_first,
        [cell_bf, cell_bf, hid_f32, hid_bf, cell_bf, msg, msg],
        [me], [x_full, rims, adj, inv, win0, wo0, slot, tags], "first",
        flops=2 * n * width * (src_rows + 3 * width),
        scratch=[pltpu.VMEM((src_rows, width), BF)])
    one, two, cotangent, coarse_weight = lax.optimization_barrier((one, two, cotangent, coarse_weight))
    one, two = two_way(one, 1), two_way(two, 2)
    own, slope0 = call(k_own, [sds((nodes, width), F32), hid_f32], [], [hott, first, pre0], "own")
    cw = gather(coarse_weight)
    got = gather(jnp.concatenate([one, two], axis=0)).reshape(2, -1, width)
    node_bf, node_f32 = sds((nodes, width), BF), sds((nodes, width), F32)
    hits, icount, coarse, cpre, corr, one, two = call(
        k_coarse, [sds((nodes, slots), F32), sds((nodes, 128), F32), node_bf, node_f32, node_bf, plain, plain],
        [me], [own, ocount, got, cw], "coarse")
    one, two, cotangent = lax.optimization_barrier((one, two, cotangent))
    one, two = two_way(one, 1), two_way(two, 2)
    ct_full = gather(cotangent)
    ctc, hg1 = call(k_cot, [cell_bf, hid_f32], [], [ct_full, wo1], "cot")
    got = gather(jnp.concatenate([one, two], axis=0)).reshape(2, -1, width)
    lifted, rims = call(
        k_lift, [cell_bf, sds((rim, width), BF)], [me],
        [first, hot, slott, corr, got, pick], "lift")
    rims = gather(two_way(rims, 1))
    agg1, hid1, new, pg1, scaled1, rims = call(
        k_second, [cell_bf, hid_bf, cell_bf, hid_bf, cell_bf, sds((rim, width), BF)],
        [me], [lifted, rims, adj, adjt, inv, win1, wo1, hg1], "second",
        scratch=[pltpu.VMEM((src_rows, width), BF)])
    rims = two_way(rims, 1)
    piece = 2 * width // domains
    small = hidden // domains
    pack = sds((domains, half + 2 * small, piece), BF)
    if packed:
        comb1, early = call(lambda *r: k_combine_pack(scale, *r), [cell_f32, pack], [me],
                            [pg1, lifted, agg1, ctc, hid1, win1, scaled1, adjt], "combine")
    else:
        comb1, = call(k_combine, [cell_f32], [], [ctc, pg1, win1, scaled1, adjt], "combine")
    rims = gather(rims)
    lg, one, two = call(
        k_lgrad, [cell_bf, plain, plain], [me], [comb1, rims, place, slot], "lgrad")
    if packed:
        one, two, early = lax.optimization_barrier((one, two, early))
    one, two = two_way(one, 1), two_way(two, 2)
    own_g, = call(k_pool, [node_f32], [], [hott, lg], "own_grad")
    new_t, = call(k_newt, [sds((half, n), BF)], [me], [new], "new")
    got = gather(jnp.concatenate([one, two], axis=0)).reshape(2, -1, width)
    pgrad, spread, one, two = call(
        k_cgrad, [node_bf, node_bf, plain, plain], [me],
        [own_g, got, hits, icount, cpre, cw], "cgrad")
    one, two = two_way(one, 1), two_way(two, 2)
    got = gather(jnp.concatenate([one, two], axis=0)).reshape(2, -1, width)
    rim_half = sds((rim, half), BF)
    back_outs = [cell_bf, hid_bf, cell_bf, rim_half, rim_half]
    back_args = [lg, hot, slott, spread, got, wo0, slope0, win0, inv, adjt]
    if packed:
        early = lax.all_to_all(early, DOM, 0, 0, tiled=True)
        gco, = call(lambda *r: k_cweight_pack(scale, *r), [sds((domains, 2 * small, piece), BF)], [me],
                    [pgrad, coarse], "cweight")
        gco = lax.all_to_all(gco, DOM, 0, 0, tiled=True)
        fb, pg0, scaled0, to_before, to_after, late = call(
            lambda *r: k_third(*r, scale=scale), back_outs + [pack], [me], back_args + [xc, agg0, hid0], "third")
        late = lax.all_to_all(late, DOM, 0, 0, tiled=True)
    else:
        gco, = call(lambda *r: k_cweight(scale, *r), [sds((half, width), F32)], [me], [pgrad, coarse], "cweight")
        fb, pg0, scaled0, to_before, to_after = call(k_third, back_outs, [me], back_args, "third")
    from_after = shifted(to_before, -1)
    from_before = shifted(to_after, 1)
    comb0, = call(k_halfcomb, [sds((n, half), F32)], [me], [fb, pg0, win0, scaled0, adjt], "halfcomb")
    fgrad, = call(k_last, [sds((half, n), F32)], [], [comb0, from_after, from_before, place], "last")
    if packed:
        ein, eout, gco = call(
            k_sum, [sds((half, piece), F32), sds((small, half), F32), sds((small, half), F32)],
            [], [early, gco], "sums")
        gin, gout = call(
            k_sum_late, [sds((2, half, piece), F32), sds((2, small, half), F32)], [], [late, ein, eout], "late")
        gout = gout.swapaxes(1, 2)
        gco = gco.T
    else:
        shapes = [sds((half, 2 * width), F32), sds((half, hidden), F32)]
        gi1, go1 = call(lambda *r: k_grads(scale, *r), shapes, [me], [pg1, lifted, agg1, ctc, hid1], "grads1")
        gi0, go0 = call(lambda *r: k_grads(scale, *r), shapes, [me], [pg0, xc, agg0, fb, hid0], "grads0")
        gin = lax.psum_scatter(jnp.stack([gi0, gi1]), DOM, scatter_dimension=2, tiled=True)
        gout = lax.psum_scatter(jnp.stack([go0, go1]), DOM, scatter_dimension=2, tiled=True)
        gco = lax.psum_scatter(gco, DOM, scatter_dimension=1, tiled=True)
    return new_t, fgrad, gin, gout, gco


def solution(mesh):
    cells = ("groups", "curve", "cross")
    in_specs = (
        P("sub", cells),
        P(None, "sub", None),
        P(None, "sub", None),
        P("sub", None),
        P(cells, None),
        P(cells, None, None, None),
        P(cells, None, None),
        P(cells),
        P("sub", cells),
    )
    out_specs = (
        P("sub", cells),
        P("sub", cells),
        P("groups", "sub", ("curve", "cross")),
        P("groups", "sub", ("curve", "cross")),
        P(("groups", "sub"), ("curve", "cross")),
    )
    return jax.shard_map(local, mesh=mesh, in_specs=in_specs, out_specs=out_specs, check_vma=False)
```

time: 177 us -> 163 us (0.921)
  between operations: 14.5 us -> 1.22 us
  starting transfers between devices: 52.3 us -> 64.8 us
  blocking collectives: 43.5 us -> 33.3 us
  waiting for transfers between devices: 24.4 us -> 19.9 us
  local copies, waits for them, and re-layouts: 15.6 us -> 18.1 us
  Pallas kernels: 26.1 us -> 23.9 us
    all_gather x21 -> x10, blocking collectives: 43.5 us -> 20.4 us  [gather(): return lax.all_gather(value, 'sub', axis=0, tiled=True)]
    all_to_all x0 -> x1, blocking collectives: none -> 12.9 us  [local(): gco = lax.all_to_all(gco, DOM, 0, 0, tiled=True)]
    all_to_all x1, waiting for transfers between devices: 17.9 us -> 7.82 us  [local(): late = lax.all_to_all(late, DOM, 0, 0, tiled=True)]
    ppermute x10, waiting for transfers between devices: 4.84 us -> 11.1 us  [two_way(): return lax.ppermute(value, LINE, pairs)]
    all_to_all x1, starting transfers between devices: 4.4 us -> 10.4 us  [local(): late = lax.all_to_all(late, DOM, 0, 0, tiled=True)]
    unnamed x89 -> x84, local copies, waits for them, and re-layouts: 13.1 us -> 18.1 us
    all_to_all x0 -> x1, starting transfers between devices: none -> 3.59 us  [local(): early = lax.all_to_all(early, DOM, 0, 0, tiled=True)]
    ppermute x10, starting transfers between devices: 35.1 us -> 38 us  [two_way(): return lax.ppermute(value, LINE, pairs)]
  transfers between devices with their start and end apart: 17 -> 18, of which waited for: 5 -> 7; matrix products, arithmetic and copies ran while one was open for 1% -> 0% of each run, Pallas kernels for 7% -> 7%
where the time goes in v2:
time: 163 us; the launch traced here: 161 us
  starting transfers between devices  64.8 us (40%)
  blocking collectives  33.3 us (20%)
  Pallas kernels  23.9 us (15%)
  waiting for transfers between devices  19.9 us (12%)
  local copies, waits for them, and re-layouts  18.1 us (11%)
    ppermute x10, starting transfers between devices, two_way(): return lax.ppermute(value, LINE, pairs)  38 us
    pallas_call x20, Pallas kernels, call(): pl.pallas_call(body, out_shape=tuple(outs), in_specs=[pl.BlockSpec(memory...  23.9 us
    all_gather x10, blocking collectives, gather(): return lax.all_gather(value, 'sub', axis=0, tiled=True)  20.4 us
    unnamed x84, local copies, waits for them, and re-layouts  18.1 us
    all_to_all x1, blocking collectives, local(): gco = lax.all_to_all(gco, DOM, 0, 0, tiled=True)  12.9 us
    ppermute x4, starting transfers between devices, shifted(): lax.ppermute(value, DOM, [(s, s + steps) for s in range(first, last)])  12.2 us
    ppermute x10, waiting for transfers between devices, two_way(): return lax.ppermute(value, LINE, pairs)  11.1 us
    all_to_all x1, starting transfers between devices, local(): late = lax.all_to_all(late, DOM, 0, 0, tiled=True)  10.4 us
  transfers between devices with their start and end apart: 18, of which 7 were waited for; matrix products, arithmetic and copies ran while one was open for 0% of the time, Pallas kernels for 7%

profile of v2, /device:TPU:0, one launch (start us, length us, event | category | flops | bytes accessed | tf_op | source)
XLA Modules:
  0.0 161.4 jit_solution(238406173909800504)
XLA Ops:
  2.6 5.0 %collective-permute-start = (bf16[256,128]{1,0:T(8,128)(2,1)S(1)}, bf16[256,128]{1,0:T(8,128)(2,1)S(1)}, u32[]{:S(2)}, u32[]{:S(2)}) collective-permute-start(bf16[256,128]{1,0:T(8,128)(2,1)S(1)} %get-tuple-element.78), channel_id=1, source_target_pairs={{0,2},{2,4},{4,6},{6,8},{8,10},{10,12},{12,14},{1,3},{3,5},{5,7},{... | collective-permute-start | bytes 196616 | tf_op jit(solution)/shard_map/ppermute | solution.py:47
  7.5 1.3 collective-permute-start.1
  8.9 2.3 %all_gather.30.x_ref = bf16[512,512]{1,0:T(8,128)(2,1)S(1)} all-gather(bf16[256,512]{1,0:T(8,128)(2,1)S(1)} %copy-done.3), channel_id=1, replica_groups=mesh['groups'=2,'curve'=4,'cross'=2,'sub'=2] {'sub'}, dimensions={0}, use_global_device_ids=true | all-gather | bytes 786432 | tf_op jit(solution)/shard_map/all_gather | solution.py:58
  11.3 1.3 prep.1
  13.7 2.0 %all_gather.31 = bf16[1024,128]{1,0:T(8,128)(2,1)S(1)} all-gather(bf16[512,128]{1,0:T(8,128)(2,1)S(1)} %pad_maximum_fusion), channel_id=1, replica_groups=mesh['groups'=2,'curve'=4,'cross'=2,'sub'=2] {'sub'}, dimensions={0}, use_global_device_ids=true | all-gather | bytes 393216 | tf_op jit(solution)/shard_map/all_gather | solution.py:58
  16.8 1.3 weights.1
  18.1 2.4 %first.1 = (bf16[512,512]{1,0:T(8,128)(2,1)S(1)}, bf16[512,512]{1,0:T(8,128)(2,1)S(1)}, f32[512,512]{1,0:T(8,128)S(1)}, bf16[512,512]{1,0:T(8,128)(2,1)S(1)}, bf...) custom-call(s32[2]{0:T(128)S(1)} %pad_add_fusion.me_ref.r_0_, ...), custom_call_target="tpu_custom_call" | custom-call | flops 1207959552 | bytes 6787072 | tf_op jit(solution)/shard_map/first/pallas_call | solution.py:31
  20.5 4.3 %collective-permute-start.4 = (bf16[48,512]{1,0:T(8,128)(2,1)S(1)}, bf16[48,512]{1,0:T(8,128)(2,1)S(1)}, u32[]{:S(2)}, u32[]{:S(2)}) collective-permute-start(bf16[48,512]{1,0:T(8,128)(2,1)S(1)} %get-tuple-element.95), channel_id=1, source_target_pairs={{0,2},{2,4},{4,6},{6,8},{8,10},{10,12},{12,14},{3,1},{5,3},{7,5},{... | collective-permute-start | bytes 147464 | tf_op jit(solution)/shard_map/ppermute | solution.py:54
  24.8 3.5 %collective-permute-start.5 = (bf16[48,512]{1,0:T(8,128)(2,1)S(1)}, bf16[48,512]{1,0:T(8,128)(2,1)S(1)}, u32[]{:S(2)}, u32[]{:S(2)}) collective-permute-start(bf16[48,512]{1,0:T(8,128)(2,1)S(1)} %get-tuple-element.96), channel_id=1, source_target_pairs={{0,4},{2,6},{4,8},{6,10},{8,12},{10,14},{5,1},{7,3},{9,5},{11,7},{... | collective-permute-start | bytes 147464 | tf_op jit(solution)/shard_map/ppermute | solution.py:54
  28.4 2.2 %all_gather.33.cw_ref = bf16[512,512]{1,0:T(8,128)(2,1)S(1)} all-gather(bf16[256,512]{1,0:T(8,128)(2,1)S(1)} %copy-done.40), channel_id=1, replica_groups=mesh['groups'=2,'curve'=4,'cross'=2,'sub'=2] {'sub'}, dimensions={0}, use_global_device_ids=true | all-gather | bytes 786432 | tf_op jit(solution)/shard_map/all_gather | solution.py:58
  31.3 1.9 %all_gather.32 = bf16[192,512]{1,0:T(8,128)(2,1)S(1)} all-gather(bf16[96,512]{1,0:T(8,128)(2,1)S(1)} %pad_maximum_fusion.1), channel_id=1, replica_groups=mesh['groups'=2,'curve'=4,'cross'=2,'sub'=2] {'sub'}, dimensions={0}, use_global_device_ids=true | all-gather | bytes 294912 | tf_op jit(solution)/shard_map/all_gather | solution.py:58
  33.3 1.1 coarse.1
  34.4 3.5 %collective-permute-start.6 = (bf16[32,512]{1,0:T(8,128)(2,1)S(1)}, bf16[32,512]{1,0:T(8,128)(2,1)S(1)}, u32[]{:S(2)}, u32[]{:S(2)}) collective-permute-start(bf16[32,512]{1,0:T(8,128)(2,1)S(1)} %get-tuple-element.102), channel_id=1, source_target_pairs={{0,2},{2,4},{4,6},{6,8},{8,10},{10,12},{12,14},{3,1},{5,3},{7,5},{... | collective-permute-start | bytes 98312 | tf_op jit(solution)/shard_map/ppermute | solution.py:54
  38.0 3.5 %collective-permute-start.7 = (bf16[32,512]{1,0:T(8,128)(2,1)S(1)}, bf16[32,512]{1,0:T(8,128)(2,1)S(1)}, u32[]{:S(2)}, u32[]{:S(2)}) collective-permute-start(bf16[32,512]{1,0:T(8,128)(2,1)S(1)} %get-tuple-element.103), channel_id=1, source_target_pairs={{0,4},{2,6},{4,8},{6,10},{8,12},{10,14},{5,1},{7,3},{9,5},{11,7},{... | collective-permute-start | bytes 98312 | tf_op jit(solution)/shard_map/ppermute | solution.py:54
  41.5 1.6 collective-permute-done.7
  43.0 1.9 %all_gather.34 = bf16[128,512]{1,0:T(8,128)(2,1)S(1)} all-gather(bf16[64,512]{1,0:T(8,128)(2,1)S(1)} %pad_maximum_fusion.2), channel_id=1, replica_groups=mesh['groups'=2,'curve'=4,'cross'=2,'sub'=2] {'sub'}, dimensions={0}, use_global_device_ids=true | all-gather | bytes 196608 | tf_op jit(solution)/shard_map/all_gather | solution.py:58
  44.9 1.1 lift.1
  46.1 2.8 %collective-permute-start.8 = (bf16[128,512]{1,0:T(8,128)(2,1)S(1)}, bf16[128,512]{1,0:T(8,128)(2,1)S(1)}, u32[]{:S(2)}, u32[]{:S(2)}) collective-permute-start(bf16[128,512]{1,0:T(8,128)(2,1)S(1)} %get-tuple-element.106), channel_id=1, source_target_pairs={{0,2},{2,4},{4,6},{6,8},{8,10},{10,12},{12,14},{3,1},{5,3},{7,5},{... | collective-permute-start | bytes 393224 | tf_op jit(solution)/shard_map/ppermute | solution.py:54
  48.9 2.2 %all_gather.36.ct_ref = bf16[512,512]{1,0:T(8,128)(2,1)S(1)} all-gather(bf16[256,512]{1,0:T(8,128)(2,1)S(1)} %copy-done.41), channel_id=1, replica_groups=mesh['groups'=2,'curve'=4,'cross'=2,'sub'=2] {'sub'}, dimensions={0}, use_global_device_ids=true | all-gather | bytes 786432 | tf_op jit(solution)/shard_map/all_gather | solution.py:58
  51.6 1.2 collective-permute-done.8
  52.8 2.0 %all_gather.35.rim_ref = bf16[256,512]{1,0:T(8,128)(2,1)S(1)} all-gather(bf16[128,512]{1,0:T(8,128)(2,1)S(1)} %collective-permute-done.8), channel_id=1, replica_groups=mesh['groups'=2,'curve'=4,'cross'=2,'sub'=2] {'sub'}, dimensions={0}, use_global_device_ids=true | all-gather | bytes 393216 | tf_op jit(solution)/shard_map/all_gather | solution.py:58
  54.8 2.7 %second.1 = (bf16[512,512]{1,0:T(8,128)(2,1)S(1)}, bf16[512,512]{1,0:T(8,128)(2,1)S(1)}, bf16[512,512]{1,0:T(8,128)(2,1)S(1)}, bf16[512,512]{1,0:T(8,128)(2,1)S(...) custom-call(s32[2]{0:T(128)S(1)} %pad_add_fusion.me_ref.r_0_, ...), custom_call_target="tpu_custom_call" | custom-call | bytes 7995392 | tf_op jit(solution)/shard_map/second/pallas_call | solution.py:31
  58.2 4.4 %collective-permute-start.9 = (bf16[128,512]{1,0:T(8,128)(2,1)S(1)}, bf16[128,512]{1,0:T(8,128)(2,1)S(1)}, u32[]{:S(2)}, u32[]{:S(2)}) collective-permute-start(bf16[128,512]{1,0:T(8,128)(2,1)S(1)} %get-tuple-element.119), channel_id=1, source_target_pairs={{0,2},{2,4},{4,6},{6,8},{8,10},{10,12},{12,14},{3,1},{5,3},{7,5},{... | collective-permute-start | bytes 393224 | tf_op jit(solution)/shard_map/ppermute | solution.py:54
  62.6 1.7 %combine.1 = (f32[512,512]{1,0:T(8,128)S(1)}, bf16[8,384,128]{2,1,0:T(8,128)(2,1)S(1)}) custom-call(s32[2]{0:T(128)S(1)} %pad_add_fusion.me_ref.r_0_, bf16[512,512]{1,0:T(8,128)(2,1)S(1)} %get-tuple-element.113.r_1_, bf16[512,512]{1,0:T(8,128)(2,1)S(1)} %get-tuple-element.105.lift_ref.r_2_, bf16[512,512]{1,0:T(8,128)(2,1)S(1)} %get-tuple-element.114.r_3_, ...), custom_call_target="tpu_custom_call" | custom-call | bytes 6815744 | tf_op jit(solution)/shard_map/combine/pallas_call | solution.py:31
  65.2 1.3 collective-permute-done.9
  66.5 2.0 %all_gather.37.rim_ref = bf16[256,512]{1,0:T(8,128)(2,1)S(1)} all-gather(bf16[128,512]{1,0:T(8,128)(2,1)S(1)} %collective-permute-done.9), channel_id=1, replica_groups=mesh['groups'=2,'curve'=4,'cross'=2,'sub'=2] {'sub'}, dimensions={0}, use_global_device_ids=true | all-gather | bytes 393216 | tf_op jit(solution)/shard_map/all_gather | solution.py:58
  68.5 1.2 lgrad.1
  69.7 4.4 %collective-permute-start.10 = (bf16[32,512]{1,0:T(8,128)(2,1)S(1)}, bf16[32,512]{1,0:T(8,128)(2,1)S(1)}, u32[]{:S(2)}, u32[]{:S(2)}) collective-permute-start(bf16[32,512]{1,0:T(8,128)(2,1)S(1)} %get-tuple-element.125), channel_id=1, source_target_pairs={{0,2},{2,4},{4,6},{6,8},{8,10},{10,12},{12,14},{3,1},{5,3},{7,5},{... | collective-permute-start | bytes 98312 | tf_op jit(solution)/shard_map/ppermute | solution.py:54
  74.1 4.2 %collective-permute-start.11 = (bf16[32,512]{1,0:T(8,128)(2,1)S(1)}, bf16[32,512]{1,0:T(8,128)(2,1)S(1)}, u32[]{:S(2)}, u32[]{:S(2)}) collective-permute-start(bf16[32,512]{1,0:T(8,128)(2,1)S(1)} %get-tuple-element.126), channel_id=1, source_target_pairs={{0,4},{2,6},{4,8},{6,10},{8,12},{10,14},{5,1},{7,3},{9,5},{11,7},{... | collective-permute-start | bytes 98312 | tf_op jit(solution)/shard_map/ppermute | solution.py:54
  78.5 1.3 collective-permute-done.11
  79.9 1.9 %all_gather.38 = bf16[128,512]{1,0:T(8,128)(2,1)S(1)} all-gather(bf16[64,512]{1,0:T(8,128)(2,1)S(1)} %pad_maximum_fusion.3), channel_id=1, replica_groups=mesh['groups'=2,'curve'=4,'cross'=2,'sub'=2] {'sub'}, dimensions={0}, use_global_device_ids=true | all-gather | bytes 196608 | tf_op jit(solution)/shard_map/all_gather | solution.py:58
  81.8 1.0 cgrad.1
  84.8 12.9 %all_to_all.15.coarse_ref = bf16[8,128,128]{2,1,0:T(8,128)(2,1)} all-to-all(bf16[8,128,128]{2,1,0:T(8,128)(2,1)S(1)} %cweight.1), channel_id=1, replica_groups=mesh['groups'=2,'curve'=4,'cross'=2,'sub'=2] {'curve','cross'}, dimensions={0} | all-to-all | bytes 524288 | tf_op jit(solution)/shard_map/all_to_all | solution.py:532
  97.8 3.6 %all-to-all-start.1 = ((bf16[8,384,128]{2,1,0:T(8,128)(2,1)}), bf16[8,384,128]{2,1,0:T(8,128)(2,1)S(1)}, u32[]{:S(2)}, u32[]{:S(2)}) async-start(bf16[8,384,128]{2,1,0:T(8,128)(2,1)} %copy-done.8), calls=%async_computation.1 | async-start | bytes 1572864 | tf_op jit(solution)/shard_map/all_to_all | solution.py:529
  101.4 3.9 %collective-permute-start.12 = (bf16[32,512]{1,0:T(8,128)(2,1)}, bf16[32,512]{1,0:T(8,128)(2,1)S(1)}, u32[]{:S(2)}, u32[]{:S(2)}) collective-permute-start(bf16[32,512]{1,0:T(8,128)(2,1)} %copy-done.39), channel_id=1, source_target_pairs={{0,2},{2,4},{4,6},{6,8},{8,10},{10,12},{12,14},{3,1},{5,3},{7,5},{... | collective-permute-start | bytes 98312 | tf_op jit(solution)/shard_map/ppermute | solution.py:54
  105.3 3.4 %collective-permute-start.13 = (bf16[32,512]{1,0:T(8,128)(2,1)}, bf16[32,512]{1,0:T(8,128)(2,1)S(1)}, u32[]{:S(2)}, u32[]{:S(2)}) collective-permute-start(bf16[32,512]{1,0:T(8,128)(2,1)} %copy-done.38), channel_id=1, source_target_pairs={{0,4},{2,6},{4,8},{6,10},{8,12},{10,14},{5,1},{7,3},{9,5},{11,7},{... | collective-permute-start | bytes 98312 | tf_op jit(solution)/shard_map/ppermute | solution.py:54
  108.7 5.7 %collective-permute-done.13 = bf16[32,512]{1,0:T(8,128)(2,1)S(1)} collective-permute-done((bf16[32,512]{1,0:T(8,128)(2,1)}, bf16[32,512]{1,0:T(8,128)(2,1)S(1)}, u32[]{:S(2)}, u32[]{:S(2)}) %collective-permute-start.13) | collective-permute-done | bytes 32800 | tf_op jit(solution)/shard_map/ppermute | solution.py:54
  114.4 2.0 %all_gather.39 = bf16[128,512]{1,0:T(8,128)(2,1)S(1)} all-gather(bf16[64,512]{1,0:T(8,128)(2,1)S(1)} %pad_maximum_fusion.4), channel_id=1, replica_groups=mesh['groups'=2,'curve'=4,'cross'=2,'sub'=2] {'sub'}, dimensions={0}, use_global_device_ids=true | all-gather | bytes 196608 | tf_op jit(solution)/shard_map/all_gather | solution.py:58
  116.4 1.2 copy-done.1
  117.6 1.0 copy-done.12
  121.8 2.6 %third.1 = (bf16[512,512]{1,0:T(8,128)(2,1)S(1)}, bf16[512,512]{1,0:T(8,128)(2,1)S(1)}, bf16[512,512]{1,0:T(8,128)(2,1)S(1)}, bf16[128,256]{1,0:T(8,128)(2,1)S(1...) custom-call(s32[2]{0:T(128)S(1)} %pad_add_fusion.me_ref.r_0_, ...), custom_call_target="tpu_custom_call" | custom-call | bytes 8781824 | tf_op jit(solution)/shard_map/third/pallas_call | solution.py:31
  129.0 10.4 %all-to-all-start = ((bf16[8,384,128]{2,1,0:T(8,128)(2,1)}), bf16[8,384,128]{2,1,0:T(8,128)(2,1)S(1)}, u32[]{:S(2)}, u32[]{:S(2)}) async-start(bf16[8,384,128]{2,1,0:T(8,128)(2,1)} %copy-done.9), calls=%async_computation | async-start | bytes 1572864 | tf_op jit(solution)/shard_map/all_to_all | solution.py:535
  139.5 1.4 collective-permute-start.14
  140.9 4.5 %collective-permute-start.15 = (bf16[128,256]{1,0:T(8,128)(2,1)S(1)}, bf16[128,256]{1,0:T(8,128)(2,1)S(1)}, u32[]{:S(2)}, u32[]{:S(2)}) collective-permute-start(bf16[128,256]{1,0:T(8,128)(2,1)S(1)} %copy-done.36), channel_id=1, source_target_pairs={{0,2},{2,4},{4,6},{6,8},{8,10},{10,12},{12,14},{1,3},{3,5},{5,7},{... | collective-permute-start | bytes 196616 | tf_op jit(solution)/shard_map/ppermute | solution.py:47
  146.5 1.4 new.1
  147.9 1.0 copy-done.22
  151.0 1.1 last.1
  152.8 7.8 %all-to-all-done.late_ref = bf16[8,384,128]{2,1,0:T(8,128)(2,1)S(1)} async-done(((bf16[8,384,128]{2,1,0:T(8,128)(2,1)}), bf16[8,384,128]{2,1,0:T(8,128)(2,1)S(1)}, u32[]{:S(2)}, u32[]{:S(2)}) %all-to-all-start) | async-done | bytes 786464 | tf_op jit(solution)/shard_map/all_to_all | solution.py:535
  (109 shorter events, 21.5 us)
Async XLA Ops:
  0.6 15.1 %collective-permute-start.2 = (bf16[2,256,1024]{2,1,0:T(8,128)(2,1)}, bf16[2,256,1024]{2,1,0:T(8,128)(2,1)S(1)}, u32[]{:S(2)}, u32[]{:S(2)}) collective-permute-start(bf16[2,256,1024]{2,1,0:T(8,128)(2,1)} %win_ref.1), channel_id=1, source_target_pairs={{0,1},{1,0},{2,3},{3,2},{4,5},{5,4},{6,7},{7,6},{8,9},{9,8},{10,11... | collective-permute-start | bytes 3145736 | tf_op jit(solution)/shard_map/ppermute | solution.py:62
  1.2 14.6 %collective-permute-start.3 = (bf16[2,256,512]{2,1,0:T(8,128)(2,1)}, bf16[2,256,512]{2,1,0:T(8,128)(2,1)}, u32[]{:S(2)}, u32[]{:S(2)}) collective-permute-start(bf16[2,256,512]{2,1,0:T(8,128)(2,1)} %wout_ref.1), channel_id=1, source_target_pairs={{0,1},{1,0},{2,3},{3,2},{4,5},{5,4},{6,7},{7,6},{8,9},{9,8},{10,11... | collective-permute-start | bytes 1572872 | tf_op jit(solution)/shard_map/ppermute | solution.py:62
  2.3 6.6 %copy-start.3 = (bf16[256,512]{1,0:T(8,128)(2,1)S(1)}, bf16[256,512]{1,0:T(8,128)(2,1)}, u32[]{:S(2)}) copy-start(bf16[256,512]{1,0:T(8,128)(2,1)} %x_ref.1) | copy-start | bytes 786436
  2.3 9.0 %copy-start.10 = (s32[4,3,128,128]{3,2,1,0:T(8,128)S(1)}, s32[4,3,128,128]{3,2,1,0:T(8,128)}, u32[]{:S(2)}) copy-start(s32[4,3,128,128]{3,2,1,0:T(8,128)} %mask_ref.1) | copy-start | bytes 2359300
  2.6 10.1 %collective-permute-start = (bf16[256,128]{1,0:T(8,128)(2,1)S(1)}, bf16[256,128]{1,0:T(8,128)(2,1)S(1)}, u32[]{:S(2)}, u32[]{:S(2)}) collective-permute-start(bf16[256,128]{1,0:T(8,128)(2,1)S(1)} %get-tuple-element.78), channel_id=1, source_target_pairs={{0,2},{2,4},{4,6},{6,8},{8,10},{10,12},{12,14},{1,3},{3,5},{5,7},{... | collective-permute-start | bytes 196616 | tf_op jit(solution)/shard_map/ppermute | solution.py:47
  7.5 6.2 %collective-permute-start.1 = (bf16[256,128]{1,0:T(8,128)(2,1)S(1)}, bf16[256,128]{1,0:T(8,128)(2,1)S(1)}, u32[]{:S(2)}, u32[]{:S(2)}) collective-permute-start(bf16[256,128]{1,0:T(8,128)(2,1)S(1)} %get-tuple-element.79), channel_id=1, source_target_pairs={{2,0},{4,2},{6,4},{8,6},{10,8},{12,10},{14,12},{3,1},{5,3},{7,5},{... | collective-permute-start | bytes 196616 | tf_op jit(solution)/shard_map/ppermute | solution.py:47
  8.8 2.4 %copy-start.33 = (s32[4,3]{1,0:T(4,128)S(1)}, s32[4,3]{1,0:T(4,128)}, u32[]{:S(2)}) copy-start(s32[4,3]{1,0:T(4,128)} %tile_ref.1) | copy-start | bytes 148
  8.9 2.4 %copy-start.34 = (s32[512]{0:T(512)S(1)}, s32[512]{0:T(512)}, u32[]{:S(2)}) copy-start(s32[512]{0:T(512)} %param.16) | copy-start | bytes 6148
  8.9 6.8 %copy-start.4 = (bf16[2,256,1024]{2,1,0:T(8,128)(2,1)S(1)}, bf16[2,256,1024]{2,1,0:T(8,128)(2,1)}, u32[]{:S(2)}) copy-start(bf16[2,256,1024]{2,1,0:T(8,128)(2,1)} %win_ref.1) | copy-start | bytes 3145732
  12.6 32.3 %copy-start.25 = (bf16[512,128]{1,0:T(8,128)(2,1)}, bf16[512,128]{1,0:T(8,128)(2,1)S(1)}, u32[]{:S(2)}) copy-start(bf16[512,128]{1,0:T(8,128)(2,1)S(1)} %get-tuple-element.88.slott_ref.r_3_) | copy-start | bytes 393220
  12.7 55.8 %copy-start.5 = (bf16[512,256]{1,0:T(8,128)(2,1)}, bf16[512,256]{1,0:T(8,128)(2,1)S(1)}, u32[]{:S(2)}) copy-start(bf16[512,256]{1,0:T(8,128)(2,1)S(1)} %get-tuple-element.120.place_ref) | copy-start | bytes 786436
  15.7 1.0 copy-start.29
  18.0 2.4 %copy-start.11 = (bf16[512,512]{1,0:T(8,128)(2,1)}, bf16[512,512]{1,0:T(8,128)(2,1)S(1)}, u32[]{:S(2)}) copy-start(bf16[512,512]{1,0:T(8,128)(2,1)S(1)} %get-tuple-element.83.wo_ref.r_6_) | copy-start | bytes 1572868
  18.0 10.3 %copy-start.40 = (bf16[256,512]{1,0:T(8,128)(2,1)S(1)}, bf16[256,512]{1,0:T(8,128)(2,1)}, u32[]{:S(2)}) copy-start(bf16[256,512]{1,0:T(8,128)(2,1)} %param.12) | copy-start | bytes 786436
  20.5 10.8 %copy-start.13 = (bf16[512,512]{1,0:T(8,128)(2,1)}, bf16[512,512]{1,0:T(8,128)(2,1)S(1)}, u32[]{:S(2)}) copy-start(bf16[512,512]{1,0:T(8,128)(2,1)S(1)} %get-tuple-element.134.r_11_) | copy-start | bytes 1572868
  20.5 10.8 %copy-start.15 = (bf16[512,512]{1,0:T(8,128)(2,1)}, bf16[512,512]{1,0:T(8,128)(2,1)S(1)}, u32[]{:S(2)}) copy-start(bf16[512,512]{1,0:T(8,128)(2,1)S(1)} %get-tuple-element.135.r_12_) | copy-start | bytes 1572868
  20.5 10.8 %copy-start.17 = (bf16[512,512]{1,0:T(8,128)(2,1)}, bf16[512,512]{1,0:T(8,128)(2,1)S(1)}, u32[]{:S(2)}) copy-start(bf16[512,512]{1,0:T(8,128)(2,1)S(1)} %get-tuple-element.136.r_13_) | copy-start | bytes 1572868
  20.5 10.8 %collective-permute-start.4 = (bf16[48,512]{1,0:T(8,128)(2,1)S(1)}, bf16[48,512]{1,0:T(8,128)(2,1)S(1)}, u32[]{:S(2)}, u32[]{:S(2)}) collective-permute-start(bf16[48,512]{1,0:T(8,128)(2,1)S(1)} %get-tuple-element.95), channel_id=1, source_target_pairs={{0,2},{2,4},{4,6},{6,8},{8,10},{10,12},{12,14},{3,1},{5,3},{7,5},{... | collective-permute-start | bytes 147464 | tf_op jit(solution)/shard_map/ppermute | solution.py:54
  24.8 6.5 %collective-permute-start.5 = (bf16[48,512]{1,0:T(8,128)(2,1)S(1)}, bf16[48,512]{1,0:T(8,128)(2,1)S(1)}, u32[]{:S(2)}, u32[]{:S(2)}) collective-permute-start(bf16[48,512]{1,0:T(8,128)(2,1)S(1)} %get-tuple-element.96), channel_id=1, source_target_pairs={{0,4},{2,6},{4,8},{6,10},{8,12},{10,14},{5,1},{7,3},{9,5},{11,7},{... | collective-permute-start | bytes 147464 | tf_op jit(solution)/shard_map/ppermute | solution.py:54
  31.3 14.8 %copy-start = (f32[512,512]{1,0:T(8,128)}, f32[512,512]{1,0:T(8,128)S(1)}, u32[]{:S(2)}) copy-start(f32[512,512]{1,0:T(8,128)S(1)} %get-tuple-element.133.r_7_) | copy-start | bytes 3145732
  34.4 7.0 %collective-permute-start.6 = (bf16[32,512]{1,0:T(8,128)(2,1)S(1)}, bf16[32,512]{1,0:T(8,128)(2,1)S(1)}, u32[]{:S(2)}, u32[]{:S(2)}) collective-permute-start(bf16[32,512]{1,0:T(8,128)(2,1)S(1)} %get-tuple-element.102), channel_id=1, source_target_pairs={{0,2},{2,4},{4,6},{6,8},{8,10},{10,12},{12,14},{3,1},{5,3},{7,5},{... | collective-permute-start | bytes 98312 | tf_op jit(solution)/shard_map/ppermute | solution.py:54
  38.0 5.1 %collective-permute-start.7 = (bf16[32,512]{1,0:T(8,128)(2,1)S(1)}, bf16[32,512]{1,0:T(8,128)(2,1)S(1)}, u32[]{:S(2)}, u32[]{:S(2)}) collective-permute-start(bf16[32,512]{1,0:T(8,128)(2,1)S(1)} %get-tuple-element.103), channel_id=1, source_target_pairs={{0,4},{2,6},{4,8},{6,10},{8,12},{10,14},{5,1},{7,3},{9,5},{11,7},{... | collective-permute-start | bytes 98312 | tf_op jit(solution)/shard_map/ppermute | solution.py:54
  44.9 4.0 %copy-start.41 = (bf16[256,512]{1,0:T(8,128)(2,1)S(1)}, bf16[256,512]{1,0:T(8,128)(2,1)}, u32[]{:S(2)}) copy-start(bf16[256,512]{1,0:T(8,128)(2,1)} %param.17) | copy-start | bytes 786436
  46.1 6.7 %collective-permute-start.8 = (bf16[128,512]{1,0:T(8,128)(2,1)S(1)}, bf16[128,512]{1,0:T(8,128)(2,1)S(1)}, u32[]{:S(2)}, u32[]{:S(2)}) collective-permute-start(bf16[128,512]{1,0:T(8,128)(2,1)S(1)} %get-tuple-element.106), channel_id=1, source_target_pairs={{0,2},{2,4},{4,6},{6,8},{8,10},{10,12},{12,14},{3,1},{5,3},{7,5},{... | collective-permute-start | bytes 393224 | tf_op jit(solution)/shard_map/ppermute | solution.py:54
  58.2 8.3 %collective-permute-start.9 = (bf16[128,512]{1,0:T(8,128)(2,1)S(1)}, bf16[128,512]{1,0:T(8,128)(2,1)S(1)}, u32[]{:S(2)}, u32[]{:S(2)}) collective-permute-start(bf16[128,512]{1,0:T(8,128)(2,1)S(1)} %get-tuple-element.119), channel_id=1, source_target_pairs={{0,2},{2,4},{4,6},{6,8},{8,10},{10,12},{12,14},{3,1},{5,3},{7,5},{... | collective-permute-start | bytes 393224 | tf_op jit(solution)/shard_map/ppermute | solution.py:54
  69.7 8.9 %collective-permute-start.10 = (bf16[32,512]{1,0:T(8,128)(2,1)S(1)}, bf16[32,512]{1,0:T(8,128)(2,1)S(1)}, u32[]{:S(2)}, u32[]{:S(2)}) collective-permute-start(bf16[32,512]{1,0:T(8,128)(2,1)S(1)} %get-tuple-element.125), channel_id=1, source_target_pairs={{0,2},{2,4},{4,6},{6,8},{8,10},{10,12},{12,14},{3,1},{5,3},{7,5},{... | collective-permute-start | bytes 98312 | tf_op jit(solution)/shard_map/ppermute | solution.py:54
  74.1 5.8 %collective-permute-start.11 = (bf16[32,512]{1,0:T(8,128)(2,1)S(1)}, bf16[32,512]{1,0:T(8,128)(2,1)S(1)}, u32[]{:S(2)}, u32[]{:S(2)}) collective-permute-start(bf16[32,512]{1,0:T(8,128)(2,1)S(1)} %get-tuple-element.126), channel_id=1, source_target_pairs={{0,4},{2,6},{4,8},{6,10},{8,12},{10,14},{5,1},{7,3},{9,5},{11,7},{... | collective-permute-start | bytes 98312 | tf_op jit(solution)/shard_map/ppermute | solution.py:54
  83.4 1.4 copy-start.30
  97.8 31.2 %all-to-all-start.1 = ((bf16[8,384,128]{2,1,0:T(8,128)(2,1)}), bf16[8,384,128]{2,1,0:T(8,128)(2,1)S(1)}, u32[]{:S(2)}, u32[]{:S(2)}) async-start(bf16[8,384,128]{2,1,0:T(8,128)(2,1)} %copy-done.8), calls=%async_computation.1 | async-start | bytes 1572864 | tf_op jit(solution)/shard_map/all_to_all | solution.py:529
  101.4 7.3 %collective-permute-start.12 = (bf16[32,512]{1,0:T(8,128)(2,1)}, bf16[32,512]{1,0:T(8,128)(2,1)S(1)}, u32[]{:S(2)}, u32[]{:S(2)}) collective-permute-start(bf16[32,512]{1,0:T(8,128)(2,1)} %copy-done.39), channel_id=1, source_target_pairs={{0,2},{2,4},{4,6},{6,8},{8,10},{10,12},{12,14},{3,1},{5,3},{7,5},{... | collective-permute-start | bytes 98312 | tf_op jit(solution)/shard_map/ppermute | solution.py:54
  105.3 9.1 %collective-permute-start.13 = (bf16[32,512]{1,0:T(8,128)(2,1)}, bf16[32,512]{1,0:T(8,128)(2,1)S(1)}, u32[]{:S(2)}, u32[]{:S(2)}) collective-permute-start(bf16[32,512]{1,0:T(8,128)(2,1)} %copy-done.38), channel_id=1, source_target_pairs={{0,4},{2,6},{4,8},{6,10},{8,12},{10,14},{5,1},{7,3},{9,5},{11,7},{... | collective-permute-start | bytes 98312 | tf_op jit(solution)/shard_map/ppermute | solution.py:54
  114.4 2.0 %copy-start.31 = (bf16[128,512]{1,0:T(8,128)(2,1)S(1)}, bf16[128,512]{1,0:T(8,128)(2,1)}, u32[]{:S(2)}) copy-start(bf16[128,512]{1,0:T(8,128)(2,1)} %copy-done.30) | copy-start | bytes 393220
  114.4 2.0 %copy-start.26 = (bf16[512,128]{1,0:T(8,128)(2,1)S(1)}, bf16[512,128]{1,0:T(8,128)(2,1)}, u32[]{:S(2)}) copy-start(bf16[512,128]{1,0:T(8,128)(2,1)} %copy-done.25) | copy-start | bytes 393220
  116.4 1.2 copy-start.1
  117.6 1.0 copy-start.12
  118.7 1.0 copy-start.14
  119.7 1.0 copy-start.16
  120.8 1.0 copy-start.18
  129.0 11.9 %copy-start.36 = (bf16[128,256]{1,0:T(8,128)(2,1)S(1)}, bf16[128,256]{1,0:T(8,128)(2,1)}, u32[]{:S(2)}) copy-start(bf16[128,256]{1,0:T(8,128)(2,1)} %copy-done.35) | copy-start | bytes 196612
  129.0 31.6 %all-to-all-start = ((bf16[8,384,128]{2,1,0:T(8,128)(2,1)}), bf16[8,384,128]{2,1,0:T(8,128)(2,1)S(1)}, u32[]{:S(2)}, u32[]{:S(2)}) async-start(bf16[8,384,128]{2,1,0:T(8,128)(2,1)} %copy-done.9), calls=%async_computation | async-start | bytes 1572864 | tf_op jit(solution)/shard_map/all_to_all | solution.py:535
  139.5 8.4 %copy-start.20 = (bf16[512,512]{1,0:T(8,128)(2,1)S(1)}, bf16[512,512]{1,0:T(8,128)(2,1)}, u32[]{:S(2)}) copy-start(bf16[512,512]{1,0:T(8,128)(2,1)} %copy-done.19) | copy-start | bytes 1572868
  139.5 11.5 %collective-permute-start.14 = (bf16[128,256]{1,0:T(8,128)(2,1)}, bf16[128,256]{1,0:T(8,128)(2,1)S(1)}, u32[]{:S(2)}, u32[]{:S(2)}) collective-permute-start(bf16[128,256]{1,0:T(8,128)(2,1)} %copy-done.37), channel_id=1, source_target_pairs={{2,0},{4,2},{6,4},{8,6},{10,8},{12,10},{14,12},{3,1},{5,3},{7,5},{... | collective-permute-start | bytes 196616 | tf_op jit(solution)/shard_map/ppermute | solution.py:47
  140.9 10.1 %collective-permute-start.15 = (bf16[128,256]{1,0:T(8,128)(2,1)S(1)}, bf16[128,256]{1,0:T(8,128)(2,1)S(1)}, u32[]{:S(2)}, u32[]{:S(2)}) collective-permute-start(bf16[128,256]{1,0:T(8,128)(2,1)S(1)} %copy-done.36), channel_id=1, source_target_pairs={{0,2},{2,4},{4,6},{6,8},{8,10},{10,12},{12,14},{1,3},{3,5},{5,7},{... | collective-permute-start | bytes 196616 | tf_op jit(solution)/shard_map/ppermute | solution.py:47
  145.5 1.0 copy-start.28
  147.9 1.0 copy-start.22
  148.9 1.0 copy-start.24
  150.0 1.0 copy-start.6
  151.0 1.2 copy-start.7
  (12 other events, 9.1 us)

commit v3 on v2

--- a/solution.py
+++ b/solution.py
@@ -62,6 +62,14 @@
     return lax.ppermute(value, "sub", [(0, 1), (1, 0)])
 
 
+def cross_swap(value):
+    return lax.ppermute(value, "cross", [(0, 1), (1, 0)])
+
+
+def curve_swap(value, step):
+    return lax.ppermute(value, "curve", [(z, z ^ step) for z in range(4)])
+
+
 def sigmoid(v):
     return 1.0 / (1.0 + jnp.exp(-v))
 
@@ -83,15 +91,14 @@
     prev_ref[...] = dot(x, (at == rows_ref[1:2, :]).astype(BF)).astype(BF)
 
 
-def k_weights(me_ref, win_ref, wout_ref, win2_ref, wout2_ref, *outs):
+def k_weights(layer, me_ref, win_ref, wout_ref, win2_ref, wout2_ref, in_ref, out_ref):
     half = win_ref.shape[1]
     own = pl.multiple_of(me_ref[1] * half, half)
     other = pl.multiple_of((1 - me_ref[1]) * half, half)
-    for layer in range(2):
-        outs[layer][pl.ds(own, half), :] = win_ref[layer]
-        outs[layer][pl.ds(other, half), :] = win2_ref[layer]
-        outs[2 + layer][pl.ds(own, half), :] = wout_ref[layer]
-        outs[2 + layer][pl.ds(other, half), :] = wout2_ref[layer]
+    in_ref[pl.ds(own, half), :] = win_ref[layer]
+    in_ref[pl.ds(other, half), :] = win2_ref[layer]
+    out_ref[pl.ds(own, half), :] = wout_ref[layer]
+    out_ref[pl.ds(other, half), :] = wout2_ref[layer]
 
 
 def k_prep(tile_ref, me_ref, mask_ref, rows_ref, par_ref,
@@ -299,41 +306,57 @@
     gout_ref[...] = dot(gt, hid_ref[...]) * scale
 
 
-def pack_grads(scale, sub, pg_ref, h_ref, agg_ref, g_ref, hid_ref, out_ref):
-    parts, _, piece = out_ref.shape
+def pack_grads(scale, me_ref, pg_ref, h_ref, agg_ref, g_ref, hid_ref, keep_ref, send_ref):
     width = h_ref.shape[1]
-    hidden = hid_ref.shape[1]
     half = width // 2
-    at = pl.multiple_of(sub * half, half)
+    piece = keep_ref.shape[2]
+    at = pl.multiple_of(me_ref[1] * half, half)
     pgt = pg_ref[:, pl.ds(at, half)].T
-    lo = (dot(pgt, h_ref[...]) * scale).astype(BF)
-    hi = (dot(pgt, agg_ref[...]) * scale).astype(BF)
-    for d in range(parts):
+    lo = dot(pgt, h_ref[...]) * scale
+    hi = dot(pgt, agg_ref[...]) * scale
+    out = dot(hid_ref[...].T, g_ref[:, pl.ds(at, half)]) * scale
+
+    def pieces(d):
         src, c = (lo, d * piece) if d * piece < width else (hi, d * piece - width)
-        out_ref[d, 0:half, :] = src[:, c:c + piece]
-    pack_small((dot(hid_ref[...].T, g_ref[:, pl.ds(at, half)]) * scale).astype(BF), out_ref, half)
-
-
-def pack_small(values, out_ref, row):
-    parts, _, piece = out_ref.shape
-    small = values.shape[0] // parts
-    for d in range(parts):
-        for c in range(values.shape[1] // piece):
-            start = row + c * small
-            out_ref[d, start:start + small, :] = values[d * small:(d + 1) * small, c * piece:(c + 1) * piece]
+        return [(0, src[:, c:c + piece])] + small_pieces(out, d, piece, half)
+
+    place_pieces(me_ref, pieces, keep_ref, send_ref)
+
+
+def small_pieces(values, d, piece, row):
+    small = values.shape[0] // 8
+    mine = values[d * small:(d + 1) * small]
+    return [
+        (row + c * small, mine[:, c * piece:(c + 1) * piece]) for c in range(values.shape[1] // piece)
+    ]
+
+
+def place_pieces(me_ref, pieces, keep_ref, send_ref):
+    for d in range(8):
+        for row, value in pieces(d):
+            rows = slice(row, row + value.shape[0])
+
+            @pl.when(me_ref[2] == d % 2)
+            def _():
+                keep_ref[d // 2, rows, :] = value
+
+            @pl.when(me_ref[2] != d % 2)
+            def _():
+                send_ref[d // 2, rows, :] = value.astype(BF)
 
 
 def k_combine_pack(scale, me_ref, pg_ref, h_ref, agg_ref, g_ref, hid_ref, win_ref, scaled_ref, adjt_ref,
-                   comb_ref, out_ref):
+                   comb_ref, keep_ref, send_ref):
     k_combine(g_ref, pg_ref, win_ref, scaled_ref, adjt_ref, comb_ref)
-    pack_grads(scale, me_ref[1], pg_ref, h_ref, agg_ref, g_ref, hid_ref, out_ref)
-
-
-def k_cweight_pack(scale, me_ref, pgrad_ref, coarse_ref, out_ref):
+    pack_grads(scale, me_ref, pg_ref, h_ref, agg_ref, g_ref, hid_ref, keep_ref, send_ref)
+
+
+def k_cweight_pack(scale, me_ref, pgrad_ref, coarse_ref, keep_ref, send_ref):
     half = pgrad_ref.shape[1] // 2
+    piece = keep_ref.shape[2]
     at = pl.multiple_of(me_ref[1] * half, half)
-    values = (dot(coarse_ref[...].T, pgrad_ref[:, pl.ds(at, half)]) * scale).astype(BF)
-    pack_small(values, out_ref, 0)
+    values = dot(coarse_ref[...].T, pgrad_ref[:, pl.ds(at, half)]) * scale
+    place_pieces(me_ref, lambda d: small_pieces(values, d, piece, 0), keep_ref, send_ref)
 
 
 def k_lgrad(me_ref, comb_ref, rim_ref, place_ref, slot_ref, lg_ref, one_ref, two_ref):
@@ -374,7 +397,7 @@
     pg_ref[...] = pg
     if scale is not None:
         xc_ref, agg_ref, hid_ref = rest[:3]
-        pack_grads(scale, me_ref[1], pg_ref, xc_ref, agg_ref, fb_ref, hid_ref, rest[8])
+        pack_grads(scale, me_ref, pg_ref, xc_ref, agg_ref, fb_ref, hid_ref, rest[8], rest[9])
     n, width = fb.shape
     half = width // 2
     rim = before_ref.shape[0]
@@ -403,11 +426,19 @@
     )
 
 
-def summed(ref):
-    total = ref[0].astype(F32)
-    for d in range(1, ref.shape[0]):
-        total = total + ref[d].astype(F32)
-    return total
+def k_stage(me_ref, *refs):
+    pairs = (len(refs) - 4) // 2
+    own_ref, outs = refs[2 * pairs], refs[2 * pairs + 1:]
+    z = me_ref[3]
+    row = 0
+    for i in range(pairs):
+        keep_ref, got_ref = refs[2 * i], refs[2 * i + 1]
+        rows = slice(row, row + keep_ref.shape[1])
+        own_ref[rows, :] = keep_ref[z] + got_ref[z].astype(F32)
+        for step in (1, 2, 3):
+            other = z ^ step
+            outs[step - 1][rows, :] = (keep_ref[other] + got_ref[other].astype(F32)).astype(BF)
+        row += keep_ref.shape[1]
 
 
 def unpack_small(total):
@@ -415,17 +446,18 @@
     return jnp.concatenate([total[0:small], total[small:]], axis=1)
 
 
-def k_sum(early_ref, coarse_ref, ein_ref, eout_ref, gco_ref):
+def k_sum(own_ref, a_ref, b_ref, c_ref, ein_ref, eout_ref, gco_ref):
     half = ein_ref.shape[0]
-    total = summed(early_ref)
+    mid = half + 2 * eout_ref.shape[0]
+    total = own_ref[...] + a_ref[...].astype(F32) + b_ref[...].astype(F32) + c_ref[...].astype(F32)
     ein_ref[...] = total[0:half]
-    eout_ref[...] = unpack_small(total[half:])
-    gco_ref[...] = unpack_small(summed(coarse_ref))
-
-
-def k_sum_late(late_ref, ein_ref, eout_ref, gin_ref, gout_ref):
+    eout_ref[...] = unpack_small(total[half:mid])
+    gco_ref[...] = unpack_small(total[mid:])
+
+
+def k_sum_late(own_ref, a_ref, b_ref, c_ref, ein_ref, eout_ref, gin_ref, gout_ref):
     half = ein_ref.shape[0]
-    total = summed(late_ref)
+    total = own_ref[...] + a_ref[...].astype(F32) + b_ref[...].astype(F32) + c_ref[...].astype(F32)
     gin_ref[0] = total[0:half]
     gin_ref[1] = ein_ref[...]
     gout_ref[0] = unpack_small(total[half:])
@@ -447,9 +479,9 @@
     slots = 4 * cap
     hidden = 2 * inward_weight.shape[1]
     scale = float(n * domains) ** -0.5
-    me = jnp.stack([lax.axis_index(DOM), lax.axis_index("sub")]).astype(I32)
+    me = jnp.stack([lax.axis_index(a) for a in (DOM, "sub", "cross", "curve")]).astype(I32)
     rows = send_rows[0]
-    packed = 2 * width // domains == 128
+    packed = cross == 2 and curve == 4 and 2 * width == 1024 and hidden == width
 
     halo_next, halo_prev = call(
         k_halo, [sds((half, rim), BF)] * 2, [], [rows, node_features], "halo")
@@ -463,9 +495,9 @@
          sds((n, nodes), BF), sds((slots, n), BF), sds((n, slots), BF), sds((2 * rim, n), BF),
          sds((n, 2 * rim), BF), sds((16, slots), BF), sds((nodes, 128), F32)],
         [tile_index, me], [tile_mask, rows, parent[None, :]], "prep")
-    win0, win1, wo0, wo1 = call(
-        k_weights, [sds((hidden, 2 * width), BF)] * 2 + [sds((width, hidden), BF)] * 2,
-        [me], [inward_weight, outward_weight, win2, wout2], "weights")
+    weight_outs = [sds((hidden, 2 * width), BF), sds((width, hidden), BF)]
+    win0, wo0 = call(lambda *r: k_weights(0, *r), weight_outs, [me],
+                     [inward_weight, outward_weight, win2, wout2], "weights0")
     rims = gather(jnp.concatenate([before_half, after_half], axis=0)).reshape(2, width, rim)
     msg = sds((cap + 16, width), BF)
     plain = sds((cap, width), BF)
@@ -477,10 +509,12 @@
         [me], [x_full, rims, adj, inv, win0, wo0, slot, tags], "first",
         flops=2 * n * width * (src_rows + 3 * width),
         scratch=[pltpu.VMEM((src_rows, width), BF)])
-    one, two, cotangent, coarse_weight = lax.optimization_barrier((one, two, cotangent, coarse_weight))
+    one, two, win2, coarse_weight = lax.optimization_barrier((one, two, win2, coarse_weight))
     one, two = two_way(one, 1), two_way(two, 2)
     own, slope0 = call(k_own, [sds((nodes, width), F32), hid_f32], [], [hott, first, pre0], "own")
     cw = gather(coarse_weight)
+    win1, wo1 = call(lambda *r: k_weights(1, *r), weight_outs, [me],
+                     [inward_weight, outward_weight, win2, wout2], "weights1")
     got = gather(jnp.concatenate([one, two], axis=0)).reshape(2, -1, width)
     node_bf, node_f32 = sds((nodes, width), BF), sds((nodes, width), F32)
     hits, icount, coarse, cpre, corr, one, two = call(
@@ -502,9 +536,10 @@
     rims = two_way(rims, 1)
     piece = 2 * width // domains
     small = hidden // domains
-    pack = sds((domains, half + 2 * small, piece), BF)
+    layer_rows = half + 2 * small
+    pack = [sds((curve, layer_rows, piece), F32), sds((curve, layer_rows, piece), BF)]
     if packed:
-        comb1, early = call(lambda *r: k_combine_pack(scale, *r), [cell_f32, pack], [me],
+        comb1, keep1, send1 = call(lambda *r: k_combine_pack(scale, *r), [cell_f32] + pack, [me],
                             [pg1, lifted, agg1, ctc, hid1, win1, scaled1, adjt], "combine")
     else:
         comb1, = call(k_combine, [cell_f32], [], [ctc, pg1, win1, scaled1, adjt], "combine")
@@ -512,7 +547,8 @@
     lg, one, two = call(
         k_lgrad, [cell_bf, plain, plain], [me], [comb1, rims, place, slot], "lgrad")
     if packed:
-        one, two, early = lax.optimization_barrier((one, two, early))
+        one, two, send1 = lax.optimization_barrier((one, two, send1))
+        got1 = cross_swap(send1)
     one, two = two_way(one, 1), two_way(two, 2)
     own_g, = call(k_pool, [node_f32], [], [hott, lg], "own_grad")
     new_t, = call(k_newt, [sds((half, n), BF)], [me], [new], "new")
@@ -526,13 +562,24 @@
     back_outs = [cell_bf, hid_bf, cell_bf, rim_half, rim_half]
     back_args = [lg, hot, slott, spread, got, wo0, slope0, win0, inv, adjt]
     if packed:
-        early = lax.all_to_all(early, DOM, 0, 0, tiled=True)
-        gco, = call(lambda *r: k_cweight_pack(scale, *r), [sds((domains, 2 * small, piece), BF)], [me],
-                    [pgrad, coarse], "cweight")
-        gco = lax.all_to_all(gco, DOM, 0, 0, tiled=True)
-        fb, pg0, scaled0, to_before, to_after, late = call(
-            lambda *r: k_third(*r, scale=scale), back_outs + [pack], [me], back_args + [xc, agg0, hid0], "third")
-        late = lax.all_to_all(late, DOM, 0, 0, tiled=True)
+        keepc, sendc = call(
+            lambda *r: k_cweight_pack(scale, *r),
+            [sds((curve, 2 * small, piece), F32), sds((curve, 2 * small, piece), BF)], [me],
+            [pgrad, coarse], "cweight")
+        gotc = cross_swap(sendc)
+        fb, pg0, scaled0, to_before, to_after, keep0, send0 = call(
+            lambda *r: k_third(*r, scale=scale), back_outs + pack, [me], back_args + [xc, agg0, hid0], "third")
+        send0, gotc = lax.optimization_barrier((send0, gotc))
+        got0 = cross_swap(send0)
+
+        def staged(pairs, name):
+            total = sum(keep.shape[1] for keep in pairs[::2])
+            own, *outs = call(k_stage, [sds((total, piece), F32)] + [sds((total, piece), BF)] * 3, [me], pairs, name)
+            return [own] + [curve_swap(value, step) for step, value in zip((1, 2, 3), outs)]
+
+        early = staged([keep1, got1, keepc, gotc], "stage1")
+        to_before, to_after, got0 = lax.optimization_barrier((to_before, to_after, got0))
+        late = staged([keep0, got0], "stage0")
     else:
         gco, = call(lambda *r: k_cweight(scale, *r), [sds((half, width), F32)], [me], [pgrad, coarse], "cweight")
         fb, pg0, scaled0, to_before, to_after = call(k_third, back_outs, [me], back_args, "third")
@@ -543,9 +590,9 @@
     if packed:
         ein, eout, gco = call(
             k_sum, [sds((half, piece), F32), sds((small, half), F32), sds((small, half), F32)],
-            [], [early, gco], "sums")
+            [], early, "sums")
         gin, gout = call(
-            k_sum_late, [sds((2, half, piece), F32), sds((2, small, half), F32)], [], [late, ein, eout], "late")
+            k_sum_late, [sds((2, half, piece), F32), sds((2, small, half), F32)], [], late + [ein, eout], "late")
         gout = gout.swapaxes(1, 2)
         gco = gco.T
     else:

time: 163 us -> 131 us (0.80)
  the two profiles are of different devices: /device:TPU:0 before, /device:TPU:8 now
where the time goes in v3:
time: 131 us; the launch traced here: 130 us
  starting transfers between devices  56.7 us (43%)
  Pallas kernels  26.4 us (20%)
  waiting for transfers between devices  23.4 us (18%)
  blocking collectives  20.4 us (16%)
  local copies, waits for them, and re-layouts  2.22 us (2%)
    ppermute x10, starting transfers between devices, two_way(): return lax.ppermute(value, LINE, pairs)  30.4 us
    pallas_call x23, Pallas kernels, call(): pl.pallas_call(body, out_shape=tuple(outs), in_specs=[pl.BlockSpec(memory...  26.4 us
    all_gather x10, blocking collectives, gather(): return lax.all_gather(value, 'sub', axis=0, tiled=True)  20.4 us
    ppermute x4, starting transfers between devices, shifted(): lax.ppermute(value, DOM, [(s, s + steps) for s in range(first, last)])  13.3 us
    ppermute x10, waiting for transfers between devices, two_way(): return lax.ppermute(value, LINE, pairs)  10.4 us
    ppermute x6, starting transfers between devices, curve_swap(): return lax.ppermute(value, 'curve', [(z, z ^ step) for z in range(4)])  8.52 us
    ppermute x3, waiting for transfers between devices, cross_swap(): return lax.ppermute(value, 'cross', [(0, 1), (1, 0)])  7.6 us
    ppermute x3, starting transfers between devices, cross_swap(): return lax.ppermute(value, 'cross', [(0, 1), (1, 0)])  3.86 us
  transfers between devices with their start and end apart: 25, of which 9 were waited for; matrix products, arithmetic and copies ran while one was open for 0% of the time, Pallas kernels for 12%

profile of v3, /device:TPU:8, one launch (start us, length us, event | category | flops | bytes accessed | tf_op | source)
XLA Modules:
  0.0 130.2 jit_solution(11984697842084956711)
XLA Ops:
  2.6 3.4 %collective-permute-start = (bf16[256,128]{1,0:T(8,128)(2,1)S(1)}, bf16[256,128]{1,0:T(8,128)(2,1)S(1)}, u32[]{:S(2)}, u32[]{:S(2)}) collective-permute-start(bf16[256,128]{1,0:T(8,128)(2,1)S(1)} %get-tuple-element.95), channel_id=1, source_target_pairs={{0,2},{2,4},{4,6},{6,8},{8,10},{10,12},{12,14},{1,3},{3,5},{5,7},{... | collective-permute-start | bytes 196616 | tf_op jit(solution)/shard_map/ppermute | solution.py:47
  6.0 3.3 %collective-permute-start.1 = (bf16[256,128]{1,0:T(8,128)(2,1)S(1)}, bf16[256,128]{1,0:T(8,128)(2,1)S(1)}, u32[]{:S(2)}, u32[]{:S(2)}) collective-permute-start(bf16[256,128]{1,0:T(8,128)(2,1)S(1)} %get-tuple-element.96), channel_id=1, source_target_pairs={{2,0},{4,2},{6,4},{8,6},{10,8},{12,10},{14,12},{3,1},{5,3},{7,5},{... | collective-permute-start | bytes 196616 | tf_op jit(solution)/shard_map/ppermute | solution.py:47
  9.4 2.3 %all_gather.30.x_ref = bf16[512,512]{1,0:T(8,128)(2,1)S(1)} all-gather(bf16[256,512]{1,0:T(8,128)(2,1)S(1)} %copy-done.3), channel_id=1, replica_groups=mesh['groups'=2,'curve'=4,'cross'=2,'sub'=2] {'sub'}, dimensions={0}, use_global_device_ids=true | all-gather | bytes 786432 | tf_op jit(solution)/shard_map/all_gather | solution.py:58
  11.8 1.1 copy-done.4
  12.9 1.3 %prep.1 = (bf16[512,768]{1,0:T(8,128)(2,1)S(1)}, bf16[768,512]{1,0:T(8,128)(2,1)S(1)}, f32[512,128]{1,0:T(8,128)S(1)}, bf16[128,512]{1,0:T(8,128)(2,1)S(1)}, bf1...) custom-call(s32[4,3]{1,0:T(4,128)S(1)} %copy-done.6, ...), custom_call_target="tpu_custom_call" | custom-call | bytes 3742720 | tf_op jit(solution)/shard_map/prep/pallas_call | solution.py:31
  14.3 2.1 %all_gather.31 = bf16[1024,128]{1,0:T(8,128)(2,1)S(1)} all-gather(bf16[512,128]{1,0:T(8,128)(2,1)S(1)} %pad_maximum_fusion), channel_id=1, replica_groups=mesh['groups'=2,'curve'=4,'cross'=2,'sub'=2] {'sub'}, dimensions={0}, use_global_device_ids=true | all-gather | bytes 393216 | tf_op jit(solution)/shard_map/all_gather | solution.py:58
  17.1 2.4 %first.1 = (bf16[512,512]{1,0:T(8,128)(2,1)S(1)}, bf16[512,512]{1,0:T(8,128)(2,1)S(1)}, f32[512,512]{1,0:T(8,128)S(1)}, bf16[512,512]{1,0:T(8,128)(2,1)S(1)}, bf...) custom-call(s32[4]{0:T(128)S(1)} %pad_add_fusion.me_ref.r_0_, ...), custom_call_target="tpu_custom_call" | custom-call | flops 1207959552 | bytes 6787072 | tf_op jit(solution)/shard_map/first/pallas_call | solution.py:31
  19.5 2.5 %collective-permute-start.4 = (bf16[48,512]{1,0:T(8,128)(2,1)S(1)}, bf16[48,512]{1,0:T(8,128)(2,1)S(1)}, u32[]{:S(2)}, u32[]{:S(2)}) collective-permute-start(bf16[48,512]{1,0:T(8,128)(2,1)S(1)} %get-tuple-element.112), channel_id=1, source_target_pairs={{0,2},{2,4},{4,6},{6,8},{8,10},{10,12},{12,14},{3,1},{5,3},{7,5},{... | collective-permute-start | bytes 147464 | tf_op jit(solution)/shard_map/ppermute | solution.py:54
  22.0 3.5 %collective-permute-start.5 = (bf16[48,512]{1,0:T(8,128)(2,1)S(1)}, bf16[48,512]{1,0:T(8,128)(2,1)S(1)}, u32[]{:S(2)}, u32[]{:S(2)}) collective-permute-start(bf16[48,512]{1,0:T(8,128)(2,1)S(1)} %get-tuple-element.113), channel_id=1, source_target_pairs={{0,4},{2,6},{4,8},{6,10},{8,12},{10,14},{5,1},{7,3},{9,5},{11,7},{... | collective-permute-start | bytes 147464 | tf_op jit(solution)/shard_map/ppermute | solution.py:54
  25.5 2.2 %all_gather.33.cw_ref = bf16[512,512]{1,0:T(8,128)(2,1)S(1)} all-gather(bf16[256,512]{1,0:T(8,128)(2,1)S(1)} %copy-done.8), channel_id=1, replica_groups=mesh['groups'=2,'curve'=4,'cross'=2,'sub'=2] {'sub'}, dimensions={0}, use_global_device_ids=true | all-gather | bytes 786432 | tf_op jit(solution)/shard_map/all_gather | solution.py:58
  28.5 1.9 %all_gather.32 = bf16[192,512]{1,0:T(8,128)(2,1)S(1)} all-gather(bf16[96,512]{1,0:T(8,128)(2,1)S(1)} %pad_maximum_fusion.1), channel_id=1, replica_groups=mesh['groups'=2,'curve'=4,'cross'=2,'sub'=2] {'sub'}, dimensions={0}, use_global_device_ids=true | all-gather | bytes 294912 | tf_op jit(solution)/shard_map/all_gather | solution.py:58
  30.4 1.1 coarse.1
  31.6 4.4 %collective-permute-start.6 = (bf16[32,512]{1,0:T(8,128)(2,1)S(1)}, bf16[32,512]{1,0:T(8,128)(2,1)S(1)}, u32[]{:S(2)}, u32[]{:S(2)}) collective-permute-start(bf16[32,512]{1,0:T(8,128)(2,1)S(1)} %get-tuple-element.118), channel_id=1, source_target_pairs={{0,2},{2,4},{4,6},{6,8},{8,10},{10,12},{12,14},{3,1},{5,3},{7,5},{... | collective-permute-start | bytes 98312 | tf_op jit(solution)/shard_map/ppermute | solution.py:54
  35.9 3.0 %collective-permute-start.7 = (bf16[32,512]{1,0:T(8,128)(2,1)S(1)}, bf16[32,512]{1,0:T(8,128)(2,1)S(1)}, u32[]{:S(2)}, u32[]{:S(2)}) collective-permute-start(bf16[32,512]{1,0:T(8,128)(2,1)S(1)} %get-tuple-element.119), channel_id=1, source_target_pairs={{0,4},{2,6},{4,8},{6,10},{8,12},{10,14},{5,1},{7,3},{9,5},{11,7},{... | collective-permute-start | bytes 98312 | tf_op jit(solution)/shard_map/ppermute | solution.py:54
  39.6 2.1 %collective-permute-done.7 = bf16[32,512]{1,0:T(8,128)(2,1)S(1)} collective-permute-done((bf16[32,512]{1,0:T(8,128)(2,1)S(1)}, bf16[32,512]{1,0:T(8,128)(2,1)S(1)}, u32[]{:S(2)}, u32[]{:S(2)}) %collective-permute-start.7) | collective-permute-done | bytes 32800 | tf_op jit(solution)/shard_map/ppermute | solution.py:54
  41.7 1.9 %all_gather.34 = bf16[128,512]{1,0:T(8,128)(2,1)S(1)} all-gather(bf16[64,512]{1,0:T(8,128)(2,1)S(1)} %pad_maximum_fusion.2), channel_id=1, replica_groups=mesh['groups'=2,'curve'=4,'cross'=2,'sub'=2] {'sub'}, dimensions={0}, use_global_device_ids=true | all-gather | bytes 196608 | tf_op jit(solution)/shard_map/all_gather | solution.py:58
  43.6 1.1 lift.1
  44.8 2.5 %collective-permute-start.8 = (bf16[128,512]{1,0:T(8,128)(2,1)S(1)}, bf16[128,512]{1,0:T(8,128)(2,1)S(1)}, u32[]{:S(2)}, u32[]{:S(2)}) collective-permute-start(bf16[128,512]{1,0:T(8,128)(2,1)S(1)} %get-tuple-element.122), channel_id=1, source_target_pairs={{0,2},{2,4},{4,6},{6,8},{8,10},{10,12},{12,14},{3,1},{5,3},{7,5},{... | collective-permute-start | bytes 393224 | tf_op jit(solution)/shard_map/ppermute | solution.py:54
  47.3 2.2 %all_gather.36.ct_ref = bf16[512,512]{1,0:T(8,128)(2,1)S(1)} all-gather(bf16[256,512]{1,0:T(8,128)(2,1)S(1)} %copy-done.9), channel_id=1, replica_groups=mesh['groups'=2,'curve'=4,'cross'=2,'sub'=2] {'sub'}, dimensions={0}, use_global_device_ids=true | all-gather | bytes 786432 | tf_op jit(solution)/shard_map/all_gather | solution.py:58
  49.9 2.6 %collective-permute-done.8 = bf16[128,512]{1,0:T(8,128)(2,1)S(1)} collective-permute-done((bf16[128,512]{1,0:T(8,128)(2,1)S(1)}, bf16[128,512]{1,0:T(8,128)(2,1)S(1)}, u32[]{:S(2)}, u32[]{:S(2)}) %collective-permute-start.8) | collective-permute-done | bytes 131104 | tf_op jit(solution)/shard_map/ppermute | solution.py:54
  52.5 2.0 %all_gather.35.rim_ref = bf16[256,512]{1,0:T(8,128)(2,1)S(1)} all-gather(bf16[128,512]{1,0:T(8,128)(2,1)S(1)} %collective-permute-done.8), channel_id=1, replica_groups=mesh['groups'=2,'curve'=4,'cross'=2,'sub'=2] {'sub'}, dimensions={0}, use_global_device_ids=true | all-gather | bytes 393216 | tf_op jit(solution)/shard_map/all_gather | solution.py:58
  54.5 2.6 %second.1 = (bf16[512,512]{1,0:T(8,128)(2,1)S(1)}, bf16[512,512]{1,0:T(8,128)(2,1)S(1)}, bf16[512,512]{1,0:T(8,128)(2,1)S(1)}, bf16[512,512]{1,0:T(8,128)(2,1)S(...) custom-call(s32[4]{0:T(128)S(1)} %pad_add_fusion.me_ref.r_0_, ...), custom_call_target="tpu_custom_call" | custom-call | bytes 7995392 | tf_op jit(solution)/shard_map/second/pallas_call | solution.py:31
  57.1 3.0 %collective-permute-start.9 = (bf16[128,512]{1,0:T(8,128)(2,1)S(1)}, bf16[128,512]{1,0:T(8,128)(2,1)S(1)}, u32[]{:S(2)}, u32[]{:S(2)}) collective-permute-start(bf16[128,512]{1,0:T(8,128)(2,1)S(1)} %get-tuple-element.136), channel_id=1, source_target_pairs={{0,2},{2,4},{4,6},{6,8},{8,10},{10,12},{12,14},{3,1},{5,3},{7,5},{... | collective-permute-start | bytes 393224 | tf_op jit(solution)/shard_map/ppermute | solution.py:54
  60.2 2.1 %combine.1 = (f32[512,512]{1,0:T(8,128)S(1)}, f32[4,384,128]{2,1,0:T(8,128)S(1)}, bf16[4,384,128]{2,1,0:T(8,128)(2,1)S(1)}) custom-call(s32[4]{0:T(128)S(1)} %pad_add_fusion.me_ref.r_0_, bf16[512,512]{1,0:T(8,128)(2,1)S(1)} %get-tuple-element.130.r_1_, bf16[512,512]{1,0:T(8,128)(2,1)S(1)} %get-tuple-element.121.lift_ref.r_2_, ...), custom_call_target="tpu_custom_call" | custom-call | bytes 7208960 | tf_op jit(solution)/shard_map/combine/pallas_call | solution.py:31
  62.3 2.6 %collective-permute-done.9 = bf16[128,512]{1,0:T(8,128)(2,1)S(1)} collective-permute-done((bf16[128,512]{1,0:T(8,128)(2,1)S(1)}, bf16[128,512]{1,0:T(8,128)(2,1)S(1)}, u32[]{:S(2)}, u32[]{:S(2)}) %collective-permute-start.9) | collective-permute-done | bytes 131104 | tf_op jit(solution)/shard_map/ppermute | solution.py:54
  64.9 2.0 %all_gather.37.rim_ref = bf16[256,512]{1,0:T(8,128)(2,1)S(1)} all-gather(bf16[128,512]{1,0:T(8,128)(2,1)S(1)} %collective-permute-done.9), channel_id=1, replica_groups=mesh['groups'=2,'curve'=4,'cross'=2,'sub'=2] {'sub'}, dimensions={0}, use_global_device_ids=true | all-gather | bytes 393216 | tf_op jit(solution)/shard_map/all_gather | solution.py:58
  66.9 1.2 lgrad.1
  68.0 3.5 %collective-permute-start.10 = (bf16[32,512]{1,0:T(8,128)(2,1)S(1)}, bf16[32,512]{1,0:T(8,128)(2,1)S(1)}, u32[]{:S(2)}, u32[]{:S(2)}) collective-permute-start(bf16[32,512]{1,0:T(8,128)(2,1)S(1)} %get-tuple-element.142), channel_id=1, source_target_pairs={{0,2},{2,4},{4,6},{6,8},{8,10},{10,12},{12,14},{3,1},{5,3},{7,5},{... | collective-permute-start | bytes 98312 | tf_op jit(solution)/shard_map/ppermute | solution.py:54
  71.6 3.0 %collective-permute-start.11 = (bf16[32,512]{1,0:T(8,128)(2,1)S(1)}, bf16[32,512]{1,0:T(8,128)(2,1)S(1)}, u32[]{:S(2)}, u32[]{:S(2)}) collective-permute-start(bf16[32,512]{1,0:T(8,128)(2,1)S(1)} %get-tuple-element.143), channel_id=1, source_target_pairs={{0,4},{2,6},{4,8},{6,10},{8,12},{10,14},{5,1},{7,3},{9,5},{11,7},{... | collective-permute-start | bytes 98312 | tf_op jit(solution)/shard_map/ppermute | solution.py:54
  74.8 2.5 %collective-permute-done.11 = bf16[32,512]{1,0:T(8,128)(2,1)S(1)} collective-permute-done((bf16[32,512]{1,0:T(8,128)(2,1)S(1)}, bf16[32,512]{1,0:T(8,128)(2,1)S(1)}, u32[]{:S(2)}, u32[]{:S(2)}) %collective-permute-start.11) | collective-permute-done | bytes 32800 | tf_op jit(solution)/shard_map/ppermute | solution.py:54
  77.4 1.9 %all_gather.38 = bf16[128,512]{1,0:T(8,128)(2,1)S(1)} all-gather(bf16[64,512]{1,0:T(8,128)(2,1)S(1)} %pad_maximum_fusion.3), channel_id=1, replica_groups=mesh['groups'=2,'curve'=4,'cross'=2,'sub'=2] {'sub'}, dimensions={0}, use_global_device_ids=true | all-gather | bytes 196608 | tf_op jit(solution)/shard_map/all_gather | solution.py:58
  79.3 1.0 cgrad.1
  80.3 2.9 %collective-permute-start.12 = (bf16[32,512]{1,0:T(8,128)(2,1)S(1)}, bf16[32,512]{1,0:T(8,128)(2,1)S(1)}, u32[]{:S(2)}, u32[]{:S(2)}) collective-permute-start(bf16[32,512]{1,0:T(8,128)(2,1)S(1)} %get-tuple-element.148), channel_id=1, source_target_pairs={{0,2},{2,4},{4,6},{6,8},{8,10},{10,12},{12,14},{3,1},{5,3},{7,5},{... | collective-permute-start | bytes 98312 | tf_op jit(solution)/shard_map/ppermute | solution.py:54
  83.2 2.1 %collective-permute-start.13 = (bf16[32,512]{1,0:T(8,128)(2,1)S(1)}, bf16[32,512]{1,0:T(8,128)(2,1)S(1)}, u32[]{:S(2)}, u32[]{:S(2)}) collective-permute-start(bf16[32,512]{1,0:T(8,128)(2,1)S(1)} %get-tuple-element.149), channel_id=1, source_target_pairs={{0,4},{2,6},{4,8},{6,10},{8,12},{10,14},{5,1},{7,3},{9,5},{11,7},{... | collective-permute-start | bytes 98312 | tf_op jit(solution)/shard_map/ppermute | solution.py:54
  85.3 1.5 %collective-permute-start.21 = (bf16[4,384,128]{2,1,0:T(8,128)(2,1)S(1)}, bf16[4,384,128]{2,1,0:T(8,128)(2,1)S(1)}, u32[]{:S(2)}, u32[]{:S(2)}) collective-permute-start(bf16[4,384,128]{2,1,0:T(8,128)(2,1)S(1)} %get-tuple-element.173), channel_id=1, source_target_pairs={{0,2},{2,0},{1,3},{3,1},{4,6},{6,4},{5,7},{7,5},{8,10},{10,8},{9,1... | collective-permute-start | bytes 1179656 | tf_op jit(solution)/shard_map/ppermute | solution.py:66
  89.0 1.9 %all_gather.39 = bf16[128,512]{1,0:T(8,128)(2,1)S(1)} all-gather(bf16[64,512]{1,0:T(8,128)(2,1)S(1)} %pad_maximum_fusion.4), channel_id=1, replica_groups=mesh['groups'=2,'curve'=4,'cross'=2,'sub'=2] {'sub'}, dimensions={0}, use_global_device_ids=true | all-gather | bytes 196608 | tf_op jit(solution)/shard_map/all_gather | solution.py:58
  90.9 3.2 %third.1 = (bf16[512,512]{1,0:T(8,128)(2,1)S(1)}, bf16[512,512]{1,0:T(8,128)(2,1)S(1)}, bf16[512,512]{1,0:T(8,128)(2,1)S(1)}, bf16[128,256]{1,0:T(8,128)(2,1)S(1...) custom-call(s32[4]{0:T(128)S(1)} %pad_add_fusion.me_ref.r_0_, ...), custom_call_target="tpu_custom_call" | custom-call | bytes 9175040 | tf_op jit(solution)/shard_map/third/pallas_call | solution.py:31
  94.1 4.1 %collective-permute-done.14.refs_3_ = bf16[4,128,128]{2,1,0:T(8,128)(2,1)S(1)} collective-permute-done((bf16[4,128,128]{2,1,0:T(8,128)(2,1)S(1)}, bf16[4,128,128]{2,1,0:T(8,128)(2,1)S(1)}, u32[]{:S(2)}, u32[]{:S(2)}) %collective-permute-start.14) | collective-permute-done | bytes 131104 | tf_op jit(solution)/shard_map/ppermute | solution.py:66
  98.3 1.7 %collective-permute-start.15 = (bf16[4,384,128]{2,1,0:T(8,128)(2,1)S(1)}, bf16[4,384,128]{2,1,0:T(8,128)(2,1)S(1)}, u32[]{:S(2)}, u32[]{:S(2)}) collective-permute-start(bf16[4,384,128]{2,1,0:T(8,128)(2,1)S(1)} %get-tuple-element.163), channel_id=1, source_target_pairs={{0,2},{2,0},{1,3},{3,1},{4,6},{6,4},{5,7},{7,5},{8,10},{10,8},{9,1... | collective-permute-start | bytes 1179656 | tf_op jit(solution)/shard_map/ppermute | solution.py:66
  100.7 3.0 %collective-permute-start.23 = (bf16[512,128]{1,0:T(8,128)(2,1)S(1)}, bf16[512,128]{1,0:T(8,128)(2,1)S(1)}, u32[]{:S(2)}, u32[]{:S(2)}) collective-permute-start(bf16[512,128]{1,0:T(8,128)(2,1)S(1)} %get-tuple-element.178), channel_id=1, source_target_pairs={{0,8},{4,12},{8,0},{12,4},{1,9},{5,13},{9,1},{13,5},{2,10},{6,14},... | collective-permute-start | bytes 393224 | tf_op jit(solution)/shard_map/ppermute | solution.py:70
  104.2 3.5 %collective-permute-done.15.refs_1_ = bf16[4,384,128]{2,1,0:T(8,128)(2,1)S(1)} collective-permute-done((bf16[4,384,128]{2,1,0:T(8,128)(2,1)S(1)}, bf16[4,384,128]{2,1,0:T(8,128)(2,1)S(1)}, u32[]{:S(2)}, u32[]{:S(2)}) %collective-permute-start.15) | collective-permute-done | bytes 393248 | tf_op jit(solution)/shard_map/ppermute | solution.py:66
  108.3 4.9 %collective-permute-start.19 = (bf16[384,128]{1,0:T(8,128)(2,1)S(1)}, bf16[384,128]{1,0:T(8,128)(2,1)S(1)}, u32[]{:S(2)}, u32[]{:S(2)}) collective-permute-start(bf16[384,128]{1,0:T(8,128)(2,1)S(1)} %get-tuple-element.170), channel_id=1, source_target_pairs={{0,8},{4,12},{8,0},{12,4},{1,9},{5,13},{9,1},{13,5},{2,10},{6,14},... | collective-permute-start | bytes 294920 | tf_op jit(solution)/shard_map/ppermute | solution.py:70
  113.3 4.4 %collective-permute-start.16 = (bf16[128,256]{1,0:T(8,128)(2,1)S(1)}, bf16[128,256]{1,0:T(8,128)(2,1)S(1)}, u32[]{:S(2)}, u32[]{:S(2)}) collective-permute-start(bf16[128,256]{1,0:T(8,128)(2,1)S(1)} %get-tuple-element.164), channel_id=1, source_target_pairs={{2,0},{4,2},{6,4},{8,6},{10,8},{12,10},{14,12},{3,1},{5,3},{7,5},{... | collective-permute-start | bytes 196616 | tf_op jit(solution)/shard_map/ppermute | solution.py:47
  117.7 3.5 %collective-permute-done.24.c_ref = bf16[512,128]{1,0:T(8,128)(2,1)S(1)} collective-permute-done((bf16[512,128]{1,0:T(8,128)(2,1)S(1)}, bf16[512,128]{1,0:T(8,128)(2,1)S(1)}, u32[]{:S(2)}, u32[]{:S(2)}) %collective-permute-start.24) | collective-permute-done | bytes 131104 | tf_op jit(solution)/shard_map/ppermute | solution.py:70
  121.2 2.2 %collective-permute-start.17 = (bf16[128,256]{1,0:T(8,128)(2,1)S(1)}, bf16[128,256]{1,0:T(8,128)(2,1)S(1)}, u32[]{:S(2)}, u32[]{:S(2)}) collective-permute-start(bf16[128,256]{1,0:T(8,128)(2,1)S(1)} %get-tuple-element.165), channel_id=1, source_target_pairs={{0,2},{2,4},{4,6},{6,8},{8,10},{10,12},{12,14},{1,3},{3,5},{5,7},{... | collective-permute-start | bytes 196616 | tf_op jit(solution)/shard_map/ppermute | solution.py:47
  123.4 1.4 %new.1 = bf16[256,512]{1,0:T(8,128)(2,1)} custom-call(s32[4]{0:T(128)S(1)} %pad_add_fusion.me_ref.r_0_, bf16[512,512]{1,0:T(8,128)(2,1)S(1)} %get-tuple-element.129.new_ref), custom_call_target="tpu_custom_call" | custom-call | bytes 786432 | tf_op jit(solution)/shard_map/new/pallas_call | solution.py:31
  126.4 1.8 %collective-permute-done.17.before_ref = bf16[128,256]{1,0:T(8,128)(2,1)S(1)} collective-permute-done((bf16[128,256]{1,0:T(8,128)(2,1)S(1)}, bf16[128,256]{1,0:T(8,128)(2,1)S(1)}, u32[]{:S(2)}, u32[]{:S(2)}) %collective-permute-start.17) | collective-permute-done | bytes 65568 | tf_op jit(solution)/shard_map/ppermute | solution.py:47
  128.2 1.1 last.1
  (61 shorter events, 11.2 us)
Async XLA Ops:
  0.6 0.7 copy-start.5
  0.6 15.8 %collective-permute-start.2 = (bf16[2,256,1024]{2,1,0:T(8,128)(2,1)}, bf16[2,256,1024]{2,1,0:T(8,128)(2,1)S(1)}, u32[]{:S(2)}, u32[]{:S(2)}) collective-permute-start(bf16[2,256,1024]{2,1,0:T(8,128)(2,1)} %r_1_.3), channel_id=1, source_target_pairs={{0,1},{1,0},{2,3},{3,2},{4,5},{5,4},{6,7},{7,6},{8,9},{9,8},{10,11... | collective-permute-start | bytes 3145736 | tf_op jit(solution)/shard_map/ppermute | solution.py:62
  0.7 15.7 %collective-permute-start.3 = (bf16[2,256,512]{2,1,0:T(8,128)(2,1)}, bf16[2,256,512]{2,1,0:T(8,128)(2,1)S(1)}, u32[]{:S(2)}, u32[]{:S(2)}) collective-permute-start(bf16[2,256,512]{2,1,0:T(8,128)(2,1)} %r_2_.3), channel_id=1, source_target_pairs={{0,1},{1,0},{2,3},{3,2},{4,5},{5,4},{6,7},{7,6},{8,9},{9,8},{10,11... | collective-permute-start | bytes 1572872 | tf_op jit(solution)/shard_map/ppermute | solution.py:62
  1.3 0.9 copy-start.2
  2.3 7.1 %copy-start.3 = (bf16[256,512]{1,0:T(8,128)(2,1)S(1)}, bf16[256,512]{1,0:T(8,128)(2,1)}, u32[]{:S(2)}) copy-start(bf16[256,512]{1,0:T(8,128)(2,1)} %x_ref.1) | copy-start | bytes 786436
  2.6 11.7 %collective-permute-start = (bf16[256,128]{1,0:T(8,128)(2,1)S(1)}, bf16[256,128]{1,0:T(8,128)(2,1)S(1)}, u32[]{:S(2)}, u32[]{:S(2)}) collective-permute-start(bf16[256,128]{1,0:T(8,128)(2,1)S(1)} %get-tuple-element.95), channel_id=1, source_target_pairs={{0,2},{2,4},{4,6},{6,8},{8,10},{10,12},{12,14},{1,3},{3,5},{5,7},{... | collective-permute-start | bytes 196616 | tf_op jit(solution)/shard_map/ppermute | solution.py:47
  6.0 8.3 %collective-permute-start.1 = (bf16[256,128]{1,0:T(8,128)(2,1)S(1)}, bf16[256,128]{1,0:T(8,128)(2,1)S(1)}, u32[]{:S(2)}, u32[]{:S(2)}) collective-permute-start(bf16[256,128]{1,0:T(8,128)(2,1)S(1)} %get-tuple-element.96), channel_id=1, source_target_pairs={{2,0},{4,2},{6,4},{8,6},{10,8},{12,10},{14,12},{3,1},{5,3},{7,5},{... | collective-permute-start | bytes 196616 | tf_op jit(solution)/shard_map/ppermute | solution.py:47
  9.3 2.4 %copy-start.6 = (s32[4,3]{1,0:T(4,128)S(1)}, s32[4,3]{1,0:T(4,128)}, u32[]{:S(2)}) copy-start(s32[4,3]{1,0:T(4,128)} %tile_ref.1) | copy-start | bytes 148
  9.3 2.4 %copy-start.7 = (s32[512]{0:T(512)S(1)}, s32[512]{0:T(512)}, u32[]{:S(2)}) copy-start(s32[512]{0:T(512)} %param.16) | copy-start | bytes 6148
  9.4 7.1 %copy-start = (bf16[2,256,1024]{2,1,0:T(8,128)(2,1)S(1)}, bf16[2,256,1024]{2,1,0:T(8,128)(2,1)}, u32[]{:S(2)}) copy-start(bf16[2,256,1024]{2,1,0:T(8,128)(2,1)} %r_1_.3) | copy-start | bytes 3145732
  11.8 1.1 copy-start.4
  14.3 2.2 %copy-start.1 = (bf16[2,256,512]{2,1,0:T(8,128)(2,1)S(1)}, bf16[2,256,512]{2,1,0:T(8,128)(2,1)}, u32[]{:S(2)}) copy-start(bf16[2,256,512]{2,1,0:T(8,128)(2,1)} %r_2_.3) | copy-start | bytes 1572868
  17.1 8.4 %copy-start.8 = (bf16[256,512]{1,0:T(8,128)(2,1)S(1)}, bf16[256,512]{1,0:T(8,128)(2,1)}, u32[]{:S(2)}) copy-start(bf16[256,512]{1,0:T(8,128)(2,1)} %param.12) | copy-start | bytes 786436
  19.5 8.9 %collective-permute-start.4 = (bf16[48,512]{1,0:T(8,128)(2,1)S(1)}, bf16[48,512]{1,0:T(8,128)(2,1)S(1)}, u32[]{:S(2)}, u32[]{:S(2)}) collective-permute-start(bf16[48,512]{1,0:T(8,128)(2,1)S(1)} %get-tuple-element.112), channel_id=1, source_target_pairs={{0,2},{2,4},{4,6},{6,8},{8,10},{10,12},{12,14},{3,1},{5,3},{7,5},{... | collective-permute-start | bytes 147464 | tf_op jit(solution)/shard_map/ppermute | solution.py:54
  22.0 6.4 %collective-permute-start.5 = (bf16[48,512]{1,0:T(8,128)(2,1)S(1)}, bf16[48,512]{1,0:T(8,128)(2,1)S(1)}, u32[]{:S(2)}, u32[]{:S(2)}) collective-permute-start(bf16[48,512]{1,0:T(8,128)(2,1)S(1)} %get-tuple-element.113), channel_id=1, source_target_pairs={{0,4},{2,6},{4,8},{6,10},{8,12},{10,14},{5,1},{7,3},{9,5},{11,7},{... | collective-permute-start | bytes 147464 | tf_op jit(solution)/shard_map/ppermute | solution.py:54
  31.6 8.1 %collective-permute-start.6 = (bf16[32,512]{1,0:T(8,128)(2,1)S(1)}, bf16[32,512]{1,0:T(8,128)(2,1)S(1)}, u32[]{:S(2)}, u32[]{:S(2)}) collective-permute-start(bf16[32,512]{1,0:T(8,128)(2,1)S(1)} %get-tuple-element.118), channel_id=1, source_target_pairs={{0,2},{2,4},{4,6},{6,8},{8,10},{10,12},{12,14},{3,1},{5,3},{7,5},{... | collective-permute-start | bytes 98312 | tf_op jit(solution)/shard_map/ppermute | solution.py:54
  35.9 5.8 %collective-permute-start.7 = (bf16[32,512]{1,0:T(8,128)(2,1)S(1)}, bf16[32,512]{1,0:T(8,128)(2,1)S(1)}, u32[]{:S(2)}, u32[]{:S(2)}) collective-permute-start(bf16[32,512]{1,0:T(8,128)(2,1)S(1)} %get-tuple-element.119), channel_id=1, source_target_pairs={{0,4},{2,6},{4,8},{6,10},{8,12},{10,14},{5,1},{7,3},{9,5},{11,7},{... | collective-permute-start | bytes 98312 | tf_op jit(solution)/shard_map/ppermute | solution.py:54
  43.6 3.7 %copy-start.9 = (bf16[256,512]{1,0:T(8,128)(2,1)S(1)}, bf16[256,512]{1,0:T(8,128)(2,1)}, u32[]{:S(2)}) copy-start(bf16[256,512]{1,0:T(8,128)(2,1)} %param.17) | copy-start | bytes 786436
  44.8 7.8 %collective-permute-start.8 = (bf16[128,512]{1,0:T(8,128)(2,1)S(1)}, bf16[128,512]{1,0:T(8,128)(2,1)S(1)}, u32[]{:S(2)}, u32[]{:S(2)}) collective-permute-start(bf16[128,512]{1,0:T(8,128)(2,1)S(1)} %get-tuple-element.122), channel_id=1, source_target_pairs={{0,2},{2,4},{4,6},{6,8},{8,10},{10,12},{12,14},{3,1},{5,3},{7,5},{... | collective-permute-start | bytes 393224 | tf_op jit(solution)/shard_map/ppermute | solution.py:54
  57.1 7.8 %collective-permute-start.9 = (bf16[128,512]{1,0:T(8,128)(2,1)S(1)}, bf16[128,512]{1,0:T(8,128)(2,1)S(1)}, u32[]{:S(2)}, u32[]{:S(2)}) collective-permute-start(bf16[128,512]{1,0:T(8,128)(2,1)S(1)} %get-tuple-element.136), channel_id=1, source_target_pairs={{0,2},{2,4},{4,6},{6,8},{8,10},{10,12},{12,14},{3,1},{5,3},{7,5},{... | collective-permute-start | bytes 393224 | tf_op jit(solution)/shard_map/ppermute | solution.py:54
  68.0 6.8 %collective-permute-start.10 = (bf16[32,512]{1,0:T(8,128)(2,1)S(1)}, bf16[32,512]{1,0:T(8,128)(2,1)S(1)}, u32[]{:S(2)}, u32[]{:S(2)}) collective-permute-start(bf16[32,512]{1,0:T(8,128)(2,1)S(1)} %get-tuple-element.142), channel_id=1, source_target_pairs={{0,2},{2,4},{4,6},{6,8},{8,10},{10,12},{12,14},{3,1},{5,3},{7,5},{... | collective-permute-start | bytes 98312 | tf_op jit(solution)/shard_map/ppermute | solution.py:54
  71.6 5.8 %collective-permute-start.11 = (bf16[32,512]{1,0:T(8,128)(2,1)S(1)}, bf16[32,512]{1,0:T(8,128)(2,1)S(1)}, u32[]{:S(2)}, u32[]{:S(2)}) collective-permute-start(bf16[32,512]{1,0:T(8,128)(2,1)S(1)} %get-tuple-element.143), channel_id=1, source_target_pairs={{0,4},{2,6},{4,8},{6,10},{8,12},{10,14},{5,1},{7,3},{9,5},{11,7},{... | collective-permute-start | bytes 98312 | tf_op jit(solution)/shard_map/ppermute | solution.py:54
  80.3 8.2 %collective-permute-start.12 = (bf16[32,512]{1,0:T(8,128)(2,1)S(1)}, bf16[32,512]{1,0:T(8,128)(2,1)S(1)}, u32[]{:S(2)}, u32[]{:S(2)}) collective-permute-start(bf16[32,512]{1,0:T(8,128)(2,1)S(1)} %get-tuple-element.148), channel_id=1, source_target_pairs={{0,2},{2,4},{4,6},{6,8},{8,10},{10,12},{12,14},{3,1},{5,3},{7,5},{... | collective-permute-start | bytes 98312 | tf_op jit(solution)/shard_map/ppermute | solution.py:54
  83.2 5.8 %collective-permute-start.13 = (bf16[32,512]{1,0:T(8,128)(2,1)S(1)}, bf16[32,512]{1,0:T(8,128)(2,1)S(1)}, u32[]{:S(2)}, u32[]{:S(2)}) collective-permute-start(bf16[32,512]{1,0:T(8,128)(2,1)S(1)} %get-tuple-element.149), channel_id=1, source_target_pairs={{0,4},{2,6},{4,8},{6,10},{8,12},{10,14},{5,1},{7,3},{9,5},{11,7},{... | collective-permute-start | bytes 98312 | tf_op jit(solution)/shard_map/ppermute | solution.py:54
  85.3 14.7 %collective-permute-start.21 = (bf16[4,384,128]{2,1,0:T(8,128)(2,1)S(1)}, bf16[4,384,128]{2,1,0:T(8,128)(2,1)S(1)}, u32[]{:S(2)}, u32[]{:S(2)}) collective-permute-start(bf16[4,384,128]{2,1,0:T(8,128)(2,1)S(1)} %get-tuple-element.173), channel_id=1, source_target_pairs={{0,2},{2,0},{1,3},{3,1},{4,6},{6,4},{5,7},{7,5},{8,10},{10,8},{9,1... | collective-permute-start | bytes 1179656 | tf_op jit(solution)/shard_map/ppermute | solution.py:66
  87.9 10.4 %collective-permute-start.14 = (bf16[4,128,128]{2,1,0:T(8,128)(2,1)S(1)}, bf16[4,128,128]{2,1,0:T(8,128)(2,1)S(1)}, u32[]{:S(2)}, u32[]{:S(2)}) collective-permute-start(bf16[4,128,128]{2,1,0:T(8,128)(2,1)S(1)} %get-tuple-element.162), channel_id=1, source_target_pairs={{0,2},{2,0},{1,3},{3,1},{4,6},{6,4},{5,7},{7,5},{8,10},{10,8},{9,1... | collective-permute-start | bytes 393224 | tf_op jit(solution)/shard_map/ppermute | solution.py:66
  98.3 9.4 %collective-permute-start.15 = (bf16[4,384,128]{2,1,0:T(8,128)(2,1)S(1)}, bf16[4,384,128]{2,1,0:T(8,128)(2,1)S(1)}, u32[]{:S(2)}, u32[]{:S(2)}) collective-permute-start(bf16[4,384,128]{2,1,0:T(8,128)(2,1)S(1)} %get-tuple-element.163), channel_id=1, source_target_pairs={{0,2},{2,0},{1,3},{3,1},{4,6},{6,4},{5,7},{7,5},{8,10},{10,8},{9,1... | collective-permute-start | bytes 1179656 | tf_op jit(solution)/shard_map/ppermute | solution.py:66
  100.6 12.6 %collective-permute-start.22 = (bf16[512,128]{1,0:T(8,128)(2,1)S(1)}, bf16[512,128]{1,0:T(8,128)(2,1)S(1)}, u32[]{:S(2)}, u32[]{:S(2)}) collective-permute-start(bf16[512,128]{1,0:T(8,128)(2,1)S(1)} %get-tuple-element.177), channel_id=1, source_target_pairs={{0,4},{4,0},{8,12},{12,8},{1,5},{5,1},{9,13},{13,9},{2,6},{6,2},{1... | collective-permute-start | bytes 393224 | tf_op jit(solution)/shard_map/ppermute | solution.py:70
  100.7 12.6 %collective-permute-start.23 = (bf16[512,128]{1,0:T(8,128)(2,1)S(1)}, bf16[512,128]{1,0:T(8,128)(2,1)S(1)}, u32[]{:S(2)}, u32[]{:S(2)}) collective-permute-start(bf16[512,128]{1,0:T(8,128)(2,1)S(1)} %get-tuple-element.178), channel_id=1, source_target_pairs={{0,8},{4,12},{8,0},{12,4},{1,9},{5,13},{9,1},{13,5},{2,10},{6,14},... | collective-permute-start | bytes 393224 | tf_op jit(solution)/shard_map/ppermute | solution.py:70
  103.7 17.5 %collective-permute-start.24 = (bf16[512,128]{1,0:T(8,128)(2,1)S(1)}, bf16[512,128]{1,0:T(8,128)(2,1)S(1)}, u32[]{:S(2)}, u32[]{:S(2)}) collective-permute-start(bf16[512,128]{1,0:T(8,128)(2,1)S(1)} %get-tuple-element.179), channel_id=1, source_target_pairs={{0,12},{4,8},{8,4},{12,0},{1,13},{5,9},{9,5},{13,1},{2,14},{6,10},... | collective-permute-start | bytes 393224 | tf_op jit(solution)/shard_map/ppermute | solution.py:70
  108.3 21.1 %collective-permute-start.18 = (bf16[384,128]{1,0:T(8,128)(2,1)S(1)}, bf16[384,128]{1,0:T(8,128)(2,1)S(1)}, u32[]{:S(2)}, u32[]{:S(2)}) collective-permute-start(bf16[384,128]{1,0:T(8,128)(2,1)S(1)} %get-tuple-element.169), channel_id=1, source_target_pairs={{0,4},{4,0},{8,12},{12,8},{1,5},{5,1},{9,13},{13,9},{2,6},{6,2},{1... | collective-permute-start | bytes 294920 | tf_op jit(solution)/shard_map/ppermute | solution.py:70
  108.3 21.1 %collective-permute-start.19 = (bf16[384,128]{1,0:T(8,128)(2,1)S(1)}, bf16[384,128]{1,0:T(8,128)(2,1)S(1)}, u32[]{:S(2)}, u32[]{:S(2)}) collective-permute-start(bf16[384,128]{1,0:T(8,128)(2,1)S(1)} %get-tuple-element.170), channel_id=1, source_target_pairs={{0,8},{4,12},{8,0},{12,4},{1,9},{5,13},{9,1},{13,5},{2,10},{6,14},... | collective-permute-start | bytes 294920 | tf_op jit(solution)/shard_map/ppermute | solution.py:70
  113.2 16.1 %collective-permute-start.20 = (bf16[384,128]{1,0:T(8,128)(2,1)S(1)}, bf16[384,128]{1,0:T(8,128)(2,1)S(1)}, u32[]{:S(2)}, u32[]{:S(2)}) collective-permute-start(bf16[384,128]{1,0:T(8,128)(2,1)S(1)} %get-tuple-element.171), channel_id=1, source_target_pairs={{0,12},{4,8},{8,4},{12,0},{1,13},{5,9},{9,5},{13,1},{2,14},{6,10},... | collective-permute-start | bytes 294920 | tf_op jit(solution)/shard_map/ppermute | solution.py:70
  113.3 13.2 %collective-permute-start.16 = (bf16[128,256]{1,0:T(8,128)(2,1)S(1)}, bf16[128,256]{1,0:T(8,128)(2,1)S(1)}, u32[]{:S(2)}, u32[]{:S(2)}) collective-permute-start(bf16[128,256]{1,0:T(8,128)(2,1)S(1)} %get-tuple-element.164), channel_id=1, source_target_pairs={{2,0},{4,2},{6,4},{8,6},{10,8},{12,10},{14,12},{3,1},{5,3},{7,5},{... | collective-permute-start | bytes 196616 | tf_op jit(solution)/shard_map/ppermute | solution.py:47
  121.2 7.0 %collective-permute-start.17 = (bf16[128,256]{1,0:T(8,128)(2,1)S(1)}, bf16[128,256]{1,0:T(8,128)(2,1)S(1)}, u32[]{:S(2)}, u32[]{:S(2)}) collective-permute-start(bf16[128,256]{1,0:T(8,128)(2,1)S(1)} %get-tuple-element.165), channel_id=1, source_target_pairs={{0,2},{2,4},{4,6},{6,8},{8,10},{10,12},{12,14},{1,3},{3,5},{5,7},{... | collective-permute-start | bytes 196616 | tf_op jit(solution)/shard_map/ppermute | solution.py:47

commit v4 on v3

--- a/solution.py
+++ b/solution.py
@@ -41,16 +41,12 @@
     )(*scalars, *arrays)
 
 
-def shifted(value, steps):
-    count = lax.axis_size(DOM)
-    first, last = (max(0, -steps), min(count, count - steps))
-    return lax.ppermute(value, DOM, [(s, s + steps) for s in range(first, last)])
-
-
 def two_way(value, steps):
     count = lax.axis_size(DOM)
     pairs = [(2 * p, 2 * (p + steps)) for p in range(count - steps)]
     pairs += [(2 * p + 1, 2 * (p - steps) + 1) for p in range(steps, count)]
+    pairs += [(2 * p, 2 * p + 1) for p in range(count - steps, count)]
+    pairs += [(2 * p + 1, 2 * p) for p in range(steps)]
     return lax.ppermute(value, LINE, pairs)
 
 
@@ -83,12 +79,13 @@
     return jnp.concatenate([col] * (width // col.shape[1]), axis=1)
 
 
-def k_halo(rows_ref, x_ref, next_ref, prev_ref):
-    x = x_ref[...]
-    n = x.shape[1]
-    at = lax.broadcasted_iota(I32, (n, rows_ref.shape[1]), 0)
-    next_ref[...] = dot(x, (at == rows_ref[0:1, :]).astype(BF)).astype(BF)
-    prev_ref[...] = dot(x, (at == rows_ref[1:2, :]).astype(BF)).astype(BF)
+def k_halo(me_ref, rows_ref, x_ref, xc_ref, msg_ref):
+    xc = x_ref[...].T
+    xc_ref[...] = xc
+    row = jnp.where(me_ref[1] == 0, rows_ref[0:1, :], rows_ref[1:2, :])
+    at = lax.broadcasted_iota(I32, (xc.shape[0], row.shape[1]), 0)
+    pick = (at == row).astype(F32).T.astype(BF)
+    msg_ref[...] = dot(pick, xc).astype(BF)
 
 
 def k_weights(layer, me_ref, win_ref, wout_ref, win2_ref, wout2_ref, in_ref, out_ref):
@@ -161,18 +158,28 @@
     two_ref[0:cap, :] = dot(slot_ref[pl.ds(a + 2 * cap, cap), :], values).astype(BF)
 
 
-def k_first(me_ref, x_ref, rims_ref, adj_ref, inv_ref, win_ref, wo_ref,
-            slot_ref, tags_ref,
-            xc_ref, agg_ref, pre_ref, hid_ref, first_ref, one_ref, two_ref, src):
-    n = x_ref.shape[1]
-    rim = rims_ref.shape[2]
-    half = rims_ref.shape[1] // 2
-    xc = x_ref[...].T
-    xc_ref[...] = xc
+def fill_sources(me_ref, xc, rims_ref, src):
+    n = xc.shape[0]
+    rim = rims_ref.shape[1]
     src[0:n, :] = xc
     for c in range(2):
-        src[n:n + rim, c * half:(c + 1) * half] = rims_ref[c, 0:half, :].T
-        src[n + rim:, c * half:(c + 1) * half] = rims_ref[c, half:, :].T
+        rows = slice(n + c * rim, n + (c + 1) * rim)
+        there = me_ref[0] >= 1 if c == 0 else me_ref[0] < me_ref[4] - 1
+
+        @pl.when(there)
+        def _():
+            src[rows, :] = rims_ref[c]
+
+        @pl.when(jnp.logical_not(there))
+        def _():
+            src[rows, :] = jnp.zeros((rim, xc.shape[1]), BF)
+
+
+def k_first(me_ref, xc_ref, rims_ref, adj_ref, inv_ref, win_ref, wo_ref,
+            slot_ref, tags_ref,
+            agg_ref, pre_ref, hid_ref, first_ref, one_ref, two_ref, src):
+    xc = xc_ref[...]
+    fill_sources(me_ref, xc, rims_ref, src)
     agg, pre, hid, out = forward(xc, src[...], adj_ref, inv_ref, win_ref, wo_ref)
     agg_ref[...] = agg
     pre_ref[...] = pre
@@ -190,10 +197,6 @@
     slope_ref[...] = slope_of(pre_ref[...])
 
 
-def k_pool(hott_ref, v_ref, pool_ref):
-    pool_ref[...] = dot(hott_ref[...], v_ref[...])
-
-
 def k_cot(ct_ref, wo_ref, ctc_ref, hg_ref):
     ctc = ct_ref[...].T
     ctc_ref[...] = ctc
@@ -216,6 +219,9 @@
     slots = 4 * cap
     lane = lax.broadcasted_iota(I32, (1, slots), 1)
     t = [got_ref[c, o + cap:o + cap + 1, 0:slots].astype(F32) for o in (0, rows) for c in range(2)]
+    domain, count = me_ref[0], me_ref[4]
+    there = (domain >= 1, domain < count - 1, domain >= 2, domain < count - 2)
+    t = [jnp.where(ok, v, 0.0) for ok, v in zip(there, t)]
     tags = jnp.where(lane < cap, t[0], jnp.where(lane < 2 * cap, t[1], jnp.where(lane < 3 * cap, t[2], t[3])))
     node = (lax.broadcasted_iota(I32, (nodes, slots), 0) + 1).astype(F32)
     hits = (node == tags).astype(F32)
@@ -267,10 +273,8 @@
 
 def k_second(me_ref, lift_ref, rim_ref, adj_ref, adjt_ref, inv_ref, win_ref, wo_ref, hg_ref,
              agg_ref, hid_ref, new_ref, pg_ref, scaled_ref, msg_ref, src):
-    n = lift_ref.shape[0]
     lifted = lift_ref[...]
-    src[0:n, :] = lifted
-    src[n:, :] = rim_ref[...]
+    fill_sources(me_ref, lifted, rim_ref, src)
     agg, pre, hid, out = forward(lifted, src[...], adj_ref, inv_ref, win_ref, wo_ref)
     agg_ref[...] = agg
     hid_ref[...] = hid
@@ -289,10 +293,11 @@
     )
 
 
-def k_newt(me_ref, new_ref, out_ref):
+def k_newt(me_ref, hott_ref, lg_ref, new_ref, pool_ref, out_ref):
     half = out_ref.shape[0]
     at = pl.multiple_of(me_ref[1] * half, half)
     out_ref[...] = new_ref[:, pl.ds(at, half)].T
+    pool_ref[...] = dot(hott_ref[...], lg_ref[...])
 
 
 def k_grads(scale, me_ref, pg_ref, h_ref, agg_ref, g_ref, hid_ref, gin_ref, gout_ref):
@@ -359,10 +364,15 @@
     place_pieces(me_ref, lambda d: small_pieces(values, d, piece, 0), keep_ref, send_ref)
 
 
+def placed(me_ref, place_ref, before, after):
+    rim = before.shape[0]
+    from_after = dot(place_ref[:, 0:rim], after)
+    from_before = dot(place_ref[:, rim:], before)
+    return jnp.where(me_ref[0] < me_ref[4] - 1, from_after, 0.0) + jnp.where(me_ref[0] >= 1, from_before, 0.0)
+
+
 def k_lgrad(me_ref, comb_ref, rim_ref, place_ref, slot_ref, lg_ref, one_ref, two_ref):
-    rim = rim_ref.shape[0] // 2
-    lg = comb_ref[...] + dot(place_ref[:, 0:rim], rim_ref[rim:, :]) + dot(place_ref[:, rim:], rim_ref[0:rim, :])
-    lg = lg.astype(BF)
+    lg = (comb_ref[...] + placed(me_ref, place_ref, rim_ref[0], rim_ref[1])).astype(BF)
     lg_ref[...] = lg
     send_slots(me_ref[1], lg, slot_ref, one_ref, two_ref)
 
@@ -390,29 +400,27 @@
 
 def k_third(me_ref, lg_ref, hot_ref, slott_ref, spread_ref, got_ref, wo_ref, slope_ref,
             win_ref, inv_ref, adjt_ref, *rest, scale=None):
-    fb_ref, pg_ref, scaled_ref, before_ref, after_ref = rest[-5:] if scale is None else rest[3:8]
+    fb_ref, pg_ref, scaled_ref, msg_ref = rest[-4:] if scale is None else rest[3:7]
     fb = spread_back(lg_ref[...], hot_ref, slott_ref, spread_ref[...], got_ref)
     fb_ref[...] = fb
     pg = (dot(fb, wo_ref[...]) * slope_ref[...]).astype(BF)
     pg_ref[...] = pg
     if scale is not None:
         xc_ref, agg_ref, hid_ref = rest[:3]
-        pack_grads(scale, me_ref, pg_ref, xc_ref, agg_ref, fb_ref, hid_ref, rest[8], rest[9])
-    n, width = fb.shape
-    half = width // 2
-    rim = before_ref.shape[0]
-    scaled = (dot(pg, win_ref[:, width:]) * wide(inv_ref[...], width)).astype(BF)
-    scaled_ref[...] = scaled
+        pack_grads(scale, me_ref, pg_ref, xc_ref, agg_ref, fb_ref, hid_ref, rest[7], rest[8])
+    rim_grads(me_ref[1], pg, win_ref, inv_ref, adjt_ref, scaled_ref, msg_ref)
+
+
+def k_last(me_ref, comb_ref, rim_ref, place_ref, *rest):
+    half = comb_ref.shape[1]
     at = pl.multiple_of(me_ref[1] * half, half)
-    both = dot(adjt_ref[n:, :], scaled_ref[:, pl.ds(at, half)]).astype(BF)
-    before_ref[...] = both[0:rim]
-    after_ref[...] = both[rim:]
-
-
-def k_last(comb_ref, after_ref, before_ref, place_ref, out_ref):
-    rim = after_ref.shape[0]
-    total = comb_ref[...] + dot(place_ref[:, 0:rim], after_ref[...]) + dot(place_ref[:, rim:], before_ref[...])
-    out_ref[...] = total.T
+    total = comb_ref[...] + placed(
+        me_ref, place_ref, rim_ref[0, :, pl.ds(at, half)], rim_ref[1, :, pl.ds(at, half)])
+    if len(rest) == 1:
+        rest[0][...] = total.T
+    else:
+        rest[4][...] = total.T
+        k_sum(*rest[:4], *rest[5:])
 
 
 def k_halfcomb(me_ref, fb_ref, pg_ref, win_ref, scaled_ref, adjt_ref, comb_ref):
@@ -439,6 +447,11 @@
             other = z ^ step
             outs[step - 1][rows, :] = (keep_ref[other] + got_ref[other].astype(F32)).astype(BF)
         row += keep_ref.shape[1]
+
+
+def k_stage_comb(me_ref, fb_ref, pg_ref, win_ref, scaled_ref, adjt_ref, *refs):
+    k_stage(me_ref, *refs[:-1])
+    k_halfcomb(me_ref, fb_ref, pg_ref, win_ref, scaled_ref, adjt_ref, refs[-1])
 
 
 def unpack_small(total):
@@ -479,16 +492,16 @@
     slots = 4 * cap
     hidden = 2 * inward_weight.shape[1]
     scale = float(n * domains) ** -0.5
-    me = jnp.stack([lax.axis_index(a) for a in (DOM, "sub", "cross", "curve")]).astype(I32)
+    me = jnp.stack(
+        [lax.axis_index(a) for a in (DOM, "sub", "cross", "curve")] + [jnp.int32(domains)]).astype(I32)
     rows = send_rows[0]
     packed = cross == 2 and curve == 4 and 2 * width == 1024 and hidden == width
 
-    halo_next, halo_prev = call(
-        k_halo, [sds((half, rim), BF)] * 2, [], [rows, node_features], "halo")
-    before_half = shifted(halo_next, 1)
-    after_half = shifted(halo_prev, -1)
+    cell_bf, cell_f32 = sds((n, width), BF), sds((n, width), F32)
     win2, wout2 = swap(inward_weight), swap(outward_weight)
     x_full = gather(node_features)
+    xc, rims = call(k_halo, [cell_bf, sds((rim, width), BF)], [me], [rows, x_full], "halo")
+    rims = two_way(rims, 1)
     (adj, adjt, inv, hott, hot, slot, slott, pick, place, tags, ocount) = call(
         k_prep,
         [sds((n, src_rows), BF), sds((src_rows, n), BF), sds((n, 128), F32), sds((nodes, n), BF),
@@ -498,15 +511,14 @@
     weight_outs = [sds((hidden, 2 * width), BF), sds((width, hidden), BF)]
     win0, wo0 = call(lambda *r: k_weights(0, *r), weight_outs, [me],
                      [inward_weight, outward_weight, win2, wout2], "weights0")
-    rims = gather(jnp.concatenate([before_half, after_half], axis=0)).reshape(2, width, rim)
+    rims = gather(rims).reshape(2, rim, width)
     msg = sds((cap + 16, width), BF)
     plain = sds((cap, width), BF)
-    cell_bf, cell_f32 = sds((n, width), BF), sds((n, width), F32)
     hid_bf, hid_f32 = sds((n, hidden), BF), sds((n, hidden), F32)
-    xc, agg0, pre0, hid0, first, one, two = call(
+    agg0, pre0, hid0, first, one, two = call(
         k_first,
-        [cell_bf, cell_bf, hid_f32, hid_bf, cell_bf, msg, msg],
-        [me], [x_full, rims, adj, inv, win0, wo0, slot, tags], "first",
+        [cell_bf, hid_f32, hid_bf, cell_bf, msg, msg],
+        [me], [xc, rims, adj, inv, win0, wo0, slot, tags], "first",
         flops=2 * n * width * (src_rows + 3 * width),
         scratch=[pltpu.VMEM((src_rows, width), BF)])
     one, two, win2, coarse_weight = lax.optimization_barrier((one, two, win2, coarse_weight))
@@ -528,7 +540,7 @@
     lifted, rims = call(
         k_lift, [cell_bf, sds((rim, width), BF)], [me],
         [first, hot, slott, corr, got, pick], "lift")
-    rims = gather(two_way(rims, 1))
+    rims = gather(two_way(rims, 1)).reshape(2, rim, width)
     agg1, hid1, new, pg1, scaled1, rims = call(
         k_second, [cell_bf, hid_bf, cell_bf, hid_bf, cell_bf, sds((rim, width), BF)],
         [me], [lifted, rims, adj, adjt, inv, win1, wo1, hg1], "second",
@@ -543,23 +555,23 @@
                             [pg1, lifted, agg1, ctc, hid1, win1, scaled1, adjt], "combine")
     else:
         comb1, = call(k_combine, [cell_f32], [], [ctc, pg1, win1, scaled1, adjt], "combine")
-    rims = gather(rims)
+    rims = gather(rims).reshape(2, rim, width)
     lg, one, two = call(
         k_lgrad, [cell_bf, plain, plain], [me], [comb1, rims, place, slot], "lgrad")
     if packed:
         one, two, send1 = lax.optimization_barrier((one, two, send1))
         got1 = cross_swap(send1)
     one, two = two_way(one, 1), two_way(two, 2)
-    own_g, = call(k_pool, [node_f32], [], [hott, lg], "own_grad")
-    new_t, = call(k_newt, [sds((half, n), BF)], [me], [new], "new")
+    own_g, new_t = call(k_newt, [node_f32, sds((half, n), BF)], [me], [hott, lg, new], "own_grad")
     got = gather(jnp.concatenate([one, two], axis=0)).reshape(2, -1, width)
+    if packed:
+        got, got1 = lax.optimization_barrier((got, got1))
     pgrad, spread, one, two = call(
         k_cgrad, [node_bf, node_bf, plain, plain], [me],
         [own_g, got, hits, icount, cpre, cw], "cgrad")
     one, two = two_way(one, 1), two_way(two, 2)
     got = gather(jnp.concatenate([one, two], axis=0)).reshape(2, -1, width)
-    rim_half = sds((rim, half), BF)
-    back_outs = [cell_bf, hid_bf, cell_bf, rim_half, rim_half]
+    back_outs = [cell_bf, hid_bf, cell_bf, sds((rim, width), BF)]
     back_args = [lg, hot, slott, spread, got, wo0, slope0, win0, inv, adjt]
     if packed:
         keepc, sendc = call(
@@ -567,35 +579,38 @@
             [sds((curve, 2 * small, piece), F32), sds((curve, 2 * small, piece), BF)], [me],
             [pgrad, coarse], "cweight")
         gotc = cross_swap(sendc)
-        fb, pg0, scaled0, to_before, to_after, keep0, send0 = call(
+        fb, pg0, scaled0, rims, keep0, send0 = call(
             lambda *r: k_third(*r, scale=scale), back_outs + pack, [me], back_args + [xc, agg0, hid0], "third")
-        send0, gotc = lax.optimization_barrier((send0, gotc))
         got0 = cross_swap(send0)
-
-        def staged(pairs, name):
+        rims = two_way(rims, 1)
+
+        def staged(body, extra, extra_outs, pairs, name):
             total = sum(keep.shape[1] for keep in pairs[::2])
-            own, *outs = call(k_stage, [sds((total, piece), F32)] + [sds((total, piece), BF)] * 3, [me], pairs, name)
-            return [own] + [curve_swap(value, step) for step, value in zip((1, 2, 3), outs)]
-
-        early = staged([keep1, got1, keepc, gotc], "stage1")
-        to_before, to_after, got0 = lax.optimization_barrier((to_before, to_after, got0))
-        late = staged([keep0, got0], "stage0")
+            own, *outs = call(
+                body, [sds((total, piece), F32)] + [sds((total, piece), BF)] * 3 + extra_outs,
+                [me], extra + pairs, name)
+            return [own] + [curve_swap(value, step) for step, value in zip((1, 2, 3), outs)], outs[3:]
+
+        early, (comb0,) = staged(
+            k_stage_comb, [fb, pg0, win0, scaled0, adjt], [sds((n, half), F32)],
+            [keep1, got1, keepc, gotc], "stage1")
+        late, _ = staged(k_stage, [], [], [keep0, got0], "stage0")
     else:
         gco, = call(lambda *r: k_cweight(scale, *r), [sds((half, width), F32)], [me], [pgrad, coarse], "cweight")
-        fb, pg0, scaled0, to_before, to_after = call(k_third, back_outs, [me], back_args, "third")
-    from_after = shifted(to_before, -1)
-    from_before = shifted(to_after, 1)
-    comb0, = call(k_halfcomb, [sds((n, half), F32)], [me], [fb, pg0, win0, scaled0, adjt], "halfcomb")
-    fgrad, = call(k_last, [sds((half, n), F32)], [], [comb0, from_after, from_before, place], "last")
+        fb, pg0, scaled0, rims = call(k_third, back_outs, [me], back_args, "third")
+        rims = two_way(rims, 1)
+        comb0, = call(k_halfcomb, [sds((n, half), F32)], [me], [fb, pg0, win0, scaled0, adjt], "halfcomb")
+    rims = gather(rims).reshape(2, rim, width)
     if packed:
-        ein, eout, gco = call(
-            k_sum, [sds((half, piece), F32), sds((small, half), F32), sds((small, half), F32)],
-            [], early, "sums")
+        fgrad, ein, eout, gco = call(
+            k_last, [sds((half, n), F32), sds((half, piece), F32), sds((small, half), F32), sds((small, half), F32)],
+            [me], [comb0, rims, place] + early, "last")
         gin, gout = call(
             k_sum_late, [sds((2, half, piece), F32), sds((2, small, half), F32)], [], late + [ein, eout], "late")
         gout = gout.swapaxes(1, 2)
         gco = gco.T
     else:
+        fgrad, = call(k_last, [sds((half, n), F32)], [me], [comb0, rims, place], "last")
         shapes = [sds((half, 2 * width), F32), sds((half, hidden), F32)]
         gi1, go1 = call(lambda *r: k_grads(scale, *r), shapes, [me], [pg1, lifted, agg1, ctc, hid1], "grads1")
         gi0, go0 = call(lambda *r: k_grads(scale, *r), shapes, [me], [pg0, xc, agg0, fb, hid0], "grads0")

time: 131 us -> 122 us (0.931)
  the two profiles are of different devices: /device:TPU:8 before, /device:TPU:0 now
where the time goes in v4:
time: 122 us
  starting transfers between devices  37.4 us (31%)
  waiting for transfers between devices  34 us (28%)
  Pallas kernels  26.3 us (22%)
  blocking collectives  23.4 us (19%)
    pallas_call x20, Pallas kernels, call(): pl.pallas_call(body, out_shape=tuple(outs), in_specs=[pl.BlockSpec(memory...  26.3 us
    all_gather x11, blocking collectives, gather(): return lax.all_gather(value, 'sub', axis=0, tiled=True)  23.4 us
    ppermute x12, starting transfers between devices, two_way(): return lax.ppermute(value, LINE, pairs)  21.5 us
    ppermute x12, waiting for transfers between devices, two_way(): return lax.ppermute(value, LINE, pairs)  13.6 us
    ppermute x3, waiting for transfers between devices, cross_swap(): return lax.ppermute(value, 'cross', [(0, 1), (1, 0)])  11.3 us
    ppermute x6, starting transfers between devices, curve_swap(): return lax.ppermute(value, 'curve', [(z, z ^ step) for z in range(4)])  10.7 us
    ppermute x6, waiting for transfers between devices, curve_swap(): return lax.ppermute(value, 'curve', [(z, z ^ step) for z in range(4)])  9.13 us
    ppermute x3, starting transfers between devices, cross_swap(): return lax.ppermute(value, 'cross', [(0, 1), (1, 0)])  4.66 us
  transfers between devices with their start and end apart: 23, of which 9 were waited for; matrix products, arithmetic and copies ran while one was open for 0% of the time, Pallas kernels for 10%

profile of v4, /device:TPU:0, one launch (start us, length us, event | category | flops | bytes accessed | tf_op | source)
XLA Modules:
  0.0 122.1 jit_solution(16078989012382693204)
XLA Ops:
  1.3 3.5 %all_gather.33.x_ref = bf16[512,512]{1,0:T(8,128)(2,1)S(1)} all-gather(bf16[256,512]{1,0:T(8,128)(2,1)} %param.9), channel_id=1, replica_groups=mesh['groups'=2,'curve'=4,'cross'=2,'sub'=2] {'sub'}, dimensions={0}, use_global_device_ids=true | all-gather | bytes 786432 | tf_op jit(solution)/shard_map/all_gather | solution.py:54
  5.7 2.9 %collective-permute-start = (bf16[128,512]{1,0:T(8,128)(2,1)S(1)}, bf16[128,512]{1,0:T(8,128)(2,1)S(1)}, u32[]{:S(2)}, u32[]{:S(2)}) collective-permute-start(bf16[128,512]{1,0:T(8,128)(2,1)S(1)} %get-tuple-element.96), channel_id=1, source_target_pairs={{0,2},{2,4},{4,6},{6,8},{8,10},{10,12},{12,14},{3,1},{5,3},{7,5},{... | collective-permute-start | bytes 393224 | tf_op jit(solution)/shard_map/ppermute | solution.py:50
  8.7 1.3 %prep.1 = (bf16[512,768]{1,0:T(8,128)(2,1)S(1)}, bf16[768,512]{1,0:T(8,128)(2,1)S(1)}, f32[512,128]{1,0:T(8,128)S(1)}, bf16[128,512]{1,0:T(8,128)(2,1)S(1)}, bf1...) custom-call(s32[4,3]{1,0:T(4,128)S(1)} %copy-done.4, ...), custom_call_target="tpu_custom_call" | custom-call | bytes 3742720 | tf_op jit(solution)/shard_map/prep/pallas_call | solution.py:31
  10.0 2.5 %collective-permute-done = bf16[128,512]{1,0:T(8,128)(2,1)S(1)} collective-permute-done((bf16[128,512]{1,0:T(8,128)(2,1)S(1)}, bf16[128,512]{1,0:T(8,128)(2,1)S(1)}, u32[]{:S(2)}, u32[]{:S(2)}) %collective-permute-start) | collective-permute-done | bytes 131104 | tf_op jit(solution)/shard_map/ppermute | solution.py:50
  12.5 2.0 %all_gather.34 = bf16[256,512]{1,0:T(8,128)(2,1)S(1)} all-gather(bf16[128,512]{1,0:T(8,128)(2,1)S(1)} %collective-permute-done), channel_id=1, replica_groups=mesh['groups'=2,'curve'=4,'cross'=2,'sub'=2] {'sub'}, dimensions={0}, use_global_device_ids=true | all-gather | bytes 393216 | tf_op jit(solution)/shard_map/all_gather | solution.py:54
  15.2 2.4 %first.1 = (bf16[512,512]{1,0:T(8,128)(2,1)S(1)}, f32[512,512]{1,0:T(8,128)S(1)}, bf16[512,512]{1,0:T(8,128)(2,1)S(1)}, bf16[512,512]{1,0:T(8,128)(2,1)S(1)}, bf...) custom-call(s32[5]{0:T(128)S(1)} %stack.19.me_ref.r_0_, bf16[512,512]{1,0:T(8,128)(2,1)S(1)} %get-tuple-element.95.xc_ref.r_11_, ...), custom_call_target="tpu_custom_call" | custom-call | flops 1207959552 | bytes 6262784 | tf_op jit(solution)/shard_map/first/pallas_call | solution.py:31
  17.6 2.5 %collective-permute-start.3 = (bf16[48,512]{1,0:T(8,128)(2,1)S(1)}, bf16[48,512]{1,0:T(8,128)(2,1)S(1)}, u32[]{:S(2)}, u32[]{:S(2)}) collective-permute-start(bf16[48,512]{1,0:T(8,128)(2,1)S(1)} %get-tuple-element.111), channel_id=1, source_target_pairs={{0,2},{2,4},{4,6},{6,8},{8,10},{10,12},{12,14},{3,1},{5,3},{7,5},{... | collective-permute-start | bytes 147464 | tf_op jit(solution)/shard_map/ppermute | solution.py:50
  20.1 1.6 %collective-permute-start.4 = (bf16[48,512]{1,0:T(8,128)(2,1)S(1)}, bf16[48,512]{1,0:T(8,128)(2,1)S(1)}, u32[]{:S(2)}, u32[]{:S(2)}) collective-permute-start(bf16[48,512]{1,0:T(8,128)(2,1)S(1)} %get-tuple-element.112), channel_id=1, source_target_pairs={{0,4},{2,6},{4,8},{6,10},{8,12},{10,14},{5,1},{7,3},{9,5},{11,7},{... | collective-permute-start | bytes 147464 | tf_op jit(solution)/shard_map/ppermute | solution.py:50
  21.7 2.2 %all_gather.36.cw_ref = bf16[512,512]{1,0:T(8,128)(2,1)S(1)} all-gather(bf16[256,512]{1,0:T(8,128)(2,1)S(1)} %copy-done.6), channel_id=1, replica_groups=mesh['groups'=2,'curve'=4,'cross'=2,'sub'=2] {'sub'}, dimensions={0}, use_global_device_ids=true | all-gather | bytes 786432 | tf_op jit(solution)/shard_map/all_gather | solution.py:54
  24.6 1.9 %all_gather.35 = bf16[192,512]{1,0:T(8,128)(2,1)S(1)} all-gather(bf16[96,512]{1,0:T(8,128)(2,1)S(1)} %pad_maximum_fusion), channel_id=1, replica_groups=mesh['groups'=2,'curve'=4,'cross'=2,'sub'=2] {'sub'}, dimensions={0}, use_global_device_ids=true | all-gather | bytes 294912 | tf_op jit(solution)/shard_map/all_gather | solution.py:54
  26.6 1.1 coarse.1
  27.7 1.1 collective-permute-start.5
  28.8 1.6 %collective-permute-start.6 = (bf16[32,512]{1,0:T(8,128)(2,1)S(1)}, bf16[32,512]{1,0:T(8,128)(2,1)S(1)}, u32[]{:S(2)}, u32[]{:S(2)}) collective-permute-start(bf16[32,512]{1,0:T(8,128)(2,1)S(1)} %get-tuple-element.118), channel_id=1, source_target_pairs={{0,4},{2,6},{4,8},{6,10},{8,12},{10,14},{5,1},{7,3},{9,5},{11,7},{... | collective-permute-start | bytes 98312 | tf_op jit(solution)/shard_map/ppermute | solution.py:50
  32.0 1.9 %all_gather.37 = bf16[128,512]{1,0:T(8,128)(2,1)S(1)} all-gather(bf16[64,512]{1,0:T(8,128)(2,1)S(1)} %pad_maximum_fusion.1), channel_id=1, replica_groups=mesh['groups'=2,'curve'=4,'cross'=2,'sub'=2] {'sub'}, dimensions={0}, use_global_device_ids=true | all-gather | bytes 196608 | tf_op jit(solution)/shard_map/all_gather | solution.py:54
  33.9 1.1 lift.1
  35.0 1.6 %collective-permute-start.7 = (bf16[128,512]{1,0:T(8,128)(2,1)S(1)}, bf16[128,512]{1,0:T(8,128)(2,1)S(1)}, u32[]{:S(2)}, u32[]{:S(2)}) collective-permute-start(bf16[128,512]{1,0:T(8,128)(2,1)S(1)} %get-tuple-element.121), channel_id=1, source_target_pairs={{0,2},{2,4},{4,6},{6,8},{8,10},{10,12},{12,14},{3,1},{5,3},{7,5},{... | collective-permute-start | bytes 393224 | tf_op jit(solution)/shard_map/ppermute | solution.py:50
  36.7 2.2 %all_gather.39.ct_ref = bf16[512,512]{1,0:T(8,128)(2,1)S(1)} all-gather(bf16[256,512]{1,0:T(8,128)(2,1)S(1)} %copy-done.7), channel_id=1, replica_groups=mesh['groups'=2,'curve'=4,'cross'=2,'sub'=2] {'sub'}, dimensions={0}, use_global_device_ids=true | all-gather | bytes 786432 | tf_op jit(solution)/shard_map/all_gather | solution.py:54
  39.3 1.2 %collective-permute-done.7 = bf16[128,512]{1,0:T(8,128)(2,1)S(1)} collective-permute-done((bf16[128,512]{1,0:T(8,128)(2,1)S(1)}, bf16[128,512]{1,0:T(8,128)(2,1)S(1)}, u32[]{:S(2)}, u32[]{:S(2)}) %collective-permute-start.7) | collective-permute-done | bytes 131104 | tf_op jit(solution)/shard_map/ppermute | solution.py:50
  40.5 2.0 %all_gather.38 = bf16[256,512]{1,0:T(8,128)(2,1)S(1)} all-gather(bf16[128,512]{1,0:T(8,128)(2,1)S(1)} %collective-permute-done.7), channel_id=1, replica_groups=mesh['groups'=2,'curve'=4,'cross'=2,'sub'=2] {'sub'}, dimensions={0}, use_global_device_ids=true | all-gather | bytes 393216 | tf_op jit(solution)/shard_map/all_gather | solution.py:54
  42.5 2.7 %second.1 = (bf16[512,512]{1,0:T(8,128)(2,1)S(1)}, bf16[512,512]{1,0:T(8,128)(2,1)S(1)}, bf16[512,512]{1,0:T(8,128)(2,1)S(1)}, bf16[512,512]{1,0:T(8,128)(2,1)S(...) custom-call(s32[5]{0:T(128)S(1)} %stack.19.me_ref.r_0_, ...), custom_call_target="tpu_custom_call" | custom-call | bytes 7995392 | tf_op jit(solution)/shard_map/second/pallas_call | solution.py:31
  45.2 2.5 %collective-permute-start.8 = (bf16[128,512]{1,0:T(8,128)(2,1)S(1)}, bf16[128,512]{1,0:T(8,128)(2,1)S(1)}, u32[]{:S(2)}, u32[]{:S(2)}) collective-permute-start(bf16[128,512]{1,0:T(8,128)(2,1)S(1)} %get-tuple-element.134), channel_id=1, source_target_pairs={{0,2},{2,4},{4,6},{6,8},{8,10},{10,12},{12,14},{3,1},{5,3},{7,5},{... | collective-permute-start | bytes 393224 | tf_op jit(solution)/shard_map/ppermute | solution.py:50
  47.8 2.1 %combine.1 = (f32[512,512]{1,0:T(8,128)S(1)}, f32[4,384,128]{2,1,0:T(8,128)S(1)}, bf16[4,384,128]{2,1,0:T(8,128)(2,1)S(1)}) custom-call(s32[5]{0:T(128)S(1)} %stack.19.me_ref.r_0_, bf16[512,512]{1,0:T(8,128)(2,1)S(1)} %get-tuple-element.128.r_1_, bf16[512,512]{1,0:T(8,128)(2,1)S(1)} %get-tuple-element.120.lift_ref.r_2_, ...), custom_call_target="tpu_custom_call" | custom-call | bytes 7208960 | tf_op jit(solution)/shard_map/combine/pallas_call | solution.py:31
  49.9 1.8 %collective-permute-done.8 = bf16[128,512]{1,0:T(8,128)(2,1)S(1)} collective-permute-done((bf16[128,512]{1,0:T(8,128)(2,1)S(1)}, bf16[128,512]{1,0:T(8,128)(2,1)S(1)}, u32[]{:S(2)}, u32[]{:S(2)}) %collective-permute-start.8) | collective-permute-done | bytes 131104 | tf_op jit(solution)/shard_map/ppermute | solution.py:50
  51.7 2.0 %all_gather.40 = bf16[256,512]{1,0:T(8,128)(2,1)S(1)} all-gather(bf16[128,512]{1,0:T(8,128)(2,1)S(1)} %collective-permute-done.8), channel_id=1, replica_groups=mesh['groups'=2,'curve'=4,'cross'=2,'sub'=2] {'sub'}, dimensions={0}, use_global_device_ids=true | all-gather | bytes 393216 | tf_op jit(solution)/shard_map/all_gather | solution.py:54
  53.6 1.2 %lgrad.1 = (bf16[512,512]{1,0:T(8,128)(2,1)S(1)}, bf16[32,512]{1,0:T(8,128)(2,1)S(1)}, bf16[32,512]{1,0:T(8,128)(2,1)S(1)}) custom-call(s32[5]{0:T(128)S(1)} %stack.19.me_ref.r_0_, f32[512,512]{1,0:T(8,128)S(1)} %get-tuple-element.133.comb_ref, bf16[2,128,512]{2,1,0:T(8,128)(2,1)S(1)} %bitcast.17, bf16[512,256]{1,0:T(8,128)(2,1)S(1)} %get-tuple-element.135.place_ref, ...), custom_call_target="tpu_custom_call" | custom-call | bytes 2293760 | tf_op jit(solution)/shard_map/lgrad/pallas_call | solution.py:31
  54.9 2.5 %collective-permute-start.11 = (bf16[4,384,128]{2,1,0:T(8,128)(2,1)S(1)}, bf16[4,384,128]{2,1,0:T(8,128)(2,1)S(1)}, u32[]{:S(2)}, u32[]{:S(2)}) collective-permute-start(bf16[4,384,128]{2,1,0:T(8,128)(2,1)S(1)} %get-tuple-element.145), channel_id=1, source_target_pairs={{0,2},{2,0},{1,3},{3,1},{4,6},{6,4},{5,7},{7,5},{8,10},{10,8},{9,1... | collective-permute-start | bytes 1179656 | tf_op jit(solution)/shard_map/ppermute | solution.py:62
  57.5 2.3 %collective-permute-start.10 = (bf16[32,512]{1,0:T(8,128)(2,1)S(1)}, bf16[32,512]{1,0:T(8,128)(2,1)S(1)}, u32[]{:S(2)}, u32[]{:S(2)}) collective-permute-start(bf16[32,512]{1,0:T(8,128)(2,1)S(1)} %get-tuple-element.144), channel_id=1, source_target_pairs={{0,4},{2,6},{4,8},{6,10},{8,12},{10,14},{5,1},{7,3},{9,5},{11,7},{... | collective-permute-start | bytes 98312 | tf_op jit(solution)/shard_map/ppermute | solution.py:50
  59.8 1.4 %own_grad.1 = (f32[128,512]{1,0:T(8,128)S(1)}, bf16[256,512]{1,0:T(8,128)(2,1)}) custom-call(s32[5]{0:T(128)S(1)} %stack.19.me_ref.r_0_, bf16[128,512]{1,0:T(8,128)(2,1)S(1)} %get-tuple-element.94.hott_ref, bf16[512,512]{1,0:T(8,128)(2,1)S(1)} %get-tuple-element.136.lg_ref.r_1_, bf16[512,512]{1,0:T(8,128)(2,1)S(1)} %get-tuple-element.137.new_ref), custom_call_target="tpu_custom_call" | custom-call | bytes 1703936 | tf_op jit(solution)/shard_map/own_grad/pallas_call | solution.py:31
  61.2 5.6 %collective-permute-done.9 = bf16[32,512]{1,0:T(8,128)(2,1)S(1)} collective-permute-done((bf16[32,512]{1,0:T(8,128)(2,1)S(1)}, bf16[32,512]{1,0:T(8,128)(2,1)S(1)}, u32[]{:S(2)}, u32[]{:S(2)}) %collective-permute-start.9) | collective-permute-done | bytes 32800 | tf_op jit(solution)/shard_map/ppermute | solution.py:50
  66.8 1.9 %all_gather.41 = bf16[128,512]{1,0:T(8,128)(2,1)S(1)} all-gather(bf16[64,512]{1,0:T(8,128)(2,1)S(1)} %pad_maximum_fusion.2), channel_id=1, replica_groups=mesh['groups'=2,'curve'=4,'cross'=2,'sub'=2] {'sub'}, dimensions={0}, use_global_device_ids=true | all-gather | bytes 196608 | tf_op jit(solution)/shard_map/all_gather | solution.py:54
  68.7 1.1 cgrad.1
  69.8 2.5 %collective-permute-start.12 = (bf16[32,512]{1,0:T(8,128)(2,1)S(1)}, bf16[32,512]{1,0:T(8,128)(2,1)S(1)}, u32[]{:S(2)}, u32[]{:S(2)}) collective-permute-start(bf16[32,512]{1,0:T(8,128)(2,1)S(1)} %get-tuple-element.151), channel_id=1, source_target_pairs={{0,2},{2,4},{4,6},{6,8},{8,10},{10,12},{12,14},{3,1},{5,3},{7,5},{... | collective-permute-start | bytes 98312 | tf_op jit(solution)/shard_map/ppermute | solution.py:50
  72.3 2.3 %collective-permute-start.13 = (bf16[32,512]{1,0:T(8,128)(2,1)S(1)}, bf16[32,512]{1,0:T(8,128)(2,1)S(1)}, u32[]{:S(2)}, u32[]{:S(2)}) collective-permute-start(bf16[32,512]{1,0:T(8,128)(2,1)S(1)} %get-tuple-element.152), channel_id=1, source_target_pairs={{0,4},{2,6},{4,8},{6,10},{8,12},{10,14},{5,1},{7,3},{9,5},{11,7},{... | collective-permute-start | bytes 98312 | tf_op jit(solution)/shard_map/ppermute | solution.py:50
  74.6 1.6 %collective-permute-done.13 = bf16[32,512]{1,0:T(8,128)(2,1)S(1)} collective-permute-done((bf16[32,512]{1,0:T(8,128)(2,1)S(1)}, bf16[32,512]{1,0:T(8,128)(2,1)S(1)}, u32[]{:S(2)}, u32[]{:S(2)}) %collective-permute-start.13) | collective-permute-done | bytes 32800 | tf_op jit(solution)/shard_map/ppermute | solution.py:50
  76.2 1.9 %all_gather.42 = bf16[128,512]{1,0:T(8,128)(2,1)S(1)} all-gather(bf16[64,512]{1,0:T(8,128)(2,1)S(1)} %pad_maximum_fusion.3), channel_id=1, replica_groups=mesh['groups'=2,'curve'=4,'cross'=2,'sub'=2] {'sub'}, dimensions={0}, use_global_device_ids=true | all-gather | bytes 196608 | tf_op jit(solution)/shard_map/all_gather | solution.py:54
  78.1 3.1 %third.1 = (bf16[512,512]{1,0:T(8,128)(2,1)S(1)}, bf16[512,512]{1,0:T(8,128)(2,1)S(1)}, bf16[512,512]{1,0:T(8,128)(2,1)S(1)}, bf16[128,512]{1,0:T(8,128)(2,1)S(1...) custom-call(s32[5]{0:T(128)S(1)} %stack.19.me_ref.r_0_, ...), custom_call_target="tpu_custom_call" | custom-call | bytes 9175040 | tf_op jit(solution)/shard_map/third/pallas_call | solution.py:31
  81.7 1.0 cweight.1
  82.7 1.7 %collective-permute-start.14 = (bf16[4,128,128]{2,1,0:T(8,128)(2,1)S(1)}, bf16[4,128,128]{2,1,0:T(8,128)(2,1)S(1)}, u32[]{:S(2)}, u32[]{:S(2)}) collective-permute-start(bf16[4,128,128]{2,1,0:T(8,128)(2,1)S(1)} %get-tuple-element.164), channel_id=1, source_target_pairs={{0,2},{2,0},{1,3},{3,1},{4,6},{6,4},{5,7},{7,5},{8,10},{10,8},{9,1... | collective-permute-start | bytes 393224 | tf_op jit(solution)/shard_map/ppermute | solution.py:62
  84.8 11.3 %collective-permute-done.14.refs_3_ = bf16[4,128,128]{2,1,0:T(8,128)(2,1)S(1)} collective-permute-done((bf16[4,128,128]{2,1,0:T(8,128)(2,1)S(1)}, bf16[4,128,128]{2,1,0:T(8,128)(2,1)S(1)}, u32[]{:S(2)}, u32[]{:S(2)}) %collective-permute-start.14) | collective-permute-done | bytes 131104 | tf_op jit(solution)/shard_map/ppermute | solution.py:62
  96.1 1.1 stage1.1
  97.2 3.8 %collective-permute-start.16 = (bf16[512,128]{1,0:T(8,128)(2,1)S(1)}, bf16[512,128]{1,0:T(8,128)(2,1)S(1)}, u32[]{:S(2)}, u32[]{:S(2)}) collective-permute-start(bf16[512,128]{1,0:T(8,128)(2,1)S(1)} %get-tuple-element.168), channel_id=1, source_target_pairs={{0,4},{4,0},{8,12},{12,8},{1,5},{5,1},{9,13},{13,9},{2,6},{6,2},{1... | collective-permute-start | bytes 393224 | tf_op jit(solution)/shard_map/ppermute | solution.py:66
  101.0 2.4 %collective-permute-start.18 = (bf16[512,128]{1,0:T(8,128)(2,1)S(1)}, bf16[512,128]{1,0:T(8,128)(2,1)S(1)}, u32[]{:S(2)}, u32[]{:S(2)}) collective-permute-start(bf16[512,128]{1,0:T(8,128)(2,1)S(1)} %get-tuple-element.170), channel_id=1, source_target_pairs={{0,12},{4,8},{8,4},{12,0},{1,13},{5,9},{9,5},{13,1},{2,14},{6,10},... | collective-permute-start | bytes 393224 | tf_op jit(solution)/shard_map/ppermute | solution.py:66
  104.0 1.1 collective-permute-start.20
  106.0 2.4 %collective-permute-start.22 = (bf16[384,128]{1,0:T(8,128)(2,1)S(1)}, bf16[384,128]{1,0:T(8,128)(2,1)S(1)}, u32[]{:S(2)}, u32[]{:S(2)}) collective-permute-start(bf16[384,128]{1,0:T(8,128)(2,1)S(1)} %get-tuple-element.177), channel_id=1, source_target_pairs={{0,12},{4,8},{8,4},{12,0},{1,13},{5,9},{9,5},{13,1},{2,14},{6,10},... | collective-permute-start | bytes 294920 | tf_op jit(solution)/shard_map/ppermute | solution.py:66
  108.5 2.0 %all_gather.43 = bf16[256,512]{1,0:T(8,128)(2,1)S(1)} all-gather(bf16[128,512]{1,0:T(8,128)(2,1)S(1)} %collective-permute-done.15), channel_id=1, replica_groups=mesh['groups'=2,'curve'=4,'cross'=2,'sub'=2] {'sub'}, dimensions={0}, use_global_device_ids=true | all-gather | bytes 393216 | tf_op jit(solution)/shard_map/all_gather | solution.py:54
  110.5 5.9 %collective-permute-done.17.rest_2_ = bf16[512,128]{1,0:T(8,128)(2,1)S(1)} collective-permute-done((bf16[512,128]{1,0:T(8,128)(2,1)S(1)}, bf16[512,128]{1,0:T(8,128)(2,1)S(1)}, u32[]{:S(2)}, u32[]{:S(2)}) %collective-permute-start.17) | collective-permute-done | bytes 131104 | tf_op jit(solution)/shard_map/ppermute | solution.py:66
  116.4 1.7 %last.1 = (f32[256,512]{1,0:T(8,128)}, f32[256,128]{1,0:T(8,128)S(1)}, f32[64,256]{1,0:T(8,128)S(1)}, f32[64,256]{1,0:T(8,128)}) custom-call(s32[5]{0:T(128)S(1)} %stack.19.me_ref.r_0_, f32[512,256]{1,0:T(8,128)S(1)} %get-tuple-element.165.comb_ref, bf16[2,128,512]{2,1,0:T(8,128)(2,1)S(1)} %bitcast.16, bf16[512,256]{1,0:T(8,128)(2,1)S(1)} %get-tuple-element.135.place_ref, ...), custom_call_target="tpu_custom_call" | custom-call | bytes 2490368 | tf_op jit(solution)/shard_map/last/pallas_call | solution.py:31
  118.1 3.2 %collective-permute-done.21.b_ref = bf16[384,128]{1,0:T(8,128)(2,1)S(1)} collective-permute-done((bf16[384,128]{1,0:T(8,128)(2,1)S(1)}, bf16[384,128]{1,0:T(8,128)(2,1)S(1)}, u32[]{:S(2)}, u32[]{:S(2)}) %collective-permute-start.21) | collective-permute-done | bytes 98336 | tf_op jit(solution)/shard_map/ppermute | solution.py:66
  (50 shorter events, 8.3 us)
Async XLA Ops:
  0.6 8.0 %copy-start.2 = (s32[4,3,128,128]{3,2,1,0:T(8,128)S(1)}, s32[4,3,128,128]{3,2,1,0:T(8,128)}, u32[]{:S(2)}) copy-start(s32[4,3,128,128]{3,2,1,0:T(8,128)} %mask_ref.1) | copy-start | bytes 2359300
  0.6 13.9 %collective-permute-start.1 = (bf16[2,256,1024]{2,1,0:T(8,128)(2,1)}, bf16[2,256,1024]{2,1,0:T(8,128)(2,1)S(1)}, u32[]{:S(2)}, u32[]{:S(2)}) collective-permute-start(bf16[2,256,1024]{2,1,0:T(8,128)(2,1)} %r_1_.3), channel_id=1, source_target_pairs={{0,1},{1,0},{2,3},{3,2},{4,5},{5,4},{6,7},{7,6},{8,9},{9,8},{10,11... | collective-permute-start | bytes 3145736 | tf_op jit(solution)/shard_map/ppermute | solution.py:58
  1.2 13.4 %collective-permute-start.2 = (bf16[2,256,512]{2,1,0:T(8,128)(2,1)}, bf16[2,256,512]{2,1,0:T(8,128)(2,1)S(1)}, u32[]{:S(2)}, u32[]{:S(2)}) collective-permute-start(bf16[2,256,512]{2,1,0:T(8,128)(2,1)} %r_2_.3), channel_id=1, source_target_pairs={{0,1},{1,0},{2,3},{3,2},{4,5},{5,4},{6,7},{7,6},{8,9},{9,8},{10,11... | collective-permute-start | bytes 1572872 | tf_op jit(solution)/shard_map/ppermute | solution.py:58
  1.3 3.5 %copy-start.3 = (s32[1,2,128]{2,1,0:T(2,128)S(1)}, s32[1,2,128]{2,1,0:T(2,128)}, u32[]{:S(2)}) copy-start(s32[1,2,128]{2,1,0:T(2,128)} %param.15) | copy-start | bytes 3076
  1.3 7.3 %copy-start.4 = (s32[4,3]{1,0:T(4,128)S(1)}, s32[4,3]{1,0:T(4,128)}, u32[]{:S(2)}) copy-start(s32[4,3]{1,0:T(4,128)} %tile_ref.1) | copy-start | bytes 148
  1.3 7.3 %copy-start.5 = (s32[512]{0:T(512)S(1)}, s32[512]{0:T(512)}, u32[]{:S(2)}) copy-start(s32[512]{0:T(512)} %param.16) | copy-start | bytes 6148
  4.8 9.7 %copy-start = (bf16[2,256,1024]{2,1,0:T(8,128)(2,1)S(1)}, bf16[2,256,1024]{2,1,0:T(8,128)(2,1)}, u32[]{:S(2)}) copy-start(bf16[2,256,1024]{2,1,0:T(8,128)(2,1)} %r_1_.3) | copy-start | bytes 3145732
  5.7 6.8 %collective-permute-start = (bf16[128,512]{1,0:T(8,128)(2,1)S(1)}, bf16[128,512]{1,0:T(8,128)(2,1)S(1)}, u32[]{:S(2)}, u32[]{:S(2)}) collective-permute-start(bf16[128,512]{1,0:T(8,128)(2,1)S(1)} %get-tuple-element.96), channel_id=1, source_target_pairs={{0,2},{2,4},{4,6},{6,8},{8,10},{10,12},{12,14},{3,1},{5,3},{7,5},{... | collective-permute-start | bytes 393224 | tf_op jit(solution)/shard_map/ppermute | solution.py:50
  8.7 5.9 %copy-start.1 = (bf16[2,256,512]{2,1,0:T(8,128)(2,1)S(1)}, bf16[2,256,512]{2,1,0:T(8,128)(2,1)}, u32[]{:S(2)}) copy-start(bf16[2,256,512]{2,1,0:T(8,128)(2,1)} %r_2_.3) | copy-start | bytes 1572868
  15.2 6.5 %copy-start.6 = (bf16[256,512]{1,0:T(8,128)(2,1)S(1)}, bf16[256,512]{1,0:T(8,128)(2,1)}, u32[]{:S(2)}) copy-start(bf16[256,512]{1,0:T(8,128)(2,1)} %param.12) | copy-start | bytes 786436
  17.6 7.0 %collective-permute-start.3 = (bf16[48,512]{1,0:T(8,128)(2,1)S(1)}, bf16[48,512]{1,0:T(8,128)(2,1)S(1)}, u32[]{:S(2)}, u32[]{:S(2)}) collective-permute-start(bf16[48,512]{1,0:T(8,128)(2,1)S(1)} %get-tuple-element.111), channel_id=1, source_target_pairs={{0,2},{2,4},{4,6},{6,8},{8,10},{10,12},{12,14},{3,1},{5,3},{7,5},{... | collective-permute-start | bytes 147464 | tf_op jit(solution)/shard_map/ppermute | solution.py:50
  20.1 4.5 %collective-permute-start.4 = (bf16[48,512]{1,0:T(8,128)(2,1)S(1)}, bf16[48,512]{1,0:T(8,128)(2,1)S(1)}, u32[]{:S(2)}, u32[]{:S(2)}) collective-permute-start(bf16[48,512]{1,0:T(8,128)(2,1)S(1)} %get-tuple-element.112), channel_id=1, source_target_pairs={{0,4},{2,6},{4,8},{6,10},{8,12},{10,14},{5,1},{7,3},{9,5},{11,7},{... | collective-permute-start | bytes 147464 | tf_op jit(solution)/shard_map/ppermute | solution.py:50
  27.7 3.3 %collective-permute-start.5 = (bf16[32,512]{1,0:T(8,128)(2,1)S(1)}, bf16[32,512]{1,0:T(8,128)(2,1)S(1)}, u32[]{:S(2)}, u32[]{:S(2)}) collective-permute-start(bf16[32,512]{1,0:T(8,128)(2,1)S(1)} %get-tuple-element.117), channel_id=1, source_target_pairs={{0,2},{2,4},{4,6},{6,8},{8,10},{10,12},{12,14},{3,1},{5,3},{7,5},{... | collective-permute-start | bytes 98312 | tf_op jit(solution)/shard_map/ppermute | solution.py:50
  28.8 3.2 %collective-permute-start.6 = (bf16[32,512]{1,0:T(8,128)(2,1)S(1)}, bf16[32,512]{1,0:T(8,128)(2,1)S(1)}, u32[]{:S(2)}, u32[]{:S(2)}) collective-permute-start(bf16[32,512]{1,0:T(8,128)(2,1)S(1)} %get-tuple-element.118), channel_id=1, source_target_pairs={{0,4},{2,6},{4,8},{6,10},{8,12},{10,14},{5,1},{7,3},{9,5},{11,7},{... | collective-permute-start | bytes 98312 | tf_op jit(solution)/shard_map/ppermute | solution.py:50
  33.9 2.8 %copy-start.7 = (bf16[256,512]{1,0:T(8,128)(2,1)S(1)}, bf16[256,512]{1,0:T(8,128)(2,1)}, u32[]{:S(2)}) copy-start(bf16[256,512]{1,0:T(8,128)(2,1)} %param.17) | copy-start | bytes 786436
  35.0 5.5 %collective-permute-start.7 = (bf16[128,512]{1,0:T(8,128)(2,1)S(1)}, bf16[128,512]{1,0:T(8,128)(2,1)S(1)}, u32[]{:S(2)}, u32[]{:S(2)}) collective-permute-start(bf16[128,512]{1,0:T(8,128)(2,1)S(1)} %get-tuple-element.121), channel_id=1, source_target_pairs={{0,2},{2,4},{4,6},{6,8},{8,10},{10,12},{12,14},{3,1},{5,3},{7,5},{... | collective-permute-start | bytes 393224 | tf_op jit(solution)/shard_map/ppermute | solution.py:50
  45.2 6.4 %collective-permute-start.8 = (bf16[128,512]{1,0:T(8,128)(2,1)S(1)}, bf16[128,512]{1,0:T(8,128)(2,1)S(1)}, u32[]{:S(2)}, u32[]{:S(2)}) collective-permute-start(bf16[128,512]{1,0:T(8,128)(2,1)S(1)} %get-tuple-element.134), channel_id=1, source_target_pairs={{0,2},{2,4},{4,6},{6,8},{8,10},{10,12},{12,14},{3,1},{5,3},{7,5},{... | collective-permute-start | bytes 393224 | tf_op jit(solution)/shard_map/ppermute | solution.py:50
  54.9 13.8 %collective-permute-start.11 = (bf16[4,384,128]{2,1,0:T(8,128)(2,1)S(1)}, bf16[4,384,128]{2,1,0:T(8,128)(2,1)S(1)}, u32[]{:S(2)}, u32[]{:S(2)}) collective-permute-start(bf16[4,384,128]{2,1,0:T(8,128)(2,1)S(1)} %get-tuple-element.145), channel_id=1, source_target_pairs={{0,2},{2,0},{1,3},{3,1},{4,6},{6,4},{5,7},{7,5},{8,10},{10,8},{9,1... | collective-permute-start | bytes 1179656 | tf_op jit(solution)/shard_map/ppermute | solution.py:62
  57.4 9.4 %collective-permute-start.9 = (bf16[32,512]{1,0:T(8,128)(2,1)S(1)}, bf16[32,512]{1,0:T(8,128)(2,1)S(1)}, u32[]{:S(2)}, u32[]{:S(2)}) collective-permute-start(bf16[32,512]{1,0:T(8,128)(2,1)S(1)} %get-tuple-element.143), channel_id=1, source_target_pairs={{0,2},{2,4},{4,6},{6,8},{8,10},{10,12},{12,14},{3,1},{5,3},{7,5},{... | collective-permute-start | bytes 98312 | tf_op jit(solution)/shard_map/ppermute | solution.py:50
  57.5 9.3 %collective-permute-start.10 = (bf16[32,512]{1,0:T(8,128)(2,1)S(1)}, bf16[32,512]{1,0:T(8,128)(2,1)S(1)}, u32[]{:S(2)}, u32[]{:S(2)}) collective-permute-start(bf16[32,512]{1,0:T(8,128)(2,1)S(1)} %get-tuple-element.144), channel_id=1, source_target_pairs={{0,4},{2,6},{4,8},{6,10},{8,12},{10,14},{5,1},{7,3},{9,5},{11,7},{... | collective-permute-start | bytes 98312 | tf_op jit(solution)/shard_map/ppermute | solution.py:50
  69.8 4.8 %collective-permute-start.12 = (bf16[32,512]{1,0:T(8,128)(2,1)S(1)}, bf16[32,512]{1,0:T(8,128)(2,1)S(1)}, u32[]{:S(2)}, u32[]{:S(2)}) collective-permute-start(bf16[32,512]{1,0:T(8,128)(2,1)S(1)} %get-tuple-element.151), channel_id=1, source_target_pairs={{0,2},{2,4},{4,6},{6,8},{8,10},{10,12},{12,14},{3,1},{5,3},{7,5},{... | collective-permute-start | bytes 98312 | tf_op jit(solution)/shard_map/ppermute | solution.py:50
  72.3 3.9 %collective-permute-start.13 = (bf16[32,512]{1,0:T(8,128)(2,1)S(1)}, bf16[32,512]{1,0:T(8,128)(2,1)S(1)}, u32[]{:S(2)}, u32[]{:S(2)}) collective-permute-start(bf16[32,512]{1,0:T(8,128)(2,1)S(1)} %get-tuple-element.152), channel_id=1, source_target_pairs={{0,4},{2,6},{4,8},{6,10},{8,12},{10,14},{5,1},{7,3},{9,5},{11,7},{... | collective-permute-start | bytes 98312 | tf_op jit(solution)/shard_map/ppermute | solution.py:50
  81.3 22.1 %collective-permute-start.19 = (bf16[4,384,128]{2,1,0:T(8,128)(2,1)S(1)}, bf16[4,384,128]{2,1,0:T(8,128)(2,1)S(1)}, u32[]{:S(2)}, u32[]{:S(2)}) collective-permute-start(bf16[4,384,128]{2,1,0:T(8,128)(2,1)S(1)} %get-tuple-element.173), channel_id=1, source_target_pairs={{0,2},{2,0},{1,3},{3,1},{4,6},{6,4},{5,7},{7,5},{8,10},{10,8},{9,1... | collective-permute-start | bytes 1179656 | tf_op jit(solution)/shard_map/ppermute | solution.py:62
  82.7 13.4 %collective-permute-start.14 = (bf16[4,128,128]{2,1,0:T(8,128)(2,1)S(1)}, bf16[4,128,128]{2,1,0:T(8,128)(2,1)S(1)}, u32[]{:S(2)}, u32[]{:S(2)}) collective-permute-start(bf16[4,128,128]{2,1,0:T(8,128)(2,1)S(1)} %get-tuple-element.164), channel_id=1, source_target_pairs={{0,2},{2,0},{1,3},{3,1},{4,6},{6,4},{5,7},{7,5},{8,10},{10,8},{9,1... | collective-permute-start | bytes 393224 | tf_op jit(solution)/shard_map/ppermute | solution.py:62
  84.4 20.7 %collective-permute-start.15 = (bf16[128,512]{1,0:T(8,128)(2,1)S(1)}, bf16[128,512]{1,0:T(8,128)(2,1)S(1)}, u32[]{:S(2)}, u32[]{:S(2)}) collective-permute-start(bf16[128,512]{1,0:T(8,128)(2,1)S(1)} %get-tuple-element.166), channel_id=1, source_target_pairs={{0,2},{2,4},{4,6},{6,8},{8,10},{10,12},{12,14},{3,1},{5,3},{7,5},{... | collective-permute-start | bytes 393224 | tf_op jit(solution)/shard_map/ppermute | solution.py:50
  97.2 8.9 %collective-permute-start.16 = (bf16[512,128]{1,0:T(8,128)(2,1)S(1)}, bf16[512,128]{1,0:T(8,128)(2,1)S(1)}, u32[]{:S(2)}, u32[]{:S(2)}) collective-permute-start(bf16[512,128]{1,0:T(8,128)(2,1)S(1)} %get-tuple-element.168), channel_id=1, source_target_pairs={{0,4},{4,0},{8,12},{12,8},{1,5},{5,1},{9,13},{13,9},{2,6},{6,2},{1... | collective-permute-start | bytes 393224 | tf_op jit(solution)/shard_map/ppermute | solution.py:66
  101.0 15.4 %collective-permute-start.17 = (bf16[512,128]{1,0:T(8,128)(2,1)S(1)}, bf16[512,128]{1,0:T(8,128)(2,1)S(1)}, u32[]{:S(2)}, u32[]{:S(2)}) collective-permute-start(bf16[512,128]{1,0:T(8,128)(2,1)S(1)} %get-tuple-element.169), channel_id=1, source_target_pairs={{0,8},{4,12},{8,0},{12,4},{1,9},{5,13},{9,1},{13,5},{2,10},{6,14},... | collective-permute-start | bytes 393224 | tf_op jit(solution)/shard_map/ppermute | solution.py:66
  101.0 15.4 %collective-permute-start.18 = (bf16[512,128]{1,0:T(8,128)(2,1)S(1)}, bf16[512,128]{1,0:T(8,128)(2,1)S(1)}, u32[]{:S(2)}, u32[]{:S(2)}) collective-permute-start(bf16[512,128]{1,0:T(8,128)(2,1)S(1)} %get-tuple-element.170), channel_id=1, source_target_pairs={{0,12},{4,8},{8,4},{12,0},{1,13},{5,9},{9,5},{13,1},{2,14},{6,10},... | collective-permute-start | bytes 393224 | tf_op jit(solution)/shard_map/ppermute | solution.py:66
  104.0 14.1 %collective-permute-start.20 = (bf16[384,128]{1,0:T(8,128)(2,1)S(1)}, bf16[384,128]{1,0:T(8,128)(2,1)S(1)}, u32[]{:S(2)}, u32[]{:S(2)}) collective-permute-start(bf16[384,128]{1,0:T(8,128)(2,1)S(1)} %get-tuple-element.175), channel_id=1, source_target_pairs={{0,4},{4,0},{8,12},{12,8},{1,5},{5,1},{9,13},{13,9},{2,6},{6,2},{1... | collective-permute-start | bytes 294920 | tf_op jit(solution)/shard_map/ppermute | solution.py:66
  105.1 16.2 %collective-permute-start.21 = (bf16[384,128]{1,0:T(8,128)(2,1)S(1)}, bf16[384,128]{1,0:T(8,128)(2,1)S(1)}, u32[]{:S(2)}, u32[]{:S(2)}) collective-permute-start(bf16[384,128]{1,0:T(8,128)(2,1)S(1)} %get-tuple-element.176), channel_id=1, source_target_pairs={{0,8},{4,12},{8,0},{12,4},{1,9},{5,13},{9,1},{13,5},{2,10},{6,14},... | collective-permute-start | bytes 294920 | tf_op jit(solution)/shard_map/ppermute | solution.py:66
  106.0 15.3 %collective-permute-start.22 = (bf16[384,128]{1,0:T(8,128)(2,1)S(1)}, bf16[384,128]{1,0:T(8,128)(2,1)S(1)}, u32[]{:S(2)}, u32[]{:S(2)}) collective-permute-start(bf16[384,128]{1,0:T(8,128)(2,1)S(1)} %get-tuple-element.177), channel_id=1, source_target_pairs={{0,12},{4,8},{8,4},{12,0},{1,13},{5,9},{9,5},{13,1},{2,14},{6,10},... | collective-permute-start | bytes 294920 | tf_op jit(solution)/shard_map/ppermute | solution.py:66

commit v5 on v4

--- a/solution.py
+++ b/solution.py
@@ -352,8 +352,8 @@
 
 def k_combine_pack(scale, me_ref, pg_ref, h_ref, agg_ref, g_ref, hid_ref, win_ref, scaled_ref, adjt_ref,
                    comb_ref, keep_ref, send_ref):
+    pack_grads(scale, me_ref, pg_ref, h_ref, agg_ref, g_ref, hid_ref, keep_ref, send_ref)
     k_combine(g_ref, pg_ref, win_ref, scaled_ref, adjt_ref, comb_ref)
-    pack_grads(scale, me_ref, pg_ref, h_ref, agg_ref, g_ref, hid_ref, keep_ref, send_ref)
 
 
 def k_cweight_pack(scale, me_ref, pgrad_ref, coarse_ref, keep_ref, send_ref):
@@ -551,21 +551,18 @@
     layer_rows = half + 2 * small
     pack = [sds((curve, layer_rows, piece), F32), sds((curve, layer_rows, piece), BF)]
     if packed:
-        comb1, keep1, send1 = call(lambda *r: k_combine_pack(scale, *r), [cell_f32] + pack, [me],
-                            [pg1, lifted, agg1, ctc, hid1, win1, scaled1, adjt], "combine")
+        comb1, keep1, send1 = call(
+            lambda *r: k_combine_pack(scale, *r), [cell_f32] + pack, [me],
+            [pg1, lifted, agg1, ctc, hid1, win1, scaled1, adjt], "combine")
+        got1 = cross_swap(send1)
     else:
         comb1, = call(k_combine, [cell_f32], [], [ctc, pg1, win1, scaled1, adjt], "combine")
     rims = gather(rims).reshape(2, rim, width)
     lg, one, two = call(
         k_lgrad, [cell_bf, plain, plain], [me], [comb1, rims, place, slot], "lgrad")
-    if packed:
-        one, two, send1 = lax.optimization_barrier((one, two, send1))
-        got1 = cross_swap(send1)
     one, two = two_way(one, 1), two_way(two, 2)
     own_g, new_t = call(k_newt, [node_f32, sds((half, n), BF)], [me], [hott, lg, new], "own_grad")
     got = gather(jnp.concatenate([one, two], axis=0)).reshape(2, -1, width)
-    if packed:
-        got, got1 = lax.optimization_barrier((got, got1))
     pgrad, spread, one, two = call(
         k_cgrad, [node_bf, node_bf, plain, plain], [me],
         [own_g, got, hits, icount, cpre, cw], "cgrad")
@@ -579,8 +576,11 @@
             [sds((curve, 2 * small, piece), F32), sds((curve, 2 * small, piece), BF)], [me],
             [pgrad, coarse], "cweight")
         gotc = cross_swap(sendc)
+        got, got1 = lax.optimization_barrier((got, got1))
+        back_args[4] = got
         fb, pg0, scaled0, rims, keep0, send0 = call(
             lambda *r: k_third(*r, scale=scale), back_outs + pack, [me], back_args + [xc, agg0, hid0], "third")
+        send0, gotc = lax.optimization_barrier((send0, gotc))
         got0 = cross_swap(send0)
         rims = two_way(rims, 1)
 

time: 122 us -> 104 us (0.85)
  waiting for transfers between devices: 34 us -> 14.7 us
    ppermute x12, waiting for transfers between devices: 13.6 us -> 5.92 us  [two_way(): return lax.ppermute(value, LINE, pairs)]
    ppermute x3, waiting for transfers between devices: 11.3 us -> 4.24 us  [cross_swap(): return lax.ppermute(value, 'cross', [(0, 1), (1, 0)])]
    ppermute x6, waiting for transfers between devices: 9.13 us -> 4.5 us  [curve_swap(): return lax.ppermute(value, 'curve', [(z, z ^ step) for z in range(4)])]
    ppermute x12, starting transfers between devices: 21.5 us -> 23.1 us  [two_way(): return lax.ppermute(value, LINE, pairs)]
  transfers between devices with their start and end apart: 23 -> 23, of which waited for: 9 -> 7; matrix products, arithmetic and copies ran while one was open for 0% -> 0% of each run, Pallas kernels for 10% -> 17%
where the time goes in v5:
time: 104 us; the launch traced here: 103 us
  starting transfers between devices  37.9 us (36%)
  Pallas kernels  26.5 us (25%)
  blocking collectives  23.3 us (22%)
  waiting for transfers between devices  14.7 us (14%)
    pallas_call x20, Pallas kernels, call(): pl.pallas_call(body, out_shape=tuple(outs), in_specs=[pl.BlockSpec(memory...  26.5 us
    all_gather x11, blocking collectives, gather(): return lax.all_gather(value, 'sub', axis=0, tiled=True)  23.3 us
    ppermute x12, starting transfers between devices, two_way(): return lax.ppermute(value, LINE, pairs)  23.1 us
    ppermute x6, starting transfers between devices, curve_swap(): return lax.ppermute(value, 'curve', [(z, z ^ step) for z in range(4)])  10.3 us
    ppermute x12, waiting for transfers between devices, two_way(): return lax.ppermute(value, LINE, pairs)  5.92 us
    ppermute x6, waiting for transfers between devices, curve_swap(): return lax.ppermute(value, 'curve', [(z, z ^ step) for z in range(4)])  4.5 us
    ppermute x3, waiting for transfers between devices, cross_swap(): return lax.ppermute(value, 'cross', [(0, 1), (1, 0)])  4.24 us
    ppermute x3, starting transfers between devices, cross_swap(): return lax.ppermute(value, 'cross', [(0, 1), (1, 0)])  3.91 us
  transfers between devices with their start and end apart: 23, of which 7 were waited for; matrix products, arithmetic and copies ran while one was open for 0% of the time, Pallas kernels for 17%

profile of v5, /device:TPU:0, one launch (start us, length us, event | category | flops | bytes accessed | tf_op | source)
XLA Modules:
  0.0 103.4 jit_solution(15576590854451455012)
XLA Ops:
  1.3 3.5 %all_gather.33.x_ref = bf16[512,512]{1,0:T(8,128)(2,1)S(1)} all-gather(bf16[256,512]{1,0:T(8,128)(2,1)} %param.9), channel_id=1, replica_groups=mesh['groups'=2,'curve'=4,'cross'=2,'sub'=2] {'sub'}, dimensions={0}, use_global_device_ids=true | all-gather | bytes 786432 | tf_op jit(solution)/shard_map/all_gather | solution.py:54
  4.8 0.9 halo.1
  5.7 2.9 %collective-permute-start = (bf16[128,512]{1,0:T(8,128)(2,1)S(1)}, bf16[128,512]{1,0:T(8,128)(2,1)S(1)}, u32[]{:S(2)}, u32[]{:S(2)}) collective-permute-start(bf16[128,512]{1,0:T(8,128)(2,1)S(1)} %get-tuple-element.95), channel_id=1, source_target_pairs={{0,2},{2,4},{4,6},{6,8},{8,10},{10,12},{12,14},{3,1},{5,3},{7,5},{... | collective-permute-start | bytes 393224 | tf_op jit(solution)/shard_map/ppermute | solution.py:50
  8.7 1.3 %prep.1 = (bf16[512,768]{1,0:T(8,128)(2,1)S(1)}, bf16[768,512]{1,0:T(8,128)(2,1)S(1)}, f32[512,128]{1,0:T(8,128)S(1)}, bf16[128,512]{1,0:T(8,128)(2,1)S(1)}, bf1...) custom-call(s32[4,3]{1,0:T(4,128)S(1)} %copy-done.4, ...), custom_call_target="tpu_custom_call" | custom-call | bytes 3742720 | tf_op jit(solution)/shard_map/prep/pallas_call | solution.py:31
  10.0 2.5 %collective-permute-done = bf16[128,512]{1,0:T(8,128)(2,1)S(1)} collective-permute-done((bf16[128,512]{1,0:T(8,128)(2,1)S(1)}, bf16[128,512]{1,0:T(8,128)(2,1)S(1)}, u32[]{:S(2)}, u32[]{:S(2)}) %collective-permute-start) | collective-permute-done | bytes 131104 | tf_op jit(solution)/shard_map/ppermute | solution.py:50
  12.5 2.0 %all_gather.34 = bf16[256,512]{1,0:T(8,128)(2,1)S(1)} all-gather(bf16[128,512]{1,0:T(8,128)(2,1)S(1)} %collective-permute-done), channel_id=1, replica_groups=mesh['groups'=2,'curve'=4,'cross'=2,'sub'=2] {'sub'}, dimensions={0}, use_global_device_ids=true | all-gather | bytes 393216 | tf_op jit(solution)/shard_map/all_gather | solution.py:54
  15.2 2.4 %first.1 = (bf16[512,512]{1,0:T(8,128)(2,1)S(1)}, f32[512,512]{1,0:T(8,128)S(1)}, bf16[512,512]{1,0:T(8,128)(2,1)S(1)}, bf16[512,512]{1,0:T(8,128)(2,1)S(1)}, bf...) custom-call(s32[5]{0:T(128)S(1)} %stack.19.me_ref.r_0_, bf16[512,512]{1,0:T(8,128)(2,1)S(1)} %get-tuple-element.94.xc_ref.r_11_, ...), custom_call_target="tpu_custom_call" | custom-call | flops 1207959552 | bytes 6262784 | tf_op jit(solution)/shard_map/first/pallas_call | solution.py:31
  17.6 2.5 %collective-permute-start.3 = (bf16[48,512]{1,0:T(8,128)(2,1)S(1)}, bf16[48,512]{1,0:T(8,128)(2,1)S(1)}, u32[]{:S(2)}, u32[]{:S(2)}) collective-permute-start(bf16[48,512]{1,0:T(8,128)(2,1)S(1)} %get-tuple-element.110), channel_id=1, source_target_pairs={{0,2},{2,4},{4,6},{6,8},{8,10},{10,12},{12,14},{3,1},{5,3},{7,5},{... | collective-permute-start | bytes 147464 | tf_op jit(solution)/shard_map/ppermute | solution.py:50
  20.1 1.6 %collective-permute-start.4 = (bf16[48,512]{1,0:T(8,128)(2,1)S(1)}, bf16[48,512]{1,0:T(8,128)(2,1)S(1)}, u32[]{:S(2)}, u32[]{:S(2)}) collective-permute-start(bf16[48,512]{1,0:T(8,128)(2,1)S(1)} %get-tuple-element.111), channel_id=1, source_target_pairs={{0,4},{2,6},{4,8},{6,10},{8,12},{10,14},{5,1},{7,3},{9,5},{11,7},{... | collective-permute-start | bytes 147464 | tf_op jit(solution)/shard_map/ppermute | solution.py:50
  21.7 2.2 %all_gather.36.cw_ref = bf16[512,512]{1,0:T(8,128)(2,1)S(1)} all-gather(bf16[256,512]{1,0:T(8,128)(2,1)S(1)} %copy-done.6), channel_id=1, replica_groups=mesh['groups'=2,'curve'=4,'cross'=2,'sub'=2] {'sub'}, dimensions={0}, use_global_device_ids=true | all-gather | bytes 786432 | tf_op jit(solution)/shard_map/all_gather | solution.py:54
  24.6 1.9 %all_gather.35 = bf16[192,512]{1,0:T(8,128)(2,1)S(1)} all-gather(bf16[96,512]{1,0:T(8,128)(2,1)S(1)} %pad_maximum_fusion), channel_id=1, replica_groups=mesh['groups'=2,'curve'=4,'cross'=2,'sub'=2] {'sub'}, dimensions={0}, use_global_device_ids=true | all-gather | bytes 294912 | tf_op jit(solution)/shard_map/all_gather | solution.py:54
  26.6 1.1 %coarse.1 = (f32[128,128]{1,0:T(8,128)S(1)}, f32[128,128]{1,0:T(8,128)S(1)}, bf16[128,512]{1,0:T(8,128)(2,1)S(1)}, f32[128,512]{1,0:T(8,128)S(1)}, bf16[128,512]...) custom-call(s32[5]{0:T(128)S(1)} %stack.19.me_ref.r_0_, ...), custom_call_target="tpu_custom_call" | custom-call | bytes 1769472 | tf_op jit(solution)/shard_map/coarse/pallas_call | solution.py:31
  27.7 1.1 %collective-permute-start.5 = (bf16[32,512]{1,0:T(8,128)(2,1)S(1)}, bf16[32,512]{1,0:T(8,128)(2,1)S(1)}, u32[]{:S(2)}, u32[]{:S(2)}) collective-permute-start(bf16[32,512]{1,0:T(8,128)(2,1)S(1)} %get-tuple-element.116), channel_id=1, source_target_pairs={{0,2},{2,4},{4,6},{6,8},{8,10},{10,12},{12,14},{3,1},{5,3},{7,5},{... | collective-permute-start | bytes 98312 | tf_op jit(solution)/shard_map/ppermute | solution.py:50
  28.8 1.6 %collective-permute-start.6 = (bf16[32,512]{1,0:T(8,128)(2,1)S(1)}, bf16[32,512]{1,0:T(8,128)(2,1)S(1)}, u32[]{:S(2)}, u32[]{:S(2)}) collective-permute-start(bf16[32,512]{1,0:T(8,128)(2,1)S(1)} %get-tuple-element.117), channel_id=1, source_target_pairs={{0,4},{2,6},{4,8},{6,10},{8,12},{10,14},{5,1},{7,3},{9,5},{11,7},{... | collective-permute-start | bytes 98312 | tf_op jit(solution)/shard_map/ppermute | solution.py:50
  32.0 1.9 %all_gather.37 = bf16[128,512]{1,0:T(8,128)(2,1)S(1)} all-gather(bf16[64,512]{1,0:T(8,128)(2,1)S(1)} %pad_maximum_fusion.1), channel_id=1, replica_groups=mesh['groups'=2,'curve'=4,'cross'=2,'sub'=2] {'sub'}, dimensions={0}, use_global_device_ids=true | all-gather | bytes 196608 | tf_op jit(solution)/shard_map/all_gather | solution.py:54
  33.9 1.1 %lift.1 = (bf16[512,512]{1,0:T(8,128)(2,1)S(1)}, bf16[128,512]{1,0:T(8,128)(2,1)S(1)}) custom-call(s32[5]{0:T(128)S(1)} %stack.19.me_ref.r_0_, bf16[512,512]{1,0:T(8,128)(2,1)S(1)} %get-tuple-element.102.v_ref.first_ref, bf16[512,128]{1,0:T(8,128)(2,1)S(1)} %get-tuple-element.103.hot_ref.r_2_, bf16[512,128]{1,0:T(8,128)(2,1)S(1)} %get-tuple-element.104.slott_ref.r_3_, ...), custom_call_target="tpu_custom_call" | custom-call | bytes 1966080 | tf_op jit(solution)/shard_map/lift/pallas_call | solution.py:31
  35.0 1.6 %collective-permute-start.7 = (bf16[128,512]{1,0:T(8,128)(2,1)S(1)}, bf16[128,512]{1,0:T(8,128)(2,1)S(1)}, u32[]{:S(2)}, u32[]{:S(2)}) collective-permute-start(bf16[128,512]{1,0:T(8,128)(2,1)S(1)} %get-tuple-element.120), channel_id=1, source_target_pairs={{0,2},{2,4},{4,6},{6,8},{8,10},{10,12},{12,14},{3,1},{5,3},{7,5},{... | collective-permute-start | bytes 393224 | tf_op jit(solution)/shard_map/ppermute | solution.py:50
  36.7 2.2 %all_gather.39.ct_ref = bf16[512,512]{1,0:T(8,128)(2,1)S(1)} all-gather(bf16[256,512]{1,0:T(8,128)(2,1)S(1)} %copy-done.7), channel_id=1, replica_groups=mesh['groups'=2,'curve'=4,'cross'=2,'sub'=2] {'sub'}, dimensions={0}, use_global_device_ids=true | all-gather | bytes 786432 | tf_op jit(solution)/shard_map/all_gather | solution.py:54
  39.3 1.2 %collective-permute-done.7 = bf16[128,512]{1,0:T(8,128)(2,1)S(1)} collective-permute-done((bf16[128,512]{1,0:T(8,128)(2,1)S(1)}, bf16[128,512]{1,0:T(8,128)(2,1)S(1)}, u32[]{:S(2)}, u32[]{:S(2)}) %collective-permute-start.7) | collective-permute-done | bytes 131104 | tf_op jit(solution)/shard_map/ppermute | solution.py:50
  40.5 2.0 %all_gather.38 = bf16[256,512]{1,0:T(8,128)(2,1)S(1)} all-gather(bf16[128,512]{1,0:T(8,128)(2,1)S(1)} %collective-permute-done.7), channel_id=1, replica_groups=mesh['groups'=2,'curve'=4,'cross'=2,'sub'=2] {'sub'}, dimensions={0}, use_global_device_ids=true | all-gather | bytes 393216 | tf_op jit(solution)/shard_map/all_gather | solution.py:54
  42.5 2.7 %second.1 = (bf16[512,512]{1,0:T(8,128)(2,1)S(1)}, bf16[512,512]{1,0:T(8,128)(2,1)S(1)}, bf16[512,512]{1,0:T(8,128)(2,1)S(1)}, bf16[512,512]{1,0:T(8,128)(2,1)S(...) custom-call(s32[5]{0:T(128)S(1)} %stack.19.me_ref.r_0_, ...), custom_call_target="tpu_custom_call" | custom-call | bytes 7995392 | tf_op jit(solution)/shard_map/second/pallas_call | solution.py:31
  45.2 2.5 %collective-permute-start.8 = (bf16[128,512]{1,0:T(8,128)(2,1)S(1)}, bf16[128,512]{1,0:T(8,128)(2,1)S(1)}, u32[]{:S(2)}, u32[]{:S(2)}) collective-permute-start(bf16[128,512]{1,0:T(8,128)(2,1)S(1)} %get-tuple-element.133), channel_id=1, source_target_pairs={{0,2},{2,4},{4,6},{6,8},{8,10},{10,12},{12,14},{3,1},{5,3},{7,5},{... | collective-permute-start | bytes 393224 | tf_op jit(solution)/shard_map/ppermute | solution.py:50
  47.8 2.3 %combine.1 = (f32[512,512]{1,0:T(8,128)S(1)}, f32[4,384,128]{2,1,0:T(8,128)S(1)}, bf16[4,384,128]{2,1,0:T(8,128)(2,1)S(1)}) custom-call(s32[5]{0:T(128)S(1)} %stack.19.me_ref.r_0_, bf16[512,512]{1,0:T(8,128)(2,1)S(1)} %get-tuple-element.127.r_1_, bf16[512,512]{1,0:T(8,128)(2,1)S(1)} %get-tuple-element.119.lift_ref.r_2_, ...), custom_call_target="tpu_custom_call" | custom-call | bytes 7208960 | tf_op jit(solution)/shard_map/combine/pallas_call | solution.py:31
  50.1 1.7 %collective-permute-start.13 = (bf16[4,384,128]{2,1,0:T(8,128)(2,1)S(1)}, bf16[4,384,128]{2,1,0:T(8,128)(2,1)S(1)}, u32[]{:S(2)}, u32[]{:S(2)}) collective-permute-start(bf16[4,384,128]{2,1,0:T(8,128)(2,1)S(1)} %get-tuple-element.147), channel_id=1, source_target_pairs={{0,2},{2,0},{1,3},{3,1},{4,6},{6,4},{5,7},{7,5},{8,10},{10,8},{9,1... | collective-permute-start | bytes 1179656 | tf_op jit(solution)/shard_map/ppermute | solution.py:62
  51.8 1.0 %collective-permute-done.8 = bf16[128,512]{1,0:T(8,128)(2,1)S(1)} collective-permute-done((bf16[128,512]{1,0:T(8,128)(2,1)S(1)}, bf16[128,512]{1,0:T(8,128)(2,1)S(1)}, u32[]{:S(2)}, u32[]{:S(2)}) %collective-permute-start.8) | collective-permute-done | bytes 131104 | tf_op jit(solution)/shard_map/ppermute | solution.py:50
  52.9 2.0 %all_gather.40 = bf16[256,512]{1,0:T(8,128)(2,1)S(1)} all-gather(bf16[128,512]{1,0:T(8,128)(2,1)S(1)} %collective-permute-done.8), channel_id=1, replica_groups=mesh['groups'=2,'curve'=4,'cross'=2,'sub'=2] {'sub'}, dimensions={0}, use_global_device_ids=true | all-gather | bytes 393216 | tf_op jit(solution)/shard_map/all_gather | solution.py:54
  54.9 1.2 %lgrad.1 = (bf16[512,512]{1,0:T(8,128)(2,1)S(1)}, bf16[32,512]{1,0:T(8,128)(2,1)S(1)}, bf16[32,512]{1,0:T(8,128)(2,1)S(1)}) custom-call(s32[5]{0:T(128)S(1)} %stack.19.me_ref.r_0_, f32[512,512]{1,0:T(8,128)S(1)} %get-tuple-element.132.comb_ref, bf16[2,128,512]{2,1,0:T(8,128)(2,1)S(1)} %bitcast.17, bf16[512,256]{1,0:T(8,128)(2,1)S(1)} %get-tuple-element.134.place_ref, ...), custom_call_target="tpu_custom_call" | custom-call | bytes 2293760 | tf_op jit(solution)/shard_map/lgrad/pallas_call | solution.py:31
  56.1 2.5 %collective-permute-start.9 = (bf16[32,512]{1,0:T(8,128)(2,1)S(1)}, bf16[32,512]{1,0:T(8,128)(2,1)S(1)}, u32[]{:S(2)}, u32[]{:S(2)}) collective-permute-start(bf16[32,512]{1,0:T(8,128)(2,1)S(1)} %get-tuple-element.139), channel_id=1, source_target_pairs={{0,2},{2,4},{4,6},{6,8},{8,10},{10,12},{12,14},{3,1},{5,3},{7,5},{... | collective-permute-start | bytes 98312 | tf_op jit(solution)/shard_map/ppermute | solution.py:50
  58.6 2.3 %collective-permute-start.10 = (bf16[32,512]{1,0:T(8,128)(2,1)S(1)}, bf16[32,512]{1,0:T(8,128)(2,1)S(1)}, u32[]{:S(2)}, u32[]{:S(2)}) collective-permute-start(bf16[32,512]{1,0:T(8,128)(2,1)S(1)} %get-tuple-element.140), channel_id=1, source_target_pairs={{0,4},{2,6},{4,8},{6,10},{8,12},{10,14},{5,1},{7,3},{9,5},{11,7},{... | collective-permute-start | bytes 98312 | tf_op jit(solution)/shard_map/ppermute | solution.py:50
  60.9 1.4 %own_grad.1 = (f32[128,512]{1,0:T(8,128)S(1)}, bf16[256,512]{1,0:T(8,128)(2,1)}) custom-call(s32[5]{0:T(128)S(1)} %stack.19.me_ref.r_0_, bf16[128,512]{1,0:T(8,128)(2,1)S(1)} %get-tuple-element.93.hott_ref, bf16[512,512]{1,0:T(8,128)(2,1)S(1)} %get-tuple-element.135.lg_ref.r_1_, bf16[512,512]{1,0:T(8,128)(2,1)S(1)} %get-tuple-element.136.new_ref), custom_call_target="tpu_custom_call" | custom-call | bytes 1703936 | tf_op jit(solution)/shard_map/own_grad/pallas_call | solution.py:31
  62.5 1.9 %all_gather.41 = bf16[128,512]{1,0:T(8,128)(2,1)S(1)} all-gather(bf16[64,512]{1,0:T(8,128)(2,1)S(1)} %pad_maximum_fusion.2), channel_id=1, replica_groups=mesh['groups'=2,'curve'=4,'cross'=2,'sub'=2] {'sub'}, dimensions={0}, use_global_device_ids=true | all-gather | bytes 196608 | tf_op jit(solution)/shard_map/all_gather | solution.py:54
  64.4 1.0 %cgrad.1 = (bf16[128,512]{1,0:T(8,128)(2,1)S(1)}, bf16[128,512]{1,0:T(8,128)(2,1)S(1)}, bf16[32,512]{1,0:T(8,128)(2,1)S(1)}, bf16[32,512]{1,0:T(8,128)(2,1)S(1)}) custom-call(s32[5]{0:T(128)S(1)} %stack.19.me_ref.r_0_, f32[128,512]{1,0:T(8,128)S(1)} %get-tuple-element.138.pool_ref, bf16[2,64,512]{2,1,0:T(8,128)(2,1)S(1)} %bitcast.21, ...), custom_call_target="tpu_custom_call" | custom-call | bytes 1638400 | tf_op jit(solution)/shard_map/cgrad/pallas_call | solution.py:31
  66.3 2.3 %collective-permute-start.12 = (bf16[32,512]{1,0:T(8,128)(2,1)S(1)}, bf16[32,512]{1,0:T(8,128)(2,1)S(1)}, u32[]{:S(2)}, u32[]{:S(2)}) collective-permute-start(bf16[32,512]{1,0:T(8,128)(2,1)S(1)} %get-tuple-element.146), channel_id=1, source_target_pairs={{0,4},{2,6},{4,8},{6,10},{8,12},{10,14},{5,1},{7,3},{9,5},{11,7},{... | collective-permute-start | bytes 98312 | tf_op jit(solution)/shard_map/ppermute | solution.py:50
  68.6 1.0 cweight.1
  69.7 1.0 collective-permute-start.14
  70.7 1.9 %all_gather.42 = bf16[128,512]{1,0:T(8,128)(2,1)S(1)} all-gather(bf16[64,512]{1,0:T(8,128)(2,1)S(1)} %pad_maximum_fusion.3), channel_id=1, replica_groups=mesh['groups'=2,'curve'=4,'cross'=2,'sub'=2] {'sub'}, dimensions={0}, use_global_device_ids=true | all-gather | bytes 196608 | tf_op jit(solution)/shard_map/all_gather | solution.py:54
  72.6 3.1 %third.1 = (bf16[512,512]{1,0:T(8,128)(2,1)S(1)}, bf16[512,512]{1,0:T(8,128)(2,1)S(1)}, bf16[512,512]{1,0:T(8,128)(2,1)S(1)}, bf16[128,512]{1,0:T(8,128)(2,1)S(1...) custom-call(s32[5]{0:T(128)S(1)} %stack.19.me_ref.r_0_, ...), custom_call_target="tpu_custom_call" | custom-call | bytes 9175040 | tf_op jit(solution)/shard_map/third/pallas_call | solution.py:31
  75.7 1.2 %collective-permute-start.19 = (bf16[4,384,128]{2,1,0:T(8,128)(2,1)S(1)}, bf16[4,384,128]{2,1,0:T(8,128)(2,1)S(1)}, u32[]{:S(2)}, u32[]{:S(2)}) collective-permute-start(bf16[4,384,128]{2,1,0:T(8,128)(2,1)S(1)} %get-tuple-element.171), channel_id=1, source_target_pairs={{0,2},{2,0},{1,3},{3,1},{4,6},{6,4},{5,7},{7,5},{8,10},{10,8},{9,1... | collective-permute-start | bytes 1179656 | tf_op jit(solution)/shard_map/ppermute | solution.py:62
  76.9 1.1 %stage1.1 = (f32[512,128]{1,0:T(8,128)S(1)}, bf16[512,128]{1,0:T(8,128)(2,1)S(1)}, bf16[512,128]{1,0:T(8,128)(2,1)S(1)}, bf16[512,128]{1,0:T(8,128)(2,1)S(1)}, f32[512,256]{1,0:T(8,128)S(1)}) custom-call(s32[5]{0:T(128)S(1)} %stack.19.me_ref.r_0_, bf16[512,512]{1,0:T(8,128)(2,1)S(1)} %get-tuple-element.152.fb_ref, ...), custom_call_target="tpu_custom_call" | custom-call | bytes 6160384 | tf_op jit(solution)/shard_map/stage1/pallas_call | solution.py:31
  78.0 1.9 %collective-permute-start.16 = (bf16[512,128]{1,0:T(8,128)(2,1)S(1)}, bf16[512,128]{1,0:T(8,128)(2,1)S(1)}, u32[]{:S(2)}, u32[]{:S(2)}) collective-permute-start(bf16[512,128]{1,0:T(8,128)(2,1)S(1)} %get-tuple-element.166), channel_id=1, source_target_pairs={{0,4},{4,0},{8,12},{12,8},{1,5},{5,1},{9,13},{13,9},{2,6},{6,2},{1... | collective-permute-start | bytes 393224 | tf_op jit(solution)/shard_map/ppermute | solution.py:66
  79.9 1.2 %collective-permute-start.15 = (bf16[128,512]{1,0:T(8,128)(2,1)S(1)}, bf16[128,512]{1,0:T(8,128)(2,1)S(1)}, u32[]{:S(2)}, u32[]{:S(2)}) collective-permute-start(bf16[128,512]{1,0:T(8,128)(2,1)S(1)} %get-tuple-element.164), channel_id=1, source_target_pairs={{0,2},{2,4},{4,6},{6,8},{8,10},{10,12},{12,14},{3,1},{5,3},{7,5},{... | collective-permute-start | bytes 393224 | tf_op jit(solution)/shard_map/ppermute | solution.py:50
  81.1 2.4 %collective-permute-start.18 = (bf16[512,128]{1,0:T(8,128)(2,1)S(1)}, bf16[512,128]{1,0:T(8,128)(2,1)S(1)}, u32[]{:S(2)}, u32[]{:S(2)}) collective-permute-start(bf16[512,128]{1,0:T(8,128)(2,1)S(1)} %get-tuple-element.168), channel_id=1, source_target_pairs={{0,12},{4,8},{8,4},{12,0},{1,13},{5,9},{9,5},{13,1},{2,14},{6,10},... | collective-permute-start | bytes 393224 | tf_op jit(solution)/shard_map/ppermute | solution.py:66
  83.5 4.2 %collective-permute-done.19.refs_1_ = bf16[4,384,128]{2,1,0:T(8,128)(2,1)S(1)} collective-permute-done((bf16[4,384,128]{2,1,0:T(8,128)(2,1)S(1)}, bf16[4,384,128]{2,1,0:T(8,128)(2,1)S(1)}, u32[]{:S(2)}, u32[]{:S(2)}) %collective-permute-start.19) | collective-permute-done | bytes 393248 | tf_op jit(solution)/shard_map/ppermute | solution.py:62
  88.4 3.6 %collective-permute-start.20 = (bf16[384,128]{1,0:T(8,128)(2,1)S(1)}, bf16[384,128]{1,0:T(8,128)(2,1)S(1)}, u32[]{:S(2)}, u32[]{:S(2)}) collective-permute-start(bf16[384,128]{1,0:T(8,128)(2,1)S(1)} %get-tuple-element.173), channel_id=1, source_target_pairs={{0,4},{4,0},{8,12},{12,8},{1,5},{5,1},{9,13},{13,9},{2,6},{6,2},{1... | collective-permute-start | bytes 294920 | tf_op jit(solution)/shard_map/ppermute | solution.py:66
  92.0 2.4 %collective-permute-start.22 = (bf16[384,128]{1,0:T(8,128)(2,1)S(1)}, bf16[384,128]{1,0:T(8,128)(2,1)S(1)}, u32[]{:S(2)}, u32[]{:S(2)}) collective-permute-start(bf16[384,128]{1,0:T(8,128)(2,1)S(1)} %get-tuple-element.175), channel_id=1, source_target_pairs={{0,12},{4,8},{8,4},{12,0},{1,13},{5,9},{9,5},{13,1},{2,14},{6,10},... | collective-permute-start | bytes 294920 | tf_op jit(solution)/shard_map/ppermute | solution.py:66
  94.4 2.0 %all_gather.43 = bf16[256,512]{1,0:T(8,128)(2,1)S(1)} all-gather(bf16[128,512]{1,0:T(8,128)(2,1)S(1)} %collective-permute-done.15), channel_id=1, replica_groups=mesh['groups'=2,'curve'=4,'cross'=2,'sub'=2] {'sub'}, dimensions={0}, use_global_device_ids=true | all-gather | bytes 393216 | tf_op jit(solution)/shard_map/all_gather | solution.py:54
  96.4 1.7 %last.1 = (f32[256,512]{1,0:T(8,128)}, f32[256,128]{1,0:T(8,128)S(1)}, f32[64,256]{1,0:T(8,128)S(1)}, f32[64,256]{1,0:T(8,128)}) custom-call(s32[5]{0:T(128)S(1)} %stack.19.me_ref.r_0_, f32[512,256]{1,0:T(8,128)S(1)} %get-tuple-element.163.comb_ref, bf16[2,128,512]{2,1,0:T(8,128)(2,1)S(1)} %bitcast.16, bf16[512,256]{1,0:T(8,128)(2,1)S(1)} %get-tuple-element.134.place_ref, ...), custom_call_target="tpu_custom_call" | custom-call | bytes 2490368 | tf_op jit(solution)/shard_map/last/pallas_call | solution.py:31
  98.1 4.5 %collective-permute-done.21.b_ref = bf16[384,128]{1,0:T(8,128)(2,1)S(1)} collective-permute-done((bf16[384,128]{1,0:T(8,128)(2,1)S(1)}, bf16[384,128]{1,0:T(8,128)(2,1)S(1)}, u32[]{:S(2)}, u32[]{:S(2)}) %collective-permute-start.21) | collective-permute-done | bytes 98336 | tf_op jit(solution)/shard_map/ppermute | solution.py:66
  (50 shorter events, 6.6 us)
Async XLA Ops:
  0.6 8.0 %copy-start.2 = (s32[4,3,128,128]{3,2,1,0:T(8,128)S(1)}, s32[4,3,128,128]{3,2,1,0:T(8,128)}, u32[]{:S(2)}) copy-start(s32[4,3,128,128]{3,2,1,0:T(8,128)} %mask_ref.1) | copy-start | bytes 2359300
  0.6 13.9 %collective-permute-start.1 = (bf16[2,256,1024]{2,1,0:T(8,128)(2,1)}, bf16[2,256,1024]{2,1,0:T(8,128)(2,1)S(1)}, u32[]{:S(2)}, u32[]{:S(2)}) collective-permute-start(bf16[2,256,1024]{2,1,0:T(8,128)(2,1)} %r_1_.3), channel_id=1, source_target_pairs={{0,1},{1,0},{2,3},{3,2},{4,5},{5,4},{6,7},{7,6},{8,9},{9,8},{10,11... | collective-permute-start | bytes 3145736 | tf_op jit(solution)/shard_map/ppermute | solution.py:58
  1.2 13.4 %collective-permute-start.2 = (bf16[2,256,512]{2,1,0:T(8,128)(2,1)}, bf16[2,256,512]{2,1,0:T(8,128)(2,1)S(1)}, u32[]{:S(2)}, u32[]{:S(2)}) collective-permute-start(bf16[2,256,512]{2,1,0:T(8,128)(2,1)} %r_2_.3), channel_id=1, source_target_pairs={{0,1},{1,0},{2,3},{3,2},{4,5},{5,4},{6,7},{7,6},{8,9},{9,8},{10,11... | collective-permute-start | bytes 1572872 | tf_op jit(solution)/shard_map/ppermute | solution.py:58
  1.3 3.5 %copy-start.3 = (s32[1,2,128]{2,1,0:T(2,128)S(1)}, s32[1,2,128]{2,1,0:T(2,128)}, u32[]{:S(2)}) copy-start(s32[1,2,128]{2,1,0:T(2,128)} %param.15) | copy-start | bytes 3076
  1.3 7.3 %copy-start.4 = (s32[4,3]{1,0:T(4,128)S(1)}, s32[4,3]{1,0:T(4,128)}, u32[]{:S(2)}) copy-start(s32[4,3]{1,0:T(4,128)} %tile_ref.1) | copy-start | bytes 148
  1.3 7.3 %copy-start.5 = (s32[512]{0:T(512)S(1)}, s32[512]{0:T(512)}, u32[]{:S(2)}) copy-start(s32[512]{0:T(512)} %param.16) | copy-start | bytes 6148
  4.8 9.7 %copy-start = (bf16[2,256,1024]{2,1,0:T(8,128)(2,1)S(1)}, bf16[2,256,1024]{2,1,0:T(8,128)(2,1)}, u32[]{:S(2)}) copy-start(bf16[2,256,1024]{2,1,0:T(8,128)(2,1)} %r_1_.3) | copy-start | bytes 3145732
  5.7 6.8 %collective-permute-start = (bf16[128,512]{1,0:T(8,128)(2,1)S(1)}, bf16[128,512]{1,0:T(8,128)(2,1)S(1)}, u32[]{:S(2)}, u32[]{:S(2)}) collective-permute-start(bf16[128,512]{1,0:T(8,128)(2,1)S(1)} %get-tuple-element.95), channel_id=1, source_target_pairs={{0,2},{2,4},{4,6},{6,8},{8,10},{10,12},{12,14},{3,1},{5,3},{7,5},{... | collective-permute-start | bytes 393224 | tf_op jit(solution)/shard_map/ppermute | solution.py:50
  8.7 5.9 %copy-start.1 = (bf16[2,256,512]{2,1,0:T(8,128)(2,1)S(1)}, bf16[2,256,512]{2,1,0:T(8,128)(2,1)}, u32[]{:S(2)}) copy-start(bf16[2,256,512]{2,1,0:T(8,128)(2,1)} %r_2_.3) | copy-start | bytes 1572868
  15.2 6.5 %copy-start.6 = (bf16[256,512]{1,0:T(8,128)(2,1)S(1)}, bf16[256,512]{1,0:T(8,128)(2,1)}, u32[]{:S(2)}) copy-start(bf16[256,512]{1,0:T(8,128)(2,1)} %param.12) | copy-start | bytes 786436
  17.6 7.0 %collective-permute-start.3 = (bf16[48,512]{1,0:T(8,128)(2,1)S(1)}, bf16[48,512]{1,0:T(8,128)(2,1)S(1)}, u32[]{:S(2)}, u32[]{:S(2)}) collective-permute-start(bf16[48,512]{1,0:T(8,128)(2,1)S(1)} %get-tuple-element.110), channel_id=1, source_target_pairs={{0,2},{2,4},{4,6},{6,8},{8,10},{10,12},{12,14},{3,1},{5,3},{7,5},{... | collective-permute-start | bytes 147464 | tf_op jit(solution)/shard_map/ppermute | solution.py:50
  20.1 4.5 %collective-permute-start.4 = (bf16[48,512]{1,0:T(8,128)(2,1)S(1)}, bf16[48,512]{1,0:T(8,128)(2,1)S(1)}, u32[]{:S(2)}, u32[]{:S(2)}) collective-permute-start(bf16[48,512]{1,0:T(8,128)(2,1)S(1)} %get-tuple-element.111), channel_id=1, source_target_pairs={{0,4},{2,6},{4,8},{6,10},{8,12},{10,14},{5,1},{7,3},{9,5},{11,7},{... | collective-permute-start | bytes 147464 | tf_op jit(solution)/shard_map/ppermute | solution.py:50
  27.7 3.3 %collective-permute-start.5 = (bf16[32,512]{1,0:T(8,128)(2,1)S(1)}, bf16[32,512]{1,0:T(8,128)(2,1)S(1)}, u32[]{:S(2)}, u32[]{:S(2)}) collective-permute-start(bf16[32,512]{1,0:T(8,128)(2,1)S(1)} %get-tuple-element.116), channel_id=1, source_target_pairs={{0,2},{2,4},{4,6},{6,8},{8,10},{10,12},{12,14},{3,1},{5,3},{7,5},{... | collective-permute-start | bytes 98312 | tf_op jit(solution)/shard_map/ppermute | solution.py:50
  28.8 3.2 %collective-permute-start.6 = (bf16[32,512]{1,0:T(8,128)(2,1)S(1)}, bf16[32,512]{1,0:T(8,128)(2,1)S(1)}, u32[]{:S(2)}, u32[]{:S(2)}) collective-permute-start(bf16[32,512]{1,0:T(8,128)(2,1)S(1)} %get-tuple-element.117), channel_id=1, source_target_pairs={{0,4},{2,6},{4,8},{6,10},{8,12},{10,14},{5,1},{7,3},{9,5},{11,7},{... | collective-permute-start | bytes 98312 | tf_op jit(solution)/shard_map/ppermute | solution.py:50
  33.9 2.8 %copy-start.7 = (bf16[256,512]{1,0:T(8,128)(2,1)S(1)}, bf16[256,512]{1,0:T(8,128)(2,1)}, u32[]{:S(2)}) copy-start(bf16[256,512]{1,0:T(8,128)(2,1)} %param.17) | copy-start | bytes 786436
  35.0 5.5 %collective-permute-start.7 = (bf16[128,512]{1,0:T(8,128)(2,1)S(1)}, bf16[128,512]{1,0:T(8,128)(2,1)S(1)}, u32[]{:S(2)}, u32[]{:S(2)}) collective-permute-start(bf16[128,512]{1,0:T(8,128)(2,1)S(1)} %get-tuple-element.120), channel_id=1, source_target_pairs={{0,2},{2,4},{4,6},{6,8},{8,10},{10,12},{12,14},{3,1},{5,3},{7,5},{... | collective-permute-start | bytes 393224 | tf_op jit(solution)/shard_map/ppermute | solution.py:50
  45.2 7.7 %collective-permute-start.8 = (bf16[128,512]{1,0:T(8,128)(2,1)S(1)}, bf16[128,512]{1,0:T(8,128)(2,1)S(1)}, u32[]{:S(2)}, u32[]{:S(2)}) collective-permute-start(bf16[128,512]{1,0:T(8,128)(2,1)S(1)} %get-tuple-element.133), channel_id=1, source_target_pairs={{0,2},{2,4},{4,6},{6,8},{8,10},{10,12},{12,14},{3,1},{5,3},{7,5},{... | collective-permute-start | bytes 393224 | tf_op jit(solution)/shard_map/ppermute | solution.py:50
  50.1 22.5 %collective-permute-start.13 = (bf16[4,384,128]{2,1,0:T(8,128)(2,1)S(1)}, bf16[4,384,128]{2,1,0:T(8,128)(2,1)S(1)}, u32[]{:S(2)}, u32[]{:S(2)}) collective-permute-start(bf16[4,384,128]{2,1,0:T(8,128)(2,1)S(1)} %get-tuple-element.147), channel_id=1, source_target_pairs={{0,2},{2,0},{1,3},{3,1},{4,6},{6,4},{5,7},{7,5},{8,10},{10,8},{9,1... | collective-permute-start | bytes 1179656 | tf_op jit(solution)/shard_map/ppermute | solution.py:62
  56.1 6.3 %collective-permute-start.9 = (bf16[32,512]{1,0:T(8,128)(2,1)S(1)}, bf16[32,512]{1,0:T(8,128)(2,1)S(1)}, u32[]{:S(2)}, u32[]{:S(2)}) collective-permute-start(bf16[32,512]{1,0:T(8,128)(2,1)S(1)} %get-tuple-element.139), channel_id=1, source_target_pairs={{0,2},{2,4},{4,6},{6,8},{8,10},{10,12},{12,14},{3,1},{5,3},{7,5},{... | collective-permute-start | bytes 98312 | tf_op jit(solution)/shard_map/ppermute | solution.py:50
  58.6 3.9 %collective-permute-start.10 = (bf16[32,512]{1,0:T(8,128)(2,1)S(1)}, bf16[32,512]{1,0:T(8,128)(2,1)S(1)}, u32[]{:S(2)}, u32[]{:S(2)}) collective-permute-start(bf16[32,512]{1,0:T(8,128)(2,1)S(1)} %get-tuple-element.140), channel_id=1, source_target_pairs={{0,4},{2,6},{4,8},{6,10},{8,12},{10,14},{5,1},{7,3},{9,5},{11,7},{... | collective-permute-start | bytes 98312 | tf_op jit(solution)/shard_map/ppermute | solution.py:50
  65.5 5.2 %collective-permute-start.11 = (bf16[32,512]{1,0:T(8,128)(2,1)S(1)}, bf16[32,512]{1,0:T(8,128)(2,1)S(1)}, u32[]{:S(2)}, u32[]{:S(2)}) collective-permute-start(bf16[32,512]{1,0:T(8,128)(2,1)S(1)} %get-tuple-element.145), channel_id=1, source_target_pairs={{0,2},{2,4},{4,6},{6,8},{8,10},{10,12},{12,14},{3,1},{5,3},{7,5},{... | collective-permute-start | bytes 98312 | tf_op jit(solution)/shard_map/ppermute | solution.py:50
  66.3 4.3 %collective-permute-start.12 = (bf16[32,512]{1,0:T(8,128)(2,1)S(1)}, bf16[32,512]{1,0:T(8,128)(2,1)S(1)}, u32[]{:S(2)}, u32[]{:S(2)}) collective-permute-start(bf16[32,512]{1,0:T(8,128)(2,1)S(1)} %get-tuple-element.146), channel_id=1, source_target_pairs={{0,4},{2,6},{4,8},{6,10},{8,12},{10,14},{5,1},{7,3},{9,5},{11,7},{... | collective-permute-start | bytes 98312 | tf_op jit(solution)/shard_map/ppermute | solution.py:50
  69.7 6.1 %collective-permute-start.14 = (bf16[4,128,128]{2,1,0:T(8,128)(2,1)S(1)}, bf16[4,128,128]{2,1,0:T(8,128)(2,1)S(1)}, u32[]{:S(2)}, u32[]{:S(2)}) collective-permute-start(bf16[4,128,128]{2,1,0:T(8,128)(2,1)S(1)} %get-tuple-element.161), channel_id=1, source_target_pairs={{0,2},{2,0},{1,3},{3,1},{4,6},{6,4},{5,7},{7,5},{8,10},{10,8},{9,1... | collective-permute-start | bytes 393224 | tf_op jit(solution)/shard_map/ppermute | solution.py:62
  75.7 12.0 %collective-permute-start.19 = (bf16[4,384,128]{2,1,0:T(8,128)(2,1)S(1)}, bf16[4,384,128]{2,1,0:T(8,128)(2,1)S(1)}, u32[]{:S(2)}, u32[]{:S(2)}) collective-permute-start(bf16[4,384,128]{2,1,0:T(8,128)(2,1)S(1)} %get-tuple-element.171), channel_id=1, source_target_pairs={{0,2},{2,0},{1,3},{3,1},{4,6},{6,4},{5,7},{7,5},{8,10},{10,8},{9,1... | collective-permute-start | bytes 1179656 | tf_op jit(solution)/shard_map/ppermute | solution.py:62
  78.0 14.0 %collective-permute-start.16 = (bf16[512,128]{1,0:T(8,128)(2,1)S(1)}, bf16[512,128]{1,0:T(8,128)(2,1)S(1)}, u32[]{:S(2)}, u32[]{:S(2)}) collective-permute-start(bf16[512,128]{1,0:T(8,128)(2,1)S(1)} %get-tuple-element.166), channel_id=1, source_target_pairs={{0,4},{4,0},{8,12},{12,8},{1,5},{5,1},{9,13},{13,9},{2,6},{6,2},{1... | collective-permute-start | bytes 393224 | tf_op jit(solution)/shard_map/ppermute | solution.py:66
  79.9 12.1 %collective-permute-start.15 = (bf16[128,512]{1,0:T(8,128)(2,1)S(1)}, bf16[128,512]{1,0:T(8,128)(2,1)S(1)}, u32[]{:S(2)}, u32[]{:S(2)}) collective-permute-start(bf16[128,512]{1,0:T(8,128)(2,1)S(1)} %get-tuple-element.164), channel_id=1, source_target_pairs={{0,2},{2,4},{4,6},{6,8},{8,10},{10,12},{12,14},{3,1},{5,3},{7,5},{... | collective-permute-start | bytes 393224 | tf_op jit(solution)/shard_map/ppermute | solution.py:50
  81.1 15.3 %collective-permute-start.17 = (bf16[512,128]{1,0:T(8,128)(2,1)S(1)}, bf16[512,128]{1,0:T(8,128)(2,1)S(1)}, u32[]{:S(2)}, u32[]{:S(2)}) collective-permute-start(bf16[512,128]{1,0:T(8,128)(2,1)S(1)} %get-tuple-element.167), channel_id=1, source_target_pairs={{0,8},{4,12},{8,0},{12,4},{1,9},{5,13},{9,1},{13,5},{2,10},{6,14},... | collective-permute-start | bytes 393224 | tf_op jit(solution)/shard_map/ppermute | solution.py:66
  81.1 15.3 %collective-permute-start.18 = (bf16[512,128]{1,0:T(8,128)(2,1)S(1)}, bf16[512,128]{1,0:T(8,128)(2,1)S(1)}, u32[]{:S(2)}, u32[]{:S(2)}) collective-permute-start(bf16[512,128]{1,0:T(8,128)(2,1)S(1)} %get-tuple-element.168), channel_id=1, source_target_pairs={{0,12},{4,8},{8,4},{12,0},{1,13},{5,9},{9,5},{13,1},{2,14},{6,10},... | collective-permute-start | bytes 393224 | tf_op jit(solution)/shard_map/ppermute | solution.py:66
  88.4 9.8 %collective-permute-start.20 = (bf16[384,128]{1,0:T(8,128)(2,1)S(1)}, bf16[384,128]{1,0:T(8,128)(2,1)S(1)}, u32[]{:S(2)}, u32[]{:S(2)}) collective-permute-start(bf16[384,128]{1,0:T(8,128)(2,1)S(1)} %get-tuple-element.173), channel_id=1, source_target_pairs={{0,4},{4,0},{8,12},{12,8},{1,5},{5,1},{9,13},{13,9},{2,6},{6,2},{1... | collective-permute-start | bytes 294920 | tf_op jit(solution)/shard_map/ppermute | solution.py:66
  92.0 10.6 %collective-permute-start.21 = (bf16[384,128]{1,0:T(8,128)(2,1)S(1)}, bf16[384,128]{1,0:T(8,128)(2,1)S(1)}, u32[]{:S(2)}, u32[]{:S(2)}) collective-permute-start(bf16[384,128]{1,0:T(8,128)(2,1)S(1)} %get-tuple-element.174), channel_id=1, source_target_pairs={{0,8},{4,12},{8,0},{12,4},{1,9},{5,13},{9,1},{13,5},{2,10},{6,14},... | collective-permute-start | bytes 294920 | tf_op jit(solution)/shard_map/ppermute | solution.py:66
  92.0 10.6 %collective-permute-start.22 = (bf16[384,128]{1,0:T(8,128)(2,1)S(1)}, bf16[384,128]{1,0:T(8,128)(2,1)S(1)}, u32[]{:S(2)}, u32[]{:S(2)}) collective-permute-start(bf16[384,128]{1,0:T(8,128)(2,1)S(1)} %get-tuple-element.175), channel_id=1, source_target_pairs={{0,12},{4,8},{8,4},{12,0},{1,13},{5,9},{9,5},{13,1},{2,14},{6,10},... | collective-permute-start | bytes 294920 | tf_op jit(solution)/shard_map/ppermute | solution.py:66

commit v6 on v5

--- a/solution.py
+++ b/solution.py
@@ -50,12 +50,21 @@
     return lax.ppermute(value, LINE, pairs)
 
 
-def gather(value):
-    return lax.all_gather(value, "sub", axis=0, tiled=True)
-
-
 def swap(value):
     return lax.ppermute(value, "sub", [(0, 1), (1, 0)])
+
+
+def gather(value):
+    return lax.all_gather(value, "sub", axis=0, tiled=False)
+
+
+def shared(*values):
+    return [v for value in values for v in (value, swap(value))]
+
+
+def directed(sub, own_ref, other_ref, rows=slice(None)):
+    own, other = own_ref[rows, :], other_ref[rows, :]
+    return jnp.where(sub == 0, own, other), jnp.where(sub == 0, other, own)
 
 
 def cross_swap(value):
@@ -77,6 +86,12 @@
 
 def wide(col, width):
     return jnp.concatenate([col] * (width // col.shape[1]), axis=1)
+
+
+def join_halves(sub, own_ref, other_ref, out_ref):
+    half = own_ref.shape[0]
+    out_ref[:, pl.ds(pl.multiple_of(sub * half, half), half)] = own_ref[...].T
+    out_ref[:, pl.ds(pl.multiple_of((1 - sub) * half, half), half)] = other_ref[...].T
 
 
 def k_halo(me_ref, rows_ref, x_ref, xc_ref, msg_ref):
@@ -158,9 +173,9 @@
     two_ref[0:cap, :] = dot(slot_ref[pl.ds(a + 2 * cap, cap), :], values).astype(BF)
 
 
-def fill_sources(me_ref, xc, rims_ref, src):
+def fill_sources(me_ref, xc, rims, src):
     n = xc.shape[0]
-    rim = rims_ref.shape[1]
+    rim = rims[0].shape[0]
     src[0:n, :] = xc
     for c in range(2):
         rows = slice(n + c * rim, n + (c + 1) * rim)
@@ -168,7 +183,7 @@
 
         @pl.when(there)
         def _():
-            src[rows, :] = rims_ref[c]
+            src[rows, :] = rims[c]
 
         @pl.when(jnp.logical_not(there))
         def _():
@@ -179,7 +194,7 @@
             slot_ref, tags_ref,
             agg_ref, pre_ref, hid_ref, first_ref, one_ref, two_ref, src):
     xc = xc_ref[...]
-    fill_sources(me_ref, xc, rims_ref, src)
+    fill_sources(me_ref, xc, (rims_ref[0], rims_ref[1]), src)
     agg, pre, hid, out = forward(xc, src[...], adj_ref, inv_ref, win_ref, wo_ref)
     agg_ref[...] = agg
     pre_ref[...] = pre
@@ -192,33 +207,36 @@
     two_ref[cap:, :] = pad
 
 
-def k_own(hott_ref, v_ref, pre_ref, pool_ref, slope_ref):
+def k_own(me_ref, hott_ref, v_ref, pre_ref, cw_ref, cw2_ref, pool_ref, slope_ref, cwf_ref):
+    half = cw_ref.shape[0]
     pool_ref[...] = dot(hott_ref[...], v_ref[...])
     slope_ref[...] = slope_of(pre_ref[...])
-
-
-def k_cot(ct_ref, wo_ref, ctc_ref, hg_ref):
-    ctc = ct_ref[...].T
-    ctc_ref[...] = ctc
-    hg_ref[...] = dot(ctc, wo_ref[...])
-
-
-def arrived_of(got_ref, cap):
-    rows = got_ref.shape[1] // 2
-    return jnp.concatenate(
-        [got_ref[0, 0:cap], got_ref[1, 0:cap], got_ref[0, rows:rows + cap], got_ref[1, rows:rows + cap]],
-        axis=0,
-    )
-
-
-def k_coarse(me_ref, pool_ref, ocount_ref, got_ref, cw_ref,
+    cwf_ref[pl.ds(pl.multiple_of(me_ref[1] * half, half), half), :] = cw_ref[...]
+    cwf_ref[pl.ds(pl.multiple_of((1 - me_ref[1]) * half, half), half), :] = cw2_ref[...]
+
+
+def k_cot(me_ref, ct_ref, ct2_ref, wo_ref, ctc_ref, hg_ref):
+    join_halves(me_ref[1], ct_ref, ct2_ref, ctc_ref)
+    hg_ref[...] = dot(ctc_ref[...], wo_ref[...])
+
+
+def arrived_of(sub, got, cap):
+    one, one2, two, two2 = got
+    rows = slice(0, cap)
+    return jnp.concatenate(directed(sub, one, one2, rows) + directed(sub, two, two2, rows), axis=0)
+
+
+def k_coarse(me_ref, pool_ref, ocount_ref, one_ref, one2_ref, two_ref, two2_ref, cw_ref,
              hits_ref, icount_ref, coarse_ref, cpre_ref, corr_ref, out1_ref, out2_ref):
     nodes, width = pool_ref.shape
     cap = out1_ref.shape[0]
-    rows = got_ref.shape[1] // 2
+    sub = me_ref[1]
+    got = (one_ref, one2_ref, two_ref, two2_ref)
     slots = 4 * cap
     lane = lax.broadcasted_iota(I32, (1, slots), 1)
-    t = [got_ref[c, o + cap:o + cap + 1, 0:slots].astype(F32) for o in (0, rows) for c in range(2)]
+    row = slice(cap, cap + 1)
+    t = directed(sub, one_ref, one2_ref, row) + directed(sub, two_ref, two2_ref, row)
+    t = [v[:, 0:slots].astype(F32) for v in t]
     domain, count = me_ref[0], me_ref[4]
     there = (domain >= 1, domain < count - 1, domain >= 2, domain < count - 2)
     t = [jnp.where(ok, v, 0.0) for ok, v in zip(there, t)]
@@ -230,7 +248,7 @@
     hits_ref[...] = hits
     icount_ref[...] = icount
     hb = hits.astype(BF)
-    total = pool_ref[...] + dot(hb, arrived_of(got_ref, cap))
+    total = pool_ref[...] + dot(hb, arrived_of(sub, got, cap))
     coarse = (total * wide(icount, width)).astype(BF)
     cpre = dot(coarse, cw_ref[...], NT)
     corr = (cpre * sigmoid(cpre)).astype(BF)
@@ -238,23 +256,21 @@
     cpre_ref[...] = cpre
     corr_ref[...] = corr
     ans = dot(hits.T.astype(BF), corr).astype(BF)
-    sub = me_ref[1]
     out1_ref[...] = jnp.where(sub == 0, ans[cap:2 * cap], ans[0:cap])
     out2_ref[...] = jnp.where(sub == 0, ans[3 * cap:], ans[2 * cap:3 * cap])
 
 
-def spread_back(first, hot_ref, slott_ref, corr, got_ref):
-    cap = got_ref.shape[1] // 2
-    returned = jnp.concatenate(
-        [got_ref[1, 0:cap], got_ref[0, 0:cap], got_ref[1, cap:], got_ref[0, cap:]], axis=0
-    )
+def spread_back(first, hot_ref, slott_ref, corr, one, two):
+    returned = jnp.concatenate([one[1], one[0], two[1], two[0]], axis=0)
     total = first.astype(F32) + dot(hot_ref[...], corr) + dot(slott_ref[...], returned)
     return total.astype(BF)
 
 
-def k_lift(me_ref, first_ref, hot_ref, slott_ref, corr_ref, got_ref, pick_ref,
+def k_lift(me_ref, first_ref, hot_ref, slott_ref, corr_ref, one_ref, one2_ref, two_ref, two2_ref, pick_ref,
            lift_ref, msg_ref):
-    lifted = spread_back(first_ref[...], hot_ref, slott_ref, corr_ref[...], got_ref)
+    lifted = spread_back(
+        first_ref[...], hot_ref, slott_ref, corr_ref[...],
+        directed(me_ref[1], one_ref, one2_ref), directed(me_ref[1], two_ref, two2_ref))
     lift_ref[...] = lifted
     rim = msg_ref.shape[0]
     at = pl.multiple_of(me_ref[1] * rim, rim)
@@ -271,10 +287,10 @@
     msg_ref[...] = dot(adjt_ref[pl.ds(at, rim), :], scaled).astype(BF)
 
 
-def k_second(me_ref, lift_ref, rim_ref, adj_ref, adjt_ref, inv_ref, win_ref, wo_ref, hg_ref,
+def k_second(me_ref, lift_ref, rim_ref, rim2_ref, adj_ref, adjt_ref, inv_ref, win_ref, wo_ref, hg_ref,
              agg_ref, hid_ref, new_ref, pg_ref, scaled_ref, msg_ref, src):
     lifted = lift_ref[...]
-    fill_sources(me_ref, lifted, rim_ref, src)
+    fill_sources(me_ref, lifted, directed(me_ref[1], rim_ref, rim2_ref), src)
     agg, pre, hid, out = forward(lifted, src[...], adj_ref, inv_ref, win_ref, wo_ref)
     agg_ref[...] = agg
     hid_ref[...] = hid
@@ -371,23 +387,23 @@
     return jnp.where(me_ref[0] < me_ref[4] - 1, from_after, 0.0) + jnp.where(me_ref[0] >= 1, from_before, 0.0)
 
 
-def k_lgrad(me_ref, comb_ref, rim_ref, place_ref, slot_ref, lg_ref, one_ref, two_ref):
-    lg = (comb_ref[...] + placed(me_ref, place_ref, rim_ref[0], rim_ref[1])).astype(BF)
+def k_lgrad(me_ref, comb_ref, rim_ref, rim2_ref, place_ref, slot_ref, lg_ref, one_ref, two_ref):
+    lg = (comb_ref[...] + placed(me_ref, place_ref, *directed(me_ref[1], rim_ref, rim2_ref))).astype(BF)
     lg_ref[...] = lg
     send_slots(me_ref[1], lg, slot_ref, one_ref, two_ref)
 
 
-def k_cgrad(me_ref, pool_ref, got_ref, hits_ref, icount_ref, cpre_ref, cw_ref,
+def k_cgrad(me_ref, pool_ref, one_ref, one2_ref, two_ref, two2_ref, hits_ref, icount_ref, cpre_ref, cw_ref,
             pgrad_ref, spread_ref, out1_ref, out2_ref):
     cap = out1_ref.shape[0]
+    sub = me_ref[1]
     hits = hits_ref[...]
-    total = pool_ref[...] + dot(hits.astype(BF), arrived_of(got_ref, cap))
+    total = pool_ref[...] + dot(hits.astype(BF), arrived_of(sub, (one_ref, one2_ref, two_ref, two2_ref), cap))
     pgrad = (total * slope_of(cpre_ref[...])).astype(BF)
     pgrad_ref[...] = pgrad
     spread = (dot(pgrad, cw_ref[...]) * wide(icount_ref[...], pgrad.shape[1])).astype(BF)
     spread_ref[...] = spread
     ans = dot(hits.T.astype(BF), spread).astype(BF)
-    sub = me_ref[1]
     out1_ref[...] = jnp.where(sub == 0, ans[cap:2 * cap], ans[0:cap])
     out2_ref[...] = jnp.where(sub == 0, ans[3 * cap:], ans[2 * cap:3 * cap])
 
@@ -398,10 +414,13 @@
     out_ref[...] = dot(pgrad_ref[:, pl.ds(at, half)].T, coarse_ref[...]) * scale
 
 
-def k_third(me_ref, lg_ref, hot_ref, slott_ref, spread_ref, got_ref, wo_ref, slope_ref,
-            win_ref, inv_ref, adjt_ref, *rest, scale=None):
-    fb_ref, pg_ref, scaled_ref, msg_ref = rest[-4:] if scale is None else rest[3:7]
-    fb = spread_back(lg_ref[...], hot_ref, slott_ref, spread_ref[...], got_ref)
+def k_third(me_ref, lg_ref, hot_ref, slott_ref, spread_ref, got_ref,
+            wo_ref, slope_ref, win_ref, inv_ref, adjt_ref, *rest, scale=None):
+    fb_ref, pg_ref, scaled_ref, msg_ref = rest if scale is None else rest[3:7]
+    cap = got_ref.shape[1] // 2
+    fb = spread_back(
+        lg_ref[...], hot_ref, slott_ref, spread_ref[...],
+        (got_ref[0, 0:cap], got_ref[1, 0:cap]), (got_ref[0, cap:], got_ref[1, cap:]))
     fb_ref[...] = fb
     pg = (dot(fb, wo_ref[...]) * slope_ref[...]).astype(BF)
     pg_ref[...] = pg
@@ -411,11 +430,11 @@
     rim_grads(me_ref[1], pg, win_ref, inv_ref, adjt_ref, scaled_ref, msg_ref)
 
 
-def k_last(me_ref, comb_ref, rim_ref, place_ref, *rest):
+def k_last(me_ref, comb_ref, rims_ref, place_ref, *rest):
     half = comb_ref.shape[1]
     at = pl.multiple_of(me_ref[1] * half, half)
     total = comb_ref[...] + placed(
-        me_ref, place_ref, rim_ref[0, :, pl.ds(at, half)], rim_ref[1, :, pl.ds(at, half)])
+        me_ref, place_ref, rims_ref[0, :, pl.ds(at, half)], rims_ref[1, :, pl.ds(at, half)])
     if len(rest) == 1:
         rest[0][...] = total.T
     else:
@@ -499,7 +518,7 @@
 
     cell_bf, cell_f32 = sds((n, width), BF), sds((n, width), F32)
     win2, wout2 = swap(inward_weight), swap(outward_weight)
-    x_full = gather(node_features)
+    x_full = gather(node_features).reshape(width, n)
     xc, rims = call(k_halo, [cell_bf, sds((rim, width), BF)], [me], [rows, x_full], "halo")
     rims = two_way(rims, 1)
     (adj, adjt, inv, hott, hot, slot, slott, pick, place, tags, ocount) = call(
@@ -511,39 +530,42 @@
     weight_outs = [sds((hidden, 2 * width), BF), sds((width, hidden), BF)]
     win0, wo0 = call(lambda *r: k_weights(0, *r), weight_outs, [me],
                      [inward_weight, outward_weight, win2, wout2], "weights0")
-    rims = gather(rims).reshape(2, rim, width)
+    rims, win0, adj = lax.optimization_barrier((rims, win0, adj))
     msg = sds((cap + 16, width), BF)
     plain = sds((cap, width), BF)
     hid_bf, hid_f32 = sds((n, hidden), BF), sds((n, hidden), F32)
     agg0, pre0, hid0, first, one, two = call(
         k_first,
         [cell_bf, hid_f32, hid_bf, cell_bf, msg, msg],
-        [me], [xc, rims, adj, inv, win0, wo0, slot, tags], "first",
+        [me], [xc, gather(rims), adj, inv, win0, wo0, slot, tags], "first",
         flops=2 * n * width * (src_rows + 3 * width),
         scratch=[pltpu.VMEM((src_rows, width), BF)])
     one, two, win2, coarse_weight = lax.optimization_barrier((one, two, win2, coarse_weight))
     one, two = two_way(one, 1), two_way(two, 2)
-    own, slope0 = call(k_own, [sds((nodes, width), F32), hid_f32], [], [hott, first, pre0], "own")
-    cw = gather(coarse_weight)
+    own, slope0, cw = call(
+        k_own, [sds((nodes, width), F32), hid_f32, sds((width, width), BF)], [me],
+        [hott, first, pre0, coarse_weight, swap(coarse_weight)], "own")
     win1, wo1 = call(lambda *r: k_weights(1, *r), weight_outs, [me],
                      [inward_weight, outward_weight, win2, wout2], "weights1")
-    got = gather(jnp.concatenate([one, two], axis=0)).reshape(2, -1, width)
+    one, two, own = lax.optimization_barrier((one, two, own))
+    got = shared(one, two)
     node_bf, node_f32 = sds((nodes, width), BF), sds((nodes, width), F32)
     hits, icount, coarse, cpre, corr, one, two = call(
         k_coarse, [sds((nodes, slots), F32), sds((nodes, 128), F32), node_bf, node_f32, node_bf, plain, plain],
-        [me], [own, ocount, got, cw], "coarse")
+        [me], [own, ocount, *got, cw], "coarse")
     one, two, cotangent = lax.optimization_barrier((one, two, cotangent))
     one, two = two_way(one, 1), two_way(two, 2)
-    ct_full = gather(cotangent)
-    ctc, hg1 = call(k_cot, [cell_bf, hid_f32], [], [ct_full, wo1], "cot")
-    got = gather(jnp.concatenate([one, two], axis=0)).reshape(2, -1, width)
+    ctc, hg1 = call(k_cot, [cell_bf, hid_f32], [me], [cotangent, swap(cotangent), wo1], "cot")
+    one, two, win1 = lax.optimization_barrier((one, two, win1))
+    got = shared(one, two)
     lifted, rims = call(
         k_lift, [cell_bf, sds((rim, width), BF)], [me],
-        [first, hot, slott, corr, got, pick], "lift")
-    rims = gather(two_way(rims, 1)).reshape(2, rim, width)
+        [first, hot, slott, corr, *got, pick], "lift")
+    rims, hg1 = lax.optimization_barrier((two_way(rims, 1), hg1))
+    rims = shared(rims)
     agg1, hid1, new, pg1, scaled1, rims = call(
         k_second, [cell_bf, hid_bf, cell_bf, hid_bf, cell_bf, sds((rim, width), BF)],
-        [me], [lifted, rims, adj, adjt, inv, win1, wo1, hg1], "second",
+        [me], [lifted, *rims, adj, adjt, inv, win1, wo1, hg1], "second",
         scratch=[pltpu.VMEM((src_rows, width), BF)])
     rims = two_way(rims, 1)
     piece = 2 * width // domains
@@ -557,31 +579,35 @@
         got1 = cross_swap(send1)
     else:
         comb1, = call(k_combine, [cell_f32], [], [ctc, pg1, win1, scaled1, adjt], "combine")
-    rims = gather(rims).reshape(2, rim, width)
+    rims, comb1 = lax.optimization_barrier((rims, comb1))
+    rims = shared(rims)
     lg, one, two = call(
-        k_lgrad, [cell_bf, plain, plain], [me], [comb1, rims, place, slot], "lgrad")
+        k_lgrad, [cell_bf, plain, plain], [me], [comb1, *rims, place, slot], "lgrad")
     one, two = two_way(one, 1), two_way(two, 2)
     own_g, new_t = call(k_newt, [node_f32, sds((half, n), BF)], [me], [hott, lg, new], "own_grad")
-    got = gather(jnp.concatenate([one, two], axis=0)).reshape(2, -1, width)
+    one, two, own_g = lax.optimization_barrier((one, two, own_g))
+    got = shared(one, two)
     pgrad, spread, one, two = call(
         k_cgrad, [node_bf, node_bf, plain, plain], [me],
-        [own_g, got, hits, icount, cpre, cw], "cgrad")
+        [own_g, *got, hits, icount, cpre, cw], "cgrad")
     one, two = two_way(one, 1), two_way(two, 2)
-    got = gather(jnp.concatenate([one, two], axis=0)).reshape(2, -1, width)
-    back_outs = [cell_bf, hid_bf, cell_bf, sds((rim, width), BF)]
-    back_args = [lg, hot, slott, spread, got, wo0, slope0, win0, inv, adjt]
     if packed:
         keepc, sendc = call(
             lambda *r: k_cweight_pack(scale, *r),
             [sds((curve, 2 * small, piece), F32), sds((curve, 2 * small, piece), BF)], [me],
             [pgrad, coarse], "cweight")
         gotc = cross_swap(sendc)
+    got = gather(jnp.concatenate([one, two], axis=0))
+    back_outs = [cell_bf, hid_bf, cell_bf, sds((rim, width), BF)]
+    if packed:
         got, got1 = lax.optimization_barrier((got, got1))
-        back_args[4] = got
+    if packed:
         fb, pg0, scaled0, rims, keep0, send0 = call(
-            lambda *r: k_third(*r, scale=scale), back_outs + pack, [me], back_args + [xc, agg0, hid0], "third")
+            lambda *r: k_third(*r, scale=scale), back_outs + pack, [me],
+            [lg, hot, slott, spread, got, wo0, slope0, win0, inv, adjt, xc, agg0, hid0], "third")
         send0, gotc = lax.optimization_barrier((send0, gotc))
         got0 = cross_swap(send0)
+        keepc, pg0 = lax.optimization_barrier((keepc, pg0))
         rims = two_way(rims, 1)
 
         def staged(body, extra, extra_outs, pairs, name):
@@ -597,10 +623,11 @@
         late, _ = staged(k_stage, [], [], [keep0, got0], "stage0")
     else:
         gco, = call(lambda *r: k_cweight(scale, *r), [sds((half, width), F32)], [me], [pgrad, coarse], "cweight")
-        fb, pg0, scaled0, rims = call(k_third, back_outs, [me], back_args, "third")
+        fb, pg0, scaled0, rims = call(
+            k_third, back_outs, [me], [lg, hot, slott, spread, got, wo0, slope0, win0, inv, adjt], "third")
         rims = two_way(rims, 1)
         comb0, = call(k_halfcomb, [sds((n, half), F32)], [me], [fb, pg0, win0, scaled0, adjt], "halfcomb")
-    rims = gather(rims).reshape(2, rim, width)
+    rims = gather(rims)
     if packed:
         fgrad, ein, eout, gco = call(
             k_last, [sds((half, n), F32), sds((half, piece), F32), sds((small, half), F32), sds((small, half), F32)],

time: 104 us -> 101 us (0.971)
  blocking collectives: 23.3 us -> 9.32 us
  waiting for transfers between devices: 14.7 us -> 20.3 us
  starting transfers between devices: 37.9 us -> 41 us
  Pallas kernels: 26.5 us -> 27.8 us
  local copies, waits for them, and re-layouts: 0.12 us -> 1.25 us
    all_gather x11 -> x4, blocking collectives: 23.3 us -> 9.32 us  [gather(): return lax.all_gather(value, 'sub', axis=0, tiled=False)]
    ppermute x2 -> x12, waiting for transfers between devices: 0.01 us -> 5.3 us  [swap(): return lax.ppermute(value, 'sub', [(0, 1), (1, 0)])]
    ppermute x2 -> x12, starting transfers between devices: 0.6 us -> 2.76 us  [swap(): return lax.ppermute(value, 'sub', [(0, 1), (1, 0)])]
    ppermute x12, starting transfers between devices: 23.1 us -> 24.6 us  [two_way(): return lax.ppermute(value, LINE, pairs)]
    pallas_call x20, Pallas kernels: 26.5 us -> 27.8 us  [call(): pl.pallas_call(body, out_shape=tuple(outs), in_specs=[pl.BlockSpec(memory...]
    unnamed x16, local copies, waits for them, and re-layouts: 0.03 us -> 1.16 us
  transfers between devices with their start and end apart: 23 -> 33, of which waited for: 7 -> 16; matrix products, arithmetic and copies ran while one was open for 0% -> 0% of each run, Pallas kernels for 17% -> 21%
where the time goes in v6:
time: 101 us
  starting transfers between devices  41 us (41%)
  Pallas kernels  27.8 us (28%)
  waiting for transfers between devices  20.3 us (20%)
  blocking collectives  9.32 us (9%)
  local copies, waits for them, and re-layouts  1.25 us (1%)
    pallas_call x20, Pallas kernels, call(): pl.pallas_call(body, out_shape=tuple(outs), in_specs=[pl.BlockSpec(memory...  27.8 us
    ppermute x12, starting transfers between devices, two_way(): return lax.ppermute(value, LINE, pairs)  24.6 us
    ppermute x6, starting transfers between devices, curve_swap(): return lax.ppermute(value, 'curve', [(z, z ^ step) for z in range(4)])  10 us
    all_gather x4, blocking collectives, gather(): return lax.all_gather(value, 'sub', axis=0, tiled=False)  9.32 us
    ppermute x12, waiting for transfers between devices, two_way(): return lax.ppermute(value, LINE, pairs)  6.34 us
    ppermute x12, waiting for transfers between devices, swap(): return lax.ppermute(value, 'sub', [(0, 1), (1, 0)])  5.3 us
    ppermute x3, waiting for transfers between devices, cross_swap(): return lax.ppermute(value, 'cross', [(0, 1), (1, 0)])  4.41 us
    ppermute x6, waiting for transfers between devices, curve_swap(): return lax.ppermute(value, 'curve', [(z, z ^ step) for z in range(4)])  4.22 us
  transfers between devices with their start and end apart: 33, of which 16 were waited for; matrix products, arithmetic and copies ran while one was open for 0% of the time, Pallas kernels for 21%

profile of v6, /device:TPU:0, one launch (start us, length us, event | category | flops | bytes accessed | tf_op | source)
XLA Modules:
  0.0 100.6 jit_solution(2130049297108824800)
XLA Ops:
  1.3 3.5 %all-gather.x_ref = bf16[512,512]{1,0:T(8,128)(2,1)S(1)} all-gather(bf16[256,512]{1,0:T(8,128)(2,1)} %param.9), channel_id=2, replica_groups=mesh['groups'=2,'curve'=4,'cross'=2,'sub'=2] {'sub'}, dimensions={0}, use_global_device_ids=true | all-gather | bytes 786432 | tf_op jit(solution)/shard_map/all_gather | solution.py:58
  4.8 0.9 halo.1
  5.7 2.9 %collective-permute-start = (bf16[128,512]{1,0:T(8,128)(2,1)S(1)}, bf16[128,512]{1,0:T(8,128)(2,1)S(1)}, u32[]{:S(2)}, u32[]{:S(2)}) collective-permute-start(bf16[128,512]{1,0:T(8,128)(2,1)S(1)} %get-tuple-element.114), channel_id=1, source_target_pairs={{0,2},{2,4},{4,6},{6,8},{8,10},{10,12},{12,14},{3,1},{5,3},{7,5},{... | collective-permute-start | bytes 393224 | tf_op jit(solution)/shard_map/ppermute | solution.py:50
  8.7 1.1 %copy-done.2 = s32[4,3,128,128]{3,2,1,0:T(8,128)S(1)} copy-done((s32[4,3,128,128]{3,2,1,0:T(8,128)S(1)}, s32[4,3,128,128]{3,2,1,0:T(8,128)}, u32[]{:S(2)}) %copy-start.2) | copy-done | bytes 786456
  9.8 1.3 %prep.1 = (bf16[512,768]{1,0:T(8,128)(2,1)S(1)}, bf16[768,512]{1,0:T(8,128)(2,1)S(1)}, f32[512,128]{1,0:T(8,128)S(1)}, bf16[128,512]{1,0:T(8,128)(2,1)S(1)}, bf1...) custom-call(s32[4,3]{1,0:T(4,128)S(1)} %copy-done.6, ...), custom_call_target="tpu_custom_call" | custom-call | bytes 3742720 | tf_op jit(solution)/shard_map/prep/pallas_call | solution.py:31
  12.5 2.0 %all-gather.1 = bf16[256,512]{1,0:T(8,128)(2,1)S(1)} all-gather(bf16[128,512]{1,0:T(8,128)(2,1)S(1)} %collective-permute-done), channel_id=3, replica_groups=mesh['groups'=2,'curve'=4,'cross'=2,'sub'=2] {'sub'}, dimensions={0}, use_global_device_ids=true | all-gather | bytes 393216 | tf_op jit(solution)/shard_map/all_gather | solution.py:58
  14.5 2.4 %first.1 = (bf16[512,512]{1,0:T(8,128)(2,1)S(1)}, f32[512,512]{1,0:T(8,128)S(1)}, bf16[512,512]{1,0:T(8,128)(2,1)S(1)}, bf16[512,512]{1,0:T(8,128)(2,1)S(1)}, bf...) custom-call(s32[5]{0:T(128)S(1)} %stack.19.me_ref.r_0_, bf16[512,512]{1,0:T(8,128)(2,1)S(1)} %get-tuple-element.113.xc_ref.r_11_, ...), custom_call_target="tpu_custom_call" | custom-call | flops 1207959552 | bytes 6262784 | tf_op jit(solution)/shard_map/first/pallas_call | solution.py:31
  17.1 2.5 %collective-permute-start.3 = (bf16[48,512]{1,0:T(8,128)(2,1)S(1)}, bf16[48,512]{1,0:T(8,128)(2,1)S(1)}, u32[]{:S(2)}, u32[]{:S(2)}) collective-permute-start(bf16[48,512]{1,0:T(8,128)(2,1)S(1)} %get-tuple-element.129), channel_id=1, source_target_pairs={{0,2},{2,4},{4,6},{6,8},{8,10},{10,12},{12,14},{3,1},{5,3},{7,5},{... | collective-permute-start | bytes 147464 | tf_op jit(solution)/shard_map/ppermute | solution.py:50
  19.6 1.6 %collective-permute-start.4 = (bf16[48,512]{1,0:T(8,128)(2,1)S(1)}, bf16[48,512]{1,0:T(8,128)(2,1)S(1)}, u32[]{:S(2)}, u32[]{:S(2)}) collective-permute-start(bf16[48,512]{1,0:T(8,128)(2,1)S(1)} %get-tuple-element.130), channel_id=1, source_target_pairs={{0,4},{2,6},{4,8},{6,10},{8,12},{10,14},{5,1},{7,3},{9,5},{11,7},{... | collective-permute-start | bytes 147464 | tf_op jit(solution)/shard_map/ppermute | solution.py:50
  21.2 1.3 %own.1 = (f32[128,512]{1,0:T(8,128)S(1)}, f32[512,512]{1,0:T(8,128)S(1)}, bf16[512,512]{1,0:T(8,128)(2,1)S(1)}) custom-call(s32[5]{0:T(128)S(1)} %stack.19.me_ref.r_0_, bf16[128,512]{1,0:T(8,128)(2,1)S(1)} %get-tuple-element.112.hott_ref, bf16[512,512]{1,0:T(8,128)(2,1)S(1)} %get-tuple-element.124.v_ref.first_ref, ...), custom_call_target="tpu_custom_call" | custom-call | bytes 4063232 | tf_op jit(solution)/shard_map/own/pallas_call | solution.py:31
  24.4 1.1 %coarse.1 = (f32[128,128]{1,0:T(8,128)S(1)}, f32[128,128]{1,0:T(8,128)S(1)}, bf16[128,512]{1,0:T(8,128)(2,1)S(1)}, f32[128,512]{1,0:T(8,128)S(1)}, bf16[128,512]...) custom-call(s32[5]{0:T(128)S(1)} %stack.19.me_ref.r_0_, ...), custom_call_target="tpu_custom_call" | custom-call | bytes 1769472 | tf_op jit(solution)/shard_map/coarse/pallas_call | solution.py:31
  25.9 1.3 %collective-permute-start.8 = (bf16[32,512]{1,0:T(8,128)(2,1)S(1)}, bf16[32,512]{1,0:T(8,128)(2,1)S(1)}, u32[]{:S(2)}, u32[]{:S(2)}) collective-permute-start(bf16[32,512]{1,0:T(8,128)(2,1)S(1)} %get-tuple-element.142), channel_id=1, source_target_pairs={{0,2},{2,4},{4,6},{6,8},{8,10},{10,12},{12,14},{3,1},{5,3},{7,5},{... | collective-permute-start | bytes 98312 | tf_op jit(solution)/shard_map/ppermute | solution.py:50
  27.2 2.1 %collective-permute-start.9 = (bf16[32,512]{1,0:T(8,128)(2,1)S(1)}, bf16[32,512]{1,0:T(8,128)(2,1)S(1)}, u32[]{:S(2)}, u32[]{:S(2)}) collective-permute-start(bf16[32,512]{1,0:T(8,128)(2,1)S(1)} %get-tuple-element.143), channel_id=1, source_target_pairs={{0,4},{2,6},{4,8},{6,10},{8,12},{10,14},{5,1},{7,3},{9,5},{11,7},{... | collective-permute-start | bytes 98312 | tf_op jit(solution)/shard_map/ppermute | solution.py:50
  30.0 0.9 collective-permute-done.9.two_ref
  32.3 1.1 %lift.1 = (bf16[512,512]{1,0:T(8,128)(2,1)S(1)}, bf16[128,512]{1,0:T(8,128)(2,1)S(1)}) custom-call(s32[5]{0:T(128)S(1)} %stack.19.me_ref.r_0_, bf16[512,512]{1,0:T(8,128)(2,1)S(1)} %get-tuple-element.124.v_ref.first_ref, bf16[512,128]{1,0:T(8,128)(2,1)S(1)} %get-tuple-element.125.hot_ref.r_2_, bf16[512,128]{1,0:T(8,128)(2,1)S(1)} %get-tuple-element.126.slott_ref.r_3_, ...), custom_call_target="tpu_custom_call" | custom-call | bytes 1966080 | tf_op jit(solution)/shard_map/lift/pallas_call | solution.py:31
  33.4 2.1 %collective-permute-start.12 = (bf16[128,512]{1,0:T(8,128)(2,1)S(1)}, bf16[128,512]{1,0:T(8,128)(2,1)S(1)}, u32[]{:S(2)}, u32[]{:S(2)}) collective-permute-start(bf16[128,512]{1,0:T(8,128)(2,1)S(1)} %get-tuple-element.150), channel_id=1, source_target_pairs={{0,2},{2,4},{4,6},{6,8},{8,10},{10,12},{12,14},{3,1},{5,3},{7,5},{... | collective-permute-start | bytes 393224 | tf_op jit(solution)/shard_map/ppermute | solution.py:50
  35.5 1.1 %cot.1 = (bf16[512,512]{1,0:T(8,128)(2,1)S(1)}, f32[512,512]{1,0:T(8,128)S(1)}) custom-call(s32[5]{0:T(128)S(1)} %stack.19.me_ref.r_0_, bf16[256,512]{1,0:T(8,128)(2,1)S(1)} %copy-done.4, bf16[256,512]{1,0:T(8,128)(2,1)S(1)} %collective-permute-done.13.ct2_ref, bf16[512,512]{1,0:T(8,128)(2,1)S(1)} %get-tuple-element.152.wo_ref), custom_call_target="tpu_custom_call" | custom-call | bytes 2621440 | tf_op jit(solution)/shard_map/cot/pallas_call | solution.py:31
  36.6 2.8 %collective-permute-done.12.rim_ref = bf16[128,512]{1,0:T(8,128)(2,1)S(1)} collective-permute-done((bf16[128,512]{1,0:T(8,128)(2,1)S(1)}, bf16[128,512]{1,0:T(8,128)(2,1)S(1)}, u32[]{:S(2)}, u32[]{:S(2)}) %collective-permute-start.12) | collective-permute-done | bytes 131104 | tf_op jit(solution)/shard_map/ppermute | solution.py:50
  39.4 1.3 %collective-permute-done.14.rim2_ref = bf16[128,512]{1,0:T(8,128)(2,1)S(1)} collective-permute-done((bf16[128,512]{1,0:T(8,128)(2,1)S(1)}, bf16[128,512]{1,0:T(8,128)(2,1)S(1)}, u32[]{:S(2)}, u32[]{:S(2)}) %collective-permute-start.14) | collective-permute-done | bytes 131104 | tf_op jit(solution)/shard_map/ppermute | solution.py:54
  40.7 2.8 %second.1 = (bf16[512,512]{1,0:T(8,128)(2,1)S(1)}, bf16[512,512]{1,0:T(8,128)(2,1)S(1)}, bf16[512,512]{1,0:T(8,128)(2,1)S(1)}, bf16[512,512]{1,0:T(8,128)(2,1)S(...) custom-call(s32[5]{0:T(128)S(1)} %stack.19.me_ref.r_0_, ...), custom_call_target="tpu_custom_call" | custom-call | bytes 7995392 | tf_op jit(solution)/shard_map/second/pallas_call | solution.py:31
  43.5 2.5 %collective-permute-start.15 = (bf16[128,512]{1,0:T(8,128)(2,1)S(1)}, bf16[128,512]{1,0:T(8,128)(2,1)S(1)}, u32[]{:S(2)}, u32[]{:S(2)}) collective-permute-start(bf16[128,512]{1,0:T(8,128)(2,1)S(1)} %get-tuple-element.158), channel_id=1, source_target_pairs={{0,2},{2,4},{4,6},{6,8},{8,10},{10,12},{12,14},{3,1},{5,3},{7,5},{... | collective-permute-start | bytes 393224 | tf_op jit(solution)/shard_map/ppermute | solution.py:50
  46.0 2.3 %combine.1 = (f32[512,512]{1,0:T(8,128)S(1)}, f32[4,384,128]{2,1,0:T(8,128)S(1)}, bf16[4,384,128]{2,1,0:T(8,128)(2,1)S(1)}) custom-call(s32[5]{0:T(128)S(1)} %stack.19.me_ref.r_0_, bf16[512,512]{1,0:T(8,128)(2,1)S(1)} %get-tuple-element.159.r_1_, bf16[512,512]{1,0:T(8,128)(2,1)S(1)} %get-tuple-element.149.lift_ref.r_2_, ...), custom_call_target="tpu_custom_call" | custom-call | bytes 7208960 | tf_op jit(solution)/shard_map/combine/pallas_call | solution.py:31
  48.3 1.4 %collective-permute-start.23 = (bf16[4,384,128]{2,1,0:T(8,128)(2,1)S(1)}, bf16[4,384,128]{2,1,0:T(8,128)(2,1)S(1)}, u32[]{:S(2)}, u32[]{:S(2)}) collective-permute-start(bf16[4,384,128]{2,1,0:T(8,128)(2,1)S(1)} %get-tuple-element.183), channel_id=1, source_target_pairs={{0,2},{2,0},{1,3},{3,1},{4,6},{6,4},{5,7},{7,5},{8,10},{10,8},{9,1... | collective-permute-start | bytes 1179656 | tf_op jit(solution)/shard_map/ppermute | solution.py:71
  49.8 1.3 %collective-permute-done.15.rim_ref = bf16[128,512]{1,0:T(8,128)(2,1)S(1)} collective-permute-done((bf16[128,512]{1,0:T(8,128)(2,1)S(1)}, bf16[128,512]{1,0:T(8,128)(2,1)S(1)}, u32[]{:S(2)}, u32[]{:S(2)}) %collective-permute-start.15) | collective-permute-done | bytes 131104 | tf_op jit(solution)/shard_map/ppermute | solution.py:50
  51.1 1.3 %collective-permute-done.16.rim2_ref = bf16[128,512]{1,0:T(8,128)(2,1)S(1)} collective-permute-done((bf16[128,512]{1,0:T(8,128)(2,1)S(1)}, bf16[128,512]{1,0:T(8,128)(2,1)S(1)}, u32[]{:S(2)}, u32[]{:S(2)}) %collective-permute-start.16) | collective-permute-done | bytes 131104 | tf_op jit(solution)/shard_map/ppermute | solution.py:54
  52.5 1.3 %lgrad.1 = (bf16[512,512]{1,0:T(8,128)(2,1)S(1)}, bf16[32,512]{1,0:T(8,128)(2,1)S(1)}, bf16[32,512]{1,0:T(8,128)(2,1)S(1)}) custom-call(s32[5]{0:T(128)S(1)} %stack.19.me_ref.r_0_, f32[512,512]{1,0:T(8,128)S(1)} %get-tuple-element.165.comb_ref, bf16[128,512]{1,0:T(8,128)(2,1)S(1)} %collective-permute-done.15.rim_ref, ...), custom_call_target="tpu_custom_call" | custom-call | bytes 2293760 | tf_op jit(solution)/shard_map/lgrad/pallas_call | solution.py:31
  53.7 2.5 %collective-permute-start.17 = (bf16[32,512]{1,0:T(8,128)(2,1)S(1)}, bf16[32,512]{1,0:T(8,128)(2,1)S(1)}, u32[]{:S(2)}, u32[]{:S(2)}) collective-permute-start(bf16[32,512]{1,0:T(8,128)(2,1)S(1)} %get-tuple-element.171), channel_id=1, source_target_pairs={{0,2},{2,4},{4,6},{6,8},{8,10},{10,12},{12,14},{3,1},{5,3},{7,5},{... | collective-permute-start | bytes 98312 | tf_op jit(solution)/shard_map/ppermute | solution.py:50
  56.2 2.3 %collective-permute-start.18 = (bf16[32,512]{1,0:T(8,128)(2,1)S(1)}, bf16[32,512]{1,0:T(8,128)(2,1)S(1)}, u32[]{:S(2)}, u32[]{:S(2)}) collective-permute-start(bf16[32,512]{1,0:T(8,128)(2,1)S(1)} %get-tuple-element.172), channel_id=1, source_target_pairs={{0,4},{2,6},{4,8},{6,10},{8,12},{10,14},{5,1},{7,3},{9,5},{11,7},{... | collective-permute-start | bytes 98312 | tf_op jit(solution)/shard_map/ppermute | solution.py:50
  58.6 1.4 %own_grad.1 = (f32[128,512]{1,0:T(8,128)S(1)}, bf16[256,512]{1,0:T(8,128)(2,1)}) custom-call(s32[5]{0:T(128)S(1)} %stack.19.me_ref.r_0_, bf16[128,512]{1,0:T(8,128)(2,1)S(1)} %get-tuple-element.112.hott_ref, bf16[512,512]{1,0:T(8,128)(2,1)S(1)} %get-tuple-element.168.lg_ref.r_1_, bf16[512,512]{1,0:T(8,128)(2,1)S(1)} %get-tuple-element.169.new_ref), custom_call_target="tpu_custom_call" | custom-call | bytes 1703936 | tf_op jit(solution)/shard_map/own_grad/pallas_call | solution.py:31
  61.5 1.1 %cgrad.1 = (bf16[128,512]{1,0:T(8,128)(2,1)S(1)}, bf16[128,512]{1,0:T(8,128)(2,1)S(1)}, bf16[32,512]{1,0:T(8,128)(2,1)S(1)}, bf16[32,512]{1,0:T(8,128)(2,1)S(1)}) custom-call(s32[5]{0:T(128)S(1)} %stack.19.me_ref.r_0_, f32[128,512]{1,0:T(8,128)S(1)} %get-tuple-element.174.pool_ref, bf16[32,512]{1,0:T(8,128)(2,1)S(1)} %collective-permute-done.17.one_ref, ...), custom_call_target="tpu_custom_call" | custom-call | bytes 1638400 | tf_op jit(solution)/shard_map/cgrad/pallas_call | solution.py:31
  62.6 1.4 %collective-permute-start.21 = (bf16[32,512]{1,0:T(8,128)(2,1)S(1)}, bf16[32,512]{1,0:T(8,128)(2,1)S(1)}, u32[]{:S(2)}, u32[]{:S(2)}) collective-permute-start(bf16[32,512]{1,0:T(8,128)(2,1)S(1)} %get-tuple-element.181), channel_id=1, source_target_pairs={{0,2},{2,4},{4,6},{6,8},{8,10},{10,12},{12,14},{3,1},{5,3},{7,5},{... | collective-permute-start | bytes 98312 | tf_op jit(solution)/shard_map/ppermute | solution.py:50
  64.0 2.3 %collective-permute-start.22 = (bf16[32,512]{1,0:T(8,128)(2,1)S(1)}, bf16[32,512]{1,0:T(8,128)(2,1)S(1)}, u32[]{:S(2)}, u32[]{:S(2)}) collective-permute-start(bf16[32,512]{1,0:T(8,128)(2,1)S(1)} %get-tuple-element.182), channel_id=1, source_target_pairs={{0,4},{2,6},{4,8},{6,10},{8,12},{10,14},{5,1},{7,3},{9,5},{11,7},{... | collective-permute-start | bytes 98312 | tf_op jit(solution)/shard_map/ppermute | solution.py:50
  66.3 1.0 %cweight.1 = (f32[4,128,128]{2,1,0:T(8,128)S(1)}, bf16[4,128,128]{2,1,0:T(8,128)(2,1)S(1)}) custom-call(s32[5]{0:T(128)S(1)} %stack.19.me_ref.r_0_, bf16[128,512]{1,0:T(8,128)(2,1)S(1)} %get-tuple-element.189.r_1_, bf16[128,512]{1,0:T(8,128)(2,1)S(1)} %get-tuple-element.190.r_2_), custom_call_target="tpu_custom_call" | custom-call | bytes 655360 | tf_op jit(solution)/shard_map/cweight/pallas_call | solution.py:31
  67.4 1.2 %collective-permute-start.24 = (bf16[4,128,128]{2,1,0:T(8,128)(2,1)S(1)}, bf16[4,128,128]{2,1,0:T(8,128)(2,1)S(1)}, u32[]{:S(2)}, u32[]{:S(2)}) collective-permute-start(bf16[4,128,128]{2,1,0:T(8,128)(2,1)S(1)} %get-tuple-element.199), channel_id=1, source_target_pairs={{0,2},{2,0},{1,3},{3,1},{4,6},{6,4},{5,7},{7,5},{8,10},{10,8},{9,1... | collective-permute-start | bytes 393224 | tf_op jit(solution)/shard_map/ppermute | solution.py:71
  68.6 1.9 %all-gather.2 = bf16[128,512]{1,0:T(8,128)(2,1)S(1)} all-gather(bf16[64,512]{1,0:T(8,128)(2,1)S(1)} %pad_maximum_fusion), channel_id=4, replica_groups=mesh['groups'=2,'curve'=4,'cross'=2,'sub'=2] {'sub'}, dimensions={0}, use_global_device_ids=true | all-gather | bytes 196608 | tf_op jit(solution)/shard_map/all_gather | solution.py:58
  70.5 3.1 %third.1 = (bf16[512,512]{1,0:T(8,128)(2,1)S(1)}, bf16[512,512]{1,0:T(8,128)(2,1)S(1)}, bf16[512,512]{1,0:T(8,128)(2,1)S(1)}, bf16[128,512]{1,0:T(8,128)(2,1)S(1...) custom-call(s32[5]{0:T(128)S(1)} %stack.19.me_ref.r_0_, ...), custom_call_target="tpu_custom_call" | custom-call | bytes 9175040 | tf_op jit(solution)/shard_map/third/pallas_call | solution.py:31
  73.6 1.0 collective-permute-start.29
  74.6 1.1 %collective-permute-start.25 = (bf16[128,512]{1,0:T(8,128)(2,1)S(1)}, bf16[128,512]{1,0:T(8,128)(2,1)S(1)}, u32[]{:S(2)}, u32[]{:S(2)}) collective-permute-start(bf16[128,512]{1,0:T(8,128)(2,1)S(1)} %get-tuple-element.202), channel_id=1, source_target_pairs={{0,2},{2,4},{4,6},{6,8},{8,10},{10,12},{12,14},{3,1},{5,3},{7,5},{... | collective-permute-start | bytes 393224 | tf_op jit(solution)/shard_map/ppermute | solution.py:50
  75.7 1.1 %stage1.1 = (f32[512,128]{1,0:T(8,128)S(1)}, bf16[512,128]{1,0:T(8,128)(2,1)S(1)}, bf16[512,128]{1,0:T(8,128)(2,1)S(1)}, bf16[512,128]{1,0:T(8,128)(2,1)S(1)}, f32[512,256]{1,0:T(8,128)S(1)}) custom-call(s32[5]{0:T(128)S(1)} %stack.19.me_ref.r_0_, bf16[512,512]{1,0:T(8,128)(2,1)S(1)} %get-tuple-element.188.fb_ref, ...), custom_call_target="tpu_custom_call" | custom-call | bytes 6160384 | tf_op jit(solution)/shard_map/stage1/pallas_call | solution.py:31
  76.8 1.7 %collective-permute-start.26 = (bf16[512,128]{1,0:T(8,128)(2,1)S(1)}, bf16[512,128]{1,0:T(8,128)(2,1)S(1)}, u32[]{:S(2)}, u32[]{:S(2)}) collective-permute-start(bf16[512,128]{1,0:T(8,128)(2,1)S(1)} %get-tuple-element.204), channel_id=1, source_target_pairs={{0,4},{4,0},{8,12},{12,8},{1,5},{5,1},{9,13},{13,9},{2,6},{6,2},{1... | collective-permute-start | bytes 393224 | tf_op jit(solution)/shard_map/ppermute | solution.py:75
  78.6 2.6 %collective-permute-start.28 = (bf16[512,128]{1,0:T(8,128)(2,1)S(1)}, bf16[512,128]{1,0:T(8,128)(2,1)S(1)}, u32[]{:S(2)}, u32[]{:S(2)}) collective-permute-start(bf16[512,128]{1,0:T(8,128)(2,1)S(1)} %get-tuple-element.206), channel_id=1, source_target_pairs={{0,12},{4,8},{8,4},{12,0},{1,13},{5,9},{9,5},{13,1},{2,14},{6,10},... | collective-permute-start | bytes 393224 | tf_op jit(solution)/shard_map/ppermute | solution.py:75
  81.2 4.4 %collective-permute-done.29.refs_1_ = bf16[4,384,128]{2,1,0:T(8,128)(2,1)S(1)} collective-permute-done((bf16[4,384,128]{2,1,0:T(8,128)(2,1)S(1)}, bf16[4,384,128]{2,1,0:T(8,128)(2,1)S(1)}, u32[]{:S(2)}, u32[]{:S(2)}) %collective-permute-start.29) | collective-permute-done | bytes 393248 | tf_op jit(solution)/shard_map/ppermute | solution.py:71
  86.3 3.1 %collective-permute-start.30 = (bf16[384,128]{1,0:T(8,128)(2,1)S(1)}, bf16[384,128]{1,0:T(8,128)(2,1)S(1)}, u32[]{:S(2)}, u32[]{:S(2)}) collective-permute-start(bf16[384,128]{1,0:T(8,128)(2,1)S(1)} %get-tuple-element.211), channel_id=1, source_target_pairs={{0,4},{4,0},{8,12},{12,8},{1,5},{5,1},{9,13},{13,9},{2,6},{6,2},{1... | collective-permute-start | bytes 294920 | tf_op jit(solution)/shard_map/ppermute | solution.py:75
  89.5 2.3 %collective-permute-start.32 = (bf16[384,128]{1,0:T(8,128)(2,1)S(1)}, bf16[384,128]{1,0:T(8,128)(2,1)S(1)}, u32[]{:S(2)}, u32[]{:S(2)}) collective-permute-start(bf16[384,128]{1,0:T(8,128)(2,1)S(1)} %get-tuple-element.213), channel_id=1, source_target_pairs={{0,12},{4,8},{8,4},{12,0},{1,13},{5,9},{9,5},{13,1},{2,14},{6,10},... | collective-permute-start | bytes 294920 | tf_op jit(solution)/shard_map/ppermute | solution.py:75
  91.9 2.0 %all-gather.3 = bf16[256,512]{1,0:T(8,128)(2,1)S(1)} all-gather(bf16[128,512]{1,0:T(8,128)(2,1)S(1)} %collective-permute-done.25), channel_id=5, replica_groups=mesh['groups'=2,'curve'=4,'cross'=2,'sub'=2] {'sub'}, dimensions={0}, use_global_device_ids=true | all-gather | bytes 393216 | tf_op jit(solution)/shard_map/all_gather | solution.py:58
  93.9 1.7 %last.1 = (f32[256,512]{1,0:T(8,128)}, f32[256,128]{1,0:T(8,128)S(1)}, f32[64,256]{1,0:T(8,128)S(1)}, f32[64,256]{1,0:T(8,128)}) custom-call(s32[5]{0:T(128)S(1)} %stack.19.me_ref.r_0_, f32[512,256]{1,0:T(8,128)S(1)} %get-tuple-element.201.comb_ref, bf16[2,128,512]{2,1,0:T(8,128)(2,1)S(1)} %bitcast.11, bf16[512,256]{1,0:T(8,128)(2,1)S(1)} %get-tuple-element.167.place_ref, ...), custom_call_target="tpu_custom_call" | custom-call | bytes 2490368 | tf_op jit(solution)/shard_map/last/pallas_call | solution.py:31
  95.6 4.2 %collective-permute-done.31.b_ref = bf16[384,128]{1,0:T(8,128)(2,1)S(1)} collective-permute-done((bf16[384,128]{1,0:T(8,128)(2,1)S(1)}, bf16[384,128]{1,0:T(8,128)(2,1)S(1)}, u32[]{:S(2)}, u32[]{:S(2)}) %collective-permute-start.31) | collective-permute-done | bytes 98336 | tf_op jit(solution)/shard_map/ppermute | solution.py:75
  99.8 0.8 late.1
  (60 shorter events, 8.9 us)
Async XLA Ops:
  0.6 10.5 %collective-permute-start.1 = (bf16[2,256,1024]{2,1,0:T(8,128)(2,1)}, bf16[2,256,1024]{2,1,0:T(8,128)(2,1)S(1)}, u32[]{:S(2)}, u32[]{:S(2)}) collective-permute-start(bf16[2,256,1024]{2,1,0:T(8,128)(2,1)} %r_1_.3), channel_id=1, source_target_pairs={{0,1},{1,0},{2,3},{3,2},{4,5},{5,4},{6,7},{7,6},{8,9},{9,8},{10,11... | collective-permute-start | bytes 3145736 | tf_op jit(solution)/shard_map/ppermute | solution.py:54
  1.1 10.0 %collective-permute-start.2 = (bf16[2,256,512]{2,1,0:T(8,128)(2,1)}, bf16[2,256,512]{2,1,0:T(8,128)(2,1)S(1)}, u32[]{:S(2)}, u32[]{:S(2)}) collective-permute-start(bf16[2,256,512]{2,1,0:T(8,128)(2,1)} %r_2_.3), channel_id=1, source_target_pairs={{0,1},{1,0},{2,3},{3,2},{4,5},{5,4},{6,7},{7,6},{8,9},{9,8},{10,11... | collective-permute-start | bytes 1572872 | tf_op jit(solution)/shard_map/ppermute | solution.py:54
  1.2 3.5 %copy-start.5 = (s32[1,2,128]{2,1,0:T(2,128)S(1)}, s32[1,2,128]{2,1,0:T(2,128)}, u32[]{:S(2)}) copy-start(s32[1,2,128]{2,1,0:T(2,128)} %param.15) | copy-start | bytes 3076
  1.3 9.9 %copy-start = (bf16[2,256,1024]{2,1,0:T(8,128)(2,1)S(1)}, bf16[2,256,1024]{2,1,0:T(8,128)(2,1)}, u32[]{:S(2)}) copy-start(bf16[2,256,1024]{2,1,0:T(8,128)(2,1)} %r_1_.3) | copy-start | bytes 3145732
  4.8 3.9 %copy-start.6 = (s32[4,3]{1,0:T(4,128)S(1)}, s32[4,3]{1,0:T(4,128)}, u32[]{:S(2)}) copy-start(s32[4,3]{1,0:T(4,128)} %tile_ref.1) | copy-start | bytes 148
  4.8 3.9 %copy-start.7 = (s32[512]{0:T(512)S(1)}, s32[512]{0:T(512)}, u32[]{:S(2)}) copy-start(s32[512]{0:T(512)} %param.16) | copy-start | bytes 6148
  5.7 5.5 %copy-start.1 = (bf16[2,256,512]{2,1,0:T(8,128)(2,1)S(1)}, bf16[2,256,512]{2,1,0:T(8,128)(2,1)}, u32[]{:S(2)}) copy-start(bf16[2,256,512]{2,1,0:T(8,128)(2,1)} %r_2_.3) | copy-start | bytes 1572868
  5.7 6.8 %collective-permute-start = (bf16[128,512]{1,0:T(8,128)(2,1)S(1)}, bf16[128,512]{1,0:T(8,128)(2,1)S(1)}, u32[]{:S(2)}, u32[]{:S(2)}) collective-permute-start(bf16[128,512]{1,0:T(8,128)(2,1)S(1)} %get-tuple-element.114), channel_id=1, source_target_pairs={{0,2},{2,4},{4,6},{6,8},{8,10},{10,12},{12,14},{3,1},{5,3},{7,5},{... | collective-permute-start | bytes 393224 | tf_op jit(solution)/shard_map/ppermute | solution.py:50
  8.7 1.1 %copy-start.2 = (s32[4,3,128,128]{3,2,1,0:T(8,128)S(1)}, s32[4,3,128,128]{3,2,1,0:T(8,128)}, u32[]{:S(2)}) copy-start(s32[4,3,128,128]{3,2,1,0:T(8,128)} %mask_ref.1) | copy-start | bytes 2359300
  14.5 2.4 %copy-start.3 = (bf16[256,512]{1,0:T(8,128)(2,1)S(1)}, bf16[256,512]{1,0:T(8,128)(2,1)}, u32[]{:S(2)}) copy-start(bf16[256,512]{1,0:T(8,128)(2,1)} %cw_ref) | copy-start | bytes 786436
  16.9 4.3 %collective-permute-start.5 = (bf16[256,512]{1,0:T(8,128)(2,1)S(1)}, bf16[256,512]{1,0:T(8,128)(2,1)S(1)}, u32[]{:S(2)}, u32[]{:S(2)}) collective-permute-start(bf16[256,512]{1,0:T(8,128)(2,1)S(1)} %copy-done.3), channel_id=1, source_target_pairs={{0,1},{1,0},{2,3},{3,2},{4,5},{5,4},{6,7},{7,6},{8,9},{9,8},{10,11... | collective-permute-start | bytes 786440 | tf_op jit(solution)/shard_map/ppermute | solution.py:54
  17.1 5.4 %collective-permute-start.3 = (bf16[48,512]{1,0:T(8,128)(2,1)S(1)}, bf16[48,512]{1,0:T(8,128)(2,1)S(1)}, u32[]{:S(2)}, u32[]{:S(2)}) collective-permute-start(bf16[48,512]{1,0:T(8,128)(2,1)S(1)} %get-tuple-element.129), channel_id=1, source_target_pairs={{0,2},{2,4},{4,6},{6,8},{8,10},{10,12},{12,14},{3,1},{5,3},{7,5},{... | collective-permute-start | bytes 147464 | tf_op jit(solution)/shard_map/ppermute | solution.py:50
  19.6 3.3 %collective-permute-start.4 = (bf16[48,512]{1,0:T(8,128)(2,1)S(1)}, bf16[48,512]{1,0:T(8,128)(2,1)S(1)}, u32[]{:S(2)}, u32[]{:S(2)}) collective-permute-start(bf16[48,512]{1,0:T(8,128)(2,1)S(1)} %get-tuple-element.130), channel_id=1, source_target_pairs={{0,4},{2,6},{4,8},{6,10},{8,12},{10,14},{5,1},{7,3},{9,5},{11,7},{... | collective-permute-start | bytes 147464 | tf_op jit(solution)/shard_map/ppermute | solution.py:50
  23.0 1.2 %collective-permute-start.6 = (bf16[48,512]{1,0:T(8,128)(2,1)S(1)}, bf16[48,512]{1,0:T(8,128)(2,1)S(1)}, u32[]{:S(2)}, u32[]{:S(2)}) collective-permute-start(bf16[48,512]{1,0:T(8,128)(2,1)S(1)} %collective-permute-done.3.one_ref), channel_id=1, source_target_pairs={{0,1},{1,0},{2,3},{3,2},{4,5},{5,4},{6,7},{7,6},{8,9},{9,8},{10,11... | collective-permute-start | bytes 147464 | tf_op jit(solution)/shard_map/ppermute | solution.py:54
  23.0 1.4 %collective-permute-start.7 = (bf16[48,512]{1,0:T(8,128)(2,1)S(1)}, bf16[48,512]{1,0:T(8,128)(2,1)S(1)}, u32[]{:S(2)}, u32[]{:S(2)}) collective-permute-start(bf16[48,512]{1,0:T(8,128)(2,1)S(1)} %collective-permute-done.4.two_ref), channel_id=1, source_target_pairs={{0,1},{1,0},{2,3},{3,2},{4,5},{5,4},{6,7},{7,6},{8,9},{9,8},{10,11... | collective-permute-start | bytes 147464 | tf_op jit(solution)/shard_map/ppermute | solution.py:54
  24.4 1.1 %copy-start.4 = (bf16[256,512]{1,0:T(8,128)(2,1)S(1)}, bf16[256,512]{1,0:T(8,128)(2,1)}, u32[]{:S(2)}) copy-start(bf16[256,512]{1,0:T(8,128)(2,1)} %ct_ref) | copy-start | bytes 786436
  25.5 10.0 %collective-permute-start.13 = (bf16[256,512]{1,0:T(8,128)(2,1)S(1)}, bf16[256,512]{1,0:T(8,128)(2,1)S(1)}, u32[]{:S(2)}, u32[]{:S(2)}) collective-permute-start(bf16[256,512]{1,0:T(8,128)(2,1)S(1)} %copy-done.4), channel_id=1, source_target_pairs={{0,1},{1,0},{2,3},{3,2},{4,5},{5,4},{6,7},{7,6},{8,9},{9,8},{10,11... | collective-permute-start | bytes 786440 | tf_op jit(solution)/shard_map/ppermute | solution.py:54
  25.9 4.0 %collective-permute-start.8 = (bf16[32,512]{1,0:T(8,128)(2,1)S(1)}, bf16[32,512]{1,0:T(8,128)(2,1)S(1)}, u32[]{:S(2)}, u32[]{:S(2)}) collective-permute-start(bf16[32,512]{1,0:T(8,128)(2,1)S(1)} %get-tuple-element.142), channel_id=1, source_target_pairs={{0,2},{2,4},{4,6},{6,8},{8,10},{10,12},{12,14},{3,1},{5,3},{7,5},{... | collective-permute-start | bytes 98312 | tf_op jit(solution)/shard_map/ppermute | solution.py:50
  27.2 3.7 %collective-permute-start.9 = (bf16[32,512]{1,0:T(8,128)(2,1)S(1)}, bf16[32,512]{1,0:T(8,128)(2,1)S(1)}, u32[]{:S(2)}, u32[]{:S(2)}) collective-permute-start(bf16[32,512]{1,0:T(8,128)(2,1)S(1)} %get-tuple-element.143), channel_id=1, source_target_pairs={{0,4},{2,6},{4,8},{6,10},{8,12},{10,14},{5,1},{7,3},{9,5},{11,7},{... | collective-permute-start | bytes 98312 | tf_op jit(solution)/shard_map/ppermute | solution.py:50
  30.9 1.2 %collective-permute-start.10 = (bf16[32,512]{1,0:T(8,128)(2,1)S(1)}, bf16[32,512]{1,0:T(8,128)(2,1)S(1)}, u32[]{:S(2)}, u32[]{:S(2)}) collective-permute-start(bf16[32,512]{1,0:T(8,128)(2,1)S(1)} %collective-permute-done.8.one_ref), channel_id=1, source_target_pairs={{0,1},{1,0},{2,3},{3,2},{4,5},{5,4},{6,7},{7,6},{8,9},{9,8},{10,11... | collective-permute-start | bytes 98312 | tf_op jit(solution)/shard_map/ppermute | solution.py:54
  30.9 1.4 %collective-permute-start.11 = (bf16[32,512]{1,0:T(8,128)(2,1)S(1)}, bf16[32,512]{1,0:T(8,128)(2,1)S(1)}, u32[]{:S(2)}, u32[]{:S(2)}) collective-permute-start(bf16[32,512]{1,0:T(8,128)(2,1)S(1)} %collective-permute-done.9.two_ref), channel_id=1, source_target_pairs={{0,1},{1,0},{2,3},{3,2},{4,5},{5,4},{6,7},{7,6},{8,9},{9,8},{10,11... | collective-permute-start | bytes 98312 | tf_op jit(solution)/shard_map/ppermute | solution.py:54
  33.4 5.9 %collective-permute-start.12 = (bf16[128,512]{1,0:T(8,128)(2,1)S(1)}, bf16[128,512]{1,0:T(8,128)(2,1)S(1)}, u32[]{:S(2)}, u32[]{:S(2)}) collective-permute-start(bf16[128,512]{1,0:T(8,128)(2,1)S(1)} %get-tuple-element.150), channel_id=1, source_target_pairs={{0,2},{2,4},{4,6},{6,8},{8,10},{10,12},{12,14},{3,1},{5,3},{7,5},{... | collective-permute-start | bytes 393224 | tf_op jit(solution)/shard_map/ppermute | solution.py:50
  39.4 1.3 %collective-permute-start.14 = (bf16[128,512]{1,0:T(8,128)(2,1)S(1)}, bf16[128,512]{1,0:T(8,128)(2,1)S(1)}, u32[]{:S(2)}, u32[]{:S(2)}) collective-permute-start(bf16[128,512]{1,0:T(8,128)(2,1)S(1)} %collective-permute-done.12.rim_ref), channel_id=1, source_target_pairs={{0,1},{1,0},{2,3},{3,2},{4,5},{5,4},{6,7},{7,6},{8,9},{9,8},{10,11... | collective-permute-start | bytes 393224 | tf_op jit(solution)/shard_map/ppermute | solution.py:54
  43.5 7.6 %collective-permute-start.15 = (bf16[128,512]{1,0:T(8,128)(2,1)S(1)}, bf16[128,512]{1,0:T(8,128)(2,1)S(1)}, u32[]{:S(2)}, u32[]{:S(2)}) collective-permute-start(bf16[128,512]{1,0:T(8,128)(2,1)S(1)} %get-tuple-element.158), channel_id=1, source_target_pairs={{0,2},{2,4},{4,6},{6,8},{8,10},{10,12},{12,14},{3,1},{5,3},{7,5},{... | collective-permute-start | bytes 393224 | tf_op jit(solution)/shard_map/ppermute | solution.py:50
  48.3 22.1 %collective-permute-start.23 = (bf16[4,384,128]{2,1,0:T(8,128)(2,1)S(1)}, bf16[4,384,128]{2,1,0:T(8,128)(2,1)S(1)}, u32[]{:S(2)}, u32[]{:S(2)}) collective-permute-start(bf16[4,384,128]{2,1,0:T(8,128)(2,1)S(1)} %get-tuple-element.183), channel_id=1, source_target_pairs={{0,2},{2,0},{1,3},{3,1},{4,6},{6,4},{5,7},{7,5},{8,10},{10,8},{9,1... | collective-permute-start | bytes 1179656 | tf_op jit(solution)/shard_map/ppermute | solution.py:71
  51.1 1.3 %collective-permute-start.16 = (bf16[128,512]{1,0:T(8,128)(2,1)S(1)}, bf16[128,512]{1,0:T(8,128)(2,1)S(1)}, u32[]{:S(2)}, u32[]{:S(2)}) collective-permute-start(bf16[128,512]{1,0:T(8,128)(2,1)S(1)} %collective-permute-done.15.rim_ref), channel_id=1, source_target_pairs={{0,1},{1,0},{2,3},{3,2},{4,5},{5,4},{6,7},{7,6},{8,9},{9,8},{10,11... | collective-permute-start | bytes 393224 | tf_op jit(solution)/shard_map/ppermute | solution.py:54
  53.7 6.3 %collective-permute-start.17 = (bf16[32,512]{1,0:T(8,128)(2,1)S(1)}, bf16[32,512]{1,0:T(8,128)(2,1)S(1)}, u32[]{:S(2)}, u32[]{:S(2)}) collective-permute-start(bf16[32,512]{1,0:T(8,128)(2,1)S(1)} %get-tuple-element.171), channel_id=1, source_target_pairs={{0,2},{2,4},{4,6},{6,8},{8,10},{10,12},{12,14},{3,1},{5,3},{7,5},{... | collective-permute-start | bytes 98312 | tf_op jit(solution)/shard_map/ppermute | solution.py:50
  56.2 3.9 %collective-permute-start.18 = (bf16[32,512]{1,0:T(8,128)(2,1)S(1)}, bf16[32,512]{1,0:T(8,128)(2,1)S(1)}, u32[]{:S(2)}, u32[]{:S(2)}) collective-permute-start(bf16[32,512]{1,0:T(8,128)(2,1)S(1)} %get-tuple-element.172), channel_id=1, source_target_pairs={{0,4},{2,6},{4,8},{6,10},{8,12},{10,14},{5,1},{7,3},{9,5},{11,7},{... | collective-permute-start | bytes 98312 | tf_op jit(solution)/shard_map/ppermute | solution.py:50
  60.2 1.2 %collective-permute-start.19 = (bf16[32,512]{1,0:T(8,128)(2,1)S(1)}, bf16[32,512]{1,0:T(8,128)(2,1)S(1)}, u32[]{:S(2)}, u32[]{:S(2)}) collective-permute-start(bf16[32,512]{1,0:T(8,128)(2,1)S(1)} %collective-permute-done.17.one_ref), channel_id=1, source_target_pairs={{0,1},{1,0},{2,3},{3,2},{4,5},{5,4},{6,7},{7,6},{8,9},{9,8},{10,11... | collective-permute-start | bytes 98312 | tf_op jit(solution)/shard_map/ppermute | solution.py:54
  60.2 1.4 %collective-permute-start.20 = (bf16[32,512]{1,0:T(8,128)(2,1)S(1)}, bf16[32,512]{1,0:T(8,128)(2,1)S(1)}, u32[]{:S(2)}, u32[]{:S(2)}) collective-permute-start(bf16[32,512]{1,0:T(8,128)(2,1)S(1)} %collective-permute-done.18.two_ref), channel_id=1, source_target_pairs={{0,1},{1,0},{2,3},{3,2},{4,5},{5,4},{6,7},{7,6},{8,9},{9,8},{10,11... | collective-permute-start | bytes 98312 | tf_op jit(solution)/shard_map/ppermute | solution.py:54
  62.6 6.0 %collective-permute-start.21 = (bf16[32,512]{1,0:T(8,128)(2,1)S(1)}, bf16[32,512]{1,0:T(8,128)(2,1)S(1)}, u32[]{:S(2)}, u32[]{:S(2)}) collective-permute-start(bf16[32,512]{1,0:T(8,128)(2,1)S(1)} %get-tuple-element.181), channel_id=1, source_target_pairs={{0,2},{2,4},{4,6},{6,8},{8,10},{10,12},{12,14},{3,1},{5,3},{7,5},{... | collective-permute-start | bytes 98312 | tf_op jit(solution)/shard_map/ppermute | solution.py:50
  64.0 4.5 %collective-permute-start.22 = (bf16[32,512]{1,0:T(8,128)(2,1)S(1)}, bf16[32,512]{1,0:T(8,128)(2,1)S(1)}, u32[]{:S(2)}, u32[]{:S(2)}) collective-permute-start(bf16[32,512]{1,0:T(8,128)(2,1)S(1)} %get-tuple-element.182), channel_id=1, source_target_pairs={{0,4},{2,6},{4,8},{6,10},{8,12},{10,14},{5,1},{7,3},{9,5},{11,7},{... | collective-permute-start | bytes 98312 | tf_op jit(solution)/shard_map/ppermute | solution.py:50
  67.4 6.2 %collective-permute-start.24 = (bf16[4,128,128]{2,1,0:T(8,128)(2,1)S(1)}, bf16[4,128,128]{2,1,0:T(8,128)(2,1)S(1)}, u32[]{:S(2)}, u32[]{:S(2)}) collective-permute-start(bf16[4,128,128]{2,1,0:T(8,128)(2,1)S(1)} %get-tuple-element.199), channel_id=1, source_target_pairs={{0,2},{2,0},{1,3},{3,1},{4,6},{6,4},{5,7},{7,5},{8,10},{10,8},{9,1... | collective-permute-start | bytes 393224 | tf_op jit(solution)/shard_map/ppermute | solution.py:71
  73.6 12.0 %collective-permute-start.29 = (bf16[4,384,128]{2,1,0:T(8,128)(2,1)S(1)}, bf16[4,384,128]{2,1,0:T(8,128)(2,1)S(1)}, u32[]{:S(2)}, u32[]{:S(2)}) collective-permute-start(bf16[4,384,128]{2,1,0:T(8,128)(2,1)S(1)} %get-tuple-element.209), channel_id=1, source_target_pairs={{0,2},{2,0},{1,3},{3,1},{4,6},{6,4},{5,7},{7,5},{8,10},{10,8},{9,1... | collective-permute-start | bytes 1179656 | tf_op jit(solution)/shard_map/ppermute | solution.py:71
  74.6 14.8 %collective-permute-start.25 = (bf16[128,512]{1,0:T(8,128)(2,1)S(1)}, bf16[128,512]{1,0:T(8,128)(2,1)S(1)}, u32[]{:S(2)}, u32[]{:S(2)}) collective-permute-start(bf16[128,512]{1,0:T(8,128)(2,1)S(1)} %get-tuple-element.202), channel_id=1, source_target_pairs={{0,2},{2,4},{4,6},{6,8},{8,10},{10,12},{12,14},{3,1},{5,3},{7,5},{... | collective-permute-start | bytes 393224 | tf_op jit(solution)/shard_map/ppermute | solution.py:50
  76.8 12.7 %collective-permute-start.26 = (bf16[512,128]{1,0:T(8,128)(2,1)S(1)}, bf16[512,128]{1,0:T(8,128)(2,1)S(1)}, u32[]{:S(2)}, u32[]{:S(2)}) collective-permute-start(bf16[512,128]{1,0:T(8,128)(2,1)S(1)} %get-tuple-element.204), channel_id=1, source_target_pairs={{0,4},{4,0},{8,12},{12,8},{1,5},{5,1},{9,13},{13,9},{2,6},{6,2},{1... | collective-permute-start | bytes 393224 | tf_op jit(solution)/shard_map/ppermute | solution.py:75
  78.5 15.3 %collective-permute-start.27 = (bf16[512,128]{1,0:T(8,128)(2,1)S(1)}, bf16[512,128]{1,0:T(8,128)(2,1)S(1)}, u32[]{:S(2)}, u32[]{:S(2)}) collective-permute-start(bf16[512,128]{1,0:T(8,128)(2,1)S(1)} %get-tuple-element.205), channel_id=1, source_target_pairs={{0,8},{4,12},{8,0},{12,4},{1,9},{5,13},{9,1},{13,5},{2,10},{6,14},... | collective-permute-start | bytes 393224 | tf_op jit(solution)/shard_map/ppermute | solution.py:75
  78.6 15.2 %collective-permute-start.28 = (bf16[512,128]{1,0:T(8,128)(2,1)S(1)}, bf16[512,128]{1,0:T(8,128)(2,1)S(1)}, u32[]{:S(2)}, u32[]{:S(2)}) collective-permute-start(bf16[512,128]{1,0:T(8,128)(2,1)S(1)} %get-tuple-element.206), channel_id=1, source_target_pairs={{0,12},{4,8},{8,4},{12,0},{1,13},{5,9},{9,5},{13,1},{2,14},{6,10},... | collective-permute-start | bytes 393224 | tf_op jit(solution)/shard_map/ppermute | solution.py:75
  86.3 9.3 %collective-permute-start.30 = (bf16[384,128]{1,0:T(8,128)(2,1)S(1)}, bf16[384,128]{1,0:T(8,128)(2,1)S(1)}, u32[]{:S(2)}, u32[]{:S(2)}) collective-permute-start(bf16[384,128]{1,0:T(8,128)(2,1)S(1)} %get-tuple-element.211), channel_id=1, source_target_pairs={{0,4},{4,0},{8,12},{12,8},{1,5},{5,1},{9,13},{13,9},{2,6},{6,2},{1... | collective-permute-start | bytes 294920 | tf_op jit(solution)/shard_map/ppermute | solution.py:75
  89.4 10.4 %collective-permute-start.31 = (bf16[384,128]{1,0:T(8,128)(2,1)S(1)}, bf16[384,128]{1,0:T(8,128)(2,1)S(1)}, u32[]{:S(2)}, u32[]{:S(2)}) collective-permute-start(bf16[384,128]{1,0:T(8,128)(2,1)S(1)} %get-tuple-element.212), channel_id=1, source_target_pairs={{0,8},{4,12},{8,0},{12,4},{1,9},{5,13},{9,1},{13,5},{2,10},{6,14},... | collective-permute-start | bytes 294920 | tf_op jit(solution)/shard_map/ppermute | solution.py:75
  89.5 10.3 %collective-permute-start.32 = (bf16[384,128]{1,0:T(8,128)(2,1)S(1)}, bf16[384,128]{1,0:T(8,128)(2,1)S(1)}, u32[]{:S(2)}, u32[]{:S(2)}) collective-permute-start(bf16[384,128]{1,0:T(8,128)(2,1)S(1)} %get-tuple-element.213), channel_id=1, source_target_pairs={{0,12},{4,8},{8,4},{12,0},{1,13},{5,9},{9,5},{13,1},{2,14},{6,10},... | collective-permute-start | bytes 294920 | tf_op jit(solution)/shard_map/ppermute | solution.py:75

commit v7 on v6

--- a/solution.py
+++ b/solution.py
@@ -41,12 +41,13 @@
     )(*scalars, *arrays)
 
 
-def two_way(value, steps):
+def two_way(value, steps, forward=0):
     count = lax.axis_size(DOM)
-    pairs = [(2 * p, 2 * (p + steps)) for p in range(count - steps)]
-    pairs += [(2 * p + 1, 2 * (p - steps) + 1) for p in range(steps, count)]
-    pairs += [(2 * p, 2 * p + 1) for p in range(count - steps, count)]
-    pairs += [(2 * p + 1, 2 * p) for p in range(steps)]
+    back = 1 - forward
+    pairs = [(2 * p + forward, 2 * (p + steps) + forward) for p in range(count - steps)]
+    pairs += [(2 * p + back, 2 * (p - steps) + back) for p in range(steps, count)]
+    pairs += [(2 * p + forward, 2 * p + back) for p in range(count - steps, count)]
+    pairs += [(2 * p + back, 2 * p + forward) for p in range(steps)]
     return lax.ppermute(value, LINE, pairs)
 
 
@@ -94,13 +95,12 @@
     out_ref[:, pl.ds(pl.multiple_of((1 - sub) * half, half), half)] = other_ref[...].T
 
 
-def k_halo(me_ref, rows_ref, x_ref, xc_ref, msg_ref):
-    xc = x_ref[...].T
-    xc_ref[...] = xc
-    row = jnp.where(me_ref[1] == 0, rows_ref[0:1, :], rows_ref[1:2, :])
-    at = lax.broadcasted_iota(I32, (xc.shape[0], row.shape[1]), 0)
-    pick = (at == row).astype(F32).T.astype(BF)
-    msg_ref[...] = dot(pick, xc).astype(BF)
+def k_halo(me_ref, rows_ref, x_ref, a_ref, b_ref):
+    half_x = x_ref[...]
+    for flip, out_ref in enumerate((a_ref, b_ref)):
+        row = jnp.where(me_ref[1] == flip, rows_ref[0:1, :], rows_ref[1:2, :])
+        at = lax.broadcasted_iota(I32, (half_x.shape[1], row.shape[1]), 0)
+        out_ref[...] = dot(half_x, (at == row).astype(F32).astype(BF)).T.astype(BF)
 
 
 def k_weights(layer, me_ref, win_ref, wout_ref, win2_ref, wout2_ref, in_ref, out_ref):
@@ -113,14 +113,15 @@
     out_ref[pl.ds(other, half), :] = wout2_ref[layer]
 
 
-def k_prep(tile_ref, me_ref, mask_ref, rows_ref, par_ref,
+def k_prep(tile_ref, me_ref, mask_ref, rows_ref, par_ref, x_ref, xc_ref,
            adj_ref, adjt_ref, inv_ref, hott_ref, hot_ref, slot_ref, slott_ref,
-           pick_ref, place_ref, tags_ref, ocount_ref):
+           pick_ref, place_ref, tags_ref, ocount_ref, rsel_ref):
     blocks, k_slots, length, _ = mask_ref.shape
     n = adj_ref.shape[0]
     nodes = hott_ref.shape[0]
     slots = slot_ref.shape[0]
     cap = slots // 4
+    xc_ref[...] = x_ref[...].T
     adj_ref[...] = jnp.zeros(adj_ref.shape, BF)
     adjt_ref[...] = jnp.zeros(adjt_ref.shape, BF)
     for b in range(blocks):
@@ -155,6 +156,10 @@
         place = (at == rows_ref[c:c + 1, :]).astype(F32)
         place_ref[:, c * width:(c + 1) * width] = place.astype(BF)
         pick_ref[c * width:(c + 1) * width, :] = place.T.astype(BF)
+    at = pl.multiple_of(me_ref[1] * width, width)
+    sent = dot(slot_ref[...], place_ref[:, pl.ds(at, width)]).astype(BF)
+    for c in range(4):
+        rsel_ref[:, c * width:(c + 1) * width] = sent[c * cap:(c + 1) * cap]
 
 
 def forward(xc, src, adj_ref, inv_ref, win_ref, wo_ref):
@@ -191,10 +196,13 @@
 
 
 def k_first(me_ref, xc_ref, rims_ref, adj_ref, inv_ref, win_ref, wo_ref,
-            slot_ref, tags_ref,
+            slot_ref, tags_ref, rsel_ref,
             agg_ref, pre_ref, hid_ref, first_ref, one_ref, two_ref, src):
     xc = xc_ref[...]
-    fill_sources(me_ref, xc, (rims_ref[0], rims_ref[1]), src)
+    rim = rims_ref.shape[1] // 2
+    before = jnp.concatenate([rims_ref[0, 0:rim], rims_ref[1, rim:]], axis=1)
+    after = jnp.concatenate([rims_ref[0, rim:], rims_ref[1, 0:rim]], axis=1)
+    fill_sources(me_ref, xc, (before, after), src)
     agg, pre, hid, out = forward(xc, src[...], adj_ref, inv_ref, win_ref, wo_ref)
     agg_ref[...] = agg
     pre_ref[...] = pre
@@ -202,8 +210,10 @@
     first_ref[...] = out
     send_slots(me_ref[1], out, slot_ref, one_ref, two_ref)
     cap = slot_ref.shape[0] // 4
-    pad = wide(tags_ref[...], one_ref.shape[1])
-    one_ref[cap:, :] = pad
+    pad = wide(tags_ref[...], two_ref.shape[1])
+    tag_rows = tags_ref.shape[0]
+    one_ref[cap:cap + tag_rows, :] = pad
+    one_ref[cap + tag_rows:, :] = rsel_ref[...]
     two_ref[cap:, :] = pad
 
 
@@ -227,7 +237,7 @@
 
 
 def k_coarse(me_ref, pool_ref, ocount_ref, one_ref, one2_ref, two_ref, two2_ref, cw_ref,
-             hits_ref, icount_ref, coarse_ref, cpre_ref, corr_ref, out1_ref, out2_ref):
+             hits_ref, icount_ref, coarse_ref, cpre_ref, corr_ref, out1_ref, out2_ref, rsb_ref, rsa_ref):
     nodes, width = pool_ref.shape
     cap = out1_ref.shape[0]
     sub = me_ref[1]
@@ -240,6 +250,12 @@
     domain, count = me_ref[0], me_ref[4]
     there = (domain >= 1, domain < count - 1, domain >= 2, domain < count - 2)
     t = [jnp.where(ok, v, 0.0) for ok, v in zip(there, t)]
+    packed = directed(sub, one_ref, one2_ref, slice(one_ref.shape[0] - cap, one_ref.shape[0]))
+    rim = width // 4
+    for ok, value, ref in zip(there, packed, (rsb_ref, rsa_ref)):
+        value = jnp.where(ok, value.astype(F32), 0.0).astype(BF)
+        for c in range(4):
+            ref[c * cap:(c + 1) * cap, :] = value[:, c * rim:(c + 1) * rim]
     tags = jnp.where(lane < cap, t[0], jnp.where(lane < 2 * cap, t[1], jnp.where(lane < 3 * cap, t[2], t[3])))
     node = (lax.broadcasted_iota(I32, (nodes, slots), 0) + 1).astype(F32)
     hits = (node == tags).astype(F32)
@@ -287,9 +303,11 @@
     msg_ref[...] = dot(adjt_ref[pl.ds(at, rim), :], scaled).astype(BF)
 
 
-def k_second(me_ref, lift_ref, rim_ref, rim2_ref, adj_ref, adjt_ref, inv_ref, win_ref, wo_ref, hg_ref,
-             agg_ref, hid_ref, new_ref, pg_ref, scaled_ref, msg_ref, src):
+def k_second(me_ref, lift_ref, rim_ref, rim2_ref, adj_ref, adjt_ref, inv_ref, win_ref, wo_ref, hg_ref, g_ref,
+             slot_ref, rsb_ref, rsa_ref,
+             agg_ref, hid_ref, new_ref, pg_ref, comb_ref, near_ref, one_ref, two_ref, three_ref, src):
     lifted = lift_ref[...]
+    n, width = lifted.shape
     fill_sources(me_ref, lifted, directed(me_ref[1], rim_ref, rim2_ref), src)
     agg, pre, hid, out = forward(lifted, src[...], adj_ref, inv_ref, win_ref, wo_ref)
     agg_ref[...] = agg
@@ -297,23 +315,42 @@
     new_ref[...] = out
     pg = (hg_ref[...] * slope_of(pre)).astype(BF)
     pg_ref[...] = pg
-    rim_grads(me_ref[1], pg, win_ref, inv_ref, adjt_ref, scaled_ref, msg_ref)
-
-
-def k_combine(g_ref, pg_ref, win_ref, scaled_ref, adjt_ref, comb_ref):
-    n, width = comb_ref.shape
-    comb_ref[...] = (
-        g_ref[...].astype(F32)
-        + dot(pg_ref[...], win_ref[:, 0:width])
-        + dot(adjt_ref[0:n, :], scaled_ref[...])
-    )
-
-
-def k_newt(me_ref, hott_ref, lg_ref, new_ref, pool_ref, out_ref):
+    scaled = (dot(pg, win_ref[:, width:]) * wide(inv_ref[...], width)).astype(BF)
+    comb = g_ref[...].astype(F32) + dot(pg, win_ref[:, 0:width]) + dot(adjt_ref[0:n, :], scaled)
+    comb_ref[...] = comb
+    rims = dot(adjt_ref[n:, :], scaled).astype(BF)
+    rim = rims.shape[0] // 2
+    before, after = rims[0:rim], rims[rim:]
+    cap = slot_ref.shape[0] // 4
+    own = dot(slot_ref[...], comb.astype(BF)).astype(BF)
+    of_before, of_after = dot(rsb_ref[...], before), dot(rsa_ref[...], after)
+    near_ref[0:cap, :] = of_before[0:cap]
+    near_ref[cap:, :] = of_after[cap:2 * cap]
+    of_before, of_after = of_before.astype(BF), of_after.astype(BF)
+
+    @pl.when(me_ref[1] == 0)
+    def _():
+        one_ref[0:rim, :] = after
+        one_ref[rim:rim + cap, :] = own[0:cap]
+        one_ref[rim + cap:, :] = of_before[2 * cap:3 * cap]
+        two_ref[0:cap, :] = own[2 * cap:3 * cap]
+        two_ref[cap:, :] = of_after[0:cap]
+        three_ref[...] = of_after[2 * cap:3 * cap]
+
+    @pl.when(me_ref[1] == 1)
+    def _():
+        one_ref[0:rim, :] = before
+        one_ref[rim:rim + cap, :] = own[cap:2 * cap]
+        one_ref[rim + cap:, :] = of_after[3 * cap:]
+        two_ref[0:cap, :] = own[3 * cap:]
+        two_ref[cap:, :] = of_before[cap:2 * cap]
+        three_ref[...] = of_before[3 * cap:]
+
+
+def k_newt(me_ref, new_ref, out_ref):
     half = out_ref.shape[0]
     at = pl.multiple_of(me_ref[1] * half, half)
     out_ref[...] = new_ref[:, pl.ds(at, half)].T
-    pool_ref[...] = dot(hott_ref[...], lg_ref[...])
 
 
 def k_grads(scale, me_ref, pg_ref, h_ref, agg_ref, g_ref, hid_ref, gin_ref, gout_ref):
@@ -366,10 +403,9 @@
                 send_ref[d // 2, rows, :] = value.astype(BF)
 
 
-def k_combine_pack(scale, me_ref, pg_ref, h_ref, agg_ref, g_ref, hid_ref, win_ref, scaled_ref, adjt_ref,
-                   comb_ref, keep_ref, send_ref):
+def k_newt_pack(scale, me_ref, new_ref, pg_ref, h_ref, agg_ref, g_ref, hid_ref, out_ref, keep_ref, send_ref):
     pack_grads(scale, me_ref, pg_ref, h_ref, agg_ref, g_ref, hid_ref, keep_ref, send_ref)
-    k_combine(g_ref, pg_ref, win_ref, scaled_ref, adjt_ref, comb_ref)
+    k_newt(me_ref, new_ref, out_ref)
 
 
 def k_cweight_pack(scale, me_ref, pgrad_ref, coarse_ref, keep_ref, send_ref):
@@ -387,18 +423,33 @@
     return jnp.where(me_ref[0] < me_ref[4] - 1, from_after, 0.0) + jnp.where(me_ref[0] >= 1, from_before, 0.0)
 
 
-def k_lgrad(me_ref, comb_ref, rim_ref, rim2_ref, place_ref, slot_ref, lg_ref, one_ref, two_ref):
-    lg = (comb_ref[...] + placed(me_ref, place_ref, *directed(me_ref[1], rim_ref, rim2_ref))).astype(BF)
+def k_cgrad(me_ref, comb_ref, place_ref, hott_ref, near_ref, one_ref, one2_ref, two_ref, two2_ref,
+            three_ref, three2_ref, hits_ref, icount_ref, cpre_ref, cw_ref,
+            lg_ref, pgrad_ref, spread_ref, out1_ref, out2_ref):
+    cap = out1_ref.shape[0]
+    rim = place_ref.shape[1] // 2
+    sub, domain, count = me_ref[1], me_ref[0], me_ref[4]
+    hits = hits_ref[...]
+    lg = comb_ref[...] + placed(me_ref, place_ref, *directed(sub, one_ref, one2_ref, slice(0, rim)))
+    lg = lg.astype(BF)
     lg_ref[...] = lg
-    send_slots(me_ref[1], lg, slot_ref, one_ref, two_ref)
-
-
-def k_cgrad(me_ref, pool_ref, one_ref, one2_ref, two_ref, two2_ref, hits_ref, icount_ref, cpre_ref, cw_ref,
-            pgrad_ref, spread_ref, out1_ref, out2_ref):
-    cap = out1_ref.shape[0]
-    sub = me_ref[1]
-    hits = hits_ref[...]
-    total = pool_ref[...] + dot(hits.astype(BF), arrived_of(sub, (one_ref, one2_ref, two_ref, two2_ref), cap))
+
+    def pieces(own_ref, other_ref, start, there=None):
+        both = directed(sub, own_ref, other_ref, slice(start, start + cap))
+        both = [v.astype(F32) for v in both]
+        if there is None:
+            return both
+        return [jnp.where(ok, v, 0.0) for ok, v in zip(there, both)]
+
+    near = pieces(one_ref, one2_ref, rim)
+    near_rim = pieces(two_ref, two2_ref, cap, (domain >= 2, domain < count - 2))
+    far = pieces(two_ref, two2_ref, 0)
+    far_rim = pieces(one_ref, one2_ref, rim + cap)
+    far_rim3 = pieces(three_ref, three2_ref, 0, (domain >= 3, domain < count - 3))
+    arrived = [near[c] + near_rim[c] + near_ref[c * cap:(c + 1) * cap, :] for c in range(2)]
+    arrived += [far[c] + far_rim[c] + far_rim3[c] for c in range(2)]
+    arrived = jnp.concatenate(arrived, axis=0).astype(BF)
+    total = dot(hott_ref[...], lg) + dot(hits.astype(BF), arrived)
     pgrad = (total * slope_of(cpre_ref[...])).astype(BF)
     pgrad_ref[...] = pgrad
     spread = (dot(pgrad, cw_ref[...]) * wide(icount_ref[...], pgrad.shape[1])).astype(BF)
@@ -517,27 +568,28 @@
     packed = cross == 2 and curve == 4 and 2 * width == 1024 and hidden == width
 
     cell_bf, cell_f32 = sds((n, width), BF), sds((n, width), F32)
+    rim_a, rim_b = call(k_halo, [sds((rim, half), BF)] * 2, [me], [rows, node_features], "halo")
+    rim_a, rim_b = two_way(rim_a, 1), two_way(rim_b, 1, forward=1)
     win2, wout2 = swap(inward_weight), swap(outward_weight)
     x_full = gather(node_features).reshape(width, n)
-    xc, rims = call(k_halo, [cell_bf, sds((rim, width), BF)], [me], [rows, x_full], "halo")
-    rims = two_way(rims, 1)
-    (adj, adjt, inv, hott, hot, slot, slott, pick, place, tags, ocount) = call(
+    (xc, adj, adjt, inv, hott, hot, slot, slott, pick, place, tags, ocount, rsel) = call(
         k_prep,
-        [sds((n, src_rows), BF), sds((src_rows, n), BF), sds((n, 128), F32), sds((nodes, n), BF),
+        [cell_bf, sds((n, src_rows), BF), sds((src_rows, n), BF), sds((n, 128), F32), sds((nodes, n), BF),
          sds((n, nodes), BF), sds((slots, n), BF), sds((n, slots), BF), sds((2 * rim, n), BF),
-         sds((n, 2 * rim), BF), sds((16, slots), BF), sds((nodes, 128), F32)],
-        [tile_index, me], [tile_mask, rows, parent[None, :]], "prep")
+         sds((n, 2 * rim), BF), sds((16, slots), BF), sds((nodes, 128), F32), sds((cap, width), BF)],
+        [tile_index, me], [tile_mask, rows, parent[None, :], x_full], "prep")
     weight_outs = [sds((hidden, 2 * width), BF), sds((width, hidden), BF)]
     win0, wo0 = call(lambda *r: k_weights(0, *r), weight_outs, [me],
                      [inward_weight, outward_weight, win2, wout2], "weights0")
-    rims, win0, adj = lax.optimization_barrier((rims, win0, adj))
+    rim_a, rim_b, win0, adj = lax.optimization_barrier((rim_a, rim_b, win0, adj))
+    rims = gather(jnp.concatenate([rim_a, rim_b], axis=0))
     msg = sds((cap + 16, width), BF)
     plain = sds((cap, width), BF)
     hid_bf, hid_f32 = sds((n, hidden), BF), sds((n, hidden), F32)
     agg0, pre0, hid0, first, one, two = call(
         k_first,
-        [cell_bf, hid_f32, hid_bf, cell_bf, msg, msg],
-        [me], [xc, gather(rims), adj, inv, win0, wo0, slot, tags], "first",
+        [cell_bf, hid_f32, hid_bf, cell_bf, sds((2 * cap + 16, width), BF), msg],
+        [me], [xc, rims, adj, inv, win0, wo0, slot, tags, rsel], "first",
         flops=2 * n * width * (src_rows + 3 * width),
         scratch=[pltpu.VMEM((src_rows, width), BF)])
     one, two, win2, coarse_weight = lax.optimization_barrier((one, two, win2, coarse_weight))
@@ -550,8 +602,10 @@
     one, two, own = lax.optimization_barrier((one, two, own))
     got = shared(one, two)
     node_bf, node_f32 = sds((nodes, width), BF), sds((nodes, width), F32)
-    hits, icount, coarse, cpre, corr, one, two = call(
-        k_coarse, [sds((nodes, slots), F32), sds((nodes, 128), F32), node_bf, node_f32, node_bf, plain, plain],
+    hits, icount, coarse, cpre, corr, one, two, rsb, rsa = call(
+        k_coarse,
+        [sds((nodes, slots), F32), sds((nodes, 128), F32), node_bf, node_f32, node_bf, plain, plain]
+        + [sds((slots, rim), BF)] * 2,
         [me], [own, ocount, *got, cw], "coarse")
     one, two, cotangent = lax.optimization_barrier((one, two, cotangent))
     one, two = two_way(one, 1), two_way(two, 2)
@@ -563,33 +617,30 @@
         [first, hot, slott, corr, *got, pick], "lift")
     rims, hg1 = lax.optimization_barrier((two_way(rims, 1), hg1))
     rims = shared(rims)
-    agg1, hid1, new, pg1, scaled1, rims = call(
-        k_second, [cell_bf, hid_bf, cell_bf, hid_bf, cell_bf, sds((rim, width), BF)],
-        [me], [lifted, *rims, adj, adjt, inv, win1, wo1, hg1], "second",
+    pair = sds((2 * cap, width), BF)
+    agg1, hid1, new, pg1, comb1, near, one, two, three = call(
+        k_second,
+        [cell_bf, hid_bf, cell_bf, hid_bf, cell_f32, sds((2 * cap, width), F32),
+         sds((rim + 2 * cap, width), BF), pair, plain],
+        [me], [lifted, *rims, adj, adjt, inv, win1, wo1, hg1, ctc, slot, rsb, rsa], "second",
         scratch=[pltpu.VMEM((src_rows, width), BF)])
-    rims = two_way(rims, 1)
+    one, two, three = two_way(one, 1), two_way(two, 2), two_way(three, 3)
     piece = 2 * width // domains
     small = hidden // domains
     layer_rows = half + 2 * small
     pack = [sds((curve, layer_rows, piece), F32), sds((curve, layer_rows, piece), BF)]
     if packed:
-        comb1, keep1, send1 = call(
-            lambda *r: k_combine_pack(scale, *r), [cell_f32] + pack, [me],
-            [pg1, lifted, agg1, ctc, hid1, win1, scaled1, adjt], "combine")
+        new_t, keep1, send1 = call(
+            lambda *r: k_newt_pack(scale, *r), [sds((half, n), BF)] + pack, [me],
+            [new, pg1, lifted, agg1, ctc, hid1], "grads1")
         got1 = cross_swap(send1)
+        one, two, three, keep1 = lax.optimization_barrier((one, two, three, keep1))
     else:
-        comb1, = call(k_combine, [cell_f32], [], [ctc, pg1, win1, scaled1, adjt], "combine")
-    rims, comb1 = lax.optimization_barrier((rims, comb1))
-    rims = shared(rims)
-    lg, one, two = call(
-        k_lgrad, [cell_bf, plain, plain], [me], [comb1, *rims, place, slot], "lgrad")
-    one, two = two_way(one, 1), two_way(two, 2)
-    own_g, new_t = call(k_newt, [node_f32, sds((half, n), BF)], [me], [hott, lg, new], "own_grad")
-    one, two, own_g = lax.optimization_barrier((one, two, own_g))
-    got = shared(one, two)
-    pgrad, spread, one, two = call(
-        k_cgrad, [node_bf, node_bf, plain, plain], [me],
-        [own_g, *got, hits, icount, cpre, cw], "cgrad")
+        new_t, = call(k_newt, [sds((half, n), BF)], [me], [new], "new")
+    got = shared(one, two, three)
+    lg, pgrad, spread, one, two = call(
+        k_cgrad, [cell_bf, node_bf, node_bf, plain, plain], [me],
+        [comb1, place, hott, near, *got, hits, icount, cpre, cw], "cgrad")
     one, two = two_way(one, 1), two_way(two, 2)
     if packed:
         keepc, sendc = call(

time: 101 us -> 95.9 us (0.950)
  waiting for transfers between devices: 20.3 us -> 16.9 us
  Pallas kernels: 27.8 us -> 26.7 us
    ppermute x12 -> x13, waiting for transfers between devices: 6.34 us -> 4.16 us  [two_way(): return lax.ppermute(value, LINE, pairs)]
    pallas_call x20 -> x18, Pallas kernels: 27.8 us -> 26.7 us  [call(): pl.pallas_call(body, out_shape=tuple(outs), in_specs=[pl.BlockSpec(memory...]
    ppermute x12 -> x13, starting transfers between devices: 24.6 us -> 23.6 us  [two_way(): return lax.ppermute(value, LINE, pairs)]
  transfers between devices with their start and end apart: 33 -> 34, of which waited for: 16 -> 10; matrix products, arithmetic and copies ran while one was open for 0% -> 0% of each run, Pallas kernels for 21% -> 20%
where the time goes in v7:
time: 95.9 us; the launch traced here: 95.7 us
  starting transfers between devices  41.1 us (43%)
  Pallas kernels  26.7 us (28%)
  waiting for transfers between devices  16.9 us (18%)
  blocking collectives  8.36 us (9%)
  local copies, waits for them, and re-layouts  1.74 us (2%)
    pallas_call x18, Pallas kernels, call(): pl.pallas_call(body, out_shape=tuple(outs), in_specs=[pl.BlockSpec(memory...  26.7 us
    ppermute x13, starting transfers between devices, two_way(): return lax.ppermute(value, LINE, pairs)  23.6 us
    ppermute x6, starting transfers between devices, curve_swap(): return lax.ppermute(value, 'curve', [(z, z ^ step) for z in range(4)])  11 us
    all_gather x4, blocking collectives, gather(): return lax.all_gather(value, 'sub', axis=0, tiled=False)  8.36 us
    ppermute x6, waiting for transfers between devices, curve_swap(): return lax.ppermute(value, 'curve', [(z, z ^ step) for z in range(4)])  4.38 us
    ppermute x12, waiting for transfers between devices, swap(): return lax.ppermute(value, 'sub', [(0, 1), (1, 0)])  4.29 us
    ppermute x13, waiting for transfers between devices, two_way(): return lax.ppermute(value, LINE, pairs)  4.16 us
    ppermute x3, waiting for transfers between devices, cross_swap(): return lax.ppermute(value, 'cross', [(0, 1), (1, 0)])  4.07 us
  transfers between devices with their start and end apart: 34, of which 10 were waited for; matrix products, arithmetic and copies ran while one was open for 0% of the time, Pallas kernels for 20%

profile of v7, /device:TPU:0, one launch (start us, length us, event | category | flops | bytes accessed | tf_op | source)
XLA Modules:
  0.0 95.7 jit_solution(2277214514978451350)
XLA Ops:
  2.0 0.9 copy-done.2
  3.0 0.9 halo.1
  3.9 3.0 %collective-permute-start = (bf16[128,256]{1,0:T(8,128)(2,1)S(1)}, bf16[128,256]{1,0:T(8,128)(2,1)S(1)}, u32[]{:S(2)}, u32[]{:S(2)}) collective-permute-start(bf16[128,256]{1,0:T(8,128)(2,1)S(1)} %get-tuple-element.116), channel_id=1, source_target_pairs={{0,2},{2,4},{4,6},{6,8},{8,10},{10,12},{12,14},{3,1},{5,3},{7,5},{... | collective-permute-start | bytes 196616 | tf_op jit(solution)/shard_map/ppermute | solution.py:51
  6.8 2.3 %all-gather.x_ref = bf16[512,512]{1,0:T(8,128)(2,1)S(1)} all-gather(bf16[256,512]{1,0:T(8,128)(2,1)S(1)} %copy-done.2), channel_id=2, replica_groups=mesh['groups'=2,'curve'=4,'cross'=2,'sub'=2] {'sub'}, dimensions={0}, use_global_device_ids=true | all-gather | bytes 786432 | tf_op jit(solution)/shard_map/all_gather | solution.py:59
  9.2 1.6 %prep.1 = (bf16[512,512]{1,0:T(8,128)(2,1)S(1)}, bf16[512,768]{1,0:T(8,128)(2,1)S(1)}, bf16[768,512]{1,0:T(8,128)(2,1)S(1)}, f32[512,128]{1,0:T(8,128)S(1)}, bf1...) custom-call(s32[4,3]{1,0:T(4,128)S(1)} %copy-done.7, ...), custom_call_target="tpu_custom_call" | custom-call | bytes 4824064 | tf_op jit(solution)/shard_map/prep/pallas_call | solution.py:31
  11.5 2.0 %all-gather.1 = bf16[512,256]{1,0:T(8,128)(2,1)S(1)} all-gather(bf16[256,256]{1,0:T(8,128)(2,1)S(1)} %pad_maximum_fusion), channel_id=3, replica_groups=mesh['groups'=2,'curve'=4,'cross'=2,'sub'=2] {'sub'}, dimensions={0}, use_global_device_ids=true | all-gather | bytes 393216 | tf_op jit(solution)/shard_map/all_gather | solution.py:59
  13.5 2.4 %first.1 = (bf16[512,512]{1,0:T(8,128)(2,1)S(1)}, f32[512,512]{1,0:T(8,128)S(1)}, bf16[512,512]{1,0:T(8,128)(2,1)S(1)}, bf16[512,512]{1,0:T(8,128)(2,1)S(1)}, bf...) custom-call(s32[5]{0:T(128)S(1)} %stack.19.me_ref.r_0_, bf16[512,512]{1,0:T(8,128)(2,1)S(1)} %get-tuple-element.115.xc_ref.r_11_, ...), custom_call_target="tpu_custom_call" | custom-call | flops 1207959552 | bytes 6328320 | tf_op jit(solution)/shard_map/first/pallas_call | solution.py:31
  16.1 2.2 %collective-permute-start.4 = (bf16[80,512]{1,0:T(8,128)(2,1)S(1)}, bf16[80,512]{1,0:T(8,128)(2,1)S(1)}, u32[]{:S(2)}, u32[]{:S(2)}) collective-permute-start(bf16[80,512]{1,0:T(8,128)(2,1)S(1)} %get-tuple-element.134), channel_id=1, source_target_pairs={{0,2},{2,4},{4,6},{6,8},{8,10},{10,12},{12,14},{3,1},{5,3},{7,5},{... | collective-permute-start | bytes 245768 | tf_op jit(solution)/shard_map/ppermute | solution.py:51
  18.2 1.6 %collective-permute-start.5 = (bf16[48,512]{1,0:T(8,128)(2,1)S(1)}, bf16[48,512]{1,0:T(8,128)(2,1)S(1)}, u32[]{:S(2)}, u32[]{:S(2)}) collective-permute-start(bf16[48,512]{1,0:T(8,128)(2,1)S(1)} %get-tuple-element.135), channel_id=1, source_target_pairs={{0,4},{2,6},{4,8},{6,10},{8,12},{10,14},{5,1},{7,3},{9,5},{11,7},{... | collective-permute-start | bytes 147464 | tf_op jit(solution)/shard_map/ppermute | solution.py:51
  19.8 1.3 %own.1 = (f32[128,512]{1,0:T(8,128)S(1)}, f32[512,512]{1,0:T(8,128)S(1)}, bf16[512,512]{1,0:T(8,128)(2,1)S(1)}) custom-call(s32[5]{0:T(128)S(1)} %stack.19.me_ref.r_0_, bf16[128,512]{1,0:T(8,128)(2,1)S(1)} %get-tuple-element.136.hott_ref, bf16[512,512]{1,0:T(8,128)(2,1)S(1)} %get-tuple-element.129.v_ref.first_ref, ...), custom_call_target="tpu_custom_call" | custom-call | bytes 4063232 | tf_op jit(solution)/shard_map/own/pallas_call | solution.py:31
  22.1 0.9 collective-permute-done.8.two2_ref
  23.0 1.1 %coarse.1 = (f32[128,128]{1,0:T(8,128)S(1)}, f32[128,128]{1,0:T(8,128)S(1)}, bf16[128,512]{1,0:T(8,128)(2,1)S(1)}, f32[128,512]{1,0:T(8,128)S(1)}, bf16[128,512]...) custom-call(s32[5]{0:T(128)S(1)} %stack.19.me_ref.r_0_, ...), custom_call_target="tpu_custom_call" | custom-call | bytes 1900544 | tf_op jit(solution)/shard_map/coarse/pallas_call | solution.py:31
  24.5 2.2 %collective-permute-start.9 = (bf16[32,512]{1,0:T(8,128)(2,1)S(1)}, bf16[32,512]{1,0:T(8,128)(2,1)S(1)}, u32[]{:S(2)}, u32[]{:S(2)}) collective-permute-start(bf16[32,512]{1,0:T(8,128)(2,1)S(1)} %get-tuple-element.148), channel_id=1, source_target_pairs={{0,2},{2,4},{4,6},{6,8},{8,10},{10,12},{12,14},{3,1},{5,3},{7,5},{... | collective-permute-start | bytes 98312 | tf_op jit(solution)/shard_map/ppermute | solution.py:51
  26.7 2.3 %collective-permute-start.10 = (bf16[32,512]{1,0:T(8,128)(2,1)S(1)}, bf16[32,512]{1,0:T(8,128)(2,1)S(1)}, u32[]{:S(2)}, u32[]{:S(2)}) collective-permute-start(bf16[32,512]{1,0:T(8,128)(2,1)S(1)} %get-tuple-element.149), channel_id=1, source_target_pairs={{0,4},{2,6},{4,8},{6,10},{8,12},{10,14},{5,1},{7,3},{9,5},{11,7},{... | collective-permute-start | bytes 98312 | tf_op jit(solution)/shard_map/ppermute | solution.py:51
  29.7 0.9 collective-permute-done.10.two_ref
  31.2 0.7 collective-permute-done.11.one2_ref
  32.0 1.1 %lift.1 = (bf16[512,512]{1,0:T(8,128)(2,1)S(1)}, bf16[128,512]{1,0:T(8,128)(2,1)S(1)}) custom-call(s32[5]{0:T(128)S(1)} %stack.19.me_ref.r_0_, bf16[512,512]{1,0:T(8,128)(2,1)S(1)} %get-tuple-element.129.v_ref.first_ref, bf16[512,128]{1,0:T(8,128)(2,1)S(1)} %get-tuple-element.130.hot_ref.r_2_, bf16[512,128]{1,0:T(8,128)(2,1)S(1)} %get-tuple-element.131.slott_ref.r_3_, ...), custom_call_target="tpu_custom_call" | custom-call | bytes 1966080 | tf_op jit(solution)/shard_map/lift/pallas_call | solution.py:31
  33.2 1.3 %collective-permute-start.13 = (bf16[128,512]{1,0:T(8,128)(2,1)S(1)}, bf16[128,512]{1,0:T(8,128)(2,1)S(1)}, u32[]{:S(2)}, u32[]{:S(2)}) collective-permute-start(bf16[128,512]{1,0:T(8,128)(2,1)S(1)} %get-tuple-element.156), channel_id=1, source_target_pairs={{0,2},{2,4},{4,6},{6,8},{8,10},{10,12},{12,14},{3,1},{5,3},{7,5},{... | collective-permute-start | bytes 393224 | tf_op jit(solution)/shard_map/ppermute | solution.py:51
  34.5 1.1 %cot.1 = (bf16[512,512]{1,0:T(8,128)(2,1)S(1)}, f32[512,512]{1,0:T(8,128)S(1)}) custom-call(s32[5]{0:T(128)S(1)} %stack.19.me_ref.r_0_, bf16[256,512]{1,0:T(8,128)(2,1)S(1)} %copy-done.5, bf16[256,512]{1,0:T(8,128)(2,1)S(1)} %collective-permute-done.14.ct2_ref, bf16[512,512]{1,0:T(8,128)(2,1)S(1)} %get-tuple-element.158.wo_ref), custom_call_target="tpu_custom_call" | custom-call | bytes 2621440 | tf_op jit(solution)/shard_map/cot/pallas_call | solution.py:31
  35.6 2.8 %collective-permute-done.13.rim_ref = bf16[128,512]{1,0:T(8,128)(2,1)S(1)} collective-permute-done((bf16[128,512]{1,0:T(8,128)(2,1)S(1)}, bf16[128,512]{1,0:T(8,128)(2,1)S(1)}, u32[]{:S(2)}, u32[]{:S(2)}) %collective-permute-start.13) | collective-permute-done | bytes 131104 | tf_op jit(solution)/shard_map/ppermute | solution.py:51
  38.4 1.3 %collective-permute-done.15.rim2_ref = bf16[128,512]{1,0:T(8,128)(2,1)S(1)} collective-permute-done((bf16[128,512]{1,0:T(8,128)(2,1)S(1)}, bf16[128,512]{1,0:T(8,128)(2,1)S(1)}, u32[]{:S(2)}, u32[]{:S(2)}) %collective-permute-start.15) | collective-permute-done | bytes 131104 | tf_op jit(solution)/shard_map/ppermute | solution.py:55
  39.7 3.5 %second.1 = (bf16[512,512]{1,0:T(8,128)(2,1)S(1)}, bf16[512,512]{1,0:T(8,128)(2,1)S(1)}, bf16[512,512]{1,0:T(8,128)(2,1)S(1)}, bf16[512,512]{1,0:T(8,128)(2,1)S(...) custom-call(s32[5]{0:T(128)S(1)} %stack.19.me_ref.r_0_, ...), custom_call_target="tpu_custom_call" | custom-call | bytes 9535488 | tf_op jit(solution)/shard_map/second/pallas_call | solution.py:31
  43.3 2.5 %collective-permute-start.16 = (bf16[192,512]{1,0:T(8,128)(2,1)S(1)}, bf16[192,512]{1,0:T(8,128)(2,1)S(1)}, u32[]{:S(2)}, u32[]{:S(2)}) collective-permute-start(bf16[192,512]{1,0:T(8,128)(2,1)S(1)} %get-tuple-element.175), channel_id=1, source_target_pairs={{0,2},{2,4},{4,6},{6,8},{8,10},{10,12},{12,14},{3,1},{5,3},{7,5},{... | collective-permute-start | bytes 589832 | tf_op jit(solution)/shard_map/ppermute | solution.py:51
  45.8 2.3 %collective-permute-start.17 = (bf16[64,512]{1,0:T(8,128)(2,1)S(1)}, bf16[64,512]{1,0:T(8,128)(2,1)S(1)}, u32[]{:S(2)}, u32[]{:S(2)}) collective-permute-start(bf16[64,512]{1,0:T(8,128)(2,1)S(1)} %get-tuple-element.176), channel_id=1, source_target_pairs={{0,4},{2,6},{4,8},{6,10},{8,12},{10,14},{5,1},{7,3},{9,5},{11,7},{... | collective-permute-start | bytes 196616 | tf_op jit(solution)/shard_map/ppermute | solution.py:51
  48.1 1.6 %collective-permute-start.18 = (bf16[32,512]{1,0:T(8,128)(2,1)S(1)}, bf16[32,512]{1,0:T(8,128)(2,1)S(1)}, u32[]{:S(2)}, u32[]{:S(2)}) collective-permute-start(bf16[32,512]{1,0:T(8,128)(2,1)S(1)} %get-tuple-element.177), channel_id=1, source_target_pairs={{0,6},{2,8},{4,10},{6,12},{8,14},{7,1},{9,3},{11,5},{13,7},{15,9},... | collective-permute-start | bytes 98312 | tf_op jit(solution)/shard_map/ppermute | solution.py:51
  49.7 2.4 %grads1.1 = (bf16[256,512]{1,0:T(8,128)(2,1)}, f32[4,384,128]{2,1,0:T(8,128)S(1)}, bf16[4,384,128]{2,1,0:T(8,128)(2,1)S(1)}) custom-call(s32[5]{0:T(128)S(1)} %stack.19.me_ref.r_0_, bf16[512,512]{1,0:T(8,128)(2,1)S(1)} %get-tuple-element.167.r_1_, bf16[512,512]{1,0:T(8,128)(2,1)S(1)} %get-tuple-element.168.r_2_, ...), custom_call_target="tpu_custom_call" | custom-call | bytes 4587520 | tf_op jit(solution)/shard_map/grads1/pallas_call | solution.py:31
  52.2 0.9 collective-permute-start.24
  53.7 1.1 %collective-permute-done.21.three2_ref = bf16[32,512]{1,0:T(8,128)(2,1)S(1)} collective-permute-done((bf16[32,512]{1,0:T(8,128)(2,1)S(1)}, bf16[32,512]{1,0:T(8,128)(2,1)S(1)}, u32[]{:S(2)}, u32[]{:S(2)}) %collective-permute-start.21) | collective-permute-done | bytes 32800 | tf_op jit(solution)/shard_map/ppermute | solution.py:55
  54.8 1.5 %cgrad.1 = (bf16[512,512]{1,0:T(8,128)(2,1)S(1)}, bf16[128,512]{1,0:T(8,128)(2,1)S(1)}, bf16[128,512]{1,0:T(8,128)(2,1)S(1)}, bf16[32,512]{1,0:T(8,128)(2,1)S(1)}, bf16[32,512]{1,0:T(8,128)(2,1)S(1)}) custom-call(s32[5]{0:T(128)S(1)} %stack.19.me_ref.r_0_, f32[512,512]{1,0:T(8,128)S(1)} %get-tuple-element.172.comb_ref, ...), custom_call_target="tpu_custom_call" | custom-call | bytes 3932160 | tf_op jit(solution)/shard_map/cgrad/pallas_call | solution.py:31
  56.4 1.2 %collective-permute-start.22 = (bf16[32,512]{1,0:T(8,128)(2,1)S(1)}, bf16[32,512]{1,0:T(8,128)(2,1)S(1)}, u32[]{:S(2)}, u32[]{:S(2)}) collective-permute-start(bf16[32,512]{1,0:T(8,128)(2,1)S(1)} %get-tuple-element.187), channel_id=1, source_target_pairs={{0,2},{2,4},{4,6},{6,8},{8,10},{10,12},{12,14},{3,1},{5,3},{7,5},{... | collective-permute-start | bytes 98312 | tf_op jit(solution)/shard_map/ppermute | solution.py:51
  57.6 3.0 %collective-permute-start.23 = (bf16[32,512]{1,0:T(8,128)(2,1)S(1)}, bf16[32,512]{1,0:T(8,128)(2,1)S(1)}, u32[]{:S(2)}, u32[]{:S(2)}) collective-permute-start(bf16[32,512]{1,0:T(8,128)(2,1)S(1)} %get-tuple-element.188), channel_id=1, source_target_pairs={{0,4},{2,6},{4,8},{6,10},{8,12},{10,14},{5,1},{7,3},{9,5},{11,7},{... | collective-permute-start | bytes 98312 | tf_op jit(solution)/shard_map/ppermute | solution.py:51
  60.6 1.0 %cweight.1 = (f32[4,128,128]{2,1,0:T(8,128)S(1)}, bf16[4,128,128]{2,1,0:T(8,128)(2,1)S(1)}) custom-call(s32[5]{0:T(128)S(1)} %stack.19.me_ref.r_0_, bf16[128,512]{1,0:T(8,128)(2,1)S(1)} %get-tuple-element.195.r_1_, bf16[128,512]{1,0:T(8,128)(2,1)S(1)} %get-tuple-element.196.r_2_), custom_call_target="tpu_custom_call" | custom-call | bytes 655360 | tf_op jit(solution)/shard_map/cweight/pallas_call | solution.py:31
  61.6 1.1 %collective-permute-start.25 = (bf16[4,128,128]{2,1,0:T(8,128)(2,1)S(1)}, bf16[4,128,128]{2,1,0:T(8,128)(2,1)S(1)}, u32[]{:S(2)}, u32[]{:S(2)}) collective-permute-start(bf16[4,128,128]{2,1,0:T(8,128)(2,1)S(1)} %get-tuple-element.205), channel_id=1, source_target_pairs={{0,2},{2,0},{1,3},{3,1},{4,6},{6,4},{5,7},{7,5},{8,10},{10,8},{9,1... | collective-permute-start | bytes 393224 | tf_op jit(solution)/shard_map/ppermute | solution.py:72
  62.7 2.1 %all-gather.2 = bf16[128,512]{1,0:T(8,128)(2,1)S(1)} all-gather(bf16[64,512]{1,0:T(8,128)(2,1)S(1)} %pad_maximum_fusion.1), channel_id=4, replica_groups=mesh['groups'=2,'curve'=4,'cross'=2,'sub'=2] {'sub'}, dimensions={0}, use_global_device_ids=true | all-gather | bytes 196608 | tf_op jit(solution)/shard_map/all_gather | solution.py:59
  64.8 3.1 %third.1 = (bf16[512,512]{1,0:T(8,128)(2,1)S(1)}, bf16[512,512]{1,0:T(8,128)(2,1)S(1)}, bf16[512,512]{1,0:T(8,128)(2,1)S(1)}, bf16[128,512]{1,0:T(8,128)(2,1)S(1...) custom-call(s32[5]{0:T(128)S(1)} %stack.19.me_ref.r_0_, bf16[512,512]{1,0:T(8,128)(2,1)S(1)} %get-tuple-element.185.r_1_, ...), custom_call_target="tpu_custom_call" | custom-call | bytes 9175040 | tf_op jit(solution)/shard_map/third/pallas_call | solution.py:31
  67.9 1.7 %collective-permute-start.30 = (bf16[4,384,128]{2,1,0:T(8,128)(2,1)S(1)}, bf16[4,384,128]{2,1,0:T(8,128)(2,1)S(1)}, u32[]{:S(2)}, u32[]{:S(2)}) collective-permute-start(bf16[4,384,128]{2,1,0:T(8,128)(2,1)S(1)} %get-tuple-element.215), channel_id=1, source_target_pairs={{0,2},{2,0},{1,3},{3,1},{4,6},{6,4},{5,7},{7,5},{8,10},{10,8},{9,1... | collective-permute-start | bytes 1179656 | tf_op jit(solution)/shard_map/ppermute | solution.py:72
  70.0 1.1 %stage1.1 = (f32[512,128]{1,0:T(8,128)S(1)}, bf16[512,128]{1,0:T(8,128)(2,1)S(1)}, bf16[512,128]{1,0:T(8,128)(2,1)S(1)}, bf16[512,128]{1,0:T(8,128)(2,1)S(1)}, f32[512,256]{1,0:T(8,128)S(1)}) custom-call(s32[5]{0:T(128)S(1)} %stack.19.me_ref.r_0_, bf16[512,512]{1,0:T(8,128)(2,1)S(1)} %get-tuple-element.194.fb_ref, ...), custom_call_target="tpu_custom_call" | custom-call | bytes 6160384 | tf_op jit(solution)/shard_map/stage1/pallas_call | solution.py:31
  71.1 2.1 %collective-permute-start.27 = (bf16[512,128]{1,0:T(8,128)(2,1)S(1)}, bf16[512,128]{1,0:T(8,128)(2,1)S(1)}, u32[]{:S(2)}, u32[]{:S(2)}) collective-permute-start(bf16[512,128]{1,0:T(8,128)(2,1)S(1)} %get-tuple-element.210), channel_id=1, source_target_pairs={{0,4},{4,0},{8,12},{12,8},{1,5},{5,1},{9,13},{13,9},{2,6},{6,2},{1... | collective-permute-start | bytes 393224 | tf_op jit(solution)/shard_map/ppermute | solution.py:76
  73.2 1.3 %collective-permute-start.28 = (bf16[512,128]{1,0:T(8,128)(2,1)S(1)}, bf16[512,128]{1,0:T(8,128)(2,1)S(1)}, u32[]{:S(2)}, u32[]{:S(2)}) collective-permute-start(bf16[512,128]{1,0:T(8,128)(2,1)S(1)} %get-tuple-element.211), channel_id=1, source_target_pairs={{0,8},{4,12},{8,0},{12,4},{1,9},{5,13},{9,1},{13,5},{2,10},{6,14},... | collective-permute-start | bytes 393224 | tf_op jit(solution)/shard_map/ppermute | solution.py:76
  74.5 1.4 %collective-permute-start.29 = (bf16[512,128]{1,0:T(8,128)(2,1)S(1)}, bf16[512,128]{1,0:T(8,128)(2,1)S(1)}, u32[]{:S(2)}, u32[]{:S(2)}) collective-permute-start(bf16[512,128]{1,0:T(8,128)(2,1)S(1)} %get-tuple-element.212), channel_id=1, source_target_pairs={{0,12},{4,8},{8,4},{12,0},{1,13},{5,9},{9,5},{13,1},{2,14},{6,10},... | collective-permute-start | bytes 393224 | tf_op jit(solution)/shard_map/ppermute | solution.py:76
  75.9 4.1 %collective-permute-done.30.refs_1_ = bf16[4,384,128]{2,1,0:T(8,128)(2,1)S(1)} collective-permute-done((bf16[4,384,128]{2,1,0:T(8,128)(2,1)S(1)}, bf16[4,384,128]{2,1,0:T(8,128)(2,1)S(1)}, u32[]{:S(2)}, u32[]{:S(2)}) %collective-permute-start.30) | collective-permute-done | bytes 393248 | tf_op jit(solution)/shard_map/ppermute | solution.py:72
  80.6 3.4 %collective-permute-start.31 = (bf16[384,128]{1,0:T(8,128)(2,1)S(1)}, bf16[384,128]{1,0:T(8,128)(2,1)S(1)}, u32[]{:S(2)}, u32[]{:S(2)}) collective-permute-start(bf16[384,128]{1,0:T(8,128)(2,1)S(1)} %get-tuple-element.217), channel_id=1, source_target_pairs={{0,4},{4,0},{8,12},{12,8},{1,5},{5,1},{9,13},{13,9},{2,6},{6,2},{1... | collective-permute-start | bytes 294920 | tf_op jit(solution)/shard_map/ppermute | solution.py:76
  84.0 1.4 %collective-permute-start.32 = (bf16[384,128]{1,0:T(8,128)(2,1)S(1)}, bf16[384,128]{1,0:T(8,128)(2,1)S(1)}, u32[]{:S(2)}, u32[]{:S(2)}) collective-permute-start(bf16[384,128]{1,0:T(8,128)(2,1)S(1)} %get-tuple-element.218), channel_id=1, source_target_pairs={{0,8},{4,12},{8,0},{12,4},{1,9},{5,13},{9,1},{13,5},{2,10},{6,14},... | collective-permute-start | bytes 294920 | tf_op jit(solution)/shard_map/ppermute | solution.py:76
  85.4 1.4 %collective-permute-start.33 = (bf16[384,128]{1,0:T(8,128)(2,1)S(1)}, bf16[384,128]{1,0:T(8,128)(2,1)S(1)}, u32[]{:S(2)}, u32[]{:S(2)}) collective-permute-start(bf16[384,128]{1,0:T(8,128)(2,1)S(1)} %get-tuple-element.219), channel_id=1, source_target_pairs={{0,12},{4,8},{8,4},{12,0},{1,13},{5,9},{9,5},{13,1},{2,14},{6,10},... | collective-permute-start | bytes 294920 | tf_op jit(solution)/shard_map/ppermute | solution.py:76
  86.8 2.0 %all-gather.3 = bf16[256,512]{1,0:T(8,128)(2,1)S(1)} all-gather(bf16[128,512]{1,0:T(8,128)(2,1)S(1)} %collective-permute-done.26), channel_id=5, replica_groups=mesh['groups'=2,'curve'=4,'cross'=2,'sub'=2] {'sub'}, dimensions={0}, use_global_device_ids=true | all-gather | bytes 393216 | tf_op jit(solution)/shard_map/all_gather | solution.py:59
  88.8 1.7 %last.1 = (f32[256,512]{1,0:T(8,128)}, f32[256,128]{1,0:T(8,128)S(1)}, f32[64,256]{1,0:T(8,128)S(1)}, f32[64,256]{1,0:T(8,128)}) custom-call(s32[5]{0:T(128)S(1)} %stack.19.me_ref.r_0_, f32[512,256]{1,0:T(8,128)S(1)} %get-tuple-element.207.comb_ref, bf16[2,128,512]{2,1,0:T(8,128)(2,1)S(1)} %bitcast.11, bf16[512,256]{1,0:T(8,128)(2,1)S(1)} %get-tuple-element.173.place_ref, ...), custom_call_target="tpu_custom_call" | custom-call | bytes 2490368 | tf_op jit(solution)/shard_map/last/pallas_call | solution.py:31
  90.5 4.4 %collective-permute-done.32.b_ref = bf16[384,128]{1,0:T(8,128)(2,1)S(1)} collective-permute-done((bf16[384,128]{1,0:T(8,128)(2,1)S(1)}, bf16[384,128]{1,0:T(8,128)(2,1)S(1)}, u32[]{:S(2)}, u32[]{:S(2)}) %collective-permute-start.32) | collective-permute-done | bytes 98336 | tf_op jit(solution)/shard_map/ppermute | solution.py:76
  94.9 0.8 late.1
  (63 shorter events, 6.6 us)
Async XLA Ops:
  0.6 10.1 %collective-permute-start.2 = (bf16[2,256,1024]{2,1,0:T(8,128)(2,1)}, bf16[2,256,1024]{2,1,0:T(8,128)(2,1)S(1)}, u32[]{:S(2)}, u32[]{:S(2)}) collective-permute-start(bf16[2,256,1024]{2,1,0:T(8,128)(2,1)} %r_1_.3), channel_id=1, source_target_pairs={{0,1},{1,0},{2,3},{3,2},{4,5},{5,4},{6,7},{7,6},{8,9},{9,8},{10,11... | collective-permute-start | bytes 3145736 | tf_op jit(solution)/shard_map/ppermute | solution.py:55
  1.1 9.6 %collective-permute-start.3 = (bf16[2,256,512]{2,1,0:T(8,128)(2,1)}, bf16[2,256,512]{2,1,0:T(8,128)(2,1)S(1)}, u32[]{:S(2)}, u32[]{:S(2)}) collective-permute-start(bf16[2,256,512]{2,1,0:T(8,128)(2,1)} %r_2_.3), channel_id=1, source_target_pairs={{0,1},{1,0},{2,3},{3,2},{4,5},{5,4},{6,7},{7,6},{8,9},{9,8},{10,11... | collective-permute-start | bytes 1572872 | tf_op jit(solution)/shard_map/ppermute | solution.py:55
  1.3 0.7 copy-start.6
  2.0 0.9 copy-start.2
  2.9 6.2 %copy-start.3 = (s32[4,3,128,128]{3,2,1,0:T(8,128)S(1)}, s32[4,3,128,128]{3,2,1,0:T(8,128)}, u32[]{:S(2)}) copy-start(s32[4,3,128,128]{3,2,1,0:T(8,128)} %mask_ref.1) | copy-start | bytes 2359300
  2.9 6.2 %copy-start.7 = (s32[4,3]{1,0:T(4,128)S(1)}, s32[4,3]{1,0:T(4,128)}, u32[]{:S(2)}) copy-start(s32[4,3]{1,0:T(4,128)} %tile_ref.1) | copy-start | bytes 148
  2.9 6.2 %copy-start.8 = (s32[512]{0:T(512)S(1)}, s32[512]{0:T(512)}, u32[]{:S(2)}) copy-start(s32[512]{0:T(512)} %param.16) | copy-start | bytes 6148
  3.9 7.6 %collective-permute-start = (bf16[128,256]{1,0:T(8,128)(2,1)S(1)}, bf16[128,256]{1,0:T(8,128)(2,1)S(1)}, u32[]{:S(2)}, u32[]{:S(2)}) collective-permute-start(bf16[128,256]{1,0:T(8,128)(2,1)S(1)} %get-tuple-element.116), channel_id=1, source_target_pairs={{0,2},{2,4},{4,6},{6,8},{8,10},{10,12},{12,14},{3,1},{5,3},{7,5},{... | collective-permute-start | bytes 196616 | tf_op jit(solution)/shard_map/ppermute | solution.py:51
  6.8 3.9 %copy-start = (bf16[2,256,1024]{2,1,0:T(8,128)(2,1)S(1)}, bf16[2,256,1024]{2,1,0:T(8,128)(2,1)}, u32[]{:S(2)}) copy-start(bf16[2,256,1024]{2,1,0:T(8,128)(2,1)} %r_1_.3) | copy-start | bytes 3145732
  6.8 4.6 %collective-permute-start.1 = (bf16[128,256]{1,0:T(8,128)(2,1)S(1)}, bf16[128,256]{1,0:T(8,128)(2,1)S(1)}, u32[]{:S(2)}, u32[]{:S(2)}) collective-permute-start(bf16[128,256]{1,0:T(8,128)(2,1)S(1)} %get-tuple-element.117), channel_id=1, source_target_pairs={{1,3},{3,5},{5,7},{7,9},{9,11},{11,13},{13,15},{2,0},{4,2},{6,4},{... | collective-permute-start | bytes 196616 | tf_op jit(solution)/shard_map/ppermute | solution.py:51
  9.1 1.6 %copy-start.1 = (bf16[2,256,512]{2,1,0:T(8,128)(2,1)S(1)}, bf16[2,256,512]{2,1,0:T(8,128)(2,1)}, u32[]{:S(2)}) copy-start(bf16[2,256,512]{2,1,0:T(8,128)(2,1)} %r_2_.3) | copy-start | bytes 1572868
  13.5 2.4 %copy-start.4 = (bf16[256,512]{1,0:T(8,128)(2,1)S(1)}, bf16[256,512]{1,0:T(8,128)(2,1)}, u32[]{:S(2)}) copy-start(bf16[256,512]{1,0:T(8,128)(2,1)} %cw_ref) | copy-start | bytes 786436
  15.9 4.0 %collective-permute-start.6 = (bf16[256,512]{1,0:T(8,128)(2,1)S(1)}, bf16[256,512]{1,0:T(8,128)(2,1)S(1)}, u32[]{:S(2)}, u32[]{:S(2)}) collective-permute-start(bf16[256,512]{1,0:T(8,128)(2,1)S(1)} %copy-done.4), channel_id=1, source_target_pairs={{0,1},{1,0},{2,3},{3,2},{4,5},{5,4},{6,7},{7,6},{8,9},{9,8},{10,11... | collective-permute-start | bytes 786440 | tf_op jit(solution)/shard_map/ppermute | solution.py:55
  16.1 5.5 %collective-permute-start.4 = (bf16[80,512]{1,0:T(8,128)(2,1)S(1)}, bf16[80,512]{1,0:T(8,128)(2,1)S(1)}, u32[]{:S(2)}, u32[]{:S(2)}) collective-permute-start(bf16[80,512]{1,0:T(8,128)(2,1)S(1)} %get-tuple-element.134), channel_id=1, source_target_pairs={{0,2},{2,4},{4,6},{6,8},{8,10},{10,12},{12,14},{3,1},{5,3},{7,5},{... | collective-permute-start | bytes 245768 | tf_op jit(solution)/shard_map/ppermute | solution.py:51
  18.2 3.3 %collective-permute-start.5 = (bf16[48,512]{1,0:T(8,128)(2,1)S(1)}, bf16[48,512]{1,0:T(8,128)(2,1)S(1)}, u32[]{:S(2)}, u32[]{:S(2)}) collective-permute-start(bf16[48,512]{1,0:T(8,128)(2,1)S(1)} %get-tuple-element.135), channel_id=1, source_target_pairs={{0,4},{2,6},{4,8},{6,10},{8,12},{10,14},{5,1},{7,3},{9,5},{11,7},{... | collective-permute-start | bytes 147464 | tf_op jit(solution)/shard_map/ppermute | solution.py:51
  21.6 1.5 %collective-permute-start.7 = (bf16[80,512]{1,0:T(8,128)(2,1)S(1)}, bf16[80,512]{1,0:T(8,128)(2,1)S(1)}, u32[]{:S(2)}, u32[]{:S(2)}) collective-permute-start(bf16[80,512]{1,0:T(8,128)(2,1)S(1)} %collective-permute-done.4.one_ref), channel_id=1, source_target_pairs={{0,1},{1,0},{2,3},{3,2},{4,5},{5,4},{6,7},{7,6},{8,9},{9,8},{10,11... | collective-permute-start | bytes 245768 | tf_op jit(solution)/shard_map/ppermute | solution.py:55
  21.8 1.2 %collective-permute-start.8 = (bf16[48,512]{1,0:T(8,128)(2,1)S(1)}, bf16[48,512]{1,0:T(8,128)(2,1)S(1)}, u32[]{:S(2)}, u32[]{:S(2)}) collective-permute-start(bf16[48,512]{1,0:T(8,128)(2,1)S(1)} %collective-permute-done.5.two_ref), channel_id=1, source_target_pairs={{0,1},{1,0},{2,3},{3,2},{4,5},{5,4},{6,7},{7,6},{8,9},{9,8},{10,11... | collective-permute-start | bytes 147464 | tf_op jit(solution)/shard_map/ppermute | solution.py:55
  23.0 1.2 %copy-start.5 = (bf16[256,512]{1,0:T(8,128)(2,1)S(1)}, bf16[256,512]{1,0:T(8,128)(2,1)}, u32[]{:S(2)}) copy-start(bf16[256,512]{1,0:T(8,128)(2,1)} %ct_ref) | copy-start | bytes 786436
  24.2 10.3 %collective-permute-start.14 = (bf16[256,512]{1,0:T(8,128)(2,1)S(1)}, bf16[256,512]{1,0:T(8,128)(2,1)S(1)}, u32[]{:S(2)}, u32[]{:S(2)}) collective-permute-start(bf16[256,512]{1,0:T(8,128)(2,1)S(1)} %copy-done.5), channel_id=1, source_target_pairs={{0,1},{1,0},{2,3},{3,2},{4,5},{5,4},{6,7},{7,6},{8,9},{9,8},{10,11... | collective-permute-start | bytes 786440 | tf_op jit(solution)/shard_map/ppermute | solution.py:55
  24.5 5.2 %collective-permute-start.9 = (bf16[32,512]{1,0:T(8,128)(2,1)S(1)}, bf16[32,512]{1,0:T(8,128)(2,1)S(1)}, u32[]{:S(2)}, u32[]{:S(2)}) collective-permute-start(bf16[32,512]{1,0:T(8,128)(2,1)S(1)} %get-tuple-element.148), channel_id=1, source_target_pairs={{0,2},{2,4},{4,6},{6,8},{8,10},{10,12},{12,14},{3,1},{5,3},{7,5},{... | collective-permute-start | bytes 98312 | tf_op jit(solution)/shard_map/ppermute | solution.py:51
  26.7 3.9 %collective-permute-start.10 = (bf16[32,512]{1,0:T(8,128)(2,1)S(1)}, bf16[32,512]{1,0:T(8,128)(2,1)S(1)}, u32[]{:S(2)}, u32[]{:S(2)}) collective-permute-start(bf16[32,512]{1,0:T(8,128)(2,1)S(1)} %get-tuple-element.149), channel_id=1, source_target_pairs={{0,4},{2,6},{4,8},{6,10},{8,12},{10,14},{5,1},{7,3},{9,5},{11,7},{... | collective-permute-start | bytes 98312 | tf_op jit(solution)/shard_map/ppermute | solution.py:51
  30.7 1.2 %collective-permute-start.11 = (bf16[32,512]{1,0:T(8,128)(2,1)S(1)}, bf16[32,512]{1,0:T(8,128)(2,1)S(1)}, u32[]{:S(2)}, u32[]{:S(2)}) collective-permute-start(bf16[32,512]{1,0:T(8,128)(2,1)S(1)} %collective-permute-done.9.one_ref), channel_id=1, source_target_pairs={{0,1},{1,0},{2,3},{3,2},{4,5},{5,4},{6,7},{7,6},{8,9},{9,8},{10,11... | collective-permute-start | bytes 98312 | tf_op jit(solution)/shard_map/ppermute | solution.py:55
  30.7 1.4 %collective-permute-start.12 = (bf16[32,512]{1,0:T(8,128)(2,1)S(1)}, bf16[32,512]{1,0:T(8,128)(2,1)S(1)}, u32[]{:S(2)}, u32[]{:S(2)}) collective-permute-start(bf16[32,512]{1,0:T(8,128)(2,1)S(1)} %collective-permute-done.10.two_ref), channel_id=1, source_target_pairs={{0,1},{1,0},{2,3},{3,2},{4,5},{5,4},{6,7},{7,6},{8,9},{9,8},{10,11... | collective-permute-start | bytes 98312 | tf_op jit(solution)/shard_map/ppermute | solution.py:55
  33.2 5.2 %collective-permute-start.13 = (bf16[128,512]{1,0:T(8,128)(2,1)S(1)}, bf16[128,512]{1,0:T(8,128)(2,1)S(1)}, u32[]{:S(2)}, u32[]{:S(2)}) collective-permute-start(bf16[128,512]{1,0:T(8,128)(2,1)S(1)} %get-tuple-element.156), channel_id=1, source_target_pairs={{0,2},{2,4},{4,6},{6,8},{8,10},{10,12},{12,14},{3,1},{5,3},{7,5},{... | collective-permute-start | bytes 393224 | tf_op jit(solution)/shard_map/ppermute | solution.py:51
  38.4 1.3 %collective-permute-start.15 = (bf16[128,512]{1,0:T(8,128)(2,1)S(1)}, bf16[128,512]{1,0:T(8,128)(2,1)S(1)}, u32[]{:S(2)}, u32[]{:S(2)}) collective-permute-start(bf16[128,512]{1,0:T(8,128)(2,1)S(1)} %collective-permute-done.13.rim_ref), channel_id=1, source_target_pairs={{0,1},{1,0},{2,3},{3,2},{4,5},{5,4},{6,7},{7,6},{8,9},{9,8},{10,11... | collective-permute-start | bytes 393224 | tf_op jit(solution)/shard_map/ppermute | solution.py:55
  43.3 9.8 %collective-permute-start.16 = (bf16[192,512]{1,0:T(8,128)(2,1)S(1)}, bf16[192,512]{1,0:T(8,128)(2,1)S(1)}, u32[]{:S(2)}, u32[]{:S(2)}) collective-permute-start(bf16[192,512]{1,0:T(8,128)(2,1)S(1)} %get-tuple-element.175), channel_id=1, source_target_pairs={{0,2},{2,4},{4,6},{6,8},{8,10},{10,12},{12,14},{3,1},{5,3},{7,5},{... | collective-permute-start | bytes 589832 | tf_op jit(solution)/shard_map/ppermute | solution.py:51
  45.8 7.2 %collective-permute-start.17 = (bf16[64,512]{1,0:T(8,128)(2,1)S(1)}, bf16[64,512]{1,0:T(8,128)(2,1)S(1)}, u32[]{:S(2)}, u32[]{:S(2)}) collective-permute-start(bf16[64,512]{1,0:T(8,128)(2,1)S(1)} %get-tuple-element.176), channel_id=1, source_target_pairs={{0,4},{2,6},{4,8},{6,10},{8,12},{10,14},{5,1},{7,3},{9,5},{11,7},{... | collective-permute-start | bytes 196616 | tf_op jit(solution)/shard_map/ppermute | solution.py:51
  48.1 4.9 %collective-permute-start.18 = (bf16[32,512]{1,0:T(8,128)(2,1)S(1)}, bf16[32,512]{1,0:T(8,128)(2,1)S(1)}, u32[]{:S(2)}, u32[]{:S(2)}) collective-permute-start(bf16[32,512]{1,0:T(8,128)(2,1)S(1)} %get-tuple-element.177), channel_id=1, source_target_pairs={{0,6},{2,8},{4,10},{6,12},{8,14},{7,1},{9,3},{11,5},{13,7},{15,9},... | collective-permute-start | bytes 98312 | tf_op jit(solution)/shard_map/ppermute | solution.py:51
  52.2 12.6 %collective-permute-start.24 = (bf16[4,384,128]{2,1,0:T(8,128)(2,1)S(1)}, bf16[4,384,128]{2,1,0:T(8,128)(2,1)S(1)}, u32[]{:S(2)}, u32[]{:S(2)}) collective-permute-start(bf16[4,384,128]{2,1,0:T(8,128)(2,1)S(1)} %get-tuple-element.189), channel_id=1, source_target_pairs={{0,2},{2,0},{1,3},{3,1},{4,6},{6,4},{5,7},{7,5},{8,10},{10,8},{9,1... | collective-permute-start | bytes 1179656 | tf_op jit(solution)/shard_map/ppermute | solution.py:72
  53.0 1.8 %collective-permute-start.19 = (bf16[192,512]{1,0:T(8,128)(2,1)S(1)}, bf16[192,512]{1,0:T(8,128)(2,1)S(1)}, u32[]{:S(2)}, u32[]{:S(2)}) collective-permute-start(bf16[192,512]{1,0:T(8,128)(2,1)S(1)} %collective-permute-done.16.one_ref), channel_id=1, source_target_pairs={{0,1},{1,0},{2,3},{3,2},{4,5},{5,4},{6,7},{7,6},{8,9},{9,8},{10,11... | collective-permute-start | bytes 589832 | tf_op jit(solution)/shard_map/ppermute | solution.py:55
  53.1 1.7 %collective-permute-start.20 = (bf16[64,512]{1,0:T(8,128)(2,1)S(1)}, bf16[64,512]{1,0:T(8,128)(2,1)S(1)}, u32[]{:S(2)}, u32[]{:S(2)}) collective-permute-start(bf16[64,512]{1,0:T(8,128)(2,1)S(1)} %collective-permute-done.17.two_ref), channel_id=1, source_target_pairs={{0,1},{1,0},{2,3},{3,2},{4,5},{5,4},{6,7},{7,6},{8,9},{9,8},{10,11... | collective-permute-start | bytes 196616 | tf_op jit(solution)/shard_map/ppermute | solution.py:55
  53.6 1.2 %collective-permute-start.21 = (bf16[32,512]{1,0:T(8,128)(2,1)S(1)}, bf16[32,512]{1,0:T(8,128)(2,1)S(1)}, u32[]{:S(2)}, u32[]{:S(2)}) collective-permute-start(bf16[32,512]{1,0:T(8,128)(2,1)S(1)} %collective-permute-done.18.three_ref), channel_id=1, source_target_pairs={{0,1},{1,0},{2,3},{3,2},{4,5},{5,4},{6,7},{7,6},{8,9},{9,8},{10,11... | collective-permute-start | bytes 98312 | tf_op jit(solution)/shard_map/ppermute | solution.py:55
  56.4 6.3 %collective-permute-start.22 = (bf16[32,512]{1,0:T(8,128)(2,1)S(1)}, bf16[32,512]{1,0:T(8,128)(2,1)S(1)}, u32[]{:S(2)}, u32[]{:S(2)}) collective-permute-start(bf16[32,512]{1,0:T(8,128)(2,1)S(1)} %get-tuple-element.187), channel_id=1, source_target_pairs={{0,2},{2,4},{4,6},{6,8},{8,10},{10,12},{12,14},{3,1},{5,3},{7,5},{... | collective-permute-start | bytes 98312 | tf_op jit(solution)/shard_map/ppermute | solution.py:51
  57.6 5.1 %collective-permute-start.23 = (bf16[32,512]{1,0:T(8,128)(2,1)S(1)}, bf16[32,512]{1,0:T(8,128)(2,1)S(1)}, u32[]{:S(2)}, u32[]{:S(2)}) collective-permute-start(bf16[32,512]{1,0:T(8,128)(2,1)S(1)} %get-tuple-element.188), channel_id=1, source_target_pairs={{0,4},{2,6},{4,8},{6,10},{8,12},{10,14},{5,1},{7,3},{9,5},{11,7},{... | collective-permute-start | bytes 98312 | tf_op jit(solution)/shard_map/ppermute | solution.py:51
  61.6 6.3 %collective-permute-start.25 = (bf16[4,128,128]{2,1,0:T(8,128)(2,1)S(1)}, bf16[4,128,128]{2,1,0:T(8,128)(2,1)S(1)}, u32[]{:S(2)}, u32[]{:S(2)}) collective-permute-start(bf16[4,128,128]{2,1,0:T(8,128)(2,1)S(1)} %get-tuple-element.205), channel_id=1, source_target_pairs={{0,2},{2,0},{1,3},{3,1},{4,6},{6,4},{5,7},{7,5},{8,10},{10,8},{9,1... | collective-permute-start | bytes 393224 | tf_op jit(solution)/shard_map/ppermute | solution.py:72
  67.9 12.0 %collective-permute-start.30 = (bf16[4,384,128]{2,1,0:T(8,128)(2,1)S(1)}, bf16[4,384,128]{2,1,0:T(8,128)(2,1)S(1)}, u32[]{:S(2)}, u32[]{:S(2)}) collective-permute-start(bf16[4,384,128]{2,1,0:T(8,128)(2,1)S(1)} %get-tuple-element.215), channel_id=1, source_target_pairs={{0,2},{2,0},{1,3},{3,1},{4,6},{6,4},{5,7},{7,5},{8,10},{10,8},{9,1... | collective-permute-start | bytes 1179656 | tf_op jit(solution)/shard_map/ppermute | solution.py:72
  69.7 14.4 %collective-permute-start.26 = (bf16[128,512]{1,0:T(8,128)(2,1)S(1)}, bf16[128,512]{1,0:T(8,128)(2,1)S(1)}, u32[]{:S(2)}, u32[]{:S(2)}) collective-permute-start(bf16[128,512]{1,0:T(8,128)(2,1)S(1)} %get-tuple-element.208), channel_id=1, source_target_pairs={{0,2},{2,4},{4,6},{6,8},{8,10},{10,12},{12,14},{3,1},{5,3},{7,5},{... | collective-permute-start | bytes 393224 | tf_op jit(solution)/shard_map/ppermute | solution.py:51
  71.1 14.3 %collective-permute-start.27 = (bf16[512,128]{1,0:T(8,128)(2,1)S(1)}, bf16[512,128]{1,0:T(8,128)(2,1)S(1)}, u32[]{:S(2)}, u32[]{:S(2)}) collective-permute-start(bf16[512,128]{1,0:T(8,128)(2,1)S(1)} %get-tuple-element.210), channel_id=1, source_target_pairs={{0,4},{4,0},{8,12},{12,8},{1,5},{5,1},{9,13},{13,9},{2,6},{6,2},{1... | collective-permute-start | bytes 393224 | tf_op jit(solution)/shard_map/ppermute | solution.py:76
  73.2 15.6 %collective-permute-start.28 = (bf16[512,128]{1,0:T(8,128)(2,1)S(1)}, bf16[512,128]{1,0:T(8,128)(2,1)S(1)}, u32[]{:S(2)}, u32[]{:S(2)}) collective-permute-start(bf16[512,128]{1,0:T(8,128)(2,1)S(1)} %get-tuple-element.211), channel_id=1, source_target_pairs={{0,8},{4,12},{8,0},{12,4},{1,9},{5,13},{9,1},{13,5},{2,10},{6,14},... | collective-permute-start | bytes 393224 | tf_op jit(solution)/shard_map/ppermute | solution.py:76
  74.5 14.3 %collective-permute-start.29 = (bf16[512,128]{1,0:T(8,128)(2,1)S(1)}, bf16[512,128]{1,0:T(8,128)(2,1)S(1)}, u32[]{:S(2)}, u32[]{:S(2)}) collective-permute-start(bf16[512,128]{1,0:T(8,128)(2,1)S(1)} %get-tuple-element.212), channel_id=1, source_target_pairs={{0,12},{4,8},{8,4},{12,0},{1,13},{5,9},{9,5},{13,1},{2,14},{6,10},... | collective-permute-start | bytes 393224 | tf_op jit(solution)/shard_map/ppermute | solution.py:76
  80.6 10.0 %collective-permute-start.31 = (bf16[384,128]{1,0:T(8,128)(2,1)S(1)}, bf16[384,128]{1,0:T(8,128)(2,1)S(1)}, u32[]{:S(2)}, u32[]{:S(2)}) collective-permute-start(bf16[384,128]{1,0:T(8,128)(2,1)S(1)} %get-tuple-element.217), channel_id=1, source_target_pairs={{0,4},{4,0},{8,12},{12,8},{1,5},{5,1},{9,13},{13,9},{2,6},{6,2},{1... | collective-permute-start | bytes 294920 | tf_op jit(solution)/shard_map/ppermute | solution.py:76
  84.0 10.9 %collective-permute-start.32 = (bf16[384,128]{1,0:T(8,128)(2,1)S(1)}, bf16[384,128]{1,0:T(8,128)(2,1)S(1)}, u32[]{:S(2)}, u32[]{:S(2)}) collective-permute-start(bf16[384,128]{1,0:T(8,128)(2,1)S(1)} %get-tuple-element.218), channel_id=1, source_target_pairs={{0,8},{4,12},{8,0},{12,4},{1,9},{5,13},{9,1},{13,5},{2,10},{6,14},... | collective-permute-start | bytes 294920 | tf_op jit(solution)/shard_map/ppermute | solution.py:76
  85.4 9.5 %collective-permute-start.33 = (bf16[384,128]{1,0:T(8,128)(2,1)S(1)}, bf16[384,128]{1,0:T(8,128)(2,1)S(1)}, u32[]{:S(2)}, u32[]{:S(2)}) collective-permute-start(bf16[384,128]{1,0:T(8,128)(2,1)S(1)} %get-tuple-element.219), channel_id=1, source_target_pairs={{0,12},{4,8},{8,4},{12,0},{1,13},{5,9},{9,5},{13,1},{2,14},{6,10},... | collective-permute-start | bytes 294920 | tf_op jit(solution)/shard_map/ppermute | solution.py:76

commit v8 on v7

--- a/solution.py
+++ b/solution.py
@@ -217,9 +217,14 @@
     two_ref[cap:, :] = pad
 
 
-def k_own(me_ref, hott_ref, v_ref, pre_ref, cw_ref, cw2_ref, pool_ref, slope_ref, cwf_ref):
+def k_own(me_ref, hott_ref, v_ref, pre_ref, cw_ref, cw2_ref, pick_ref, hot_ref,
+          pool_ref, slope_ref, cwf_ref, rim_ref, psel_ref):
     half = cw_ref.shape[0]
     pool_ref[...] = dot(hott_ref[...], v_ref[...])
+    rim = rim_ref.shape[0]
+    pick = pick_ref[pl.ds(pl.multiple_of(me_ref[1] * rim, rim), rim), :]
+    rim_ref[...] = dot(pick, v_ref[...]).astype(BF)
+    psel_ref[...] = dot(pick, hot_ref[...]).astype(BF)
     slope_ref[...] = slope_of(pre_ref[...])
     cwf_ref[pl.ds(pl.multiple_of(me_ref[1] * half, half), half), :] = cw_ref[...]
     cwf_ref[pl.ds(pl.multiple_of((1 - me_ref[1]) * half, half), half), :] = cw2_ref[...]
@@ -236,10 +241,11 @@
     return jnp.concatenate(directed(sub, one, one2, rows) + directed(sub, two, two2, rows), axis=0)
 
 
-def k_coarse(me_ref, pool_ref, ocount_ref, one_ref, one2_ref, two_ref, two2_ref, cw_ref,
-             hits_ref, icount_ref, coarse_ref, cpre_ref, corr_ref, out1_ref, out2_ref, rsb_ref, rsa_ref):
+def k_coarse(me_ref, pool_ref, ocount_ref, one_ref, one2_ref, two_ref, two2_ref, cw_ref, rim_ref, psel_ref,
+             hits_ref, icount_ref, coarse_ref, cpre_ref, corr_ref, near_ref, out1_ref, out2_ref, out3_ref,
+             rsb_ref, rsa_ref):
     nodes, width = pool_ref.shape
-    cap = out1_ref.shape[0]
+    cap = out3_ref.shape[0]
     sub = me_ref[1]
     got = (one_ref, one2_ref, two_ref, two2_ref)
     slots = 4 * cap
@@ -272,25 +278,23 @@
     cpre_ref[...] = cpre
     corr_ref[...] = corr
     ans = dot(hits.T.astype(BF), corr).astype(BF)
-    out1_ref[...] = jnp.where(sub == 0, ans[cap:2 * cap], ans[0:cap])
-    out2_ref[...] = jnp.where(sub == 0, ans[3 * cap:], ans[2 * cap:3 * cap])
+    near_ref[...] = ans[0:2 * cap]
+    rims = (rim_ref[...].astype(F32) + dot(psel_ref[...], corr)).astype(BF)
+    rim_rows = rims.shape[0]
+    out1_ref[0:rim_rows, :] = rims
+    near = jnp.where(sub == 0, ans[cap:2 * cap], ans[0:cap])
+    far = jnp.where(sub == 0, ans[3 * cap:], ans[2 * cap:3 * cap])
+    out1_ref[rim_rows:rim_rows + cap, :] = near
+    out1_ref[rim_rows + cap:, :] = far
+    out2_ref[0:cap, :] = far
+    out2_ref[cap:, :] = near
+    out3_ref[...] = far
 
 
 def spread_back(first, hot_ref, slott_ref, corr, one, two):
     returned = jnp.concatenate([one[1], one[0], two[1], two[0]], axis=0)
     total = first.astype(F32) + dot(hot_ref[...], corr) + dot(slott_ref[...], returned)
     return total.astype(BF)
-
-
-def k_lift(me_ref, first_ref, hot_ref, slott_ref, corr_ref, one_ref, one2_ref, two_ref, two2_ref, pick_ref,
-           lift_ref, msg_ref):
-    lifted = spread_back(
-        first_ref[...], hot_ref, slott_ref, corr_ref[...],
-        directed(me_ref[1], one_ref, one2_ref), directed(me_ref[1], two_ref, two2_ref))
-    lift_ref[...] = lifted
-    rim = msg_ref.shape[0]
-    at = pl.multiple_of(me_ref[1] * rim, rim)
-    msg_ref[...] = dot(pick_ref[pl.ds(at, rim), :], lifted).astype(BF)
 
 
 def rim_grads(sub, pg, win_ref, inv_ref, adjt_ref, scaled_ref, msg_ref):
@@ -303,12 +307,29 @@
     msg_ref[...] = dot(adjt_ref[pl.ds(at, rim), :], scaled).astype(BF)
 
 
-def k_second(me_ref, lift_ref, rim_ref, rim2_ref, adj_ref, adjt_ref, inv_ref, win_ref, wo_ref, hg_ref, g_ref,
+def k_second(me_ref, first_ref, hot_ref, slott_ref, corr_ref, ans_ref, aone_ref, aone2_ref, atwo_ref, atwo2_ref,
+             athree_ref, athree2_ref, adj_ref, adjt_ref, inv_ref, win_ref, wo_ref, hg_ref, g_ref,
              slot_ref, rsb_ref, rsa_ref,
-             agg_ref, hid_ref, new_ref, pg_ref, comb_ref, near_ref, one_ref, two_ref, three_ref, src):
-    lifted = lift_ref[...]
-    n, width = lifted.shape
-    fill_sources(me_ref, lifted, directed(me_ref[1], rim_ref, rim2_ref), src)
+             lift_ref, agg_ref, hid_ref, new_ref, pg_ref, comb_ref, near_ref, one_ref, two_ref, three_ref, src):
+    n, width = first_ref.shape
+    cap = slot_ref.shape[0] // 4
+    sub = me_ref[1]
+    rim = aone_ref.shape[0] - 2 * cap
+
+    def answers(own_ref, other_ref, start):
+        return directed(sub, own_ref, other_ref, slice(start, start + cap))
+
+    near, far = answers(aone_ref, aone2_ref, rim), answers(atwo_ref, atwo2_ref, 0)
+    lifted = spread_back(first_ref[...], hot_ref, slott_ref, corr_ref[...], near, far)
+    lift_ref[...] = lifted
+    rims = directed(sub, aone_ref, aone2_ref, slice(0, rim))
+    across, near_rim = answers(aone_ref, aone2_ref, rim + cap), answers(atwo_ref, atwo2_ref, cap)
+    far_rim = answers(athree_ref, athree2_ref, 0)
+    of_before = jnp.concatenate([ans_ref[0:cap, :], near_rim[0], across[1], far_rim[0]], axis=0)
+    of_after = jnp.concatenate([near_rim[1], ans_ref[cap:, :], far_rim[1], across[0]], axis=0)
+    before = (rims[0].astype(F32) + dot(rsb_ref[...].astype(F32).T.astype(BF), of_before)).astype(BF)
+    after = (rims[1].astype(F32) + dot(rsa_ref[...].astype(F32).T.astype(BF), of_after)).astype(BF)
+    fill_sources(me_ref, lifted, (before, after), src)
     agg, pre, hid, out = forward(lifted, src[...], adj_ref, inv_ref, win_ref, wo_ref)
     agg_ref[...] = agg
     hid_ref[...] = hid
@@ -319,9 +340,7 @@
     comb = g_ref[...].astype(F32) + dot(pg, win_ref[:, 0:width]) + dot(adjt_ref[0:n, :], scaled)
     comb_ref[...] = comb
     rims = dot(adjt_ref[n:, :], scaled).astype(BF)
-    rim = rims.shape[0] // 2
     before, after = rims[0:rim], rims[rim:]
-    cap = slot_ref.shape[0] // 4
     own = dot(slot_ref[...], comb.astype(BF)).astype(BF)
     of_before, of_after = dot(rsb_ref[...], before), dot(rsa_ref[...], after)
     near_ref[0:cap, :] = of_before[0:cap]
@@ -594,35 +613,31 @@
         scratch=[pltpu.VMEM((src_rows, width), BF)])
     one, two, win2, coarse_weight = lax.optimization_barrier((one, two, win2, coarse_weight))
     one, two = two_way(one, 1), two_way(two, 2)
-    own, slope0, cw = call(
-        k_own, [sds((nodes, width), F32), hid_f32, sds((width, width), BF)], [me],
-        [hott, first, pre0, coarse_weight, swap(coarse_weight)], "own")
+    rim_bf = sds((rim, width), BF)
+    own, slope0, cw, rims, psel = call(
+        k_own, [sds((nodes, width), F32), hid_f32, sds((width, width), BF), rim_bf, sds((rim, nodes), BF)], [me],
+        [hott, first, pre0, coarse_weight, swap(coarse_weight), pick, hot], "own")
     win1, wo1 = call(lambda *r: k_weights(1, *r), weight_outs, [me],
                      [inward_weight, outward_weight, win2, wout2], "weights1")
     one, two, own = lax.optimization_barrier((one, two, own))
     got = shared(one, two)
     node_bf, node_f32 = sds((nodes, width), BF), sds((nodes, width), F32)
-    hits, icount, coarse, cpre, corr, one, two, rsb, rsa = call(
+    pair, rim_msg = sds((2 * cap, width), BF), sds((rim + 2 * cap, width), BF)
+    hits, icount, coarse, cpre, corr, near, one, two, three, rsb, rsa = call(
         k_coarse,
-        [sds((nodes, slots), F32), sds((nodes, 128), F32), node_bf, node_f32, node_bf, plain, plain]
+        [sds((nodes, slots), F32), sds((nodes, 128), F32), node_bf, node_f32, node_bf, pair, rim_msg, pair, plain]
         + [sds((slots, rim), BF)] * 2,
-        [me], [own, ocount, *got, cw], "coarse")
-    one, two, cotangent = lax.optimization_barrier((one, two, cotangent))
-    one, two = two_way(one, 1), two_way(two, 2)
+        [me], [own, ocount, *got, cw, rims, psel], "coarse")
+    one, two, three, cotangent = lax.optimization_barrier((one, two, three, cotangent))
+    one, two, three = two_way(one, 1), two_way(two, 2), two_way(three, 3)
     ctc, hg1 = call(k_cot, [cell_bf, hid_f32], [me], [cotangent, swap(cotangent), wo1], "cot")
-    one, two, win1 = lax.optimization_barrier((one, two, win1))
-    got = shared(one, two)
-    lifted, rims = call(
-        k_lift, [cell_bf, sds((rim, width), BF)], [me],
-        [first, hot, slott, corr, *got, pick], "lift")
-    rims, hg1 = lax.optimization_barrier((two_way(rims, 1), hg1))
-    rims = shared(rims)
-    pair = sds((2 * cap, width), BF)
-    agg1, hid1, new, pg1, comb1, near, one, two, three = call(
+    one, two, three, win1, hg1 = lax.optimization_barrier((one, two, three, win1, hg1))
+    got = shared(one, two, three)
+    lifted, agg1, hid1, new, pg1, comb1, near, one, two, three = call(
         k_second,
-        [cell_bf, hid_bf, cell_bf, hid_bf, cell_f32, sds((2 * cap, width), F32),
-         sds((rim + 2 * cap, width), BF), pair, plain],
-        [me], [lifted, *rims, adj, adjt, inv, win1, wo1, hg1, ctc, slot, rsb, rsa], "second",
+        [cell_bf, cell_bf, hid_bf, cell_bf, hid_bf, cell_f32, sds((2 * cap, width), F32), rim_msg, pair, plain],
+        [me],
+        [first, hot, slott, corr, near, *got, adj, adjt, inv, win1, wo1, hg1, ctc, slot, rsb, rsa], "second",
         scratch=[pltpu.VMEM((src_rows, width), BF)])
     one, two, three = two_way(one, 1), two_way(two, 2), two_way(three, 3)
     piece = 2 * width // domains

time: 95.9 us -> 91 us (0.949)
  waiting for transfers between devices: 16.9 us -> 11.8 us
    ppermute x13, waiting for transfers between devices: 4.16 us -> 0.34 us  [two_way(): return lax.ppermute(value, LINE, pairs)]
    ppermute x13, starting transfers between devices: 23.6 us -> 25.2 us  [two_way(): return lax.ppermute(value, LINE, pairs)]
    ppermute x12, waiting for transfers between devices: 4.29 us -> 3.22 us  [swap(): return lax.ppermute(value, 'sub', [(0, 1), (1, 0)])]
    ppermute x3, starting transfers between devices: 3.66 us -> 2.6 us  [cross_swap(): return lax.ppermute(value, 'cross', [(0, 1), (1, 0)])]
    pallas_call x18 -> x17, Pallas kernels: 26.7 us -> 26.2 us  [call(): pl.pallas_call(body, out_shape=tuple(outs), in_specs=[pl.BlockSpec(memory...]
  transfers between devices with their start and end apart: 34 -> 34, of which waited for: 10 -> 6; matrix products, arithmetic and copies ran while one was open for 0% -> 0% of each run, Pallas kernels for 20% -> 20%
where the time goes in v8:
time: 91 us; the launch traced here: 90.8 us
  starting transfers between devices  41.7 us (46%)
  Pallas kernels  26.2 us (29%)
  waiting for transfers between devices  11.8 us (13%)
  blocking collectives  8.36 us (9%)
  local copies, waits for them, and re-layouts  1.74 us (2%)
  between operations  0.91 us (1%)
    pallas_call x17, Pallas kernels, call(): pl.pallas_call(body, out_shape=tuple(outs), in_specs=[pl.BlockSpec(memory...  26.2 us
    ppermute x13, starting transfers between devices, two_way(): return lax.ppermute(value, LINE, pairs)  25.2 us
    ppermute x6, starting transfers between devices, curve_swap(): return lax.ppermute(value, 'curve', [(z, z ^ step) for z in range(4)])  11 us
    all_gather x4, blocking collectives, gather(): return lax.all_gather(value, 'sub', axis=0, tiled=False)  8.36 us
    ppermute x6, waiting for transfers between devices, curve_swap(): return lax.ppermute(value, 'curve', [(z, z ^ step) for z in range(4)])  4.18 us
    ppermute x3, waiting for transfers between devices, cross_swap(): return lax.ppermute(value, 'cross', [(0, 1), (1, 0)])  4.09 us
    ppermute x12, waiting for transfers between devices, swap(): return lax.ppermute(value, 'sub', [(0, 1), (1, 0)])  3.22 us
    ppermute x12, starting transfers between devices, swap(): return lax.ppermute(value, 'sub', [(0, 1), (1, 0)])  2.97 us
  transfers between devices with their start and end apart: 34, of which 6 were waited for; matrix products, arithmetic and copies ran while one was open for 0% of the time, Pallas kernels for 20%

profile of v8, /device:TPU:0, one launch (start us, length us, event | category | flops | bytes accessed | tf_op | source)
XLA Modules:
  0.0 90.8 jit_solution(9507718228485309532)
XLA Ops:
  1.3 0.7 copy-done.6
  2.0 0.9 %copy-done.2 = bf16[256,512]{1,0:T(8,128)(2,1)S(1)} copy-done((bf16[256,512]{1,0:T(8,128)(2,1)S(1)}, bf16[256,512]{1,0:T(8,128)(2,1)}, u32[]{:S(2)}) %copy-start.2) | copy-done | bytes 262168
  3.0 0.9 halo.1
  3.9 3.0 %collective-permute-start = (bf16[128,256]{1,0:T(8,128)(2,1)S(1)}, bf16[128,256]{1,0:T(8,128)(2,1)S(1)}, u32[]{:S(2)}, u32[]{:S(2)}) collective-permute-start(bf16[128,256]{1,0:T(8,128)(2,1)S(1)} %get-tuple-element.120), channel_id=1, source_target_pairs={{0,2},{2,4},{4,6},{6,8},{8,10},{10,12},{12,14},{3,1},{5,3},{7,5},{... | collective-permute-start | bytes 196616 | tf_op jit(solution)/shard_map/ppermute | solution.py:51
  6.8 2.3 %all-gather.x_ref = bf16[512,512]{1,0:T(8,128)(2,1)S(1)} all-gather(bf16[256,512]{1,0:T(8,128)(2,1)S(1)} %copy-done.2), channel_id=2, replica_groups=mesh['groups'=2,'curve'=4,'cross'=2,'sub'=2] {'sub'}, dimensions={0}, use_global_device_ids=true | all-gather | bytes 786432 | tf_op jit(solution)/shard_map/all_gather | solution.py:59
  9.2 1.6 %prep.1 = (bf16[512,512]{1,0:T(8,128)(2,1)S(1)}, bf16[512,768]{1,0:T(8,128)(2,1)S(1)}, bf16[768,512]{1,0:T(8,128)(2,1)S(1)}, f32[512,128]{1,0:T(8,128)S(1)}, bf1...) custom-call(s32[4,3]{1,0:T(4,128)S(1)} %copy-done.7, ...), custom_call_target="tpu_custom_call" | custom-call | bytes 4824064 | tf_op jit(solution)/shard_map/prep/pallas_call | solution.py:31
  10.8 0.6 weights0.1
  11.5 2.0 %all-gather.1 = bf16[512,256]{1,0:T(8,128)(2,1)S(1)} all-gather(bf16[256,256]{1,0:T(8,128)(2,1)S(1)} %pad_maximum_fusion), channel_id=3, replica_groups=mesh['groups'=2,'curve'=4,'cross'=2,'sub'=2] {'sub'}, dimensions={0}, use_global_device_ids=true | all-gather | bytes 393216 | tf_op jit(solution)/shard_map/all_gather | solution.py:59
  13.5 2.4 %first.1 = (bf16[512,512]{1,0:T(8,128)(2,1)S(1)}, f32[512,512]{1,0:T(8,128)S(1)}, bf16[512,512]{1,0:T(8,128)(2,1)S(1)}, bf16[512,512]{1,0:T(8,128)(2,1)S(1)}, bf...) custom-call(s32[5]{0:T(128)S(1)} %stack.19.me_ref.r_0_, bf16[512,512]{1,0:T(8,128)(2,1)S(1)} %get-tuple-element.119.xc_ref.r_11_, ...), custom_call_target="tpu_custom_call" | custom-call | flops 1207959552 | bytes 6328320 | tf_op jit(solution)/shard_map/first/pallas_call | solution.py:31
  16.1 2.2 %collective-permute-start.4 = (bf16[80,512]{1,0:T(8,128)(2,1)S(1)}, bf16[80,512]{1,0:T(8,128)(2,1)S(1)}, u32[]{:S(2)}, u32[]{:S(2)}) collective-permute-start(bf16[80,512]{1,0:T(8,128)(2,1)S(1)} %get-tuple-element.138), channel_id=1, source_target_pairs={{0,2},{2,4},{4,6},{6,8},{8,10},{10,12},{12,14},{3,1},{5,3},{7,5},{... | collective-permute-start | bytes 245768 | tf_op jit(solution)/shard_map/ppermute | solution.py:51
  18.2 1.6 %collective-permute-start.5 = (bf16[48,512]{1,0:T(8,128)(2,1)S(1)}, bf16[48,512]{1,0:T(8,128)(2,1)S(1)}, u32[]{:S(2)}, u32[]{:S(2)}) collective-permute-start(bf16[48,512]{1,0:T(8,128)(2,1)S(1)} %get-tuple-element.139), channel_id=1, source_target_pairs={{0,4},{2,6},{4,8},{6,10},{8,12},{10,14},{5,1},{7,3},{9,5},{11,7},{... | collective-permute-start | bytes 147464 | tf_op jit(solution)/shard_map/ppermute | solution.py:51
  19.8 1.4 %own.1 = (f32[128,512]{1,0:T(8,128)S(1)}, f32[512,512]{1,0:T(8,128)S(1)}, bf16[512,512]{1,0:T(8,128)(2,1)S(1)}, bf16[128,512]{1,0:T(8,128)(2,1)S(1)}, bf16[128,128]{1,0:T(8,128)(2,1)S(1)}) custom-call(s32[5]{0:T(128)S(1)} %stack.19.me_ref.r_0_, bf16[128,512]{1,0:T(8,128)(2,1)S(1)} %get-tuple-element.140.hott_ref, ...), custom_call_target="tpu_custom_call" | custom-call | bytes 4620288 | tf_op jit(solution)/shard_map/own/pallas_call | solution.py:31
  22.1 0.9 %collective-permute-done.8.two2_ref = bf16[48,512]{1,0:T(8,128)(2,1)S(1)} collective-permute-done((bf16[48,512]{1,0:T(8,128)(2,1)S(1)}, bf16[48,512]{1,0:T(8,128)(2,1)S(1)}, u32[]{:S(2)}, u32[]{:S(2)}) %collective-permute-start.8) | collective-permute-done | bytes 49184 | tf_op jit(solution)/shard_map/ppermute | solution.py:55
  23.0 1.2 %coarse.1 = (f32[128,128]{1,0:T(8,128)S(1)}, f32[128,128]{1,0:T(8,128)S(1)}, bf16[128,512]{1,0:T(8,128)(2,1)S(1)}, f32[128,512]{1,0:T(8,128)S(1)}, bf16[128,512]...) custom-call(s32[5]{0:T(128)S(1)} %stack.19.me_ref.r_0_, ...), custom_call_target="tpu_custom_call" | custom-call | bytes 2359296 | tf_op jit(solution)/shard_map/coarse/pallas_call | solution.py:31
  24.6 2.2 %collective-permute-start.9 = (bf16[192,512]{1,0:T(8,128)(2,1)S(1)}, bf16[192,512]{1,0:T(8,128)(2,1)S(1)}, u32[]{:S(2)}, u32[]{:S(2)}) collective-permute-start(bf16[192,512]{1,0:T(8,128)(2,1)S(1)} %get-tuple-element.157), channel_id=1, source_target_pairs={{0,2},{2,4},{4,6},{6,8},{8,10},{10,12},{12,14},{3,1},{5,3},{7,5},{... | collective-permute-start | bytes 589832 | tf_op jit(solution)/shard_map/ppermute | solution.py:51
  26.8 2.3 %collective-permute-start.10 = (bf16[64,512]{1,0:T(8,128)(2,1)S(1)}, bf16[64,512]{1,0:T(8,128)(2,1)S(1)}, u32[]{:S(2)}, u32[]{:S(2)}) collective-permute-start(bf16[64,512]{1,0:T(8,128)(2,1)S(1)} %get-tuple-element.158), channel_id=1, source_target_pairs={{0,4},{2,6},{4,8},{6,10},{8,12},{10,14},{5,1},{7,3},{9,5},{11,7},{... | collective-permute-start | bytes 196616 | tf_op jit(solution)/shard_map/ppermute | solution.py:51
  29.1 2.3 %collective-permute-start.11 = (bf16[32,512]{1,0:T(8,128)(2,1)S(1)}, bf16[32,512]{1,0:T(8,128)(2,1)S(1)}, u32[]{:S(2)}, u32[]{:S(2)}) collective-permute-start(bf16[32,512]{1,0:T(8,128)(2,1)S(1)} %get-tuple-element.159), channel_id=1, source_target_pairs={{0,6},{2,8},{4,10},{6,12},{8,14},{7,1},{9,3},{11,5},{13,7},{15,9},... | collective-permute-start | bytes 98312 | tf_op jit(solution)/shard_map/ppermute | solution.py:51
  31.4 0.6 weights1.1
  32.0 1.1 %cot.1 = (bf16[512,512]{1,0:T(8,128)(2,1)S(1)}, f32[512,512]{1,0:T(8,128)S(1)}) custom-call(s32[5]{0:T(128)S(1)} %stack.19.me_ref.r_0_, bf16[256,512]{1,0:T(8,128)(2,1)S(1)} %copy-done.4, bf16[256,512]{1,0:T(8,128)(2,1)S(1)} %collective-permute-done.12.ct2_ref, bf16[512,512]{1,0:T(8,128)(2,1)S(1)} %get-tuple-element.163.wo_ref), custom_call_target="tpu_custom_call" | custom-call | bytes 2621440 | tf_op jit(solution)/shard_map/cot/pallas_call | solution.py:31
  33.9 1.1 %collective-permute-done.15.athree2_ref = bf16[32,512]{1,0:T(8,128)(2,1)S(1)} collective-permute-done((bf16[32,512]{1,0:T(8,128)(2,1)S(1)}, bf16[32,512]{1,0:T(8,128)(2,1)S(1)}, u32[]{:S(2)}, u32[]{:S(2)}) %collective-permute-start.15) | collective-permute-done | bytes 32800 | tf_op jit(solution)/shard_map/ppermute | solution.py:55
  35.0 3.9 %second.1 = (bf16[512,512]{1,0:T(8,128)(2,1)S(1)}, bf16[512,512]{1,0:T(8,128)(2,1)S(1)}, bf16[512,512]{1,0:T(8,128)(2,1)S(1)}, bf16[512,512]{1,0:T(8,128)(2,1)S(...) custom-call(s32[5]{0:T(128)S(1)} %stack.19.me_ref.r_0_, ...), custom_call_target="tpu_custom_call" | custom-call | bytes 10846208 | tf_op jit(solution)/shard_map/second/pallas_call | solution.py:31
  38.9 1.7 %collective-permute-start.16 = (bf16[192,512]{1,0:T(8,128)(2,1)S(1)}, bf16[192,512]{1,0:T(8,128)(2,1)S(1)}, u32[]{:S(2)}, u32[]{:S(2)}) collective-permute-start(bf16[192,512]{1,0:T(8,128)(2,1)S(1)} %get-tuple-element.183), channel_id=1, source_target_pairs={{0,2},{2,4},{4,6},{6,8},{8,10},{10,12},{12,14},{3,1},{5,3},{7,5},{... | collective-permute-start | bytes 589832 | tf_op jit(solution)/shard_map/ppermute | solution.py:51
  40.6 2.7 %collective-permute-start.17 = (bf16[64,512]{1,0:T(8,128)(2,1)S(1)}, bf16[64,512]{1,0:T(8,128)(2,1)S(1)}, u32[]{:S(2)}, u32[]{:S(2)}) collective-permute-start(bf16[64,512]{1,0:T(8,128)(2,1)S(1)} %get-tuple-element.184), channel_id=1, source_target_pairs={{0,4},{2,6},{4,8},{6,10},{8,12},{10,14},{5,1},{7,3},{9,5},{11,7},{... | collective-permute-start | bytes 196616 | tf_op jit(solution)/shard_map/ppermute | solution.py:51
  43.3 1.7 %collective-permute-start.18 = (bf16[32,512]{1,0:T(8,128)(2,1)S(1)}, bf16[32,512]{1,0:T(8,128)(2,1)S(1)}, u32[]{:S(2)}, u32[]{:S(2)}) collective-permute-start(bf16[32,512]{1,0:T(8,128)(2,1)S(1)} %get-tuple-element.185), channel_id=1, source_target_pairs={{0,6},{2,8},{4,10},{6,12},{8,14},{7,1},{9,3},{11,5},{13,7},{15,9},... | collective-permute-start | bytes 98312 | tf_op jit(solution)/shard_map/ppermute | solution.py:51
  45.0 2.4 %grads1.1 = (bf16[256,512]{1,0:T(8,128)(2,1)}, f32[4,384,128]{2,1,0:T(8,128)S(1)}, bf16[4,384,128]{2,1,0:T(8,128)(2,1)S(1)}) custom-call(s32[5]{0:T(128)S(1)} %stack.19.me_ref.r_0_, bf16[512,512]{1,0:T(8,128)(2,1)S(1)} %get-tuple-element.174.r_1_, bf16[512,512]{1,0:T(8,128)(2,1)S(1)} %get-tuple-element.175.r_2_, ...), custom_call_target="tpu_custom_call" | custom-call | bytes 4587520 | tf_op jit(solution)/shard_map/grads1/pallas_call | solution.py:31
  48.6 1.1 %collective-permute-done.21.three2_ref = bf16[32,512]{1,0:T(8,128)(2,1)S(1)} collective-permute-done((bf16[32,512]{1,0:T(8,128)(2,1)S(1)}, bf16[32,512]{1,0:T(8,128)(2,1)S(1)}, u32[]{:S(2)}, u32[]{:S(2)}) %collective-permute-start.21) | collective-permute-done | bytes 32800 | tf_op jit(solution)/shard_map/ppermute | solution.py:55
  49.7 1.5 %cgrad.1 = (bf16[512,512]{1,0:T(8,128)(2,1)S(1)}, bf16[128,512]{1,0:T(8,128)(2,1)S(1)}, bf16[128,512]{1,0:T(8,128)(2,1)S(1)}, bf16[32,512]{1,0:T(8,128)(2,1)S(1)}, bf16[32,512]{1,0:T(8,128)(2,1)S(1)}) custom-call(s32[5]{0:T(128)S(1)} %stack.19.me_ref.r_0_, f32[512,512]{1,0:T(8,128)S(1)} %get-tuple-element.180.comb_ref, ...), custom_call_target="tpu_custom_call" | custom-call | bytes 3932160 | tf_op jit(solution)/shard_map/cgrad/pallas_call | solution.py:31
  51.2 1.7 %collective-permute-start.22 = (bf16[32,512]{1,0:T(8,128)(2,1)S(1)}, bf16[32,512]{1,0:T(8,128)(2,1)S(1)}, u32[]{:S(2)}, u32[]{:S(2)}) collective-permute-start(bf16[32,512]{1,0:T(8,128)(2,1)S(1)} %get-tuple-element.195), channel_id=1, source_target_pairs={{0,2},{2,4},{4,6},{6,8},{8,10},{10,12},{12,14},{3,1},{5,3},{7,5},{... | collective-permute-start | bytes 98312 | tf_op jit(solution)/shard_map/ppermute | solution.py:51
  52.9 3.1 %collective-permute-start.23 = (bf16[32,512]{1,0:T(8,128)(2,1)S(1)}, bf16[32,512]{1,0:T(8,128)(2,1)S(1)}, u32[]{:S(2)}, u32[]{:S(2)}) collective-permute-start(bf16[32,512]{1,0:T(8,128)(2,1)S(1)} %get-tuple-element.196), channel_id=1, source_target_pairs={{0,4},{2,6},{4,8},{6,10},{8,12},{10,14},{5,1},{7,3},{9,5},{11,7},{... | collective-permute-start | bytes 98312 | tf_op jit(solution)/shard_map/ppermute | solution.py:51
  56.0 1.0 %cweight.1 = (f32[4,128,128]{2,1,0:T(8,128)S(1)}, bf16[4,128,128]{2,1,0:T(8,128)(2,1)S(1)}) custom-call(s32[5]{0:T(128)S(1)} %stack.19.me_ref.r_0_, bf16[128,512]{1,0:T(8,128)(2,1)S(1)} %get-tuple-element.203.r_1_, bf16[128,512]{1,0:T(8,128)(2,1)S(1)} %get-tuple-element.204.r_2_), custom_call_target="tpu_custom_call" | custom-call | bytes 655360 | tf_op jit(solution)/shard_map/cweight/pallas_call | solution.py:31
  57.1 0.9 collective-permute-start.25
  58.0 2.1 %all-gather.2 = bf16[128,512]{1,0:T(8,128)(2,1)S(1)} all-gather(bf16[64,512]{1,0:T(8,128)(2,1)S(1)} %pad_maximum_fusion.1), channel_id=4, replica_groups=mesh['groups'=2,'curve'=4,'cross'=2,'sub'=2] {'sub'}, dimensions={0}, use_global_device_ids=true | all-gather | bytes 196608 | tf_op jit(solution)/shard_map/all_gather | solution.py:59
  60.0 3.1 %third.1 = (bf16[512,512]{1,0:T(8,128)(2,1)S(1)}, bf16[512,512]{1,0:T(8,128)(2,1)S(1)}, bf16[512,512]{1,0:T(8,128)(2,1)S(1)}, bf16[128,512]{1,0:T(8,128)(2,1)S(1...) custom-call(s32[5]{0:T(128)S(1)} %stack.19.me_ref.r_0_, bf16[512,512]{1,0:T(8,128)(2,1)S(1)} %get-tuple-element.193.r_1_, ...), custom_call_target="tpu_custom_call" | custom-call | bytes 9175040 | tf_op jit(solution)/shard_map/third/pallas_call | solution.py:31
  63.2 1.3 %collective-permute-start.30 = (bf16[4,384,128]{2,1,0:T(8,128)(2,1)S(1)}, bf16[4,384,128]{2,1,0:T(8,128)(2,1)S(1)}, u32[]{:S(2)}, u32[]{:S(2)}) collective-permute-start(bf16[4,384,128]{2,1,0:T(8,128)(2,1)S(1)} %get-tuple-element.223), channel_id=1, source_target_pairs={{0,2},{2,0},{1,3},{3,1},{4,6},{6,4},{5,7},{7,5},{8,10},{10,8},{9,1... | collective-permute-start | bytes 1179656 | tf_op jit(solution)/shard_map/ppermute | solution.py:72
  64.5 0.8 collective-permute-start.26
  65.3 1.1 %stage1.1 = (f32[512,128]{1,0:T(8,128)S(1)}, bf16[512,128]{1,0:T(8,128)(2,1)S(1)}, bf16[512,128]{1,0:T(8,128)(2,1)S(1)}, bf16[512,128]{1,0:T(8,128)(2,1)S(1)}, f32[512,256]{1,0:T(8,128)S(1)}) custom-call(s32[5]{0:T(128)S(1)} %stack.19.me_ref.r_0_, bf16[512,512]{1,0:T(8,128)(2,1)S(1)} %get-tuple-element.202.fb_ref, ...), custom_call_target="tpu_custom_call" | custom-call | bytes 6160384 | tf_op jit(solution)/shard_map/stage1/pallas_call | solution.py:31
  66.4 2.0 %collective-permute-start.27 = (bf16[512,128]{1,0:T(8,128)(2,1)S(1)}, bf16[512,128]{1,0:T(8,128)(2,1)S(1)}, u32[]{:S(2)}, u32[]{:S(2)}) collective-permute-start(bf16[512,128]{1,0:T(8,128)(2,1)S(1)} %get-tuple-element.218), channel_id=1, source_target_pairs={{0,4},{4,0},{8,12},{12,8},{1,5},{5,1},{9,13},{13,9},{2,6},{6,2},{1... | collective-permute-start | bytes 393224 | tf_op jit(solution)/shard_map/ppermute | solution.py:76
  68.4 1.4 %collective-permute-start.28 = (bf16[512,128]{1,0:T(8,128)(2,1)S(1)}, bf16[512,128]{1,0:T(8,128)(2,1)S(1)}, u32[]{:S(2)}, u32[]{:S(2)}) collective-permute-start(bf16[512,128]{1,0:T(8,128)(2,1)S(1)} %get-tuple-element.219), channel_id=1, source_target_pairs={{0,8},{4,12},{8,0},{12,4},{1,9},{5,13},{9,1},{13,5},{2,10},{6,14},... | collective-permute-start | bytes 393224 | tf_op jit(solution)/shard_map/ppermute | solution.py:76
  69.8 1.4 %collective-permute-start.29 = (bf16[512,128]{1,0:T(8,128)(2,1)S(1)}, bf16[512,128]{1,0:T(8,128)(2,1)S(1)}, u32[]{:S(2)}, u32[]{:S(2)}) collective-permute-start(bf16[512,128]{1,0:T(8,128)(2,1)S(1)} %get-tuple-element.220), channel_id=1, source_target_pairs={{0,12},{4,8},{8,4},{12,0},{1,13},{5,9},{9,5},{13,1},{2,14},{6,10},... | collective-permute-start | bytes 393224 | tf_op jit(solution)/shard_map/ppermute | solution.py:76
  71.1 4.1 %collective-permute-done.30.refs_1_ = bf16[4,384,128]{2,1,0:T(8,128)(2,1)S(1)} collective-permute-done((bf16[4,384,128]{2,1,0:T(8,128)(2,1)S(1)}, bf16[4,384,128]{2,1,0:T(8,128)(2,1)S(1)}, u32[]{:S(2)}, u32[]{:S(2)}) %collective-permute-start.30) | collective-permute-done | bytes 393248 | tf_op jit(solution)/shard_map/ppermute | solution.py:72
  75.2 0.6 stage0.1
  75.9 3.4 %collective-permute-start.31 = (bf16[384,128]{1,0:T(8,128)(2,1)S(1)}, bf16[384,128]{1,0:T(8,128)(2,1)S(1)}, u32[]{:S(2)}, u32[]{:S(2)}) collective-permute-start(bf16[384,128]{1,0:T(8,128)(2,1)S(1)} %get-tuple-element.225), channel_id=1, source_target_pairs={{0,4},{4,0},{8,12},{12,8},{1,5},{5,1},{9,13},{13,9},{2,6},{6,2},{1... | collective-permute-start | bytes 294920 | tf_op jit(solution)/shard_map/ppermute | solution.py:76
  79.3 1.4 %collective-permute-start.32 = (bf16[384,128]{1,0:T(8,128)(2,1)S(1)}, bf16[384,128]{1,0:T(8,128)(2,1)S(1)}, u32[]{:S(2)}, u32[]{:S(2)}) collective-permute-start(bf16[384,128]{1,0:T(8,128)(2,1)S(1)} %get-tuple-element.226), channel_id=1, source_target_pairs={{0,8},{4,12},{8,0},{12,4},{1,9},{5,13},{9,1},{13,5},{2,10},{6,14},... | collective-permute-start | bytes 294920 | tf_op jit(solution)/shard_map/ppermute | solution.py:76
  80.7 1.4 %collective-permute-start.33 = (bf16[384,128]{1,0:T(8,128)(2,1)S(1)}, bf16[384,128]{1,0:T(8,128)(2,1)S(1)}, u32[]{:S(2)}, u32[]{:S(2)}) collective-permute-start(bf16[384,128]{1,0:T(8,128)(2,1)S(1)} %get-tuple-element.227), channel_id=1, source_target_pairs={{0,12},{4,8},{8,4},{12,0},{1,13},{5,9},{9,5},{13,1},{2,14},{6,10},... | collective-permute-start | bytes 294920 | tf_op jit(solution)/shard_map/ppermute | solution.py:76
  82.1 2.0 %all-gather.3 = bf16[256,512]{1,0:T(8,128)(2,1)S(1)} all-gather(bf16[128,512]{1,0:T(8,128)(2,1)S(1)} %collective-permute-done.26), channel_id=5, replica_groups=mesh['groups'=2,'curve'=4,'cross'=2,'sub'=2] {'sub'}, dimensions={0}, use_global_device_ids=true | all-gather | bytes 393216 | tf_op jit(solution)/shard_map/all_gather | solution.py:59
  84.1 1.7 %last.1 = (f32[256,512]{1,0:T(8,128)}, f32[256,128]{1,0:T(8,128)S(1)}, f32[64,256]{1,0:T(8,128)S(1)}, f32[64,256]{1,0:T(8,128)}) custom-call(s32[5]{0:T(128)S(1)} %stack.19.me_ref.r_0_, f32[512,256]{1,0:T(8,128)S(1)} %get-tuple-element.215.comb_ref, bf16[2,128,512]{2,1,0:T(8,128)(2,1)S(1)} %bitcast.11, bf16[512,256]{1,0:T(8,128)(2,1)S(1)} %get-tuple-element.181.place_ref, ...), custom_call_target="tpu_custom_call" | custom-call | bytes 2490368 | tf_op jit(solution)/shard_map/last/pallas_call | solution.py:31
  85.8 4.2 %collective-permute-done.32.b_ref = bf16[384,128]{1,0:T(8,128)(2,1)S(1)} collective-permute-done((bf16[384,128]{1,0:T(8,128)(2,1)S(1)}, bf16[384,128]{1,0:T(8,128)(2,1)S(1)}, u32[]{:S(2)}, u32[]{:S(2)}) %collective-permute-start.32) | collective-permute-done | bytes 98336 | tf_op jit(solution)/shard_map/ppermute | solution.py:76
  90.0 0.8 late.1
  (62 shorter events, 3.9 us)
Async XLA Ops:
  0.6 10.1 %collective-permute-start.2 = (bf16[2,256,1024]{2,1,0:T(8,128)(2,1)}, bf16[2,256,1024]{2,1,0:T(8,128)(2,1)S(1)}, u32[]{:S(2)}, u32[]{:S(2)}) collective-permute-start(bf16[2,256,1024]{2,1,0:T(8,128)(2,1)} %r_1_.3), channel_id=1, source_target_pairs={{0,1},{1,0},{2,3},{3,2},{4,5},{5,4},{6,7},{7,6},{8,9},{9,8},{10,11... | collective-permute-start | bytes 3145736 | tf_op jit(solution)/shard_map/ppermute | solution.py:55
  1.1 9.6 %collective-permute-start.3 = (bf16[2,256,512]{2,1,0:T(8,128)(2,1)}, bf16[2,256,512]{2,1,0:T(8,128)(2,1)S(1)}, u32[]{:S(2)}, u32[]{:S(2)}) collective-permute-start(bf16[2,256,512]{2,1,0:T(8,128)(2,1)} %r_2_.3), channel_id=1, source_target_pairs={{0,1},{1,0},{2,3},{3,2},{4,5},{5,4},{6,7},{7,6},{8,9},{9,8},{10,11... | collective-permute-start | bytes 1572872 | tf_op jit(solution)/shard_map/ppermute | solution.py:55
  1.3 0.7 copy-start.6
  2.0 0.9 %copy-start.2 = (bf16[256,512]{1,0:T(8,128)(2,1)S(1)}, bf16[256,512]{1,0:T(8,128)(2,1)}, u32[]{:S(2)}) copy-start(bf16[256,512]{1,0:T(8,128)(2,1)} %x_ref.1) | copy-start | bytes 786436
  2.9 6.2 %copy-start.3 = (s32[4,3,128,128]{3,2,1,0:T(8,128)S(1)}, s32[4,3,128,128]{3,2,1,0:T(8,128)}, u32[]{:S(2)}) copy-start(s32[4,3,128,128]{3,2,1,0:T(8,128)} %mask_ref.1) | copy-start | bytes 2359300
  2.9 6.2 %copy-start.7 = (s32[4,3]{1,0:T(4,128)S(1)}, s32[4,3]{1,0:T(4,128)}, u32[]{:S(2)}) copy-start(s32[4,3]{1,0:T(4,128)} %tile_ref.1) | copy-start | bytes 148
  2.9 6.2 %copy-start.8 = (s32[512]{0:T(512)S(1)}, s32[512]{0:T(512)}, u32[]{:S(2)}) copy-start(s32[512]{0:T(512)} %param.16) | copy-start | bytes 6148
  3.9 7.6 %collective-permute-start = (bf16[128,256]{1,0:T(8,128)(2,1)S(1)}, bf16[128,256]{1,0:T(8,128)(2,1)S(1)}, u32[]{:S(2)}, u32[]{:S(2)}) collective-permute-start(bf16[128,256]{1,0:T(8,128)(2,1)S(1)} %get-tuple-element.120), channel_id=1, source_target_pairs={{0,2},{2,4},{4,6},{6,8},{8,10},{10,12},{12,14},{3,1},{5,3},{7,5},{... | collective-permute-start | bytes 196616 | tf_op jit(solution)/shard_map/ppermute | solution.py:51
  6.8 3.9 %copy-start = (bf16[2,256,1024]{2,1,0:T(8,128)(2,1)S(1)}, bf16[2,256,1024]{2,1,0:T(8,128)(2,1)}, u32[]{:S(2)}) copy-start(bf16[2,256,1024]{2,1,0:T(8,128)(2,1)} %r_1_.3) | copy-start | bytes 3145732
  6.8 4.6 %collective-permute-start.1 = (bf16[128,256]{1,0:T(8,128)(2,1)S(1)}, bf16[128,256]{1,0:T(8,128)(2,1)S(1)}, u32[]{:S(2)}, u32[]{:S(2)}) collective-permute-start(bf16[128,256]{1,0:T(8,128)(2,1)S(1)} %get-tuple-element.121), channel_id=1, source_target_pairs={{1,3},{3,5},{5,7},{7,9},{9,11},{11,13},{13,15},{2,0},{4,2},{6,4},{... | collective-permute-start | bytes 196616 | tf_op jit(solution)/shard_map/ppermute | solution.py:51
  9.1 1.6 %copy-start.1 = (bf16[2,256,512]{2,1,0:T(8,128)(2,1)S(1)}, bf16[2,256,512]{2,1,0:T(8,128)(2,1)}, u32[]{:S(2)}) copy-start(bf16[2,256,512]{2,1,0:T(8,128)(2,1)} %r_2_.3) | copy-start | bytes 1572868
  13.5 2.4 %copy-start.5 = (bf16[256,512]{1,0:T(8,128)(2,1)S(1)}, bf16[256,512]{1,0:T(8,128)(2,1)}, u32[]{:S(2)}) copy-start(bf16[256,512]{1,0:T(8,128)(2,1)} %cw_ref) | copy-start | bytes 786436
  15.9 4.0 %collective-permute-start.6 = (bf16[256,512]{1,0:T(8,128)(2,1)S(1)}, bf16[256,512]{1,0:T(8,128)(2,1)S(1)}, u32[]{:S(2)}, u32[]{:S(2)}) collective-permute-start(bf16[256,512]{1,0:T(8,128)(2,1)S(1)} %copy-done.5), channel_id=1, source_target_pairs={{0,1},{1,0},{2,3},{3,2},{4,5},{5,4},{6,7},{7,6},{8,9},{9,8},{10,11... | collective-permute-start | bytes 786440 | tf_op jit(solution)/shard_map/ppermute | solution.py:55
  16.1 5.5 %collective-permute-start.4 = (bf16[80,512]{1,0:T(8,128)(2,1)S(1)}, bf16[80,512]{1,0:T(8,128)(2,1)S(1)}, u32[]{:S(2)}, u32[]{:S(2)}) collective-permute-start(bf16[80,512]{1,0:T(8,128)(2,1)S(1)} %get-tuple-element.138), channel_id=1, source_target_pairs={{0,2},{2,4},{4,6},{6,8},{8,10},{10,12},{12,14},{3,1},{5,3},{7,5},{... | collective-permute-start | bytes 245768 | tf_op jit(solution)/shard_map/ppermute | solution.py:51
  18.2 3.3 %collective-permute-start.5 = (bf16[48,512]{1,0:T(8,128)(2,1)S(1)}, bf16[48,512]{1,0:T(8,128)(2,1)S(1)}, u32[]{:S(2)}, u32[]{:S(2)}) collective-permute-start(bf16[48,512]{1,0:T(8,128)(2,1)S(1)} %get-tuple-element.139), channel_id=1, source_target_pairs={{0,4},{2,6},{4,8},{6,10},{8,12},{10,14},{5,1},{7,3},{9,5},{11,7},{... | collective-permute-start | bytes 147464 | tf_op jit(solution)/shard_map/ppermute | solution.py:51
  21.6 1.5 %collective-permute-start.7 = (bf16[80,512]{1,0:T(8,128)(2,1)S(1)}, bf16[80,512]{1,0:T(8,128)(2,1)S(1)}, u32[]{:S(2)}, u32[]{:S(2)}) collective-permute-start(bf16[80,512]{1,0:T(8,128)(2,1)S(1)} %collective-permute-done.4.one_ref), channel_id=1, source_target_pairs={{0,1},{1,0},{2,3},{3,2},{4,5},{5,4},{6,7},{7,6},{8,9},{9,8},{10,11... | collective-permute-start | bytes 245768 | tf_op jit(solution)/shard_map/ppermute | solution.py:55
  21.8 1.2 %collective-permute-start.8 = (bf16[48,512]{1,0:T(8,128)(2,1)S(1)}, bf16[48,512]{1,0:T(8,128)(2,1)S(1)}, u32[]{:S(2)}, u32[]{:S(2)}) collective-permute-start(bf16[48,512]{1,0:T(8,128)(2,1)S(1)} %collective-permute-done.5.two_ref), channel_id=1, source_target_pairs={{0,1},{1,0},{2,3},{3,2},{4,5},{5,4},{6,7},{7,6},{8,9},{9,8},{10,11... | collective-permute-start | bytes 147464 | tf_op jit(solution)/shard_map/ppermute | solution.py:55
  23.0 1.2 %copy-start.4 = (bf16[256,512]{1,0:T(8,128)(2,1)S(1)}, bf16[256,512]{1,0:T(8,128)(2,1)}, u32[]{:S(2)}) copy-start(bf16[256,512]{1,0:T(8,128)(2,1)} %ct_ref) | copy-start | bytes 786436
  24.2 7.8 %collective-permute-start.12 = (bf16[256,512]{1,0:T(8,128)(2,1)S(1)}, bf16[256,512]{1,0:T(8,128)(2,1)S(1)}, u32[]{:S(2)}, u32[]{:S(2)}) collective-permute-start(bf16[256,512]{1,0:T(8,128)(2,1)S(1)} %copy-done.4), channel_id=1, source_target_pairs={{0,1},{1,0},{2,3},{3,2},{4,5},{5,4},{6,7},{7,6},{8,9},{9,8},{10,11... | collective-permute-start | bytes 786440 | tf_op jit(solution)/shard_map/ppermute | solution.py:55
  24.6 8.6 %collective-permute-start.9 = (bf16[192,512]{1,0:T(8,128)(2,1)S(1)}, bf16[192,512]{1,0:T(8,128)(2,1)S(1)}, u32[]{:S(2)}, u32[]{:S(2)}) collective-permute-start(bf16[192,512]{1,0:T(8,128)(2,1)S(1)} %get-tuple-element.157), channel_id=1, source_target_pairs={{0,2},{2,4},{4,6},{6,8},{8,10},{10,12},{12,14},{3,1},{5,3},{7,5},{... | collective-permute-start | bytes 589832 | tf_op jit(solution)/shard_map/ppermute | solution.py:51
  26.8 6.4 %collective-permute-start.10 = (bf16[64,512]{1,0:T(8,128)(2,1)S(1)}, bf16[64,512]{1,0:T(8,128)(2,1)S(1)}, u32[]{:S(2)}, u32[]{:S(2)}) collective-permute-start(bf16[64,512]{1,0:T(8,128)(2,1)S(1)} %get-tuple-element.158), channel_id=1, source_target_pairs={{0,4},{2,6},{4,8},{6,10},{8,12},{10,14},{5,1},{7,3},{9,5},{11,7},{... | collective-permute-start | bytes 196616 | tf_op jit(solution)/shard_map/ppermute | solution.py:51
  29.1 4.1 %collective-permute-start.11 = (bf16[32,512]{1,0:T(8,128)(2,1)S(1)}, bf16[32,512]{1,0:T(8,128)(2,1)S(1)}, u32[]{:S(2)}, u32[]{:S(2)}) collective-permute-start(bf16[32,512]{1,0:T(8,128)(2,1)S(1)} %get-tuple-element.159), channel_id=1, source_target_pairs={{0,6},{2,8},{4,10},{6,12},{8,14},{7,1},{9,3},{11,5},{13,7},{15,9},... | collective-permute-start | bytes 98312 | tf_op jit(solution)/shard_map/ppermute | solution.py:51
  33.2 1.8 %collective-permute-start.13 = (bf16[192,512]{1,0:T(8,128)(2,1)S(1)}, bf16[192,512]{1,0:T(8,128)(2,1)S(1)}, u32[]{:S(2)}, u32[]{:S(2)}) collective-permute-start(bf16[192,512]{1,0:T(8,128)(2,1)S(1)} %collective-permute-done.9.aone_ref), channel_id=1, source_target_pairs={{0,1},{1,0},{2,3},{3,2},{4,5},{5,4},{6,7},{7,6},{8,9},{9,8},{10,11... | collective-permute-start | bytes 589832 | tf_op jit(solution)/shard_map/ppermute | solution.py:55
  33.3 1.7 %collective-permute-start.14 = (bf16[64,512]{1,0:T(8,128)(2,1)S(1)}, bf16[64,512]{1,0:T(8,128)(2,1)S(1)}, u32[]{:S(2)}, u32[]{:S(2)}) collective-permute-start(bf16[64,512]{1,0:T(8,128)(2,1)S(1)} %collective-permute-done.10.atwo_ref), channel_id=1, source_target_pairs={{0,1},{1,0},{2,3},{3,2},{4,5},{5,4},{6,7},{7,6},{8,9},{9,8},{10,11... | collective-permute-start | bytes 196616 | tf_op jit(solution)/shard_map/ppermute | solution.py:55
  33.8 1.2 %collective-permute-start.15 = (bf16[32,512]{1,0:T(8,128)(2,1)S(1)}, bf16[32,512]{1,0:T(8,128)(2,1)S(1)}, u32[]{:S(2)}, u32[]{:S(2)}) collective-permute-start(bf16[32,512]{1,0:T(8,128)(2,1)S(1)} %collective-permute-done.11.athree_ref), channel_id=1, source_target_pairs={{0,1},{1,0},{2,3},{3,2},{4,5},{5,4},{6,7},{7,6},{8,9},{9,8},{10,11... | collective-permute-start | bytes 98312 | tf_op jit(solution)/shard_map/ppermute | solution.py:55
  38.9 9.0 %collective-permute-start.16 = (bf16[192,512]{1,0:T(8,128)(2,1)S(1)}, bf16[192,512]{1,0:T(8,128)(2,1)S(1)}, u32[]{:S(2)}, u32[]{:S(2)}) collective-permute-start(bf16[192,512]{1,0:T(8,128)(2,1)S(1)} %get-tuple-element.183), channel_id=1, source_target_pairs={{0,2},{2,4},{4,6},{6,8},{8,10},{10,12},{12,14},{3,1},{5,3},{7,5},{... | collective-permute-start | bytes 589832 | tf_op jit(solution)/shard_map/ppermute | solution.py:51
  40.6 7.3 %collective-permute-start.17 = (bf16[64,512]{1,0:T(8,128)(2,1)S(1)}, bf16[64,512]{1,0:T(8,128)(2,1)S(1)}, u32[]{:S(2)}, u32[]{:S(2)}) collective-permute-start(bf16[64,512]{1,0:T(8,128)(2,1)S(1)} %get-tuple-element.184), channel_id=1, source_target_pairs={{0,4},{2,6},{4,8},{6,10},{8,12},{10,14},{5,1},{7,3},{9,5},{11,7},{... | collective-permute-start | bytes 196616 | tf_op jit(solution)/shard_map/ppermute | solution.py:51
  43.3 4.6 %collective-permute-start.18 = (bf16[32,512]{1,0:T(8,128)(2,1)S(1)}, bf16[32,512]{1,0:T(8,128)(2,1)S(1)}, u32[]{:S(2)}, u32[]{:S(2)}) collective-permute-start(bf16[32,512]{1,0:T(8,128)(2,1)S(1)} %get-tuple-element.185), channel_id=1, source_target_pairs={{0,6},{2,8},{4,10},{6,12},{8,14},{7,1},{9,3},{11,5},{13,7},{15,9},... | collective-permute-start | bytes 98312 | tf_op jit(solution)/shard_map/ppermute | solution.py:51
  47.5 12.6 %collective-permute-start.24 = (bf16[4,384,128]{2,1,0:T(8,128)(2,1)S(1)}, bf16[4,384,128]{2,1,0:T(8,128)(2,1)S(1)}, u32[]{:S(2)}, u32[]{:S(2)}) collective-permute-start(bf16[4,384,128]{2,1,0:T(8,128)(2,1)S(1)} %get-tuple-element.197), channel_id=1, source_target_pairs={{0,2},{2,0},{1,3},{3,1},{4,6},{6,4},{5,7},{7,5},{8,10},{10,8},{9,1... | collective-permute-start | bytes 1179656 | tf_op jit(solution)/shard_map/ppermute | solution.py:72
  47.9 1.8 %collective-permute-start.19 = (bf16[192,512]{1,0:T(8,128)(2,1)S(1)}, bf16[192,512]{1,0:T(8,128)(2,1)S(1)}, u32[]{:S(2)}, u32[]{:S(2)}) collective-permute-start(bf16[192,512]{1,0:T(8,128)(2,1)S(1)} %collective-permute-done.16.one_ref), channel_id=1, source_target_pairs={{0,1},{1,0},{2,3},{3,2},{4,5},{5,4},{6,7},{7,6},{8,9},{9,8},{10,11... | collective-permute-start | bytes 589832 | tf_op jit(solution)/shard_map/ppermute | solution.py:55
  48.0 1.7 %collective-permute-start.20 = (bf16[64,512]{1,0:T(8,128)(2,1)S(1)}, bf16[64,512]{1,0:T(8,128)(2,1)S(1)}, u32[]{:S(2)}, u32[]{:S(2)}) collective-permute-start(bf16[64,512]{1,0:T(8,128)(2,1)S(1)} %collective-permute-done.17.two_ref), channel_id=1, source_target_pairs={{0,1},{1,0},{2,3},{3,2},{4,5},{5,4},{6,7},{7,6},{8,9},{9,8},{10,11... | collective-permute-start | bytes 196616 | tf_op jit(solution)/shard_map/ppermute | solution.py:55
  48.5 1.2 %collective-permute-start.21 = (bf16[32,512]{1,0:T(8,128)(2,1)S(1)}, bf16[32,512]{1,0:T(8,128)(2,1)S(1)}, u32[]{:S(2)}, u32[]{:S(2)}) collective-permute-start(bf16[32,512]{1,0:T(8,128)(2,1)S(1)} %collective-permute-done.18.three_ref), channel_id=1, source_target_pairs={{0,1},{1,0},{2,3},{3,2},{4,5},{5,4},{6,7},{7,6},{8,9},{9,8},{10,11... | collective-permute-start | bytes 98312 | tf_op jit(solution)/shard_map/ppermute | solution.py:55
  51.2 6.7 %collective-permute-start.22 = (bf16[32,512]{1,0:T(8,128)(2,1)S(1)}, bf16[32,512]{1,0:T(8,128)(2,1)S(1)}, u32[]{:S(2)}, u32[]{:S(2)}) collective-permute-start(bf16[32,512]{1,0:T(8,128)(2,1)S(1)} %get-tuple-element.195), channel_id=1, source_target_pairs={{0,2},{2,4},{4,6},{6,8},{8,10},{10,12},{12,14},{3,1},{5,3},{7,5},{... | collective-permute-start | bytes 98312 | tf_op jit(solution)/shard_map/ppermute | solution.py:51
  52.9 5.1 %collective-permute-start.23 = (bf16[32,512]{1,0:T(8,128)(2,1)S(1)}, bf16[32,512]{1,0:T(8,128)(2,1)S(1)}, u32[]{:S(2)}, u32[]{:S(2)}) collective-permute-start(bf16[32,512]{1,0:T(8,128)(2,1)S(1)} %get-tuple-element.196), channel_id=1, source_target_pairs={{0,4},{2,6},{4,8},{6,10},{8,12},{10,14},{5,1},{7,3},{9,5},{11,7},{... | collective-permute-start | bytes 98312 | tf_op jit(solution)/shard_map/ppermute | solution.py:51
  57.1 6.1 %collective-permute-start.25 = (bf16[4,128,128]{2,1,0:T(8,128)(2,1)S(1)}, bf16[4,128,128]{2,1,0:T(8,128)(2,1)S(1)}, u32[]{:S(2)}, u32[]{:S(2)}) collective-permute-start(bf16[4,128,128]{2,1,0:T(8,128)(2,1)S(1)} %get-tuple-element.213), channel_id=1, source_target_pairs={{0,2},{2,0},{1,3},{3,1},{4,6},{6,4},{5,7},{7,5},{8,10},{10,8},{9,1... | collective-permute-start | bytes 393224 | tf_op jit(solution)/shard_map/ppermute | solution.py:72
  63.2 12.0 %collective-permute-start.30 = (bf16[4,384,128]{2,1,0:T(8,128)(2,1)S(1)}, bf16[4,384,128]{2,1,0:T(8,128)(2,1)S(1)}, u32[]{:S(2)}, u32[]{:S(2)}) collective-permute-start(bf16[4,384,128]{2,1,0:T(8,128)(2,1)S(1)} %get-tuple-element.223), channel_id=1, source_target_pairs={{0,2},{2,0},{1,3},{3,1},{4,6},{6,4},{5,7},{7,5},{8,10},{10,8},{9,1... | collective-permute-start | bytes 1179656 | tf_op jit(solution)/shard_map/ppermute | solution.py:72
  64.5 14.8 %collective-permute-start.26 = (bf16[128,512]{1,0:T(8,128)(2,1)S(1)}, bf16[128,512]{1,0:T(8,128)(2,1)S(1)}, u32[]{:S(2)}, u32[]{:S(2)}) collective-permute-start(bf16[128,512]{1,0:T(8,128)(2,1)S(1)} %get-tuple-element.216), channel_id=1, source_target_pairs={{0,2},{2,4},{4,6},{6,8},{8,10},{10,12},{12,14},{3,1},{5,3},{7,5},{... | collective-permute-start | bytes 393224 | tf_op jit(solution)/shard_map/ppermute | solution.py:51
  66.4 14.3 %collective-permute-start.27 = (bf16[512,128]{1,0:T(8,128)(2,1)S(1)}, bf16[512,128]{1,0:T(8,128)(2,1)S(1)}, u32[]{:S(2)}, u32[]{:S(2)}) collective-permute-start(bf16[512,128]{1,0:T(8,128)(2,1)S(1)} %get-tuple-element.218), channel_id=1, source_target_pairs={{0,4},{4,0},{8,12},{12,8},{1,5},{5,1},{9,13},{13,9},{2,6},{6,2},{1... | collective-permute-start | bytes 393224 | tf_op jit(solution)/shard_map/ppermute | solution.py:76
  68.4 15.7 %collective-permute-start.28 = (bf16[512,128]{1,0:T(8,128)(2,1)S(1)}, bf16[512,128]{1,0:T(8,128)(2,1)S(1)}, u32[]{:S(2)}, u32[]{:S(2)}) collective-permute-start(bf16[512,128]{1,0:T(8,128)(2,1)S(1)} %get-tuple-element.219), channel_id=1, source_target_pairs={{0,8},{4,12},{8,0},{12,4},{1,9},{5,13},{9,1},{13,5},{2,10},{6,14},... | collective-permute-start | bytes 393224 | tf_op jit(solution)/shard_map/ppermute | solution.py:76
  69.8 14.3 %collective-permute-start.29 = (bf16[512,128]{1,0:T(8,128)(2,1)S(1)}, bf16[512,128]{1,0:T(8,128)(2,1)S(1)}, u32[]{:S(2)}, u32[]{:S(2)}) collective-permute-start(bf16[512,128]{1,0:T(8,128)(2,1)S(1)} %get-tuple-element.220), channel_id=1, source_target_pairs={{0,12},{4,8},{8,4},{12,0},{1,13},{5,9},{9,5},{13,1},{2,14},{6,10},... | collective-permute-start | bytes 393224 | tf_op jit(solution)/shard_map/ppermute | solution.py:76
  75.9 10.0 %collective-permute-start.31 = (bf16[384,128]{1,0:T(8,128)(2,1)S(1)}, bf16[384,128]{1,0:T(8,128)(2,1)S(1)}, u32[]{:S(2)}, u32[]{:S(2)}) collective-permute-start(bf16[384,128]{1,0:T(8,128)(2,1)S(1)} %get-tuple-element.225), channel_id=1, source_target_pairs={{0,4},{4,0},{8,12},{12,8},{1,5},{5,1},{9,13},{13,9},{2,6},{6,2},{1... | collective-permute-start | bytes 294920 | tf_op jit(solution)/shard_map/ppermute | solution.py:76
  79.3 10.7 %collective-permute-start.32 = (bf16[384,128]{1,0:T(8,128)(2,1)S(1)}, bf16[384,128]{1,0:T(8,128)(2,1)S(1)}, u32[]{:S(2)}, u32[]{:S(2)}) collective-permute-start(bf16[384,128]{1,0:T(8,128)(2,1)S(1)} %get-tuple-element.226), channel_id=1, source_target_pairs={{0,8},{4,12},{8,0},{12,4},{1,9},{5,13},{9,1},{13,5},{2,10},{6,14},... | collective-permute-start | bytes 294920 | tf_op jit(solution)/shard_map/ppermute | solution.py:76
  80.7 9.3 %collective-permute-start.33 = (bf16[384,128]{1,0:T(8,128)(2,1)S(1)}, bf16[384,128]{1,0:T(8,128)(2,1)S(1)}, u32[]{:S(2)}, u32[]{:S(2)}) collective-permute-start(bf16[384,128]{1,0:T(8,128)(2,1)S(1)} %get-tuple-element.227), channel_id=1, source_target_pairs={{0,12},{4,8},{8,4},{12,0},{1,13},{5,9},{9,5},{13,1},{2,14},{6,10},... | collective-permute-start | bytes 294920 | tf_op jit(solution)/shard_map/ppermute | solution.py:76

commit v9 on v8

--- a/solution.py
+++ b/solution.py
@@ -195,13 +195,13 @@
             src[rows, :] = jnp.zeros((rim, xc.shape[1]), BF)
 
 
-def k_first(me_ref, xc_ref, rims_ref, adj_ref, inv_ref, win_ref, wo_ref,
+def k_first(me_ref, xc_ref, a_ref, a2_ref, b_ref, b2_ref, adj_ref, inv_ref, win_ref, wo_ref,
             slot_ref, tags_ref, rsel_ref,
             agg_ref, pre_ref, hid_ref, first_ref, one_ref, two_ref, src):
     xc = xc_ref[...]
-    rim = rims_ref.shape[1] // 2
-    before = jnp.concatenate([rims_ref[0, 0:rim], rims_ref[1, rim:]], axis=1)
-    after = jnp.concatenate([rims_ref[0, rim:], rims_ref[1, 0:rim]], axis=1)
+    (before0, after1), (after0, before1) = directed(me_ref[1], a_ref, a2_ref), directed(me_ref[1], b_ref, b2_ref)
+    before = jnp.concatenate([before0, before1], axis=1)
+    after = jnp.concatenate([after0, after1], axis=1)
     fill_sources(me_ref, xc, (before, after), src)
     agg, pre, hid, out = forward(xc, src[...], adj_ref, inv_ref, win_ref, wo_ref)
     agg_ref[...] = agg
@@ -366,12 +366,6 @@
         three_ref[...] = of_before[3 * cap:]
 
 
-def k_newt(me_ref, new_ref, out_ref):
-    half = out_ref.shape[0]
-    at = pl.multiple_of(me_ref[1] * half, half)
-    out_ref[...] = new_ref[:, pl.ds(at, half)].T
-
-
 def k_grads(scale, me_ref, pg_ref, h_ref, agg_ref, g_ref, hid_ref, gin_ref, gout_ref):
     half = gin_ref.shape[0]
     width = h_ref.shape[1]
@@ -420,11 +414,6 @@
             @pl.when(me_ref[2] != d % 2)
             def _():
                 send_ref[d // 2, rows, :] = value.astype(BF)
-
-
-def k_newt_pack(scale, me_ref, new_ref, pg_ref, h_ref, agg_ref, g_ref, hid_ref, out_ref, keep_ref, send_ref):
-    pack_grads(scale, me_ref, pg_ref, h_ref, agg_ref, g_ref, hid_ref, keep_ref, send_ref)
-    k_newt(me_ref, new_ref, out_ref)
 
 
 def k_cweight_pack(scale, me_ref, pgrad_ref, coarse_ref, keep_ref, send_ref):
@@ -500,27 +489,21 @@
     rim_grads(me_ref[1], pg, win_ref, inv_ref, adjt_ref, scaled_ref, msg_ref)
 
 
-def k_last(me_ref, comb_ref, rims_ref, place_ref, *rest):
-    half = comb_ref.shape[1]
-    at = pl.multiple_of(me_ref[1] * half, half)
-    total = comb_ref[...] + placed(
-        me_ref, place_ref, rims_ref[0, :, pl.ds(at, half)], rims_ref[1, :, pl.ds(at, half)])
-    if len(rest) == 1:
-        rest[0][...] = total.T
-    else:
-        rest[4][...] = total.T
-        k_sum(*rest[:4], *rest[5:])
-
-
-def k_halfcomb(me_ref, fb_ref, pg_ref, win_ref, scaled_ref, adjt_ref, comb_ref):
-    n, half = comb_ref.shape
-    at = pl.multiple_of(me_ref[1] * half, half)
-    cols = pl.ds(at, half)
-    comb_ref[...] = (
+def k_last(me_ref, fb_ref, pg_ref, win_ref, scaled_ref, adjt_ref, rims_ref, place_ref, new_ref, *rest):
+    n, width = fb_ref.shape
+    half = width // 2
+    cols = pl.ds(pl.multiple_of(me_ref[1] * half, half), half)
+    grad_ref, out_ref = rest[-2:]
+    total = (
         fb_ref[:, cols].astype(F32)
         + dot(pg_ref[...], win_ref[:, cols])
         + dot(adjt_ref[0:n, :], scaled_ref[:, cols])
+        + placed(me_ref, place_ref, rims_ref[0, :, cols], rims_ref[1, :, cols])
     )
+    grad_ref[...] = total.T
+    out_ref[...] = new_ref[:, cols].T
+    if len(rest) > 2:
+        k_sum(*rest[:-2])
 
 
 def k_stage(me_ref, *refs):
@@ -536,11 +519,6 @@
             other = z ^ step
             outs[step - 1][rows, :] = (keep_ref[other] + got_ref[other].astype(F32)).astype(BF)
         row += keep_ref.shape[1]
-
-
-def k_stage_comb(me_ref, fb_ref, pg_ref, win_ref, scaled_ref, adjt_ref, *refs):
-    k_stage(me_ref, *refs[:-1])
-    k_halfcomb(me_ref, fb_ref, pg_ref, win_ref, scaled_ref, adjt_ref, refs[-1])
 
 
 def unpack_small(total):
@@ -601,14 +579,13 @@
     win0, wo0 = call(lambda *r: k_weights(0, *r), weight_outs, [me],
                      [inward_weight, outward_weight, win2, wout2], "weights0")
     rim_a, rim_b, win0, adj = lax.optimization_barrier((rim_a, rim_b, win0, adj))
-    rims = gather(jnp.concatenate([rim_a, rim_b], axis=0))
     msg = sds((cap + 16, width), BF)
     plain = sds((cap, width), BF)
     hid_bf, hid_f32 = sds((n, hidden), BF), sds((n, hidden), F32)
     agg0, pre0, hid0, first, one, two = call(
         k_first,
         [cell_bf, hid_f32, hid_bf, cell_bf, sds((2 * cap + 16, width), BF), msg],
-        [me], [xc, rims, adj, inv, win0, wo0, slot, tags, rsel], "first",
+        [me], [xc, *shared(rim_a, rim_b), adj, inv, win0, wo0, slot, tags, rsel], "first",
         flops=2 * n * width * (src_rows + 3 * width),
         scratch=[pltpu.VMEM((src_rows, width), BF)])
     one, two, win2, coarse_weight = lax.optimization_barrier((one, two, win2, coarse_weight))
@@ -645,13 +622,10 @@
     layer_rows = half + 2 * small
     pack = [sds((curve, layer_rows, piece), F32), sds((curve, layer_rows, piece), BF)]
     if packed:
-        new_t, keep1, send1 = call(
-            lambda *r: k_newt_pack(scale, *r), [sds((half, n), BF)] + pack, [me],
-            [new, pg1, lifted, agg1, ctc, hid1], "grads1")
+        keep1, send1 = call(
+            lambda *r: pack_grads(scale, *r), pack, [me], [pg1, lifted, agg1, ctc, hid1], "grads1")
         got1 = cross_swap(send1)
         one, two, three, keep1 = lax.optimization_barrier((one, two, three, keep1))
-    else:
-        new_t, = call(k_newt, [sds((half, n), BF)], [me], [new], "new")
     got = shared(one, two, three)
     lg, pgrad, spread, one, two = call(
         k_cgrad, [cell_bf, node_bf, node_bf, plain, plain], [me],
@@ -676,34 +650,31 @@
         keepc, pg0 = lax.optimization_barrier((keepc, pg0))
         rims = two_way(rims, 1)
 
-        def staged(body, extra, extra_outs, pairs, name):
+        def staged(pairs, name):
             total = sum(keep.shape[1] for keep in pairs[::2])
             own, *outs = call(
-                body, [sds((total, piece), F32)] + [sds((total, piece), BF)] * 3 + extra_outs,
-                [me], extra + pairs, name)
-            return [own] + [curve_swap(value, step) for step, value in zip((1, 2, 3), outs)], outs[3:]
-
-        early, (comb0,) = staged(
-            k_stage_comb, [fb, pg0, win0, scaled0, adjt], [sds((n, half), F32)],
-            [keep1, got1, keepc, gotc], "stage1")
-        late, _ = staged(k_stage, [], [], [keep0, got0], "stage0")
+                k_stage, [sds((total, piece), F32)] + [sds((total, piece), BF)] * 3, [me], pairs, name)
+            return [own] + [curve_swap(value, step) for step, value in zip((1, 2, 3), outs)]
+
+        early = staged([keep1, got1, keepc, gotc], "stage1")
+        late = staged([keep0, got0], "stage0")
     else:
         gco, = call(lambda *r: k_cweight(scale, *r), [sds((half, width), F32)], [me], [pgrad, coarse], "cweight")
         fb, pg0, scaled0, rims = call(
             k_third, back_outs, [me], [lg, hot, slott, spread, got, wo0, slope0, win0, inv, adjt], "third")
         rims = two_way(rims, 1)
-        comb0, = call(k_halfcomb, [sds((n, half), F32)], [me], [fb, pg0, win0, scaled0, adjt], "halfcomb")
-    rims = gather(rims)
+    last_args = [fb, pg0, win0, scaled0, adjt, gather(rims), place, new]
+    last_outs = [sds((half, n), F32), sds((half, n), BF)]
     if packed:
-        fgrad, ein, eout, gco = call(
-            k_last, [sds((half, n), F32), sds((half, piece), F32), sds((small, half), F32), sds((small, half), F32)],
-            [me], [comb0, rims, place] + early, "last")
+        ein, eout, gco, fgrad, new_t = call(
+            k_last, [sds((half, piece), F32), sds((small, half), F32), sds((small, half), F32)] + last_outs,
+            [me], last_args + early, "last")
         gin, gout = call(
             k_sum_late, [sds((2, half, piece), F32), sds((2, small, half), F32)], [], late + [ein, eout], "late")
         gout = gout.swapaxes(1, 2)
         gco = gco.T
     else:
-        fgrad, = call(k_last, [sds((half, n), F32)], [me], [comb0, rims, place], "last")
+        fgrad, new_t = call(k_last, last_outs, [me], last_args, "last")
         shapes = [sds((half, 2 * width), F32), sds((half, hidden), F32)]
         gi1, go1 = call(lambda *r: k_grads(scale, *r), shapes, [me], [pg1, lifted, agg1, ctc, hid1], "grads1")
         gi0, go0 = call(lambda *r: k_grads(scale, *r), shapes, [me], [pg0, xc, agg0, fb, hid0], "grads0")

time: 91 us -> 90.3 us (level)
  blocking collectives: 8.36 us -> 6.35 us
  starting transfers between devices: 41.7 us -> 43.5 us
    all_gather x4 -> x3, blocking collectives: 8.36 us -> 6.35 us  [gather(): return lax.all_gather(value, 'sub', axis=0, tiled=False)]
    ppermute x6, waiting for transfers between devices: 4.18 us -> 3.24 us  [curve_swap(): return lax.ppermute(value, 'curve', [(z, z ^ step) for z in range(4)])]
    ppermute x13, starting transfers between devices: 25.2 us -> 26.1 us  [two_way(): return lax.ppermute(value, LINE, pairs)]
    ppermute x12 -> x14, waiting for transfers between devices: 3.22 us -> 4.11 us  [swap(): return lax.ppermute(value, 'sub', [(0, 1), (1, 0)])]
    ppermute x12 -> x14, starting transfers between devices: 2.97 us -> 3.76 us  [swap(): return lax.ppermute(value, 'sub', [(0, 1), (1, 0)])]
  transfers between devices with their start and end apart: 34 -> 36, of which waited for: 6 -> 9; matrix products, arithmetic and copies ran while one was open for 0% -> 0% of each run, Pallas kernels for 20% -> 19%
where the time goes in v9:
time: 90.3 us; the launch traced here: 90.1 us
  starting transfers between devices  43.5 us (48%)
  Pallas kernels  25.3 us (28%)
  waiting for transfers between devices  12.3 us (14%)
  blocking collectives  6.35 us (7%)
  local copies, waits for them, and re-layouts  1.74 us (2%)
  between operations  0.91 us (1%)
    ppermute x13, starting transfers between devices, two_way(): return lax.ppermute(value, LINE, pairs)  26.1 us
    pallas_call x17, Pallas kernels, call(): pl.pallas_call(body, out_shape=tuple(outs), in_specs=[pl.BlockSpec(memory...  25.3 us
    ppermute x6, starting transfers between devices, curve_swap(): return lax.ppermute(value, 'curve', [(z, z ^ step) for z in range(4)])  11.1 us
    all_gather x3, blocking collectives, gather(): return lax.all_gather(value, 'sub', axis=0, tiled=False)  6.35 us
    ppermute x3, waiting for transfers between devices, cross_swap(): return lax.ppermute(value, 'cross', [(0, 1), (1, 0)])  4.48 us
    ppermute x14, waiting for transfers between devices, swap(): return lax.ppermute(value, 'sub', [(0, 1), (1, 0)])  4.11 us
    ppermute x14, starting transfers between devices, swap(): return lax.ppermute(value, 'sub', [(0, 1), (1, 0)])  3.76 us
    ppermute x6, waiting for transfers between devices, curve_swap(): return lax.ppermute(value, 'curve', [(z, z ^ step) for z in range(4)])  3.24 us
  transfers between devices with their start and end apart: 36, of which 9 were waited for; matrix products, arithmetic and copies ran while one was open for 0% of the time, Pallas kernels for 19%

profile of v9, /device:TPU:0, one launch (start us, length us, event | category | flops | bytes accessed | tf_op | source)
XLA Modules:
  0.0 90.1 jit_solution(503340203376902681)
XLA Ops:
  0.6 0.5 collective-permute-start.2
  1.3 0.7 copy-done.6
  2.0 0.9 %copy-done.2 = bf16[256,512]{1,0:T(8,128)(2,1)S(1)} copy-done((bf16[256,512]{1,0:T(8,128)(2,1)S(1)}, bf16[256,512]{1,0:T(8,128)(2,1)}, u32[]{:S(2)}) %copy-start.2) | copy-done | bytes 262168
  3.0 0.9 halo.1
  3.9 3.0 %collective-permute-start = (bf16[128,256]{1,0:T(8,128)(2,1)S(1)}, bf16[128,256]{1,0:T(8,128)(2,1)S(1)}, u32[]{:S(2)}, u32[]{:S(2)}) collective-permute-start(bf16[128,256]{1,0:T(8,128)(2,1)S(1)} %get-tuple-element.119), channel_id=1, source_target_pairs={{0,2},{2,4},{4,6},{6,8},{8,10},{10,12},{12,14},{3,1},{5,3},{7,5},{... | collective-permute-start | bytes 196616 | tf_op jit(solution)/shard_map/ppermute | solution.py:51
  6.8 2.3 %all-gather.x_ref = bf16[512,512]{1,0:T(8,128)(2,1)S(1)} all-gather(bf16[256,512]{1,0:T(8,128)(2,1)S(1)} %copy-done.2), channel_id=2, replica_groups=mesh['groups'=2,'curve'=4,'cross'=2,'sub'=2] {'sub'}, dimensions={0}, use_global_device_ids=true | all-gather | bytes 786432 | tf_op jit(solution)/shard_map/all_gather | solution.py:59
  9.2 1.6 %prep.1 = (bf16[512,512]{1,0:T(8,128)(2,1)S(1)}, bf16[512,768]{1,0:T(8,128)(2,1)S(1)}, bf16[768,512]{1,0:T(8,128)(2,1)S(1)}, f32[512,128]{1,0:T(8,128)S(1)}, bf1...) custom-call(s32[4,3]{1,0:T(4,128)S(1)} %copy-done.7, ...), custom_call_target="tpu_custom_call" | custom-call | bytes 4824064 | tf_op jit(solution)/shard_map/prep/pallas_call | solution.py:31
  10.8 0.6 weights0.1
  12.0 0.7 collective-permute-done.4.a2_ref
  12.9 2.4 %first.1 = (bf16[512,512]{1,0:T(8,128)(2,1)S(1)}, f32[512,512]{1,0:T(8,128)S(1)}, bf16[512,512]{1,0:T(8,128)(2,1)S(1)}, bf16[512,512]{1,0:T(8,128)(2,1)S(1)}, bf...) custom-call(s32[5]{0:T(128)S(1)} %stack.19.me_ref.r_0_, bf16[512,512]{1,0:T(8,128)(2,1)S(1)} %get-tuple-element.118.xc_ref.r_11_, ...), custom_call_target="tpu_custom_call" | custom-call | flops 1207959552 | bytes 6328320 | tf_op jit(solution)/shard_map/first/pallas_call | solution.py:31
  15.7 2.0 %collective-permute-start.6 = (bf16[80,512]{1,0:T(8,128)(2,1)S(1)}, bf16[80,512]{1,0:T(8,128)(2,1)S(1)}, u32[]{:S(2)}, u32[]{:S(2)}) collective-permute-start(bf16[80,512]{1,0:T(8,128)(2,1)S(1)} %get-tuple-element.137), channel_id=1, source_target_pairs={{0,2},{2,4},{4,6},{6,8},{8,10},{10,12},{12,14},{3,1},{5,3},{7,5},{... | collective-permute-start | bytes 245768 | tf_op jit(solution)/shard_map/ppermute | solution.py:51
  17.8 1.6 %collective-permute-start.7 = (bf16[48,512]{1,0:T(8,128)(2,1)S(1)}, bf16[48,512]{1,0:T(8,128)(2,1)S(1)}, u32[]{:S(2)}, u32[]{:S(2)}) collective-permute-start(bf16[48,512]{1,0:T(8,128)(2,1)S(1)} %get-tuple-element.138), channel_id=1, source_target_pairs={{0,4},{2,6},{4,8},{6,10},{8,12},{10,14},{5,1},{7,3},{9,5},{11,7},{... | collective-permute-start | bytes 147464 | tf_op jit(solution)/shard_map/ppermute | solution.py:51
  19.4 1.4 %own.1 = (f32[128,512]{1,0:T(8,128)S(1)}, f32[512,512]{1,0:T(8,128)S(1)}, bf16[512,512]{1,0:T(8,128)(2,1)S(1)}, bf16[128,512]{1,0:T(8,128)(2,1)S(1)}, bf16[128,128]{1,0:T(8,128)(2,1)S(1)}) custom-call(s32[5]{0:T(128)S(1)} %stack.19.me_ref.r_0_, bf16[128,512]{1,0:T(8,128)(2,1)S(1)} %get-tuple-element.139.hott_ref, ...), custom_call_target="tpu_custom_call" | custom-call | bytes 4620288 | tf_op jit(solution)/shard_map/own/pallas_call | solution.py:31
  21.6 0.9 %collective-permute-done.10.two2_ref = bf16[48,512]{1,0:T(8,128)(2,1)S(1)} collective-permute-done((bf16[48,512]{1,0:T(8,128)(2,1)S(1)}, bf16[48,512]{1,0:T(8,128)(2,1)S(1)}, u32[]{:S(2)}, u32[]{:S(2)}) %collective-permute-start.10) | collective-permute-done | bytes 49184 | tf_op jit(solution)/shard_map/ppermute | solution.py:55
  22.6 1.2 %coarse.1 = (f32[128,128]{1,0:T(8,128)S(1)}, f32[128,128]{1,0:T(8,128)S(1)}, bf16[128,512]{1,0:T(8,128)(2,1)S(1)}, f32[128,512]{1,0:T(8,128)S(1)}, bf16[128,512]...) custom-call(s32[5]{0:T(128)S(1)} %stack.19.me_ref.r_0_, ...), custom_call_target="tpu_custom_call" | custom-call | bytes 2359296 | tf_op jit(solution)/shard_map/coarse/pallas_call | solution.py:31
  24.1 2.3 %collective-permute-start.11 = (bf16[192,512]{1,0:T(8,128)(2,1)S(1)}, bf16[192,512]{1,0:T(8,128)(2,1)S(1)}, u32[]{:S(2)}, u32[]{:S(2)}) collective-permute-start(bf16[192,512]{1,0:T(8,128)(2,1)S(1)} %get-tuple-element.156), channel_id=1, source_target_pairs={{0,2},{2,4},{4,6},{6,8},{8,10},{10,12},{12,14},{3,1},{5,3},{7,5},{... | collective-permute-start | bytes 589832 | tf_op jit(solution)/shard_map/ppermute | solution.py:51
  26.4 2.3 %collective-permute-start.12 = (bf16[64,512]{1,0:T(8,128)(2,1)S(1)}, bf16[64,512]{1,0:T(8,128)(2,1)S(1)}, u32[]{:S(2)}, u32[]{:S(2)}) collective-permute-start(bf16[64,512]{1,0:T(8,128)(2,1)S(1)} %get-tuple-element.157), channel_id=1, source_target_pairs={{0,4},{2,6},{4,8},{6,10},{8,12},{10,14},{5,1},{7,3},{9,5},{11,7},{... | collective-permute-start | bytes 196616 | tf_op jit(solution)/shard_map/ppermute | solution.py:51
  28.8 2.3 %collective-permute-start.13 = (bf16[32,512]{1,0:T(8,128)(2,1)S(1)}, bf16[32,512]{1,0:T(8,128)(2,1)S(1)}, u32[]{:S(2)}, u32[]{:S(2)}) collective-permute-start(bf16[32,512]{1,0:T(8,128)(2,1)S(1)} %get-tuple-element.158), channel_id=1, source_target_pairs={{0,6},{2,8},{4,10},{6,12},{8,14},{7,1},{9,3},{11,5},{13,7},{15,9},... | collective-permute-start | bytes 98312 | tf_op jit(solution)/shard_map/ppermute | solution.py:51
  31.0 0.6 weights1.1
  31.7 1.1 %cot.1 = (bf16[512,512]{1,0:T(8,128)(2,1)S(1)}, f32[512,512]{1,0:T(8,128)S(1)}) custom-call(s32[5]{0:T(128)S(1)} %stack.19.me_ref.r_0_, bf16[256,512]{1,0:T(8,128)(2,1)S(1)} %copy-done.4, bf16[256,512]{1,0:T(8,128)(2,1)S(1)} %collective-permute-done.14.ct2_ref, bf16[512,512]{1,0:T(8,128)(2,1)S(1)} %get-tuple-element.162.wo_ref), custom_call_target="tpu_custom_call" | custom-call | bytes 2621440 | tf_op jit(solution)/shard_map/cot/pallas_call | solution.py:31
  33.5 1.1 %collective-permute-done.17.athree2_ref = bf16[32,512]{1,0:T(8,128)(2,1)S(1)} collective-permute-done((bf16[32,512]{1,0:T(8,128)(2,1)S(1)}, bf16[32,512]{1,0:T(8,128)(2,1)S(1)}, u32[]{:S(2)}, u32[]{:S(2)}) %collective-permute-start.17) | collective-permute-done | bytes 32800 | tf_op jit(solution)/shard_map/ppermute | solution.py:55
  34.7 3.9 %second.1 = (bf16[512,512]{1,0:T(8,128)(2,1)S(1)}, bf16[512,512]{1,0:T(8,128)(2,1)S(1)}, bf16[512,512]{1,0:T(8,128)(2,1)S(1)}, bf16[512,512]{1,0:T(8,128)(2,1)S(...) custom-call(s32[5]{0:T(128)S(1)} %stack.19.me_ref.r_0_, ...), custom_call_target="tpu_custom_call" | custom-call | bytes 10846208 | tf_op jit(solution)/shard_map/second/pallas_call | solution.py:31
  38.6 1.7 %collective-permute-start.18 = (bf16[192,512]{1,0:T(8,128)(2,1)S(1)}, bf16[192,512]{1,0:T(8,128)(2,1)S(1)}, u32[]{:S(2)}, u32[]{:S(2)}) collective-permute-start(bf16[192,512]{1,0:T(8,128)(2,1)S(1)} %get-tuple-element.176), channel_id=1, source_target_pairs={{0,2},{2,4},{4,6},{6,8},{8,10},{10,12},{12,14},{3,1},{5,3},{7,5},{... | collective-permute-start | bytes 589832 | tf_op jit(solution)/shard_map/ppermute | solution.py:51
  40.3 2.7 %collective-permute-start.19 = (bf16[64,512]{1,0:T(8,128)(2,1)S(1)}, bf16[64,512]{1,0:T(8,128)(2,1)S(1)}, u32[]{:S(2)}, u32[]{:S(2)}) collective-permute-start(bf16[64,512]{1,0:T(8,128)(2,1)S(1)} %get-tuple-element.177), channel_id=1, source_target_pairs={{0,4},{2,6},{4,8},{6,10},{8,12},{10,14},{5,1},{7,3},{9,5},{11,7},{... | collective-permute-start | bytes 196616 | tf_op jit(solution)/shard_map/ppermute | solution.py:51
  43.0 1.7 %collective-permute-start.20 = (bf16[32,512]{1,0:T(8,128)(2,1)S(1)}, bf16[32,512]{1,0:T(8,128)(2,1)S(1)}, u32[]{:S(2)}, u32[]{:S(2)}) collective-permute-start(bf16[32,512]{1,0:T(8,128)(2,1)S(1)} %get-tuple-element.178), channel_id=1, source_target_pairs={{0,6},{2,8},{4,10},{6,12},{8,14},{7,1},{9,3},{11,5},{13,7},{15,9},... | collective-permute-start | bytes 98312 | tf_op jit(solution)/shard_map/ppermute | solution.py:51
  44.7 1.6 %grads1.1 = (f32[4,384,128]{2,1,0:T(8,128)S(1)}, bf16[4,384,128]{2,1,0:T(8,128)(2,1)S(1)}) custom-call(s32[5]{0:T(128)S(1)} %stack.19.me_ref.r_0_, bf16[512,512]{1,0:T(8,128)(2,1)S(1)} %get-tuple-element.179.r_1_, bf16[512,512]{1,0:T(8,128)(2,1)S(1)} %get-tuple-element.180.r_2_, bf16[512,512]{1,0:T(8,128)(2,1)S(1)} %get-tuple-element.181.r_3_, ...), custom_call_target="tpu_custom_call" | custom-call | bytes 3801088 | tf_op jit(solution)/shard_map/grads1/pallas_call | solution.py:31
  46.3 0.5 collective-permute-start.26
  47.5 1.1 %collective-permute-done.23.three2_ref = bf16[32,512]{1,0:T(8,128)(2,1)S(1)} collective-permute-done((bf16[32,512]{1,0:T(8,128)(2,1)S(1)}, bf16[32,512]{1,0:T(8,128)(2,1)S(1)}, u32[]{:S(2)}, u32[]{:S(2)}) %collective-permute-start.23) | collective-permute-done | bytes 32800 | tf_op jit(solution)/shard_map/ppermute | solution.py:55
  48.6 1.6 %cgrad.1 = (bf16[512,512]{1,0:T(8,128)(2,1)S(1)}, bf16[128,512]{1,0:T(8,128)(2,1)S(1)}, bf16[128,512]{1,0:T(8,128)(2,1)S(1)}, bf16[32,512]{1,0:T(8,128)(2,1)S(1)}, bf16[32,512]{1,0:T(8,128)(2,1)S(1)}) custom-call(s32[5]{0:T(128)S(1)} %stack.19.me_ref.r_0_, f32[512,512]{1,0:T(8,128)S(1)} %get-tuple-element.173.comb_ref, ...), custom_call_target="tpu_custom_call" | custom-call | bytes 3932160 | tf_op jit(solution)/shard_map/cgrad/pallas_call | solution.py:31
  50.2 2.0 %collective-permute-start.24 = (bf16[32,512]{1,0:T(8,128)(2,1)S(1)}, bf16[32,512]{1,0:T(8,128)(2,1)S(1)}, u32[]{:S(2)}, u32[]{:S(2)}) collective-permute-start(bf16[32,512]{1,0:T(8,128)(2,1)S(1)} %get-tuple-element.192), channel_id=1, source_target_pairs={{0,2},{2,4},{4,6},{6,8},{8,10},{10,12},{12,14},{3,1},{5,3},{7,5},{... | collective-permute-start | bytes 98312 | tf_op jit(solution)/shard_map/ppermute | solution.py:51
  52.2 4.1 %collective-permute-start.25 = (bf16[32,512]{1,0:T(8,128)(2,1)S(1)}, bf16[32,512]{1,0:T(8,128)(2,1)S(1)}, u32[]{:S(2)}, u32[]{:S(2)}) collective-permute-start(bf16[32,512]{1,0:T(8,128)(2,1)S(1)} %get-tuple-element.193), channel_id=1, source_target_pairs={{0,4},{2,6},{4,8},{6,10},{8,12},{10,14},{5,1},{7,3},{9,5},{11,7},{... | collective-permute-start | bytes 98312 | tf_op jit(solution)/shard_map/ppermute | solution.py:51
  56.2 1.0 %cweight.1 = (f32[4,128,128]{2,1,0:T(8,128)S(1)}, bf16[4,128,128]{2,1,0:T(8,128)(2,1)S(1)}) custom-call(s32[5]{0:T(128)S(1)} %stack.19.me_ref.r_0_, bf16[128,512]{1,0:T(8,128)(2,1)S(1)} %get-tuple-element.200.r_1_, bf16[128,512]{1,0:T(8,128)(2,1)S(1)} %get-tuple-element.201.r_2_), custom_call_target="tpu_custom_call" | custom-call | bytes 655360 | tf_op jit(solution)/shard_map/cweight/pallas_call | solution.py:31
  57.8 2.1 %all-gather.1 = bf16[128,512]{1,0:T(8,128)(2,1)S(1)} all-gather(bf16[64,512]{1,0:T(8,128)(2,1)S(1)} %pad_maximum_fusion), channel_id=3, replica_groups=mesh['groups'=2,'curve'=4,'cross'=2,'sub'=2] {'sub'}, dimensions={0}, use_global_device_ids=true | all-gather | bytes 196608 | tf_op jit(solution)/shard_map/all_gather | solution.py:59
  59.9 3.1 %third.1 = (bf16[512,512]{1,0:T(8,128)(2,1)S(1)}, bf16[512,512]{1,0:T(8,128)(2,1)S(1)}, bf16[512,512]{1,0:T(8,128)(2,1)S(1)}, bf16[128,512]{1,0:T(8,128)(2,1)S(1...) custom-call(s32[5]{0:T(128)S(1)} %stack.19.me_ref.r_0_, bf16[512,512]{1,0:T(8,128)(2,1)S(1)} %get-tuple-element.190.r_1_, ...), custom_call_target="tpu_custom_call" | custom-call | bytes 9175040 | tf_op jit(solution)/shard_map/third/pallas_call | solution.py:31
  63.0 1.6 %collective-permute-start.32 = (bf16[4,384,128]{2,1,0:T(8,128)(2,1)S(1)}, bf16[4,384,128]{2,1,0:T(8,128)(2,1)S(1)}, u32[]{:S(2)}, u32[]{:S(2)}) collective-permute-start(bf16[4,384,128]{2,1,0:T(8,128)(2,1)S(1)} %get-tuple-element.221), channel_id=1, source_target_pairs={{0,2},{2,0},{1,3},{3,1},{4,6},{6,4},{5,7},{7,5},{8,10},{10,8},{9,1... | collective-permute-start | bytes 1179656 | tf_op jit(solution)/shard_map/ppermute | solution.py:72
  65.1 0.6 stage1.1
  65.8 2.4 %collective-permute-start.29 = (bf16[512,128]{1,0:T(8,128)(2,1)S(1)}, bf16[512,128]{1,0:T(8,128)(2,1)S(1)}, u32[]{:S(2)}, u32[]{:S(2)}) collective-permute-start(bf16[512,128]{1,0:T(8,128)(2,1)S(1)} %get-tuple-element.215), channel_id=1, source_target_pairs={{0,4},{4,0},{8,12},{12,8},{1,5},{5,1},{9,13},{13,9},{2,6},{6,2},{1... | collective-permute-start | bytes 393224 | tf_op jit(solution)/shard_map/ppermute | solution.py:76
  68.2 0.9 %collective-permute-start.30 = (bf16[512,128]{1,0:T(8,128)(2,1)S(1)}, bf16[512,128]{1,0:T(8,128)(2,1)S(1)}, u32[]{:S(2)}, u32[]{:S(2)}) collective-permute-start(bf16[512,128]{1,0:T(8,128)(2,1)S(1)} %get-tuple-element.216), channel_id=1, source_target_pairs={{0,8},{4,12},{8,0},{12,4},{1,9},{5,13},{9,1},{13,5},{2,10},{6,14},... | collective-permute-start | bytes 393224 | tf_op jit(solution)/shard_map/ppermute | solution.py:76
  69.1 1.5 %collective-permute-start.31 = (bf16[512,128]{1,0:T(8,128)(2,1)S(1)}, bf16[512,128]{1,0:T(8,128)(2,1)S(1)}, u32[]{:S(2)}, u32[]{:S(2)}) collective-permute-start(bf16[512,128]{1,0:T(8,128)(2,1)S(1)} %get-tuple-element.217), channel_id=1, source_target_pairs={{0,12},{4,8},{8,4},{12,0},{1,13},{5,9},{9,5},{13,1},{2,14},{6,10},... | collective-permute-start | bytes 393224 | tf_op jit(solution)/shard_map/ppermute | solution.py:76
  70.6 4.5 %collective-permute-done.32.refs_1_ = bf16[4,384,128]{2,1,0:T(8,128)(2,1)S(1)} collective-permute-done((bf16[4,384,128]{2,1,0:T(8,128)(2,1)S(1)}, bf16[4,384,128]{2,1,0:T(8,128)(2,1)S(1)}, u32[]{:S(2)}, u32[]{:S(2)}) %collective-permute-start.32) | collective-permute-done | bytes 393248 | tf_op jit(solution)/shard_map/ppermute | solution.py:72
  75.1 0.6 stage0.1
  75.7 3.8 %collective-permute-start.33 = (bf16[384,128]{1,0:T(8,128)(2,1)S(1)}, bf16[384,128]{1,0:T(8,128)(2,1)S(1)}, u32[]{:S(2)}, u32[]{:S(2)}) collective-permute-start(bf16[384,128]{1,0:T(8,128)(2,1)S(1)} %get-tuple-element.223), channel_id=1, source_target_pairs={{0,4},{4,0},{8,12},{12,8},{1,5},{5,1},{9,13},{13,9},{2,6},{6,2},{1... | collective-permute-start | bytes 294920 | tf_op jit(solution)/shard_map/ppermute | solution.py:76
  79.5 0.9 %collective-permute-start.34 = (bf16[384,128]{1,0:T(8,128)(2,1)S(1)}, bf16[384,128]{1,0:T(8,128)(2,1)S(1)}, u32[]{:S(2)}, u32[]{:S(2)}) collective-permute-start(bf16[384,128]{1,0:T(8,128)(2,1)S(1)} %get-tuple-element.224), channel_id=1, source_target_pairs={{0,8},{4,12},{8,0},{12,4},{1,9},{5,13},{9,1},{13,5},{2,10},{6,14},... | collective-permute-start | bytes 294920 | tf_op jit(solution)/shard_map/ppermute | solution.py:76
  80.4 1.5 %collective-permute-start.35 = (bf16[384,128]{1,0:T(8,128)(2,1)S(1)}, bf16[384,128]{1,0:T(8,128)(2,1)S(1)}, u32[]{:S(2)}, u32[]{:S(2)}) collective-permute-start(bf16[384,128]{1,0:T(8,128)(2,1)S(1)} %get-tuple-element.225), channel_id=1, source_target_pairs={{0,12},{4,8},{8,4},{12,0},{1,13},{5,9},{9,5},{13,1},{2,14},{6,10},... | collective-permute-start | bytes 294920 | tf_op jit(solution)/shard_map/ppermute | solution.py:76
  81.9 2.0 %all-gather.2 = bf16[256,512]{1,0:T(8,128)(2,1)S(1)} all-gather(bf16[128,512]{1,0:T(8,128)(2,1)S(1)} %collective-permute-done.27), channel_id=4, replica_groups=mesh['groups'=2,'curve'=4,'cross'=2,'sub'=2] {'sub'}, dimensions={0}, use_global_device_ids=true | all-gather | bytes 393216 | tf_op jit(solution)/shard_map/all_gather | solution.py:59
  83.9 2.1 %last.1 = (f32[256,128]{1,0:T(8,128)S(1)}, f32[64,256]{1,0:T(8,128)S(1)}, f32[64,256]{1,0:T(8,128)}, f32[256,512]{1,0:T(8,128)}, bf16[256,512]{1,0:T(8,128)(2,1)}) custom-call(s32[5]{0:T(128)S(1)} %stack.19.me_ref.r_0_, bf16[512,512]{1,0:T(8,128)(2,1)S(1)} %get-tuple-element.199.fb_ref, bf16[512,512]{1,0:T(8,128)(2,1)S(1)} %get-tuple-element.204.pg_ref, ...), custom_call_target="tpu_custom_call" | custom-call | bytes 6160384 | tf_op jit(solution)/shard_map/last/pallas_call | solution.py:31
  86.0 3.2 %collective-permute-done.34.b_ref = bf16[384,128]{1,0:T(8,128)(2,1)S(1)} collective-permute-done((bf16[384,128]{1,0:T(8,128)(2,1)S(1)}, bf16[384,128]{1,0:T(8,128)(2,1)S(1)}, u32[]{:S(2)}, u32[]{:S(2)}) %collective-permute-start.34) | collective-permute-done | bytes 98336 | tf_op jit(solution)/shard_map/ppermute | solution.py:76
  89.3 0.8 late.1
  (64 shorter events, 4.9 us)
Async XLA Ops:
  0.6 10.1 %collective-permute-start.2 = (bf16[2,256,1024]{2,1,0:T(8,128)(2,1)}, bf16[2,256,1024]{2,1,0:T(8,128)(2,1)S(1)}, u32[]{:S(2)}, u32[]{:S(2)}) collective-permute-start(bf16[2,256,1024]{2,1,0:T(8,128)(2,1)} %r_1_.3), channel_id=1, source_target_pairs={{0,1},{1,0},{2,3},{3,2},{4,5},{5,4},{6,7},{7,6},{8,9},{9,8},{10,11... | collective-permute-start | bytes 3145736 | tf_op jit(solution)/shard_map/ppermute | solution.py:55
  1.1 9.6 %collective-permute-start.3 = (bf16[2,256,512]{2,1,0:T(8,128)(2,1)}, bf16[2,256,512]{2,1,0:T(8,128)(2,1)S(1)}, u32[]{:S(2)}, u32[]{:S(2)}) collective-permute-start(bf16[2,256,512]{2,1,0:T(8,128)(2,1)} %r_2_.3), channel_id=1, source_target_pairs={{0,1},{1,0},{2,3},{3,2},{4,5},{5,4},{6,7},{7,6},{8,9},{9,8},{10,11... | collective-permute-start | bytes 1572872 | tf_op jit(solution)/shard_map/ppermute | solution.py:55
  1.3 0.7 copy-start.6
  2.0 0.9 %copy-start.2 = (bf16[256,512]{1,0:T(8,128)(2,1)S(1)}, bf16[256,512]{1,0:T(8,128)(2,1)}, u32[]{:S(2)}) copy-start(bf16[256,512]{1,0:T(8,128)(2,1)} %x_ref.1) | copy-start | bytes 786436
  2.9 6.2 %copy-start.3 = (s32[4,3,128,128]{3,2,1,0:T(8,128)S(1)}, s32[4,3,128,128]{3,2,1,0:T(8,128)}, u32[]{:S(2)}) copy-start(s32[4,3,128,128]{3,2,1,0:T(8,128)} %mask_ref.1) | copy-start | bytes 2359300
  2.9 6.2 %copy-start.7 = (s32[4,3]{1,0:T(4,128)S(1)}, s32[4,3]{1,0:T(4,128)}, u32[]{:S(2)}) copy-start(s32[4,3]{1,0:T(4,128)} %tile_ref.1) | copy-start | bytes 148
  2.9 6.2 %copy-start.8 = (s32[512]{0:T(512)S(1)}, s32[512]{0:T(512)}, u32[]{:S(2)}) copy-start(s32[512]{0:T(512)} %param.16) | copy-start | bytes 6148
  3.9 7.6 %collective-permute-start = (bf16[128,256]{1,0:T(8,128)(2,1)S(1)}, bf16[128,256]{1,0:T(8,128)(2,1)S(1)}, u32[]{:S(2)}, u32[]{:S(2)}) collective-permute-start(bf16[128,256]{1,0:T(8,128)(2,1)S(1)} %get-tuple-element.119), channel_id=1, source_target_pairs={{0,2},{2,4},{4,6},{6,8},{8,10},{10,12},{12,14},{3,1},{5,3},{7,5},{... | collective-permute-start | bytes 196616 | tf_op jit(solution)/shard_map/ppermute | solution.py:51
  6.8 3.9 %copy-start = (bf16[2,256,1024]{2,1,0:T(8,128)(2,1)S(1)}, bf16[2,256,1024]{2,1,0:T(8,128)(2,1)}, u32[]{:S(2)}) copy-start(bf16[2,256,1024]{2,1,0:T(8,128)(2,1)} %r_1_.3) | copy-start | bytes 3145732
  6.8 4.6 %collective-permute-start.1 = (bf16[128,256]{1,0:T(8,128)(2,1)S(1)}, bf16[128,256]{1,0:T(8,128)(2,1)S(1)}, u32[]{:S(2)}, u32[]{:S(2)}) collective-permute-start(bf16[128,256]{1,0:T(8,128)(2,1)S(1)} %get-tuple-element.120), channel_id=1, source_target_pairs={{1,3},{3,5},{5,7},{7,9},{9,11},{11,13},{13,15},{2,0},{4,2},{6,4},{... | collective-permute-start | bytes 196616 | tf_op jit(solution)/shard_map/ppermute | solution.py:51
  9.1 1.6 %copy-start.1 = (bf16[2,256,512]{2,1,0:T(8,128)(2,1)S(1)}, bf16[2,256,512]{2,1,0:T(8,128)(2,1)}, u32[]{:S(2)}) copy-start(bf16[2,256,512]{2,1,0:T(8,128)(2,1)} %r_2_.3) | copy-start | bytes 1572868
  11.4 1.3 %collective-permute-start.4 = (bf16[128,256]{1,0:T(8,128)(2,1)S(1)}, bf16[128,256]{1,0:T(8,128)(2,1)S(1)}, u32[]{:S(2)}, u32[]{:S(2)}) collective-permute-start(bf16[128,256]{1,0:T(8,128)(2,1)S(1)} %collective-permute-done.a_ref), channel_id=1, source_target_pairs={{0,1},{1,0},{2,3},{3,2},{4,5},{5,4},{6,7},{7,6},{8,9},{9,8},{10,11... | collective-permute-start | bytes 196616 | tf_op jit(solution)/shard_map/ppermute | solution.py:55
  11.6 1.3 %collective-permute-start.5 = (bf16[128,256]{1,0:T(8,128)(2,1)S(1)}, bf16[128,256]{1,0:T(8,128)(2,1)S(1)}, u32[]{:S(2)}, u32[]{:S(2)}) collective-permute-start(bf16[128,256]{1,0:T(8,128)(2,1)S(1)} %collective-permute-done.1.b_ref), channel_id=1, source_target_pairs={{0,1},{1,0},{2,3},{3,2},{4,5},{5,4},{6,7},{7,6},{8,9},{9,8},{10,11... | collective-permute-start | bytes 196616 | tf_op jit(solution)/shard_map/ppermute | solution.py:55
  12.9 2.4 %copy-start.5 = (bf16[256,512]{1,0:T(8,128)(2,1)S(1)}, bf16[256,512]{1,0:T(8,128)(2,1)}, u32[]{:S(2)}) copy-start(bf16[256,512]{1,0:T(8,128)(2,1)} %cw_ref) | copy-start | bytes 786436
  15.3 4.0 %collective-permute-start.8 = (bf16[256,512]{1,0:T(8,128)(2,1)S(1)}, bf16[256,512]{1,0:T(8,128)(2,1)S(1)}, u32[]{:S(2)}, u32[]{:S(2)}) collective-permute-start(bf16[256,512]{1,0:T(8,128)(2,1)S(1)} %copy-done.5), channel_id=1, source_target_pairs={{0,1},{1,0},{2,3},{3,2},{4,5},{5,4},{6,7},{7,6},{8,9},{9,8},{10,11... | collective-permute-start | bytes 786440 | tf_op jit(solution)/shard_map/ppermute | solution.py:55
  15.7 5.4 %collective-permute-start.6 = (bf16[80,512]{1,0:T(8,128)(2,1)S(1)}, bf16[80,512]{1,0:T(8,128)(2,1)S(1)}, u32[]{:S(2)}, u32[]{:S(2)}) collective-permute-start(bf16[80,512]{1,0:T(8,128)(2,1)S(1)} %get-tuple-element.137), channel_id=1, source_target_pairs={{0,2},{2,4},{4,6},{6,8},{8,10},{10,12},{12,14},{3,1},{5,3},{7,5},{... | collective-permute-start | bytes 245768 | tf_op jit(solution)/shard_map/ppermute | solution.py:51
  17.8 3.3 %collective-permute-start.7 = (bf16[48,512]{1,0:T(8,128)(2,1)S(1)}, bf16[48,512]{1,0:T(8,128)(2,1)S(1)}, u32[]{:S(2)}, u32[]{:S(2)}) collective-permute-start(bf16[48,512]{1,0:T(8,128)(2,1)S(1)} %get-tuple-element.138), channel_id=1, source_target_pairs={{0,4},{2,6},{4,8},{6,10},{8,12},{10,14},{5,1},{7,3},{9,5},{11,7},{... | collective-permute-start | bytes 147464 | tf_op jit(solution)/shard_map/ppermute | solution.py:51
  21.1 1.4 %collective-permute-start.9 = (bf16[80,512]{1,0:T(8,128)(2,1)S(1)}, bf16[80,512]{1,0:T(8,128)(2,1)S(1)}, u32[]{:S(2)}, u32[]{:S(2)}) collective-permute-start(bf16[80,512]{1,0:T(8,128)(2,1)S(1)} %collective-permute-done.6.one_ref), channel_id=1, source_target_pairs={{0,1},{1,0},{2,3},{3,2},{4,5},{5,4},{6,7},{7,6},{8,9},{9,8},{10,11... | collective-permute-start | bytes 245768 | tf_op jit(solution)/shard_map/ppermute | solution.py:55
  21.3 1.2 %collective-permute-start.10 = (bf16[48,512]{1,0:T(8,128)(2,1)S(1)}, bf16[48,512]{1,0:T(8,128)(2,1)S(1)}, u32[]{:S(2)}, u32[]{:S(2)}) collective-permute-start(bf16[48,512]{1,0:T(8,128)(2,1)S(1)} %collective-permute-done.7.two_ref), channel_id=1, source_target_pairs={{0,1},{1,0},{2,3},{3,2},{4,5},{5,4},{6,7},{7,6},{8,9},{9,8},{10,11... | collective-permute-start | bytes 147464 | tf_op jit(solution)/shard_map/ppermute | solution.py:55
  22.6 1.2 %copy-start.4 = (bf16[256,512]{1,0:T(8,128)(2,1)S(1)}, bf16[256,512]{1,0:T(8,128)(2,1)}, u32[]{:S(2)}) copy-start(bf16[256,512]{1,0:T(8,128)(2,1)} %ct_ref) | copy-start | bytes 786436
  23.8 7.9 %collective-permute-start.14 = (bf16[256,512]{1,0:T(8,128)(2,1)S(1)}, bf16[256,512]{1,0:T(8,128)(2,1)S(1)}, u32[]{:S(2)}, u32[]{:S(2)}) collective-permute-start(bf16[256,512]{1,0:T(8,128)(2,1)S(1)} %copy-done.4), channel_id=1, source_target_pairs={{0,1},{1,0},{2,3},{3,2},{4,5},{5,4},{6,7},{7,6},{8,9},{9,8},{10,11... | collective-permute-start | bytes 786440 | tf_op jit(solution)/shard_map/ppermute | solution.py:55
  24.1 8.7 %collective-permute-start.11 = (bf16[192,512]{1,0:T(8,128)(2,1)S(1)}, bf16[192,512]{1,0:T(8,128)(2,1)S(1)}, u32[]{:S(2)}, u32[]{:S(2)}) collective-permute-start(bf16[192,512]{1,0:T(8,128)(2,1)S(1)} %get-tuple-element.156), channel_id=1, source_target_pairs={{0,2},{2,4},{4,6},{6,8},{8,10},{10,12},{12,14},{3,1},{5,3},{7,5},{... | collective-permute-start | bytes 589832 | tf_op jit(solution)/shard_map/ppermute | solution.py:51
  26.4 6.4 %collective-permute-start.12 = (bf16[64,512]{1,0:T(8,128)(2,1)S(1)}, bf16[64,512]{1,0:T(8,128)(2,1)S(1)}, u32[]{:S(2)}, u32[]{:S(2)}) collective-permute-start(bf16[64,512]{1,0:T(8,128)(2,1)S(1)} %get-tuple-element.157), channel_id=1, source_target_pairs={{0,4},{2,6},{4,8},{6,10},{8,12},{10,14},{5,1},{7,3},{9,5},{11,7},{... | collective-permute-start | bytes 196616 | tf_op jit(solution)/shard_map/ppermute | solution.py:51
  28.8 4.1 %collective-permute-start.13 = (bf16[32,512]{1,0:T(8,128)(2,1)S(1)}, bf16[32,512]{1,0:T(8,128)(2,1)S(1)}, u32[]{:S(2)}, u32[]{:S(2)}) collective-permute-start(bf16[32,512]{1,0:T(8,128)(2,1)S(1)} %get-tuple-element.158), channel_id=1, source_target_pairs={{0,6},{2,8},{4,10},{6,12},{8,14},{7,1},{9,3},{11,5},{13,7},{15,9},... | collective-permute-start | bytes 98312 | tf_op jit(solution)/shard_map/ppermute | solution.py:51
  32.9 1.8 %collective-permute-start.15 = (bf16[192,512]{1,0:T(8,128)(2,1)S(1)}, bf16[192,512]{1,0:T(8,128)(2,1)S(1)}, u32[]{:S(2)}, u32[]{:S(2)}) collective-permute-start(bf16[192,512]{1,0:T(8,128)(2,1)S(1)} %collective-permute-done.11.aone_ref), channel_id=1, source_target_pairs={{0,1},{1,0},{2,3},{3,2},{4,5},{5,4},{6,7},{7,6},{8,9},{9,8},{10,11... | collective-permute-start | bytes 589832 | tf_op jit(solution)/shard_map/ppermute | solution.py:55
  33.0 1.7 %collective-permute-start.16 = (bf16[64,512]{1,0:T(8,128)(2,1)S(1)}, bf16[64,512]{1,0:T(8,128)(2,1)S(1)}, u32[]{:S(2)}, u32[]{:S(2)}) collective-permute-start(bf16[64,512]{1,0:T(8,128)(2,1)S(1)} %collective-permute-done.12.atwo_ref), channel_id=1, source_target_pairs={{0,1},{1,0},{2,3},{3,2},{4,5},{5,4},{6,7},{7,6},{8,9},{9,8},{10,11... | collective-permute-start | bytes 196616 | tf_op jit(solution)/shard_map/ppermute | solution.py:55
  33.5 1.2 %collective-permute-start.17 = (bf16[32,512]{1,0:T(8,128)(2,1)S(1)}, bf16[32,512]{1,0:T(8,128)(2,1)S(1)}, u32[]{:S(2)}, u32[]{:S(2)}) collective-permute-start(bf16[32,512]{1,0:T(8,128)(2,1)S(1)} %collective-permute-done.13.athree_ref), channel_id=1, source_target_pairs={{0,1},{1,0},{2,3},{3,2},{4,5},{5,4},{6,7},{7,6},{8,9},{9,8},{10,11... | collective-permute-start | bytes 98312 | tf_op jit(solution)/shard_map/ppermute | solution.py:55
  38.6 8.2 %collective-permute-start.18 = (bf16[192,512]{1,0:T(8,128)(2,1)S(1)}, bf16[192,512]{1,0:T(8,128)(2,1)S(1)}, u32[]{:S(2)}, u32[]{:S(2)}) collective-permute-start(bf16[192,512]{1,0:T(8,128)(2,1)S(1)} %get-tuple-element.176), channel_id=1, source_target_pairs={{0,2},{2,4},{4,6},{6,8},{8,10},{10,12},{12,14},{3,1},{5,3},{7,5},{... | collective-permute-start | bytes 589832 | tf_op jit(solution)/shard_map/ppermute | solution.py:51
  40.3 6.5 %collective-permute-start.19 = (bf16[64,512]{1,0:T(8,128)(2,1)S(1)}, bf16[64,512]{1,0:T(8,128)(2,1)S(1)}, u32[]{:S(2)}, u32[]{:S(2)}) collective-permute-start(bf16[64,512]{1,0:T(8,128)(2,1)S(1)} %get-tuple-element.177), channel_id=1, source_target_pairs={{0,4},{2,6},{4,8},{6,10},{8,12},{10,14},{5,1},{7,3},{9,5},{11,7},{... | collective-permute-start | bytes 196616 | tf_op jit(solution)/shard_map/ppermute | solution.py:51
  43.0 3.8 %collective-permute-start.20 = (bf16[32,512]{1,0:T(8,128)(2,1)S(1)}, bf16[32,512]{1,0:T(8,128)(2,1)S(1)}, u32[]{:S(2)}, u32[]{:S(2)}) collective-permute-start(bf16[32,512]{1,0:T(8,128)(2,1)S(1)} %get-tuple-element.178), channel_id=1, source_target_pairs={{0,6},{2,8},{4,10},{6,12},{8,14},{7,1},{9,3},{11,5},{13,7},{15,9},... | collective-permute-start | bytes 98312 | tf_op jit(solution)/shard_map/ppermute | solution.py:51
  46.3 13.6 %collective-permute-start.26 = (bf16[4,384,128]{2,1,0:T(8,128)(2,1)S(1)}, bf16[4,384,128]{2,1,0:T(8,128)(2,1)S(1)}, u32[]{:S(2)}, u32[]{:S(2)}) collective-permute-start(bf16[4,384,128]{2,1,0:T(8,128)(2,1)S(1)} %get-tuple-element.194), channel_id=1, source_target_pairs={{0,2},{2,0},{1,3},{3,1},{4,6},{6,4},{5,7},{7,5},{8,10},{10,8},{9,1... | collective-permute-start | bytes 1179656 | tf_op jit(solution)/shard_map/ppermute | solution.py:72
  46.8 1.8 %collective-permute-start.21 = (bf16[192,512]{1,0:T(8,128)(2,1)S(1)}, bf16[192,512]{1,0:T(8,128)(2,1)S(1)}, u32[]{:S(2)}, u32[]{:S(2)}) collective-permute-start(bf16[192,512]{1,0:T(8,128)(2,1)S(1)} %collective-permute-done.18.one_ref), channel_id=1, source_target_pairs={{0,1},{1,0},{2,3},{3,2},{4,5},{5,4},{6,7},{7,6},{8,9},{9,8},{10,11... | collective-permute-start | bytes 589832 | tf_op jit(solution)/shard_map/ppermute | solution.py:55
  46.9 1.7 %collective-permute-start.22 = (bf16[64,512]{1,0:T(8,128)(2,1)S(1)}, bf16[64,512]{1,0:T(8,128)(2,1)S(1)}, u32[]{:S(2)}, u32[]{:S(2)}) collective-permute-start(bf16[64,512]{1,0:T(8,128)(2,1)S(1)} %collective-permute-done.19.two_ref), channel_id=1, source_target_pairs={{0,1},{1,0},{2,3},{3,2},{4,5},{5,4},{6,7},{7,6},{8,9},{9,8},{10,11... | collective-permute-start | bytes 196616 | tf_op jit(solution)/shard_map/ppermute | solution.py:55
  47.4 1.2 %collective-permute-start.23 = (bf16[32,512]{1,0:T(8,128)(2,1)S(1)}, bf16[32,512]{1,0:T(8,128)(2,1)S(1)}, u32[]{:S(2)}, u32[]{:S(2)}) collective-permute-start(bf16[32,512]{1,0:T(8,128)(2,1)S(1)} %collective-permute-done.20.three_ref), channel_id=1, source_target_pairs={{0,1},{1,0},{2,3},{3,2},{4,5},{5,4},{6,7},{7,6},{8,9},{9,8},{10,11... | collective-permute-start | bytes 98312 | tf_op jit(solution)/shard_map/ppermute | solution.py:55
  50.2 7.5 %collective-permute-start.24 = (bf16[32,512]{1,0:T(8,128)(2,1)S(1)}, bf16[32,512]{1,0:T(8,128)(2,1)S(1)}, u32[]{:S(2)}, u32[]{:S(2)}) collective-permute-start(bf16[32,512]{1,0:T(8,128)(2,1)S(1)} %get-tuple-element.192), channel_id=1, source_target_pairs={{0,2},{2,4},{4,6},{6,8},{8,10},{10,12},{12,14},{3,1},{5,3},{7,5},{... | collective-permute-start | bytes 98312 | tf_op jit(solution)/shard_map/ppermute | solution.py:51
  52.2 5.7 %collective-permute-start.25 = (bf16[32,512]{1,0:T(8,128)(2,1)S(1)}, bf16[32,512]{1,0:T(8,128)(2,1)S(1)}, u32[]{:S(2)}, u32[]{:S(2)}) collective-permute-start(bf16[32,512]{1,0:T(8,128)(2,1)S(1)} %get-tuple-element.193), channel_id=1, source_target_pairs={{0,4},{2,6},{4,8},{6,10},{8,12},{10,14},{5,1},{7,3},{9,5},{11,7},{... | collective-permute-start | bytes 98312 | tf_op jit(solution)/shard_map/ppermute | solution.py:51
  57.2 5.8 %collective-permute-start.28 = (bf16[4,128,128]{2,1,0:T(8,128)(2,1)S(1)}, bf16[4,128,128]{2,1,0:T(8,128)(2,1)S(1)}, u32[]{:S(2)}, u32[]{:S(2)}) collective-permute-start(bf16[4,128,128]{2,1,0:T(8,128)(2,1)S(1)} %get-tuple-element.212), channel_id=1, source_target_pairs={{0,2},{2,0},{1,3},{3,1},{4,6},{6,4},{5,7},{7,5},{8,10},{10,8},{9,1... | collective-permute-start | bytes 393224 | tf_op jit(solution)/shard_map/ppermute | solution.py:72
  63.0 12.0 %collective-permute-start.32 = (bf16[4,384,128]{2,1,0:T(8,128)(2,1)S(1)}, bf16[4,384,128]{2,1,0:T(8,128)(2,1)S(1)}, u32[]{:S(2)}, u32[]{:S(2)}) collective-permute-start(bf16[4,384,128]{2,1,0:T(8,128)(2,1)S(1)} %get-tuple-element.221), channel_id=1, source_target_pairs={{0,2},{2,0},{1,3},{3,1},{4,6},{6,4},{5,7},{7,5},{8,10},{10,8},{9,1... | collective-permute-start | bytes 1179656 | tf_op jit(solution)/shard_map/ppermute | solution.py:72
  64.7 14.8 %collective-permute-start.27 = (bf16[128,512]{1,0:T(8,128)(2,1)S(1)}, bf16[128,512]{1,0:T(8,128)(2,1)S(1)}, u32[]{:S(2)}, u32[]{:S(2)}) collective-permute-start(bf16[128,512]{1,0:T(8,128)(2,1)S(1)} %get-tuple-element.206), channel_id=1, source_target_pairs={{0,2},{2,4},{4,6},{6,8},{8,10},{10,12},{12,14},{3,1},{5,3},{7,5},{... | collective-permute-start | bytes 393224 | tf_op jit(solution)/shard_map/ppermute | solution.py:51
  65.8 14.7 %collective-permute-start.29 = (bf16[512,128]{1,0:T(8,128)(2,1)S(1)}, bf16[512,128]{1,0:T(8,128)(2,1)S(1)}, u32[]{:S(2)}, u32[]{:S(2)}) collective-permute-start(bf16[512,128]{1,0:T(8,128)(2,1)S(1)} %get-tuple-element.215), channel_id=1, source_target_pairs={{0,4},{4,0},{8,12},{12,8},{1,5},{5,1},{9,13},{13,9},{2,6},{6,2},{1... | collective-permute-start | bytes 393224 | tf_op jit(solution)/shard_map/ppermute | solution.py:76
  68.2 15.8 %collective-permute-start.30 = (bf16[512,128]{1,0:T(8,128)(2,1)S(1)}, bf16[512,128]{1,0:T(8,128)(2,1)S(1)}, u32[]{:S(2)}, u32[]{:S(2)}) collective-permute-start(bf16[512,128]{1,0:T(8,128)(2,1)S(1)} %get-tuple-element.216), channel_id=1, source_target_pairs={{0,8},{4,12},{8,0},{12,4},{1,9},{5,13},{9,1},{13,5},{2,10},{6,14},... | collective-permute-start | bytes 393224 | tf_op jit(solution)/shard_map/ppermute | solution.py:76
  69.1 14.8 %collective-permute-start.31 = (bf16[512,128]{1,0:T(8,128)(2,1)S(1)}, bf16[512,128]{1,0:T(8,128)(2,1)S(1)}, u32[]{:S(2)}, u32[]{:S(2)}) collective-permute-start(bf16[512,128]{1,0:T(8,128)(2,1)S(1)} %get-tuple-element.217), channel_id=1, source_target_pairs={{0,12},{4,8},{8,4},{12,0},{1,13},{5,9},{9,5},{13,1},{2,14},{6,10},... | collective-permute-start | bytes 393224 | tf_op jit(solution)/shard_map/ppermute | solution.py:76
  75.7 10.4 %collective-permute-start.33 = (bf16[384,128]{1,0:T(8,128)(2,1)S(1)}, bf16[384,128]{1,0:T(8,128)(2,1)S(1)}, u32[]{:S(2)}, u32[]{:S(2)}) collective-permute-start(bf16[384,128]{1,0:T(8,128)(2,1)S(1)} %get-tuple-element.223), channel_id=1, source_target_pairs={{0,4},{4,0},{8,12},{12,8},{1,5},{5,1},{9,13},{13,9},{2,6},{6,2},{1... | collective-permute-start | bytes 294920 | tf_op jit(solution)/shard_map/ppermute | solution.py:76
  79.5 9.8 %collective-permute-start.34 = (bf16[384,128]{1,0:T(8,128)(2,1)S(1)}, bf16[384,128]{1,0:T(8,128)(2,1)S(1)}, u32[]{:S(2)}, u32[]{:S(2)}) collective-permute-start(bf16[384,128]{1,0:T(8,128)(2,1)S(1)} %get-tuple-element.224), channel_id=1, source_target_pairs={{0,8},{4,12},{8,0},{12,4},{1,9},{5,13},{9,1},{13,5},{2,10},{6,14},... | collective-permute-start | bytes 294920 | tf_op jit(solution)/shard_map/ppermute | solution.py:76
  80.4 8.8 %collective-permute-start.35 = (bf16[384,128]{1,0:T(8,128)(2,1)S(1)}, bf16[384,128]{1,0:T(8,128)(2,1)S(1)}, u32[]{:S(2)}, u32[]{:S(2)}) collective-permute-start(bf16[384,128]{1,0:T(8,128)(2,1)S(1)} %get-tuple-element.225), channel_id=1, source_target_pairs={{0,12},{4,8},{8,4},{12,0},{1,13},{5,9},{9,5},{13,1},{2,14},{6,10},... | collective-permute-start | bytes 294920 | tf_op jit(solution)/shard_map/ppermute | solution.py:76
